TPU v7x, 32 devices: a whole 2x2x4 slice. The times are simulated.
32 devices in a mesh: groups: 2 (over x), bl: 16 (over z, y, core).
Axes of the slice: x: 2, y: 2, z: 4, core: 2. Of those that a mesh axis runs over, the one named last changes fastest.
Arguments:
- visibilities: bfloat16 [4096, 8, 384], P(('groups', 'bl')), parts along dimension 0, may hold values from -6 to 6
- row_owner: int32 [4096, 1], P(('groups', 'bl')), parts along dimension 0, may hold values from 0 to 15; in each aligned block of 128 rows (0 to 127, 128 to 255, ...) at most 16 rows name the same one
- row_slot: int32 [4096], P(('groups', 'bl')), parts along dimension 0, may hold values from 0 to 63
- baseline_station_pairs: int32 [1024, 2], P('bl'), may hold values from 0 to 511
- gains_coarse: float32 [1024, 8, 6], P(('groups', 'bl')), parts along dimension 0, may hold values from -3 to 3
- band_weights: float32 [768, 3], P('groups'), parts along dimension 0, may hold values from 0.2 to 1
- band_offset: int32 [768], P('groups'), parts along dimension 0, may hold values from 0 to 3
Outputs:
- averaged: bfloat16 [2048, 8, 384], P(('groups', 'bl')), parts along dimension 0
There are 2 independent parts, one for each index of `groups`. A program takes and returns all parts, laid end to end along the dimension named above; an argument that names none is the same for every part. Nothing has to cross between parts.
Inputs may be any that keep to these rules, and one draw needn't show every extreme that they name: `row_owner`: among the rows of one device no owner is named by more than 16 rows, a bound that some block reaches.
All inputs are finite; a program needn't handle non-finite values.
Results may differ from a plain program's by a relative error of at most 0.0062.
Values may be sent and summed in bfloat16 or wider, within the bound.
No kernel may reach another device: no remote copies, remote signals or barrier semaphores. Data moves between devices by JAX's collectives and lax.ppermute only.
A program may use at most 64 MiB of HBM per device.

v0:
```python
import functools

import jax
import jax.numpy as jnp
from jax import lax
from jax.experimental import pallas as pl
from jax.experimental.pallas import tpu as pltpu
from jax.sharding import PartitionSpec as P

LANES = 128
SUB = 8
USED = 48
ALL_VMEM = 60 * 1024 * 1024
SOME_VMEM = 24 * 1024 * 1024


def round_up(value, unit):
    return -(-value // unit) * unit


def schedule(near):
    even, odd = list(range(near, 2 * near, 2)), list(range(near + 1, 2 * near, 2))
    close = list(range(near // 2, near)) + list(range(1, near // 2))
    cross, late = even[2:] + odd[1:-2], odd[-2:]
    order = [0] + even[:2] + close[:3]
    close = close[3:]
    while cross:
        order += cross[:1] + close[:1]
        cross, close = cross[1:], close[1:]
    return order + close + odd[:1], late


def with_gains(near):
    return list(range(near)) + list(range(near, 2 * near, 2))


def start_all(pairs, sems):
    moves = [pltpu.make_async_copy(src, dst, sems.at[i]) for i, (src, dst) in enumerate(pairs)]
    for move in moves:
        move.start()
    return moves


def pack_kernel(
    capacity,
    near,
    me_s,
    owner_hbm,
    owner_row_hbm,
    slot_row_hbm,
    vis_hbm,
    coarse_hbm,
    weights_hbm,
    offset_hbm,
    pairs_hbm,
    *rest,
):
    outs = rest[:-14]
    (
        weights_ref,
        offset_ref,
        pairs_ref,
        small_ref,
        owner_s,
        count_s,
        owner_ref,
        slot_ref,
        vis_ref,
        coarse_ref,
        turn_ref,
        meta_ref,
        block_ref,
        sems,
    ) = rest[-14:]
    rows = vis_ref.shape[0]
    chunks = vis_ref.shape[2] // LANES
    devices = block_ref.shape[0]
    terms, stations = coarse_ref.shape
    half = stations // 2
    depth = meta_ref.shape[0]
    gain_tiles = (depth - 1) // 2
    moves = start_all(
        (
            (vis_hbm, vis_ref),
            (coarse_hbm, coarse_ref),
            (owner_hbm, owner_s),
            (owner_row_hbm, owner_ref),
            (slot_row_hbm, slot_ref),
            (weights_hbm, weights_ref),
            (offset_hbm, offset_ref),
            (pairs_hbm, pairs_ref),
        ),
        sems,
    )
    turn_ref[...] = jnp.zeros_like(turn_ref)
    for d in range(devices):
        count_s[d] = 0
    me = me_s[0]
    for move in moves[1:]:
        move.wait()

    turn_ref[0:terms, 0:half] = coarse_ref[:, 0:half]
    turn_ref[64 : 64 + terms, 0:half] = coarse_ref[:, half:stations]
    gains = turn_ref[...].T
    high = gains.astype(jnp.bfloat16)
    low = (gains - high.astype(jnp.float32)).astype(jnp.bfloat16)
    for i in range(gain_tiles):
        meta_ref[i] = high[i * SUB : (i + 1) * SUB, :]
        meta_ref[gain_tiles + i] = low[i * SUB : (i + 1) * SUB, :]
    sub = lax.broadcasted_iota(jnp.int32, (SUB, LANES), 0)
    codes = jnp.where(sub == 0, owner_ref[...], slot_ref[...])
    meta_ref[2 * gain_tiles] = codes.astype(jnp.float32).astype(jnp.bfloat16)
    steps = weights_ref.shape[0]
    small_ref[...] = jnp.zeros_like(small_ref)
    small_ref[0:steps, :] = weights_ref[...]
    for c in range(chunks):
        lanes = slice(c * LANES, (c + 1) * LANES)
        small_ref[steps : steps + 1, lanes] = offset_ref[c : c + 1, :].astype(jnp.float32)
    small_ref[4:6, 0 : pairs_ref.shape[1]] = pairs_ref[...].astype(jnp.float32)

    at = chunks * capacity
    if near > 1:
        pairs = [(meta_ref, outs[x].at[pl.ds(at, depth)]) for x in with_gains(near)]
    else:
        pairs = [(meta_ref, outs[1])]
    pairs += [(small_ref, outs[-1])]
    sends = start_all(pairs, sems.at[pl.ds(8, len(pairs))])
    moves[0].wait()

    def place(r, carry):
        x = owner_s[r] ^ me
        k = count_s[x]
        count_s[x] = k + 1
        for c in range(chunks):
            block_ref[x, chunks * k + c] = vis_ref[r, :, c * LANES : (c + 1) * LANES]
        return carry

    lax.fori_loop(0, rows, place, 0, unroll=8)
    start = 8 + len(pairs)
    if near > 1:
        pairs = [(block_ref.at[x], outs[x].at[pl.ds(0, at)]) for x in range(devices)]
    else:
        pairs = [(block_ref, outs[0])]
    sends += start_all(pairs, sems.at[pl.ds(start, len(pairs))])
    for send in sends:
        send.wait()


def interpolation(small):
    channels = small.shape[1]
    index = lax.broadcasted_iota(jnp.int32, (LANES, channels), 0)
    knot = ((index & 63) >> 3).astype(jnp.float32)
    basis = jnp.zeros((LANES, channels), jnp.float32)
    for step in range(3):
        basis = basis + jnp.where(knot == small[3:4, :] + float(step), small[step : step + 1, :], 0.0)
    high = basis.astype(jnp.bfloat16).astype(jnp.float32)
    part = index & 7
    return [
        (
            jnp.where(part == j, high, 0.0).astype(jnp.bfloat16),
            jnp.where(part == j, basis - high, 0.0).astype(jnp.bfloat16),
        )
        for j in range(8)
    ]


def collect_kernel(at, depth, *rest):
    blocks, (out_ref, sems) = rest[:-2], rest[-2:]
    moves = start_all(
        [
            (block.at[pl.ds(at, depth)], out_ref.at[pl.ds(i * depth, depth)])
            for i, block in enumerate(blocks)
        ],
        sems,
    )
    for move in moves:
        move.wait()


def list_rows(owner, slot, target, capacity):
    senders = owner.shape[0]
    mine = owner == target
    counted = mine.astype(jnp.float32)
    before = lax.broadcasted_iota(jnp.int32, (LANES, LANES), 0) < lax.broadcasted_iota(
        jnp.int32, (LANES, LANES), 1
    )
    rank = jnp.dot(
        counted.astype(jnp.bfloat16),
        before.astype(jnp.float32).astype(jnp.bfloat16),
        preferred_element_type=jnp.float32,
    )
    lane = lax.broadcasted_iota(jnp.int32, (senders, LANES), 1)
    count = jnp.sum(counted, axis=1, keepdims=True)
    listing = jnp.where(lane == capacity, count, 0.0)
    for k in range(capacity):
        here = jnp.logical_and(mine, rank == float(k))
        kth = jnp.sum(jnp.where(here, slot, 0.0), axis=1, keepdims=True)
        listing = jnp.where(lane == k, kth, listing)
    return listing.astype(jnp.int32), mine


def add_rows(acc_ref, slots_s, line, capacity, rows_ref):
    chunks = acc_ref.shape[0]

    def add(k, carry):
        b = slots_s[line, k]
        for c in range(chunks):
            acc_ref[c, b] += rows_ref[chunks * k + c].astype(jnp.float32)
        return carry

    lax.fori_loop(0, slots_s[line, capacity], add, 0)


def add_table(table_ref, x, block, at, depth):
    gain_tiles = (depth - 1) // 2
    for i in range(gain_tiles):
        table_ref[x, i * SUB : (i + 1) * SUB, :] = block[at + i].astype(jnp.float32) + block[
            at + gain_tiles + i
        ].astype(jnp.float32)
    return block[at + 2 * gain_tiles].astype(jnp.float32)


def count_rows(hits, mine, slot):
    which = lax.broadcasted_iota(jnp.int32, hits.shape, 0).astype(jnp.float32)
    slot = jnp.where(mine, slot, -1.0)
    for x in range(slot.shape[0]):
        hits = hits + (slot[x : x + 1, :] == which).astype(jnp.float32)
    return hits


def middle_kernel(capacity, near, stations, order, turn_s, me_s, small_ref, *rest):
    arrived, passed = dict(zip(order, rest)), rest[len(order) : -13]
    gains_ref, recip_ref, slots_ref, sums_ref = rest[-13:-9]
    table_ref, pick_ref, owner_ref, slot_ref, slots_v, slots_s, pairs_v, pairs_s, sems = rest[-9:]
    devices = table_ref.shape[0]
    owned = recip_ref.shape[0]
    chunks = sums_ref.shape[0]
    half = stations // 2
    depth = 2 * (table_ref.shape[1] // SUB) + 1
    small = small_ref[...]
    pairs_v[...] = small[0:SUB, 0:LANES].astype(jnp.int32)
    scalars = [pltpu.make_async_copy(pairs_v, pairs_s, sems.at[0])]
    scalars[0].start()
    for x in range(devices):
        if near == 1:
            code = add_table(table_ref, x, arrived[0].at[x], 0, depth)
        elif x in with_gains(near):
            code = add_table(table_ref, x, arrived[x], chunks * capacity, depth)
        else:
            code = add_table(table_ref, x, passed[0], (x - near) // 2 * depth, depth)
        owner_ref[x : x + 1, :] = code[0:1, :]
        slot_ref[x : x + 1, :] = code[1:2, :]
    slot = slot_ref[...]
    listing, mine = list_rows(owner_ref[...], slot, me_s[0].astype(jnp.float32), capacity)
    slots_ref[...] = listing
    slots_v[...] = listing
    scalars.append(pltpu.make_async_copy(slots_v, slots_s, sems.at[1]))
    scalars[1].start()
    hits = count_rows(jnp.zeros((owned, LANES), jnp.float32), mine, slot)
    tally = jnp.sum(hits, axis=1, keepdims=True)
    recip_ref[...] = jnp.broadcast_to(1.0 / jnp.maximum(tally, 1.0), recip_ref.shape)

    scalars[0].wait()
    turn = turn_s[0]
    column = lax.broadcasted_iota(jnp.int32, (1, LANES), 1)
    used = (column & 63) < USED
    upper = column >> 6

    def pick(b, carry):
        for side in range(2):
            s = pairs_s[4 + side, b]
            d = s // stations
            within = s - d * stations
            second = jnp.where(within >= half, 1, 0)
            row = table_ref[d ^ turn, pl.ds(within - second * half, 1), :]
            keep = jnp.logical_and(used, upper == second)
            pick_ref[pl.ds(side * owned + b, 1), :] = jnp.where(keep, row, 0.0)
        return carry

    lax.fori_loop(0, owned, pick, 0, unroll=8)
    both = pick_ref[...]
    both_high = both.astype(jnp.bfloat16)
    both_low = (both - both_high.astype(jnp.float32)).astype(jnp.bfloat16)
    both_two = jnp.concatenate([both_high, both_low], axis=1)
    for j, (high, low) in enumerate(interpolation(small)):
        fine = jnp.dot(
            both_two, jnp.concatenate([high, high], axis=0), preferred_element_type=jnp.float32
        ) + jnp.dot(both_high, low, preferred_element_type=jnp.float32)
        gains_ref[j] = fine.astype(jnp.bfloat16).astype(jnp.float32)

    sums_ref[...] = jnp.zeros_like(sums_ref)
    scalars[1].wait()
    if near > 1:
        for x in order:
            add_rows(sums_ref, slots_s, x, capacity, arrived[x])


def finish_kernel(capacity, late, slots_s, gains_ref, recip_ref, sums_ref, *rest):
    far = rest[: len(late)]
    out_hbm, acc_ref, res_ref, out_ref, sems = rest[len(late) :]
    owned, parts, channels = out_hbm.shape
    chunks = channels // LANES
    acc_ref[...] = sums_ref[...]
    if len(late) > 1:
        for x, rows_ref in zip(late, far):
            add_rows(acc_ref, slots_s, x, capacity, rows_ref)
    else:

        def from_device(d, carry):
            add_rows(acc_ref, slots_s, d, capacity, far[0].at[d])
            return carry

        lax.fori_loop(0, far[0].shape[0], from_device, 0)

    flat = acc_ref.reshape(chunks * owned * parts, LANES)
    done = res_ref.reshape(chunks * owned * parts, LANES)
    sends = []
    for c in range(chunks):
        cols = slice(c * LANES, (c + 1) * LANES)
        for b0 in range(0, owned, SUB):
            scale = recip_ref[b0 : b0 + SUB, :]
            row = (c * owned + b0) * parts
            vis = [flat[pl.ds(row + j, SUB, stride=parts), :] for j in range(parts)]
            lhs = [gains_ref[j, b0 : b0 + SUB, cols] for j in range(parts)]
            rhs = [gains_ref[j, owned + b0 : owned + b0 + SUB, cols] for j in range(parts)]
            mid_re, mid_im = [], []
            for row_a in range(2):
                for col_b in range(2):
                    re = im = 0.0
                    for inner in range(2):
                        lr, li = lhs[2 * row_a + inner], lhs[4 + 2 * row_a + inner]
                        vr, vi = vis[2 * inner + col_b], vis[4 + 2 * inner + col_b]
                        re = re + lr * vr - li * vi
                        im = im + lr * vi + li * vr
                    mid_re.append(re * scale)
                    mid_im.append(im * scale)
            for row_a in range(2):
                for col_b in range(2):
                    re = im = 0.0
                    for inner in range(2):
                        mr, mi = mid_re[2 * row_a + inner], mid_im[2 * row_a + inner]
                        rr, ri = rhs[2 * col_b + inner], rhs[4 + 2 * col_b + inner]
                        re = re + mr * rr + mi * ri
                        im = im + mi * rr - mr * ri
                    j = 2 * row_a + col_b
                    done[pl.ds(row + j, SUB, stride=parts), :] = re
                    done[pl.ds(row + 4 + j, SUB, stride=parts), :] = im
        out_ref[c] = res_ref[c].astype(out_ref.dtype)
        sends.append(
            pltpu.make_async_copy(
                out_ref.at[c], out_hbm.at[:, :, pl.ds(c * LANES, LANES)], sems.at[c]
            )
        )
        sends[-1].start()
    for send in sends:
        send.wait()


def on_device(
    visibilities,
    row_owner,
    row_slot,
    baseline_station_pairs,
    gains_coarse,
    band_weights,
    band_offset,
):
    devices = lax.axis_size("bl")
    rows, parts, channels = visibilities.shape
    capacity = 2 * rows // devices
    owned = baseline_station_pairs.shape[0]
    stations, _, knots = gains_coarse.shape
    chunks = channels // LANES
    gain_tiles = round_up(stations // 2, SUB) // SUB
    depth = 2 * gain_tiles + 1
    near = devices // 2 if devices <= 16 else 1
    halves = near > 1
    f32, bf16, i32 = jnp.float32, jnp.bfloat16, jnp.int32
    vmem = pl.BlockSpec(memory_space=pltpu.VMEM)
    smem = pl.BlockSpec(memory_space=pltpu.SMEM)
    hbm = pl.BlockSpec(memory_space=pltpu.HBM)
    anywhere = pl.BlockSpec(memory_space=pl.ANY)
    most = pltpu.CompilerParams(vmem_limit_bytes=ALL_VMEM)
    some = pltpu.CompilerParams(vmem_limit_bytes=SOME_VMEM)
    shape = jax.ShapeDtypeStruct
    dma = pltpu.SemaphoreType.DMA

    me = lax.axis_index("bl").astype(i32).reshape(1)
    turn = me if halves else jnp.zeros_like(me)
    owner = row_owner.reshape(rows)
    coarse = gains_coarse.transpose(2, 1, 0).reshape(knots * parts, stations)
    block = (chunks * capacity, parts, LANES)
    rows_at = chunks * capacity
    if halves:
        long = with_gains(near) + [near + 3]
        outs = [
            shape((rows_at + (depth if x in long else 0), parts, LANES), bf16)
            for x in range(devices)
        ]
    else:
        outs = [shape((devices,) + block, bf16), shape((depth, SUB, LANES), bf16)]
    outs += [shape((SUB, channels), f32)]
    pairs = baseline_station_pairs.T
    weights = band_weights.T
    offset = band_offset.reshape(chunks, LANES)
    sent = pl.pallas_call(
        functools.partial(pack_kernel, capacity, near),
        out_shape=outs,
        in_specs=[smem] + [hbm] * 8,
        out_specs=[hbm] * len(outs),
        scratch_shapes=[
            pltpu.VMEM(weights.shape, f32),
            pltpu.VMEM(offset.shape, i32),
            pltpu.VMEM(pairs.shape, i32),
            pltpu.VMEM((SUB, channels), f32),
            pltpu.SMEM((rows,), i32),
            pltpu.SMEM((devices,), i32),
            pltpu.VMEM((1, rows), i32),
            pltpu.VMEM((1, rows), i32),
            pltpu.VMEM((rows, parts, channels), bf16),
            pltpu.VMEM((knots * parts, stations), f32),
            pltpu.VMEM((LANES, LANES), f32),
            pltpu.VMEM((depth, SUB, LANES), bf16),
            pltpu.VMEM((devices,) + block, bf16),
            dma((9 + 2 * devices,)),
        ],
        compiler_params=most,
        name="pack_rows",
    )(
        turn,
        owner,
        row_owner.reshape(1, rows),
        row_slot.reshape(1, rows),
        visibilities,
        coarse,
        weights,
        offset,
        pairs,
    )


    def swap(array, x):
        return lax.ppermute(array, "bl", [(d, d ^ x) for d in range(devices)])

    if halves:
        arrived = {x: swap(sent[x], x) if x else sent[x] for x in range(devices)}
        order, late = schedule(near)
        even = list(range(near, devices, 2))
        collected = pl.pallas_call(
            functools.partial(collect_kernel, rows_at, depth),
            out_shape=shape((len(even) * depth, parts, LANES), bf16),
            in_specs=[anywhere] * len(even),
            out_specs=vmem,
            scratch_shapes=[dma((len(even),))],
            compiler_params=some,
            name="collect_gains",
        )(*[arrived[x] for x in even])
        passed = [swap(collected, 1)]
    else:
        arrived = {
            0: lax.all_gather(sent[1], "bl", axis=0),
            1: lax.all_to_all(sent[0], "bl", split_axis=0, concat_axis=0, tiled=True),
        }
        order, late, passed = [0], [1], []

    gains, recip, slots, sums = pl.pallas_call(
        functools.partial(middle_kernel, capacity, near, stations, order),
        out_shape=(
            shape((parts, 2 * owned, channels), f32),
            shape((owned, LANES), f32),
            shape((devices, LANES), i32),
            shape((chunks, owned, parts, LANES), f32),
        ),
        in_specs=[smem] * 2 + [vmem] * (1 + len(order) + len(passed)),
        out_specs=(vmem,) * 4,
        scratch_shapes=[
            pltpu.VMEM((devices, gain_tiles * SUB, LANES), f32),
            pltpu.VMEM((2 * owned, LANES), f32),
            pltpu.VMEM((devices, LANES), f32),
            pltpu.VMEM((devices, LANES), f32),
            pltpu.VMEM((devices, LANES), i32),
            pltpu.SMEM((devices, LANES), i32),
            pltpu.VMEM((SUB, LANES), i32),
            pltpu.SMEM((SUB, LANES), i32),
            dma((2,)),
        ],
        compiler_params=some,
        name="gains_and_sums",
    )(turn, me, sent[-1], *[arrived[x] for x in order], *passed)
    return pl.pallas_call(
        functools.partial(finish_kernel, capacity, late),
        out_shape=shape((owned, parts, channels), bf16),
        in_specs=[smem] + [vmem] * (3 + len(late)),
        out_specs=hbm,
        scratch_shapes=[
            pltpu.VMEM((chunks, owned, parts, LANES), f32),
            pltpu.VMEM((chunks, owned, parts, LANES), f32),
            pltpu.VMEM((chunks, owned, parts, LANES), bf16),
            dma((chunks,)),
        ],
        compiler_params=some,
        name="sum_and_apply",
    )(slots, gains, recip, sums, *[arrived[x] for x in late])


def solution(mesh):
    placed = (
        P(("groups", "bl"), None, None),
        P(("groups", "bl"), None),
        P(("groups", "bl")),
        P("bl", None),
        P(("groups", "bl"), None, None),
        P("groups", None),
        P("groups"),
    )
    return jax.shard_map(
        on_device,
        mesh=mesh,
        in_specs=placed,
        out_specs=P(("groups", "bl"), None, None),
        check_vma=False,
    )
```

profile of v0, /device:TPU:1, one launch (start us, length us, event | category | flops | bytes accessed | tf_op | source)
XLA Modules:
  0.0 50.5 jit_solution(1047098540033138650)
XLA Ops:
  0.0 3.3 %pack_rows.1 = (bf16[53,8,128]{2,1,0:T(8,128)(2,1)}, bf16[53,8,128]{2,1,0:T(8,128)(2,1)}, bf16[53,8,128]{2,1,0:T(8,128)(2,1)}, bf16[53,8,128]{2,1,0:T(8,128)(2,1...) custom-call(s32[1]{0:T(128)} %bitcast.me_s.turn_s, ...), custom_call_target="tpu_custom_call" | custom-call | tf_op jit(solution)/shard_map/pack_rows/pallas_call | solution.py:406
  3.3 3.8 %collective-permute-start.12 = (bf16[48,8,128]{2,1,0:T(8,128)(2,1)}, bf16[48,8,128]{2,1,0:T(8,128)(2,1)S(1)}, u32[]{:S(2)}, u32[]{:S(2)}) collective-permute-start(bf16[48,8,128]{2,1,0:T(8,128)(2,1)} %get-tuple-element.40), channel_id=1, source_target_pairs={{0,9},{1,8},{2,11},{3,10},{4,13},{5,12},{6,15},{7,14},{8,1},{9,0},... | collective-permute-start | bytes 294920 | tf_op jit(solution)/shard_map/ppermute | solution.py:443
  7.0 3.4 %collective-permute-start.1 = (bf16[53,8,128]{2,1,0:T(8,128)(2,1)}, bf16[53,8,128]{2,1,0:T(8,128)(2,1)S(1)}, u32[]{:S(2)}, u32[]{:S(2)}) collective-permute-start(bf16[53,8,128]{2,1,0:T(8,128)(2,1)} %get-tuple-element.29), channel_id=1, source_target_pairs={{0,10},{1,11},{2,8},{3,9},{4,14},{5,15},{6,12},{7,13},{8,2},{9,3},... | collective-permute-start | bytes 325640 | tf_op jit(solution)/shard_map/ppermute | solution.py:443
  10.4 1.3 %collective-permute-start.2 = (bf16[53,8,128]{2,1,0:T(8,128)(2,1)}, bf16[53,8,128]{2,1,0:T(8,128)(2,1)S(1)}, u32[]{:S(2)}, u32[]{:S(2)}) collective-permute-start(bf16[53,8,128]{2,1,0:T(8,128)(2,1)} %get-tuple-element.30), channel_id=1, source_target_pairs={{0,4},{1,5},{2,6},{3,7},{4,0},{5,1},{6,2},{7,3},{8,12},{9,13},{10,... | collective-permute-start | bytes 325640 | tf_op jit(solution)/shard_map/ppermute | solution.py:443
  11.7 0.7 %collective-permute-start.3 = (bf16[53,8,128]{2,1,0:T(8,128)(2,1)}, bf16[53,8,128]{2,1,0:T(8,128)(2,1)S(1)}, u32[]{:S(2)}, u32[]{:S(2)}) collective-permute-start(bf16[53,8,128]{2,1,0:T(8,128)(2,1)} %get-tuple-element.31), channel_id=1, source_target_pairs={{0,5},{1,4},{2,7},{3,6},{4,1},{5,0},{6,3},{7,2},{8,13},{9,12},{10,... | collective-permute-start | bytes 325640 | tf_op jit(solution)/shard_map/ppermute | solution.py:443
  12.4 4.5 %collective-permute-done.12.rest_13_ = bf16[48,8,128]{2,1,0:T(8,128)(2,1)S(1)} collective-permute-done((bf16[48,8,128]{2,1,0:T(8,128)(2,1)}, bf16[48,8,128]{2,1,0:T(8,128)(2,1)S(1)}, u32[]{:S(2)}, u32[]{:S(2)}) %collective-permute-start.12) | collective-permute-done | bytes 98336 | tf_op jit(solution)/shard_map/ppermute | solution.py:443
  16.9 1.9 %collective-permute-start.4 = (bf16[53,8,128]{2,1,0:T(8,128)(2,1)}, bf16[53,8,128]{2,1,0:T(8,128)(2,1)S(1)}, u32[]{:S(2)}, u32[]{:S(2)}) collective-permute-start(bf16[53,8,128]{2,1,0:T(8,128)(2,1)} %get-tuple-element.32), channel_id=1, source_target_pairs={{0,6},{1,7},{2,4},{3,5},{4,2},{5,3},{6,0},{7,1},{8,14},{9,15},{10,... | collective-permute-start | bytes 325640 | tf_op jit(solution)/shard_map/ppermute | solution.py:443
  18.9 4.1 %collective-permute-start.5 = (bf16[53,8,128]{2,1,0:T(8,128)(2,1)}, bf16[53,8,128]{2,1,0:T(8,128)(2,1)S(1)}, u32[]{:S(2)}, u32[]{:S(2)}) collective-permute-start(bf16[53,8,128]{2,1,0:T(8,128)(2,1)} %get-tuple-element.33), channel_id=1, source_target_pairs={{0,12},{1,13},{2,14},{3,15},{4,8},{5,9},{6,10},{7,11},{8,4},{9,5},... | collective-permute-start | bytes 325640 | tf_op jit(solution)/shard_map/ppermute | solution.py:443
  23.0 0.8 %collective-permute-start.6 = (bf16[53,8,128]{2,1,0:T(8,128)(2,1)}, bf16[53,8,128]{2,1,0:T(8,128)(2,1)S(1)}, u32[]{:S(2)}, u32[]{:S(2)}) collective-permute-start(bf16[53,8,128]{2,1,0:T(8,128)(2,1)} %get-tuple-element.34), channel_id=1, source_target_pairs={{0,7},{1,6},{2,5},{3,4},{4,3},{5,2},{6,1},{7,0},{8,15},{9,14},{10,... | collective-permute-start | bytes 325640 | tf_op jit(solution)/shard_map/ppermute | solution.py:443
  23.8 2.4 %collective-permute-start.7 = (bf16[53,8,128]{2,1,0:T(8,128)(2,1)}, bf16[53,8,128]{2,1,0:T(8,128)(2,1)S(1)}, u32[]{:S(2)}, u32[]{:S(2)}) collective-permute-start(bf16[53,8,128]{2,1,0:T(8,128)(2,1)} %get-tuple-element.35), channel_id=1, source_target_pairs={{0,14},{1,15},{2,12},{3,13},{4,10},{5,11},{6,8},{7,9},{8,6},{9,7},... | collective-permute-start | bytes 325640 | tf_op jit(solution)/shard_map/ppermute | solution.py:443
  26.2 0.7 %collective-permute-start.8 = (bf16[53,8,128]{2,1,0:T(8,128)(2,1)}, bf16[53,8,128]{2,1,0:T(8,128)(2,1)S(1)}, u32[]{:S(2)}, u32[]{:S(2)}) collective-permute-start(bf16[53,8,128]{2,1,0:T(8,128)(2,1)} %get-tuple-element.36), channel_id=1, source_target_pairs={{0,1},{1,0},{2,3},{3,2},{4,5},{5,4},{6,7},{7,6},{8,9},{9,8},{10,11... | collective-permute-start | bytes 325640 | tf_op jit(solution)/shard_map/ppermute | solution.py:443
  27.0 0.8 %collective-permute-done.4.rest_5_ = bf16[53,8,128]{2,1,0:T(8,128)(2,1)S(1)} collective-permute-done((bf16[53,8,128]{2,1,0:T(8,128)(2,1)}, bf16[53,8,128]{2,1,0:T(8,128)(2,1)S(1)}, u32[]{:S(2)}, u32[]{:S(2)}) %collective-permute-start.4) | collective-permute-done | bytes 108576 | tf_op jit(solution)/shard_map/ppermute | solution.py:443
  27.7 0.7 %collective-permute-start.9 = (bf16[53,8,128]{2,1,0:T(8,128)(2,1)}, bf16[53,8,128]{2,1,0:T(8,128)(2,1)S(1)}, u32[]{:S(2)}, u32[]{:S(2)}) collective-permute-start(bf16[53,8,128]{2,1,0:T(8,128)(2,1)} %get-tuple-element.37), channel_id=1, source_target_pairs={{0,11},{1,10},{2,9},{3,8},{4,15},{5,14},{6,13},{7,12},{8,3},{9,2},... | collective-permute-start | bytes 325640 | tf_op jit(solution)/shard_map/ppermute | solution.py:443
  28.4 0.3 collective-permute-start.10
  28.8 3.8 %collective-permute-done.6.rest_7_ = bf16[53,8,128]{2,1,0:T(8,128)(2,1)S(1)} collective-permute-done((bf16[53,8,128]{2,1,0:T(8,128)(2,1)}, bf16[53,8,128]{2,1,0:T(8,128)(2,1)S(1)}, u32[]{:S(2)}, u32[]{:S(2)}) %collective-permute-start.6) | collective-permute-done | bytes 108576 | tf_op jit(solution)/shard_map/ppermute | solution.py:443
  32.6 4.2 %collective-permute-start.14 = (bf16[48,8,128]{2,1,0:T(8,128)(2,1)}, bf16[48,8,128]{2,1,0:T(8,128)(2,1)S(1)}, u32[]{:S(2)}, u32[]{:S(2)}) collective-permute-start(bf16[48,8,128]{2,1,0:T(8,128)(2,1)} %get-tuple-element.45), channel_id=1, source_target_pairs={{0,13},{1,12},{2,15},{3,14},{4,9},{5,8},{6,11},{7,10},{8,5},{9,4},... | collective-permute-start | bytes 294920 | tf_op jit(solution)/shard_map/ppermute | solution.py:443
  36.8 0.1 collective-permute-start.15
  36.9 0.1 collect_gains.1
  37.0 3.7 %collective-permute-done.9.rest_10_ = bf16[53,8,128]{2,1,0:T(8,128)(2,1)S(1)} collective-permute-done((bf16[53,8,128]{2,1,0:T(8,128)(2,1)}, bf16[53,8,128]{2,1,0:T(8,128)(2,1)S(1)}, u32[]{:S(2)}, u32[]{:S(2)}) %collective-permute-start.9) | collective-permute-done | bytes 108576 | tf_op jit(solution)/shard_map/ppermute | solution.py:443
  40.7 1.2 %collective-permute-done.13.rest_14_ = bf16[20,8,128]{2,1,0:T(8,128)(2,1)S(1)} collective-permute-done((bf16[20,8,128]{2,1,0:T(8,128)(2,1)S(1)}, bf16[20,8,128]{2,1,0:T(8,128)(2,1)S(1)}, u32[]{:S(2)}, u32[]{:S(2)}) %collective-permute-start.13) | collective-permute-done | bytes 40992 | tf_op jit(solution)/shard_map/ppermute | solution.py:443
  41.9 0.9 %copy-done = bf16[53,8,128]{2,1,0:T(8,128)(2,1)S(1)} copy-done((bf16[53,8,128]{2,1,0:T(8,128)(2,1)S(1)}, bf16[53,8,128]{2,1,0:T(8,128)(2,1)}, u32[]{:S(2)}) %copy-start) | copy-done | bytes 108568
  42.8 0.7 %copy-done.1 = f32[8,384]{1,0:T(8,128)S(1)} copy-done((f32[8,384]{1,0:T(8,128)S(1)}, f32[8,384]{1,0:T(8,128)}, u32[]{:S(2)}) %copy-start.1) | copy-done | bytes 12312
  43.5 4.8 %gains_and_sums.1 = (f32[8,128,384]{2,1,0:T(8,128)S(1)}, f32[64,128]{1,0:T(8,128)S(1)}, s32[16,128]{1,0:T(8,128)S(1)}, f32[3,64,8,128]{3,2,1,0:T(8,128)S(1)}) custom-call(s32[1]{0:T(128)} %bitcast.me_s.turn_s, s32[1]{0:T(128)} %bitcast.me_s.turn_s, f32[8,384]{1,0:T(8,128)S(1)} %copy-done.1, bf16[53,8,128]{2,1,0:T(8,128)(2,1)S(1)} %copy-done, ...), custom_call_target="tpu_custom_call" | custom-call | tf_op jit(solution)/shard_map/gains_and_sums/pallas_call | solution.py:466
  48.4 2.2 %sum_and_apply.1 = bf16[64,8,384]{2,1,0:T(8,128)(2,1)} custom-call(s32[16,128]{1,0:T(8,128)S(1)} %get-tuple-element.41.slots_s, f32[8,128,384]{2,1,0:T(8,128)S(1)} %get-tuple-element.42.gains_ref, f32[64,128]{1,0:T(8,128)S(1)} %get-tuple-element.43.recip_ref, f32[3,64,8,128]{3,2,1,0:T(8,128)S(1)} %get-tuple-element.44.sums_ref, ...), custom_call_target="tpu_custom_call" | custom-call | tf_op jit(solution)/shard_map/sum_and_apply/pallas_call | solution.py:490
  (16 shorter events, 0.0 us)
Async XLA Ops:
  3.3 13.7 %collective-permute-start.12 = (bf16[48,8,128]{2,1,0:T(8,128)(2,1)}, bf16[48,8,128]{2,1,0:T(8,128)(2,1)S(1)}, u32[]{:S(2)}, u32[]{:S(2)}) collective-permute-start(bf16[48,8,128]{2,1,0:T(8,128)(2,1)} %get-tuple-element.40), channel_id=1, source_target_pairs={{0,9},{1,8},{2,11},{3,10},{4,13},{5,12},{6,15},{7,14},{8,1},{9,0},... | collective-permute-start | bytes 294920 | tf_op jit(solution)/shard_map/ppermute | solution.py:443
  7.0 11.8 %collective-permute-start = (bf16[53,8,128]{2,1,0:T(8,128)(2,1)}, bf16[53,8,128]{2,1,0:T(8,128)(2,1)S(1)}, u32[]{:S(2)}, u32[]{:S(2)}) collective-permute-start(bf16[53,8,128]{2,1,0:T(8,128)(2,1)} %get-tuple-element.28), channel_id=1, source_target_pairs={{0,8},{1,9},{2,10},{3,11},{4,12},{5,13},{6,14},{7,15},{8,0},{9,1},... | collective-permute-start | bytes 325640 | tf_op jit(solution)/shard_map/ppermute | solution.py:443
  7.0 15.9 %collective-permute-start.1 = (bf16[53,8,128]{2,1,0:T(8,128)(2,1)}, bf16[53,8,128]{2,1,0:T(8,128)(2,1)S(1)}, u32[]{:S(2)}, u32[]{:S(2)}) collective-permute-start(bf16[53,8,128]{2,1,0:T(8,128)(2,1)} %get-tuple-element.29), channel_id=1, source_target_pairs={{0,10},{1,11},{2,8},{3,9},{4,14},{5,15},{6,12},{7,13},{8,2},{9,3},... | collective-permute-start | bytes 325640 | tf_op jit(solution)/shard_map/ppermute | solution.py:443
  10.4 13.4 %collective-permute-start.2 = (bf16[53,8,128]{2,1,0:T(8,128)(2,1)}, bf16[53,8,128]{2,1,0:T(8,128)(2,1)S(1)}, u32[]{:S(2)}, u32[]{:S(2)}) collective-permute-start(bf16[53,8,128]{2,1,0:T(8,128)(2,1)} %get-tuple-element.30), channel_id=1, source_target_pairs={{0,4},{1,5},{2,6},{3,7},{4,0},{5,1},{6,2},{7,3},{8,12},{9,13},{10,... | collective-permute-start | bytes 325640 | tf_op jit(solution)/shard_map/ppermute | solution.py:443
  11.7 14.5 %collective-permute-start.3 = (bf16[53,8,128]{2,1,0:T(8,128)(2,1)}, bf16[53,8,128]{2,1,0:T(8,128)(2,1)S(1)}, u32[]{:S(2)}, u32[]{:S(2)}) collective-permute-start(bf16[53,8,128]{2,1,0:T(8,128)(2,1)} %get-tuple-element.31), channel_id=1, source_target_pairs={{0,5},{1,4},{2,7},{3,6},{4,1},{5,0},{6,3},{7,2},{8,13},{9,12},{10,... | collective-permute-start | bytes 325640 | tf_op jit(solution)/shard_map/ppermute | solution.py:443
  16.9 10.8 %collective-permute-start.4 = (bf16[53,8,128]{2,1,0:T(8,128)(2,1)}, bf16[53,8,128]{2,1,0:T(8,128)(2,1)S(1)}, u32[]{:S(2)}, u32[]{:S(2)}) collective-permute-start(bf16[53,8,128]{2,1,0:T(8,128)(2,1)} %get-tuple-element.32), channel_id=1, source_target_pairs={{0,6},{1,7},{2,4},{3,5},{4,2},{5,3},{6,0},{7,1},{8,14},{9,15},{10,... | collective-permute-start | bytes 325640 | tf_op jit(solution)/shard_map/ppermute | solution.py:443
  18.9 9.5 %collective-permute-start.5 = (bf16[53,8,128]{2,1,0:T(8,128)(2,1)}, bf16[53,8,128]{2,1,0:T(8,128)(2,1)S(1)}, u32[]{:S(2)}, u32[]{:S(2)}) collective-permute-start(bf16[53,8,128]{2,1,0:T(8,128)(2,1)} %get-tuple-element.33), channel_id=1, source_target_pairs={{0,12},{1,13},{2,14},{3,15},{4,8},{5,9},{6,10},{7,11},{8,4},{9,5},... | collective-permute-start | bytes 325640 | tf_op jit(solution)/shard_map/ppermute | solution.py:443
  23.0 9.6 %collective-permute-start.6 = (bf16[53,8,128]{2,1,0:T(8,128)(2,1)}, bf16[53,8,128]{2,1,0:T(8,128)(2,1)S(1)}, u32[]{:S(2)}, u32[]{:S(2)}) collective-permute-start(bf16[53,8,128]{2,1,0:T(8,128)(2,1)} %get-tuple-element.34), channel_id=1, source_target_pairs={{0,7},{1,6},{2,5},{3,4},{4,3},{5,2},{6,1},{7,0},{8,15},{9,14},{10,... | collective-permute-start | bytes 325640 | tf_op jit(solution)/shard_map/ppermute | solution.py:443
  23.8 8.7 %collective-permute-start.7 = (bf16[53,8,128]{2,1,0:T(8,128)(2,1)}, bf16[53,8,128]{2,1,0:T(8,128)(2,1)S(1)}, u32[]{:S(2)}, u32[]{:S(2)}) collective-permute-start(bf16[53,8,128]{2,1,0:T(8,128)(2,1)} %get-tuple-element.35), channel_id=1, source_target_pairs={{0,14},{1,15},{2,12},{3,13},{4,10},{5,11},{6,8},{7,9},{8,6},{9,7},... | collective-permute-start | bytes 325640 | tf_op jit(solution)/shard_map/ppermute | solution.py:443
  26.2 10.6 %collective-permute-start.8 = (bf16[53,8,128]{2,1,0:T(8,128)(2,1)}, bf16[53,8,128]{2,1,0:T(8,128)(2,1)S(1)}, u32[]{:S(2)}, u32[]{:S(2)}) collective-permute-start(bf16[53,8,128]{2,1,0:T(8,128)(2,1)} %get-tuple-element.36), channel_id=1, source_target_pairs={{0,1},{1,0},{2,3},{3,2},{4,5},{5,4},{6,7},{7,6},{8,9},{9,8},{10,11... | collective-permute-start | bytes 325640 | tf_op jit(solution)/shard_map/ppermute | solution.py:443
  27.7 12.9 %collective-permute-start.9 = (bf16[53,8,128]{2,1,0:T(8,128)(2,1)}, bf16[53,8,128]{2,1,0:T(8,128)(2,1)S(1)}, u32[]{:S(2)}, u32[]{:S(2)}) collective-permute-start(bf16[53,8,128]{2,1,0:T(8,128)(2,1)} %get-tuple-element.37), channel_id=1, source_target_pairs={{0,11},{1,10},{2,9},{3,8},{4,15},{5,14},{6,13},{7,12},{8,3},{9,2},... | collective-permute-start | bytes 325640 | tf_op jit(solution)/shard_map/ppermute | solution.py:443
  28.4 12.3 %collective-permute-start.10 = (bf16[53,8,128]{2,1,0:T(8,128)(2,1)}, bf16[53,8,128]{2,1,0:T(8,128)(2,1)S(1)}, u32[]{:S(2)}, u32[]{:S(2)}) collective-permute-start(bf16[53,8,128]{2,1,0:T(8,128)(2,1)} %get-tuple-element.38), channel_id=1, source_target_pairs={{0,2},{1,3},{2,0},{3,1},{4,6},{5,7},{6,4},{7,5},{8,10},{9,11},{10,... | collective-permute-start | bytes 325640 | tf_op jit(solution)/shard_map/ppermute | solution.py:443
  32.6 8.1 %collective-permute-start.11 = (bf16[53,8,128]{2,1,0:T(8,128)(2,1)}, bf16[53,8,128]{2,1,0:T(8,128)(2,1)S(1)}, u32[]{:S(2)}, u32[]{:S(2)}) collective-permute-start(bf16[53,8,128]{2,1,0:T(8,128)(2,1)} %get-tuple-element.39), channel_id=1, source_target_pairs={{0,3},{1,2},{2,1},{3,0},{4,7},{5,6},{6,5},{7,4},{8,11},{9,10},{10,... | collective-permute-start | bytes 325640 | tf_op jit(solution)/shard_map/ppermute | solution.py:443
  32.6 15.8 %collective-permute-start.14 = (bf16[48,8,128]{2,1,0:T(8,128)(2,1)}, bf16[48,8,128]{2,1,0:T(8,128)(2,1)S(1)}, u32[]{:S(2)}, u32[]{:S(2)}) collective-permute-start(bf16[48,8,128]{2,1,0:T(8,128)(2,1)} %get-tuple-element.45), channel_id=1, source_target_pairs={{0,13},{1,12},{2,15},{3,14},{4,9},{5,8},{6,11},{7,10},{8,5},{9,4},... | collective-permute-start | bytes 294920 | tf_op jit(solution)/shard_map/ppermute | solution.py:443
  36.8 11.5 %collective-permute-start.15 = (bf16[48,8,128]{2,1,0:T(8,128)(2,1)}, bf16[48,8,128]{2,1,0:T(8,128)(2,1)S(1)}, u32[]{:S(2)}, u32[]{:S(2)}) collective-permute-start(bf16[48,8,128]{2,1,0:T(8,128)(2,1)} %get-tuple-element.46), channel_id=1, source_target_pairs={{0,15},{1,14},{2,13},{3,12},{4,11},{5,10},{6,9},{7,8},{8,7},{9,6},... | collective-permute-start | bytes 294920 | tf_op jit(solution)/shard_map/ppermute | solution.py:443
  40.7 1.2 %collective-permute-start.13 = (bf16[20,8,128]{2,1,0:T(8,128)(2,1)S(1)}, bf16[20,8,128]{2,1,0:T(8,128)(2,1)S(1)}, u32[]{:S(2)}, u32[]{:S(2)}) collective-permute-start(bf16[20,8,128]{2,1,0:T(8,128)(2,1)S(1)} %collect_gains.1), channel_id=1, source_target_pairs={{0,1},{1,0},{2,3},{3,2},{4,5},{5,4},{6,7},{7,6},{8,9},{9,8},{10,11... | collective-permute-start | bytes 122888 | tf_op jit(solution)/shard_map/ppermute | solution.py:443
  41.9 0.9 %copy-start = (bf16[53,8,128]{2,1,0:T(8,128)(2,1)S(1)}, bf16[53,8,128]{2,1,0:T(8,128)(2,1)}, u32[]{:S(2)}) copy-start(bf16[53,8,128]{2,1,0:T(8,128)(2,1)} %get-tuple-element.27.rest_0_) | copy-start | bytes 325636
  42.8 0.7 %copy-start.1 = (f32[8,384]{1,0:T(8,128)S(1)}, f32[8,384]{1,0:T(8,128)}, u32[]{:S(2)}) copy-start(f32[8,384]{1,0:T(8,128)} %get-tuple-element.26.small_ref) | copy-start | bytes 36868
where the time goes:
time: 50.2 us; the launch traced here: 50.5 us
  starting transfers between devices  24.5 us (49%)
  waiting for transfers between devices  14.1 us (28%)
  Pallas kernels  10.3 us (21%)
  local copies, waits for them, and re-layouts  1.6 us (3%)
    ppermute x16, starting transfers between devices, swap(): return lax.ppermute(array, 'bl', [(d, d ^ x) for d in range(devices)])  24.5 us
    ppermute x16, waiting for transfers between devices, swap(): return lax.ppermute(array, 'bl', [(d, d ^ x) for d in range(devices)])  14.1 us
    pallas_call x1, Pallas kernels, on_device(): pl.pallas_call(functools.partial(middle_kernel, capacity, near, stations,...  4.84 us
    pallas_call x1, Pallas kernels, on_device(): pl.pallas_call(functools.partial(pack_kernel, capacity, near), out_shape=...  3.27 us
    pallas_call x1, Pallas kernels, on_device(): pl.pallas_call(functools.partial(finish_kernel, capacity, late), out_shap...  2.18 us
    unnamed x4, local copies, waits for them, and re-layouts  1.6 us
  transfers between devices with their start and end apart: 16, of which 5 were waited for; matrix products, arithmetic and copies ran while one was open for 0% of the time, Pallas kernels for 10%

commit v1 on v0

--- a/solution.py
+++ b/solution.py
@@ -10,6 +10,7 @@
 LANES = 128
 SUB = 8
 USED = 48
+PARTS = 4
 ALL_VMEM = 60 * 1024 * 1024
 SOME_VMEM = 24 * 1024 * 1024
 
@@ -22,8 +23,8 @@
     even, odd = list(range(near, 2 * near, 2)), list(range(near + 1, 2 * near, 2))
     close = list(range(near // 2, near)) + list(range(1, near // 2))
     cross, late = even[2:] + odd[1:-2], odd[-2:]
-    order = [0] + even[:2] + close[:3]
-    close = close[3:]
+    order = [0] + even[:2] + close[:2]
+    close = close[2:]
     while cross:
         order += cross[:1] + close[:1]
         cross, close = cross[1:], close[1:]
@@ -55,13 +56,14 @@
     pairs_hbm,
     *rest,
 ):
-    outs = rest[:-14]
+    outs = rest[:-15]
     (
         weights_ref,
         offset_ref,
         pairs_ref,
         small_ref,
         owner_s,
+        place_s,
         count_s,
         owner_ref,
         slot_ref,
@@ -71,7 +73,7 @@
         meta_ref,
         block_ref,
         sems,
-    ) = rest[-14:]
+    ) = rest[-15:]
     rows = vis_ref.shape[0]
     chunks = vis_ref.shape[2] // LANES
     devices = block_ref.shape[0]
@@ -79,11 +81,11 @@
     half = stations // 2
     depth = meta_ref.shape[0]
     gain_tiles = (depth - 1) // 2
+    span = rows // PARTS
     moves = start_all(
         (
-            (vis_hbm, vis_ref),
+            (owner_hbm, owner_s),
             (coarse_hbm, coarse_ref),
-            (owner_hbm, owner_s),
             (owner_row_hbm, owner_ref),
             (slot_row_hbm, slot_ref),
             (weights_hbm, weights_ref),
@@ -92,10 +94,27 @@
         ),
         sems,
     )
+    fetches = start_all(
+        [
+            (vis_hbm.at[pl.ds(i * span, span)], vis_ref.at[pl.ds(i * span, span)])
+            for i in range(PARTS)
+        ],
+        sems.at[pl.ds(len(moves), PARTS)],
+    )
     turn_ref[...] = jnp.zeros_like(turn_ref)
     for d in range(devices):
         count_s[d] = 0
     me = me_s[0]
+    moves[0].wait()
+
+    def rank(r, carry):
+        x = owner_s[r] ^ me
+        k = count_s[x]
+        count_s[x] = k + 1
+        place_s[r] = x * capacity + k
+        return carry
+
+    lax.fori_loop(0, rows, rank, 0, unroll=8)
     for move in moves[1:]:
         move.wait()
 
@@ -124,19 +143,20 @@
     else:
         pairs = [(meta_ref, outs[1])]
     pairs += [(small_ref, outs[-1])]
-    sends = start_all(pairs, sems.at[pl.ds(8, len(pairs))])
-    moves[0].wait()
+    start = len(moves) + PARTS
+    sends = start_all(pairs, sems.at[pl.ds(start, len(pairs))])
+    start += len(pairs)
 
     def place(r, carry):
-        x = owner_s[r] ^ me
-        k = count_s[x]
-        count_s[x] = k + 1
+        p = place_s[r]
         for c in range(chunks):
-            block_ref[x, chunks * k + c] = vis_ref[r, :, c * LANES : (c + 1) * LANES]
+            flat_ref[p * chunks + c] = vis_ref[r, :, c * LANES : (c + 1) * LANES]
         return carry
 
-    lax.fori_loop(0, rows, place, 0, unroll=8)
-    start = 8 + len(pairs)
+    flat_ref = block_ref.reshape(devices * at, SUB, LANES)
+    for i in range(PARTS):
+        fetches[i].wait()
+        lax.fori_loop(i * span, (i + 1) * span, place, 0, unroll=8)
     if near > 1:
         pairs = [(block_ref.at[x], outs[x].at[pl.ds(0, at)]) for x in range(devices)]
     else:
@@ -414,6 +434,7 @@
             pltpu.VMEM(pairs.shape, i32),
             pltpu.VMEM((SUB, channels), f32),
             pltpu.SMEM((rows,), i32),
+            pltpu.SMEM((rows,), i32),
             pltpu.SMEM((devices,), i32),
             pltpu.VMEM((1, rows), i32),
             pltpu.VMEM((1, rows), i32),
@@ -422,7 +443,7 @@
             pltpu.VMEM((LANES, LANES), f32),
             pltpu.VMEM((depth, SUB, LANES), bf16),
             pltpu.VMEM((devices,) + block, bf16),
-            dma((9 + 2 * devices,)),
+            dma((9 + PARTS + 2 * devices,)),
         ],
         compiler_params=most,
         name="pack_rows",

time: 50.2 us -> 49.7 us (0.990)
  the two profiles are of different devices: /device:TPU:1 before, /device:TPU:0 now
where the time goes in v1:
time: 49.7 us; the launch traced here: 49.4 us
  starting transfers between devices  28.1 us (57%)
  waiting for transfers between devices  10.6 us (21%)
  Pallas kernels  9.06 us (18%)
  local copies, waits for them, and re-layouts  1.6 us (3%)
    ppermute x16, starting transfers between devices, swap(): return lax.ppermute(array, 'bl', [(d, d ^ x) for d in range(devices)])  28.1 us
    ppermute x16, waiting for transfers between devices, swap(): return lax.ppermute(array, 'bl', [(d, d ^ x) for d in range(devices)])  10.6 us
    pallas_call x1, Pallas kernels, on_device(): pl.pallas_call(functools.partial(middle_kernel, capacity, near, stations,...  3.77 us
    pallas_call x1, Pallas kernels, on_device(): pl.pallas_call(functools.partial(pack_kernel, capacity, near), out_shape=...  3.23 us
    pallas_call x1, Pallas kernels, on_device(): pl.pallas_call(functools.partial(finish_kernel, capacity, late), out_shap...  1.99 us
    unnamed x4, local copies, waits for them, and re-layouts  1.6 us
  transfers between devices with their start and end apart: 16, of which 7 were waited for; matrix products, arithmetic and copies ran while one was open for 0% of the time, Pallas kernels for 8%

profile of v1, /device:TPU:0, one launch (start us, length us, event | category | flops | bytes accessed | tf_op | source)
XLA Modules:
  0.0 49.4 jit_solution(7715855051070922344)
XLA Ops:
  0.0 3.2 %pack_rows.1 = (bf16[53,8,128]{2,1,0:T(8,128)(2,1)}, bf16[53,8,128]{2,1,0:T(8,128)(2,1)}, bf16[53,8,128]{2,1,0:T(8,128)(2,1)}, bf16[53,8,128]{2,1,0:T(8,128)(2,1...) custom-call(s32[1]{0:T(128)} %bitcast.me_s.turn_s, ...), custom_call_target="tpu_custom_call" | custom-call | tf_op jit(solution)/shard_map/pack_rows/pallas_call | solution.py:426
  3.2 3.5 %collective-permute-start.12 = (bf16[48,8,128]{2,1,0:T(8,128)(2,1)}, bf16[48,8,128]{2,1,0:T(8,128)(2,1)S(1)}, u32[]{:S(2)}, u32[]{:S(2)}) collective-permute-start(bf16[48,8,128]{2,1,0:T(8,128)(2,1)} %get-tuple-element.40), channel_id=1, source_target_pairs={{0,9},{1,8},{2,11},{3,10},{4,13},{5,12},{6,15},{7,14},{8,1},{9,0},... | collective-permute-start | bytes 294920 | tf_op jit(solution)/shard_map/ppermute | solution.py:464
  6.8 0.6 %collective-permute-start = (bf16[53,8,128]{2,1,0:T(8,128)(2,1)}, bf16[53,8,128]{2,1,0:T(8,128)(2,1)S(1)}, u32[]{:S(2)}, u32[]{:S(2)}) collective-permute-start(bf16[53,8,128]{2,1,0:T(8,128)(2,1)} %get-tuple-element.28), channel_id=1, source_target_pairs={{0,8},{1,9},{2,10},{3,11},{4,12},{5,13},{6,14},{7,15},{8,0},{9,1},... | collective-permute-start | bytes 325640 | tf_op jit(solution)/shard_map/ppermute | solution.py:464
  7.4 3.2 %collective-permute-start.1 = (bf16[53,8,128]{2,1,0:T(8,128)(2,1)}, bf16[53,8,128]{2,1,0:T(8,128)(2,1)S(1)}, u32[]{:S(2)}, u32[]{:S(2)}) collective-permute-start(bf16[53,8,128]{2,1,0:T(8,128)(2,1)} %get-tuple-element.29), channel_id=1, source_target_pairs={{0,10},{1,11},{2,8},{3,9},{4,14},{5,15},{6,12},{7,13},{8,2},{9,3},... | collective-permute-start | bytes 325640 | tf_op jit(solution)/shard_map/ppermute | solution.py:464
  10.7 1.6 %collective-permute-start.2 = (bf16[53,8,128]{2,1,0:T(8,128)(2,1)}, bf16[53,8,128]{2,1,0:T(8,128)(2,1)S(1)}, u32[]{:S(2)}, u32[]{:S(2)}) collective-permute-start(bf16[53,8,128]{2,1,0:T(8,128)(2,1)} %get-tuple-element.30), channel_id=1, source_target_pairs={{0,4},{1,5},{2,6},{3,7},{4,0},{5,1},{6,2},{7,3},{8,12},{9,13},{10,... | collective-permute-start | bytes 325640 | tf_op jit(solution)/shard_map/ppermute | solution.py:464
  12.2 9.1 %collective-permute-start.4 = (bf16[53,8,128]{2,1,0:T(8,128)(2,1)}, bf16[53,8,128]{2,1,0:T(8,128)(2,1)S(1)}, u32[]{:S(2)}, u32[]{:S(2)}) collective-permute-start(bf16[53,8,128]{2,1,0:T(8,128)(2,1)} %get-tuple-element.32), channel_id=1, source_target_pairs={{0,12},{1,13},{2,14},{3,15},{4,8},{5,9},{6,10},{7,11},{8,4},{9,5},... | collective-permute-start | bytes 325640 | tf_op jit(solution)/shard_map/ppermute | solution.py:464
  21.3 0.5 collective-permute-start.5
  21.8 4.2 %collective-permute-done.1.rest_1_.rest_2_ = bf16[53,8,128]{2,1,0:T(8,128)(2,1)S(1)} collective-permute-done((bf16[53,8,128]{2,1,0:T(8,128)(2,1)}, bf16[53,8,128]{2,1,0:T(8,128)(2,1)S(1)}, u32[]{:S(2)}, u32[]{:S(2)}) %collective-permute-start.1) | collective-permute-done | bytes 108576 | tf_op jit(solution)/shard_map/ppermute | solution.py:464
  26.0 0.9 %collective-permute-start.6 = (bf16[53,8,128]{2,1,0:T(8,128)(2,1)}, bf16[53,8,128]{2,1,0:T(8,128)(2,1)S(1)}, u32[]{:S(2)}, u32[]{:S(2)}) collective-permute-start(bf16[53,8,128]{2,1,0:T(8,128)(2,1)} %get-tuple-element.34), channel_id=1, source_target_pairs={{0,14},{1,15},{2,12},{3,13},{4,10},{5,11},{6,8},{7,9},{8,6},{9,7},... | collective-permute-start | bytes 325640 | tf_op jit(solution)/shard_map/ppermute | solution.py:464
  26.9 1.2 %collective-permute-start.8 = (bf16[53,8,128]{2,1,0:T(8,128)(2,1)}, bf16[53,8,128]{2,1,0:T(8,128)(2,1)S(1)}, u32[]{:S(2)}, u32[]{:S(2)}) collective-permute-start(bf16[53,8,128]{2,1,0:T(8,128)(2,1)} %get-tuple-element.36), channel_id=1, source_target_pairs={{0,11},{1,10},{2,9},{3,8},{4,15},{5,14},{6,13},{7,12},{8,3},{9,2},... | collective-permute-start | bytes 325640 | tf_op jit(solution)/shard_map/ppermute | solution.py:464
  28.1 0.3 collective-permute-done.5.rest_6_
  28.4 4.1 %collective-permute-start.10 = (bf16[53,8,128]{2,1,0:T(8,128)(2,1)}, bf16[53,8,128]{2,1,0:T(8,128)(2,1)S(1)}, u32[]{:S(2)}, u32[]{:S(2)}) collective-permute-start(bf16[53,8,128]{2,1,0:T(8,128)(2,1)} %get-tuple-element.38), channel_id=1, source_target_pairs={{0,2},{1,3},{2,0},{3,1},{4,6},{5,7},{6,4},{7,5},{8,10},{9,11},{10,... | collective-permute-start | bytes 325640 | tf_op jit(solution)/shard_map/ppermute | solution.py:464
  32.5 1.3 %collective-permute-done.6.rest_3_.rest_7_ = bf16[53,8,128]{2,1,0:T(8,128)(2,1)S(1)} collective-permute-done((bf16[53,8,128]{2,1,0:T(8,128)(2,1)}, bf16[53,8,128]{2,1,0:T(8,128)(2,1)S(1)}, u32[]{:S(2)}, u32[]{:S(2)}) %collective-permute-start.6) | collective-permute-done | bytes 108576 | tf_op jit(solution)/shard_map/ppermute | solution.py:464
  33.8 2.4 %collective-permute-done.7.rest_8_ = bf16[53,8,128]{2,1,0:T(8,128)(2,1)S(1)} collective-permute-done((bf16[53,8,128]{2,1,0:T(8,128)(2,1)}, bf16[53,8,128]{2,1,0:T(8,128)(2,1)S(1)}, u32[]{:S(2)}, u32[]{:S(2)}) %collective-permute-start.7) | collective-permute-done | bytes 108576 | tf_op jit(solution)/shard_map/ppermute | solution.py:464
  36.2 0.1 collective-permute-start.14
  36.3 1.5 %collective-permute-done.8.rest_9_ = bf16[53,8,128]{2,1,0:T(8,128)(2,1)S(1)} collective-permute-done((bf16[53,8,128]{2,1,0:T(8,128)(2,1)}, bf16[53,8,128]{2,1,0:T(8,128)(2,1)S(1)}, u32[]{:S(2)}, u32[]{:S(2)}) %collective-permute-start.8) | collective-permute-done | bytes 108576 | tf_op jit(solution)/shard_map/ppermute | solution.py:464
  37.9 2.6 %collective-permute-start.15 = (bf16[48,8,128]{2,1,0:T(8,128)(2,1)}, bf16[48,8,128]{2,1,0:T(8,128)(2,1)S(1)}, u32[]{:S(2)}, u32[]{:S(2)}) collective-permute-start(bf16[48,8,128]{2,1,0:T(8,128)(2,1)} %get-tuple-element.46), channel_id=1, source_target_pairs={{0,15},{1,14},{2,13},{3,12},{4,11},{5,10},{6,9},{7,8},{8,7},{9,6},... | collective-permute-start | bytes 294920 | tf_op jit(solution)/shard_map/ppermute | solution.py:464
  40.6 0.6 %collective-permute-start.13 = (bf16[20,8,128]{2,1,0:T(8,128)(2,1)S(1)}, bf16[20,8,128]{2,1,0:T(8,128)(2,1)S(1)}, u32[]{:S(2)}, u32[]{:S(2)}) collective-permute-start(bf16[20,8,128]{2,1,0:T(8,128)(2,1)S(1)} %collect_gains.1), channel_id=1, source_target_pairs={{0,1},{1,0},{2,3},{3,2},{4,5},{5,4},{6,7},{7,6},{8,9},{9,8},{10,11... | collective-permute-start | bytes 122888 | tf_op jit(solution)/shard_map/ppermute | solution.py:464
  41.1 0.2 collective-permute-done.11.rest_12_
  41.4 0.6 %collective-permute-done.13.rest_14_ = bf16[20,8,128]{2,1,0:T(8,128)(2,1)S(1)} collective-permute-done((bf16[20,8,128]{2,1,0:T(8,128)(2,1)S(1)}, bf16[20,8,128]{2,1,0:T(8,128)(2,1)S(1)}, u32[]{:S(2)}, u32[]{:S(2)}) %collective-permute-start.13) | collective-permute-done | bytes 40992 | tf_op jit(solution)/shard_map/ppermute | solution.py:464
  42.0 0.9 %copy-done = bf16[53,8,128]{2,1,0:T(8,128)(2,1)S(1)} copy-done((bf16[53,8,128]{2,1,0:T(8,128)(2,1)S(1)}, bf16[53,8,128]{2,1,0:T(8,128)(2,1)}, u32[]{:S(2)}) %copy-start) | copy-done | bytes 108568
  42.9 0.7 %copy-done.1 = f32[8,384]{1,0:T(8,128)S(1)} copy-done((f32[8,384]{1,0:T(8,128)S(1)}, f32[8,384]{1,0:T(8,128)}, u32[]{:S(2)}) %copy-start.1) | copy-done | bytes 12312
  43.6 3.8 %gains_and_sums.1 = (f32[8,128,384]{2,1,0:T(8,128)S(1)}, f32[64,128]{1,0:T(8,128)S(1)}, s32[16,128]{1,0:T(8,128)S(1)}, f32[3,64,8,128]{3,2,1,0:T(8,128)S(1)}) custom-call(s32[1]{0:T(128)} %bitcast.me_s.turn_s, s32[1]{0:T(128)} %bitcast.me_s.turn_s, f32[8,384]{1,0:T(8,128)S(1)} %copy-done.1, bf16[53,8,128]{2,1,0:T(8,128)(2,1)S(1)} %copy-done, ...), custom_call_target="tpu_custom_call" | custom-call | tf_op jit(solution)/shard_map/gains_and_sums/pallas_call | solution.py:487
  47.4 2.0 %sum_and_apply.1 = bf16[64,8,384]{2,1,0:T(8,128)(2,1)} custom-call(s32[16,128]{1,0:T(8,128)S(1)} %get-tuple-element.41.slots_s, f32[8,128,384]{2,1,0:T(8,128)S(1)} %get-tuple-element.42.gains_ref, f32[64,128]{1,0:T(8,128)S(1)} %get-tuple-element.43.recip_ref, f32[3,64,8,128]{3,2,1,0:T(8,128)S(1)} %get-tuple-element.44.sums_ref, ...), custom_call_target="tpu_custom_call" | custom-call | tf_op jit(solution)/shard_map/sum_and_apply/pallas_call | solution.py:511
  (16 shorter events, 0.2 us)
Async XLA Ops:
  3.2 9.0 %collective-permute-start.12 = (bf16[48,8,128]{2,1,0:T(8,128)(2,1)}, bf16[48,8,128]{2,1,0:T(8,128)(2,1)S(1)}, u32[]{:S(2)}, u32[]{:S(2)}) collective-permute-start(bf16[48,8,128]{2,1,0:T(8,128)(2,1)} %get-tuple-element.40), channel_id=1, source_target_pairs={{0,9},{1,8},{2,11},{3,10},{4,13},{5,12},{6,15},{7,14},{8,1},{9,0},... | collective-permute-start | bytes 294920 | tf_op jit(solution)/shard_map/ppermute | solution.py:464
  6.8 14.5 %collective-permute-start = (bf16[53,8,128]{2,1,0:T(8,128)(2,1)}, bf16[53,8,128]{2,1,0:T(8,128)(2,1)S(1)}, u32[]{:S(2)}, u32[]{:S(2)}) collective-permute-start(bf16[53,8,128]{2,1,0:T(8,128)(2,1)} %get-tuple-element.28), channel_id=1, source_target_pairs={{0,8},{1,9},{2,10},{3,11},{4,12},{5,13},{6,14},{7,15},{8,0},{9,1},... | collective-permute-start | bytes 325640 | tf_op jit(solution)/shard_map/ppermute | solution.py:464
  7.4 18.5 %collective-permute-start.1 = (bf16[53,8,128]{2,1,0:T(8,128)(2,1)}, bf16[53,8,128]{2,1,0:T(8,128)(2,1)S(1)}, u32[]{:S(2)}, u32[]{:S(2)}) collective-permute-start(bf16[53,8,128]{2,1,0:T(8,128)(2,1)} %get-tuple-element.29), channel_id=1, source_target_pairs={{0,10},{1,11},{2,8},{3,9},{4,14},{5,15},{6,12},{7,13},{8,2},{9,3},... | collective-permute-start | bytes 325640 | tf_op jit(solution)/shard_map/ppermute | solution.py:464
  10.7 16.2 %collective-permute-start.2 = (bf16[53,8,128]{2,1,0:T(8,128)(2,1)}, bf16[53,8,128]{2,1,0:T(8,128)(2,1)S(1)}, u32[]{:S(2)}, u32[]{:S(2)}) collective-permute-start(bf16[53,8,128]{2,1,0:T(8,128)(2,1)} %get-tuple-element.30), channel_id=1, source_target_pairs={{0,4},{1,5},{2,6},{3,7},{4,0},{5,1},{6,2},{7,3},{8,12},{9,13},{10,... | collective-permute-start | bytes 325640 | tf_op jit(solution)/shard_map/ppermute | solution.py:464
  12.2 14.6 %collective-permute-start.3 = (bf16[53,8,128]{2,1,0:T(8,128)(2,1)}, bf16[53,8,128]{2,1,0:T(8,128)(2,1)S(1)}, u32[]{:S(2)}, u32[]{:S(2)}) collective-permute-start(bf16[53,8,128]{2,1,0:T(8,128)(2,1)} %get-tuple-element.31), channel_id=1, source_target_pairs={{0,5},{1,4},{2,7},{3,6},{4,1},{5,0},{6,3},{7,2},{8,13},{9,12},{10,... | collective-permute-start | bytes 325640 | tf_op jit(solution)/shard_map/ppermute | solution.py:464
  12.2 15.8 %collective-permute-start.4 = (bf16[53,8,128]{2,1,0:T(8,128)(2,1)}, bf16[53,8,128]{2,1,0:T(8,128)(2,1)S(1)}, u32[]{:S(2)}, u32[]{:S(2)}) collective-permute-start(bf16[53,8,128]{2,1,0:T(8,128)(2,1)} %get-tuple-element.32), channel_id=1, source_target_pairs={{0,12},{1,13},{2,14},{3,15},{4,8},{5,9},{6,10},{7,11},{8,4},{9,5},... | collective-permute-start | bytes 325640 | tf_op jit(solution)/shard_map/ppermute | solution.py:464
  21.3 7.1 %collective-permute-start.5 = (bf16[53,8,128]{2,1,0:T(8,128)(2,1)}, bf16[53,8,128]{2,1,0:T(8,128)(2,1)S(1)}, u32[]{:S(2)}, u32[]{:S(2)}) collective-permute-start(bf16[53,8,128]{2,1,0:T(8,128)(2,1)} %get-tuple-element.33), channel_id=1, source_target_pairs={{0,6},{1,7},{2,4},{3,5},{4,2},{5,3},{6,0},{7,1},{8,14},{9,15},{10,... | collective-permute-start | bytes 325640 | tf_op jit(solution)/shard_map/ppermute | solution.py:464
  26.0 7.8 %collective-permute-start.6 = (bf16[53,8,128]{2,1,0:T(8,128)(2,1)}, bf16[53,8,128]{2,1,0:T(8,128)(2,1)S(1)}, u32[]{:S(2)}, u32[]{:S(2)}) collective-permute-start(bf16[53,8,128]{2,1,0:T(8,128)(2,1)} %get-tuple-element.34), channel_id=1, source_target_pairs={{0,14},{1,15},{2,12},{3,13},{4,10},{5,11},{6,8},{7,9},{8,6},{9,7},... | collective-permute-start | bytes 325640 | tf_op jit(solution)/shard_map/ppermute | solution.py:464
  26.9 9.4 %collective-permute-start.7 = (bf16[53,8,128]{2,1,0:T(8,128)(2,1)}, bf16[53,8,128]{2,1,0:T(8,128)(2,1)S(1)}, u32[]{:S(2)}, u32[]{:S(2)}) collective-permute-start(bf16[53,8,128]{2,1,0:T(8,128)(2,1)} %get-tuple-element.35), channel_id=1, source_target_pairs={{0,7},{1,6},{2,5},{3,4},{4,3},{5,2},{6,1},{7,0},{8,15},{9,14},{10,... | collective-permute-start | bytes 325640 | tf_op jit(solution)/shard_map/ppermute | solution.py:464
  26.9 11.0 %collective-permute-start.8 = (bf16[53,8,128]{2,1,0:T(8,128)(2,1)}, bf16[53,8,128]{2,1,0:T(8,128)(2,1)S(1)}, u32[]{:S(2)}, u32[]{:S(2)}) collective-permute-start(bf16[53,8,128]{2,1,0:T(8,128)(2,1)} %get-tuple-element.36), channel_id=1, source_target_pairs={{0,11},{1,10},{2,9},{3,8},{4,15},{5,14},{6,13},{7,12},{8,3},{9,2},... | collective-permute-start | bytes 325640 | tf_op jit(solution)/shard_map/ppermute | solution.py:464
  28.1 12.5 %collective-permute-start.9 = (bf16[53,8,128]{2,1,0:T(8,128)(2,1)}, bf16[53,8,128]{2,1,0:T(8,128)(2,1)S(1)}, u32[]{:S(2)}, u32[]{:S(2)}) collective-permute-start(bf16[53,8,128]{2,1,0:T(8,128)(2,1)} %get-tuple-element.37), channel_id=1, source_target_pairs={{0,1},{1,0},{2,3},{3,2},{4,5},{5,4},{6,7},{7,6},{8,9},{9,8},{10,11... | collective-permute-start | bytes 325640 | tf_op jit(solution)/shard_map/ppermute | solution.py:464
  28.4 12.7 %collective-permute-start.10 = (bf16[53,8,128]{2,1,0:T(8,128)(2,1)}, bf16[53,8,128]{2,1,0:T(8,128)(2,1)S(1)}, u32[]{:S(2)}, u32[]{:S(2)}) collective-permute-start(bf16[53,8,128]{2,1,0:T(8,128)(2,1)} %get-tuple-element.38), channel_id=1, source_target_pairs={{0,2},{1,3},{2,0},{3,1},{4,6},{5,7},{6,4},{7,5},{8,10},{9,11},{10,... | collective-permute-start | bytes 325640 | tf_op jit(solution)/shard_map/ppermute | solution.py:464
  33.8 7.6 %collective-permute-start.11 = (bf16[53,8,128]{2,1,0:T(8,128)(2,1)}, bf16[53,8,128]{2,1,0:T(8,128)(2,1)S(1)}, u32[]{:S(2)}, u32[]{:S(2)}) collective-permute-start(bf16[53,8,128]{2,1,0:T(8,128)(2,1)} %get-tuple-element.39), channel_id=1, source_target_pairs={{0,3},{1,2},{2,1},{3,0},{4,7},{5,6},{6,5},{7,4},{8,11},{9,10},{10,... | collective-permute-start | bytes 325640 | tf_op jit(solution)/shard_map/ppermute | solution.py:464
  36.2 11.2 %collective-permute-start.14 = (bf16[48,8,128]{2,1,0:T(8,128)(2,1)}, bf16[48,8,128]{2,1,0:T(8,128)(2,1)S(1)}, u32[]{:S(2)}, u32[]{:S(2)}) collective-permute-start(bf16[48,8,128]{2,1,0:T(8,128)(2,1)} %get-tuple-element.45), channel_id=1, source_target_pairs={{0,13},{1,12},{2,15},{3,14},{4,9},{5,8},{6,11},{7,10},{8,5},{9,4},... | collective-permute-start | bytes 294920 | tf_op jit(solution)/shard_map/ppermute | solution.py:464
  37.9 9.5 %collective-permute-start.15 = (bf16[48,8,128]{2,1,0:T(8,128)(2,1)}, bf16[48,8,128]{2,1,0:T(8,128)(2,1)S(1)}, u32[]{:S(2)}, u32[]{:S(2)}) collective-permute-start(bf16[48,8,128]{2,1,0:T(8,128)(2,1)} %get-tuple-element.46), channel_id=1, source_target_pairs={{0,15},{1,14},{2,13},{3,12},{4,11},{5,10},{6,9},{7,8},{8,7},{9,6},... | collective-permute-start | bytes 294920 | tf_op jit(solution)/shard_map/ppermute | solution.py:464
  40.6 1.4 %collective-permute-start.13 = (bf16[20,8,128]{2,1,0:T(8,128)(2,1)S(1)}, bf16[20,8,128]{2,1,0:T(8,128)(2,1)S(1)}, u32[]{:S(2)}, u32[]{:S(2)}) collective-permute-start(bf16[20,8,128]{2,1,0:T(8,128)(2,1)S(1)} %collect_gains.1), channel_id=1, source_target_pairs={{0,1},{1,0},{2,3},{3,2},{4,5},{5,4},{6,7},{7,6},{8,9},{9,8},{10,11... | collective-permute-start | bytes 122888 | tf_op jit(solution)/shard_map/ppermute | solution.py:464
  42.0 0.9 %copy-start = (bf16[53,8,128]{2,1,0:T(8,128)(2,1)S(1)}, bf16[53,8,128]{2,1,0:T(8,128)(2,1)}, u32[]{:S(2)}) copy-start(bf16[53,8,128]{2,1,0:T(8,128)(2,1)} %get-tuple-element.27.rest_0_) | copy-start | bytes 325636
  42.9 0.7 %copy-start.1 = (f32[8,384]{1,0:T(8,128)S(1)}, f32[8,384]{1,0:T(8,128)}, u32[]{:S(2)}) copy-start(f32[8,384]{1,0:T(8,128)} %get-tuple-element.26.small_ref) | copy-start | bytes 36868

commit v2 on v1

--- a/solution.py
+++ b/solution.py
@@ -22,13 +22,12 @@
 def schedule(near):
     even, odd = list(range(near, 2 * near, 2)), list(range(near + 1, 2 * near, 2))
     close = list(range(near // 2, near)) + list(range(1, near // 2))
-    cross, late = even[2:] + odd[1:-2], odd[-2:]
     order = [0] + even[:2] + close[:2]
-    close = close[2:]
+    cross, close = even[2:], close[2:]
     while cross:
         order += cross[:1] + close[:1]
         cross, close = cross[1:], close[1:]
-    return order + close + odd[:1], late
+    return order + close + odd[:1], odd[1:]
 
 
 def with_gains(near):
@@ -45,6 +44,7 @@
 def pack_kernel(
     capacity,
     near,
+    targets,
     me_s,
     owner_hbm,
     owner_row_hbm,
@@ -139,10 +139,15 @@
 
     at = chunks * capacity
     if near > 1:
-        pairs = [(meta_ref, outs[x].at[pl.ds(at, depth)]) for x in with_gains(near)]
+        pairs = [
+            (meta_ref, out.at[pl.ds(at, depth)])
+            for x, out in zip(targets, outs)
+            if x in with_gains(near)
+        ]
     else:
         pairs = [(meta_ref, outs[1])]
-    pairs += [(small_ref, outs[-1])]
+    if len(outs) > len(targets):
+        pairs += [(small_ref, outs[-1])]
     start = len(moves) + PARTS
     sends = start_all(pairs, sems.at[pl.ds(start, len(pairs))])
     start += len(pairs)
@@ -158,7 +163,7 @@
         fetches[i].wait()
         lax.fori_loop(i * span, (i + 1) * span, place, 0, unroll=8)
     if near > 1:
-        pairs = [(block_ref.at[x], outs[x].at[pl.ds(0, at)]) for x in range(devices)]
+        pairs = [(block_ref.at[x], out.at[pl.ds(0, at)]) for x, out in zip(targets, outs)]
     else:
         pairs = [(block_ref, outs[0])]
     sends += start_all(pairs, sems.at[pl.ds(start, len(pairs))])
@@ -411,54 +416,59 @@
     coarse = gains_coarse.transpose(2, 1, 0).reshape(knots * parts, stations)
     block = (chunks * capacity, parts, LANES)
     rows_at = chunks * capacity
-    if halves:
-        long = with_gains(near) + [near + 3]
-        outs = [
-            shape((rows_at + (depth if x in long else 0), parts, LANES), bf16)
-            for x in range(devices)
-        ]
-    else:
-        outs = [shape((devices,) + block, bf16), shape((depth, SUB, LANES), bf16)]
-    outs += [shape((SUB, channels), f32)]
+    def pack(targets, outs):
+        return pl.pallas_call(
+            functools.partial(pack_kernel, capacity, near, targets),
+            out_shape=outs,
+            in_specs=[smem] + [hbm] * 8,
+            out_specs=[hbm] * len(outs),
+            scratch_shapes=[
+                pltpu.VMEM(weights.shape, f32),
+                pltpu.VMEM(offset.shape, i32),
+                pltpu.VMEM(pairs.shape, i32),
+                pltpu.VMEM((SUB, channels), f32),
+                pltpu.SMEM((rows,), i32),
+                pltpu.SMEM((rows,), i32),
+                pltpu.SMEM((devices,), i32),
+                pltpu.VMEM((1, rows), i32),
+                pltpu.VMEM((1, rows), i32),
+                pltpu.VMEM((rows, parts, channels), bf16),
+                pltpu.VMEM((knots * parts, stations), f32),
+                pltpu.VMEM((LANES, LANES), f32),
+                pltpu.VMEM((depth, SUB, LANES), bf16),
+                pltpu.VMEM((devices,) + block, bf16),
+                dma((9 + PARTS + 2 * devices,)),
+            ],
+            compiler_params=most,
+            name="pack_rows",
+        )(
+            turn,
+            owner,
+            row_owner.reshape(1, rows),
+            row_slot.reshape(1, rows),
+            visibilities,
+            coarse,
+            weights,
+            offset,
+            pairs,
+        )
+
     pairs = baseline_station_pairs.T
     weights = band_weights.T
     offset = band_offset.reshape(chunks, LANES)
-    sent = pl.pallas_call(
-        functools.partial(pack_kernel, capacity, near),
-        out_shape=outs,
-        in_specs=[smem] + [hbm] * 8,
-        out_specs=[hbm] * len(outs),
-        scratch_shapes=[
-            pltpu.VMEM(weights.shape, f32),
-            pltpu.VMEM(offset.shape, i32),
-            pltpu.VMEM(pairs.shape, i32),
-            pltpu.VMEM((SUB, channels), f32),
-            pltpu.SMEM((rows,), i32),
-            pltpu.SMEM((rows,), i32),
-            pltpu.SMEM((devices,), i32),
-            pltpu.VMEM((1, rows), i32),
-            pltpu.VMEM((1, rows), i32),
-            pltpu.VMEM((rows, parts, channels), bf16),
-            pltpu.VMEM((knots * parts, stations), f32),
-            pltpu.VMEM((LANES, LANES), f32),
-            pltpu.VMEM((depth, SUB, LANES), bf16),
-            pltpu.VMEM((devices,) + block, bf16),
-            dma((9 + PARTS + 2 * devices,)),
-        ],
-        compiler_params=most,
-        name="pack_rows",
-    )(
-        turn,
-        owner,
-        row_owner.reshape(1, rows),
-        row_slot.reshape(1, rows),
-        visibilities,
-        coarse,
-        weights,
-        offset,
-        pairs,
-    )
-
+    small = shape((SUB, channels), f32)
+    if halves:
+        length = {x: rows_at + (depth if x in with_gains(near) else 0) for x in range(devices)}
+        ahead = [near, near + 1, near + 2]
+        behind = [x for x in range(devices) if x not in ahead]
+        sent = dict(zip(ahead, pack(ahead, [shape((length[x], parts, LANES), bf16) for x in ahead])))
+        *others, small = pack(
+            behind, [shape((length[x], parts, LANES), bf16) for x in behind] + [small]
+        )
+        sent.update(zip(behind, others))
+    else:
+        outs = [shape((devices,) + block, bf16), shape((depth, SUB, LANES), bf16)]
+        *sent, small = pack([0, 1], outs + [small])
 
     def swap(array, x):
         return lax.ppermute(array, "bl", [(d, d ^ x) for d in range(devices)])
@@ -507,7 +517,7 @@
         ],
         compiler_params=some,
         name="gains_and_sums",
-    )(turn, me, sent[-1], *[arrived[x] for x in order], *passed)
+    )(turn, me, small, *[arrived[x] for x in order], *passed)
     return pl.pallas_call(
         functools.partial(finish_kernel, capacity, late),
         out_shape=shape((owned, parts, channels), bf16),

time: 49.7 us -> 52 us (1.046)
  the two profiles are of different devices: /device:TPU:0 before, /device:TPU:9 now
where the time goes in v2:
time: 52 us; the launch traced here: 51.8 us
  starting transfers between devices  28 us (54%)
  Pallas kernels  12.3 us (24%)
  waiting for transfers between devices  9.75 us (19%)
  local copies, waits for them, and re-layouts  1.6 us (3%)
    ppermute x16, starting transfers between devices, swap(): return lax.ppermute(array, 'bl', [(d, d ^ x) for d in range(devices)])  28 us
    ppermute x16, waiting for transfers between devices, swap(): return lax.ppermute(array, 'bl', [(d, d ^ x) for d in range(devices)])  9.75 us
    pallas_call x2, Pallas kernels, pack(): pl.pallas_call(functools.partial(pack_kernel, capacity, near, targets), o...  5.96 us
    pallas_call x1, Pallas kernels, on_device(): pl.pallas_call(functools.partial(middle_kernel, capacity, near, stations,...  4.14 us
    pallas_call x1, Pallas kernels, on_device(): pl.pallas_call(functools.partial(finish_kernel, capacity, late), out_shap...  2.14 us
    unnamed x4, local copies, waits for them, and re-layouts  1.6 us
  transfers between devices with their start and end apart: 16, of which 7 were waited for; matrix products, arithmetic and copies ran while one was open for 0% of the time, Pallas kernels for 14%

profile of v2, /device:TPU:9, one launch (start us, length us, event | category | flops | bytes accessed | tf_op | source)
XLA Modules:
  0.0 51.8 jit_solution(5228608168552308051)
XLA Ops:
  0.0 2.8 %pack_rows.3 = (bf16[53,8,128]{2,1,0:T(8,128)(2,1)}, bf16[48,8,128]{2,1,0:T(8,128)(2,1)}, bf16[53,8,128]{2,1,0:T(8,128)(2,1)}) custom-call(s32[1]{0:T(128)} %bitcast.me_s.turn_s, s32[128]{0:T(128)} %bitcast.16, s32[1,128]{1,0:T(1,128)} %bitcast.17, s32[1,128]{1,0:T(1,128)} %bitcast.22, bf16[128,8,384]{2,1,0:T(8,128)(2,1)} %vis_hbm.3, f32[48,32]{1,0:T(8,128)} %bitcast.10, ...), custom_call_target="tpu_custom_call" | custom-call | tf_op jit(solution)/shard_map/pack_rows/pallas_call | solution.py:420
  2.8 2.9 %collective-permute-start.11 = (bf16[48,8,128]{2,1,0:T(8,128)(2,1)}, bf16[48,8,128]{2,1,0:T(8,128)(2,1)S(1)}, u32[]{:S(2)}, u32[]{:S(2)}) collective-permute-start(bf16[48,8,128]{2,1,0:T(8,128)(2,1)} %get-tuple-element.39), channel_id=1, source_target_pairs={{0,9},{1,8},{2,11},{3,10},{4,13},{5,12},{6,15},{7,14},{8,1},{9,0},... | collective-permute-start | bytes 294920 | tf_op jit(solution)/shard_map/ppermute | solution.py:474
  5.8 3.3 %collective-permute-start.1 = (bf16[53,8,128]{2,1,0:T(8,128)(2,1)}, bf16[53,8,128]{2,1,0:T(8,128)(2,1)S(1)}, u32[]{:S(2)}, u32[]{:S(2)}) collective-permute-start(bf16[53,8,128]{2,1,0:T(8,128)(2,1)} %get-tuple-element.29), channel_id=1, source_target_pairs={{0,10},{1,11},{2,8},{3,9},{4,14},{5,15},{6,12},{7,13},{8,2},{9,3},... | collective-permute-start | bytes 325640 | tf_op jit(solution)/shard_map/ppermute | solution.py:474
  9.1 3.1 %pack_rows.2 = (bf16[53,8,128]{2,1,0:T(8,128)(2,1)}, bf16[53,8,128]{2,1,0:T(8,128)(2,1)}, bf16[53,8,128]{2,1,0:T(8,128)(2,1)}, bf16[53,8,128]{2,1,0:T(8,128)(2,1...) custom-call(s32[1]{0:T(128)} %bitcast.me_s.turn_s, ...), custom_call_target="tpu_custom_call" | custom-call | tf_op jit(solution)/shard_map/pack_rows/pallas_call | solution.py:420
  12.5 1.8 %collective-permute-start.3 = (bf16[53,8,128]{2,1,0:T(8,128)(2,1)}, bf16[53,8,128]{2,1,0:T(8,128)(2,1)S(1)}, u32[]{:S(2)}, u32[]{:S(2)}) collective-permute-start(bf16[53,8,128]{2,1,0:T(8,128)(2,1)} %get-tuple-element.31), channel_id=1, source_target_pairs={{0,5},{1,4},{2,7},{3,6},{4,1},{5,0},{6,3},{7,2},{8,13},{9,12},{10,... | collective-permute-start | bytes 325640 | tf_op jit(solution)/shard_map/ppermute | solution.py:474
  14.3 1.1 %collective-permute-done.11.rest_12_ = bf16[48,8,128]{2,1,0:T(8,128)(2,1)S(1)} collective-permute-done((bf16[48,8,128]{2,1,0:T(8,128)(2,1)}, bf16[48,8,128]{2,1,0:T(8,128)(2,1)S(1)}, u32[]{:S(2)}, u32[]{:S(2)}) %collective-permute-start.11) | collective-permute-done | bytes 98336 | tf_op jit(solution)/shard_map/ppermute | solution.py:474
  15.4 2.3 %collective-permute-done.rest_0_.rest_1_ = bf16[53,8,128]{2,1,0:T(8,128)(2,1)S(1)} collective-permute-done((bf16[53,8,128]{2,1,0:T(8,128)(2,1)}, bf16[53,8,128]{2,1,0:T(8,128)(2,1)S(1)}, u32[]{:S(2)}, u32[]{:S(2)}) %collective-permute-start) | collective-permute-done | bytes 108576 | tf_op jit(solution)/shard_map/ppermute | solution.py:474
  17.7 2.8 %collective-permute-start.5 = (bf16[53,8,128]{2,1,0:T(8,128)(2,1)}, bf16[53,8,128]{2,1,0:T(8,128)(2,1)S(1)}, u32[]{:S(2)}, u32[]{:S(2)}) collective-permute-start(bf16[53,8,128]{2,1,0:T(8,128)(2,1)} %get-tuple-element.33), channel_id=1, source_target_pairs={{0,6},{1,7},{2,4},{3,5},{4,2},{5,3},{6,0},{7,1},{8,14},{9,15},{10,... | collective-permute-start | bytes 325640 | tf_op jit(solution)/shard_map/ppermute | solution.py:474
  20.5 1.4 %collective-permute-start.6 = (bf16[53,8,128]{2,1,0:T(8,128)(2,1)}, bf16[53,8,128]{2,1,0:T(8,128)(2,1)S(1)}, u32[]{:S(2)}, u32[]{:S(2)}) collective-permute-start(bf16[53,8,128]{2,1,0:T(8,128)(2,1)} %get-tuple-element.34), channel_id=1, source_target_pairs={{0,14},{1,15},{2,12},{3,13},{4,10},{5,11},{6,8},{7,9},{8,6},{9,7},... | collective-permute-start | bytes 325640 | tf_op jit(solution)/shard_map/ppermute | solution.py:474
  21.9 0.7 %collective-permute-done.2.rest_3_ = bf16[53,8,128]{2,1,0:T(8,128)(2,1)S(1)} collective-permute-done((bf16[53,8,128]{2,1,0:T(8,128)(2,1)}, bf16[53,8,128]{2,1,0:T(8,128)(2,1)S(1)}, u32[]{:S(2)}, u32[]{:S(2)}) %collective-permute-start.2) | collective-permute-done | bytes 108576 | tf_op jit(solution)/shard_map/ppermute | solution.py:474
  22.6 4.1 %collective-permute-start.7 = (bf16[53,8,128]{2,1,0:T(8,128)(2,1)}, bf16[53,8,128]{2,1,0:T(8,128)(2,1)S(1)}, u32[]{:S(2)}, u32[]{:S(2)}) collective-permute-start(bf16[53,8,128]{2,1,0:T(8,128)(2,1)} %get-tuple-element.35), channel_id=1, source_target_pairs={{0,7},{1,6},{2,5},{3,4},{4,3},{5,2},{6,1},{7,0},{8,15},{9,14},{10,... | collective-permute-start | bytes 325640 | tf_op jit(solution)/shard_map/ppermute | solution.py:474
  26.7 1.2 %collective-permute-start.8 = (bf16[53,8,128]{2,1,0:T(8,128)(2,1)}, bf16[53,8,128]{2,1,0:T(8,128)(2,1)S(1)}, u32[]{:S(2)}, u32[]{:S(2)}) collective-permute-start(bf16[53,8,128]{2,1,0:T(8,128)(2,1)} %get-tuple-element.36), channel_id=1, source_target_pairs={{0,1},{1,0},{2,3},{3,2},{4,5},{5,4},{6,7},{7,6},{8,9},{9,8},{10,11... | collective-permute-start | bytes 325640 | tf_op jit(solution)/shard_map/ppermute | solution.py:474
  28.4 1.2 %collective-permute-done.5.rest_6_ = bf16[53,8,128]{2,1,0:T(8,128)(2,1)S(1)} collective-permute-done((bf16[53,8,128]{2,1,0:T(8,128)(2,1)}, bf16[53,8,128]{2,1,0:T(8,128)(2,1)S(1)}, u32[]{:S(2)}, u32[]{:S(2)}) %collective-permute-start.5) | collective-permute-done | bytes 108576 | tf_op jit(solution)/shard_map/ppermute | solution.py:474
  29.6 1.6 %collective-permute-start.10 = (bf16[53,8,128]{2,1,0:T(8,128)(2,1)}, bf16[53,8,128]{2,1,0:T(8,128)(2,1)S(1)}, u32[]{:S(2)}, u32[]{:S(2)}) collective-permute-start(bf16[53,8,128]{2,1,0:T(8,128)(2,1)} %get-tuple-element.38), channel_id=1, source_target_pairs={{0,3},{1,2},{2,1},{3,0},{4,7},{5,6},{6,5},{7,4},{8,11},{9,10},{10,... | collective-permute-start | bytes 325640 | tf_op jit(solution)/shard_map/ppermute | solution.py:474
  31.2 4.8 %collective-permute-start.13 = (bf16[48,8,128]{2,1,0:T(8,128)(2,1)}, bf16[48,8,128]{2,1,0:T(8,128)(2,1)S(1)}, u32[]{:S(2)}, u32[]{:S(2)}) collective-permute-start(bf16[48,8,128]{2,1,0:T(8,128)(2,1)} %get-tuple-element.44), channel_id=1, source_target_pairs={{0,11},{1,10},{2,9},{3,8},{4,15},{5,14},{6,13},{7,12},{8,3},{9,2},... | collective-permute-start | bytes 294920 | tf_op jit(solution)/shard_map/ppermute | solution.py:474
  36.2 1.4 %collective-permute-start.15 = (bf16[48,8,128]{2,1,0:T(8,128)(2,1)}, bf16[48,8,128]{2,1,0:T(8,128)(2,1)S(1)}, u32[]{:S(2)}, u32[]{:S(2)}) collective-permute-start(bf16[48,8,128]{2,1,0:T(8,128)(2,1)} %get-tuple-element.46), channel_id=1, source_target_pairs={{0,15},{1,14},{2,13},{3,12},{4,11},{5,10},{6,9},{7,8},{8,7},{9,6},... | collective-permute-start | bytes 294920 | tf_op jit(solution)/shard_map/ppermute | solution.py:474
  37.6 1.8 %collective-permute-start.12 = (bf16[20,8,128]{2,1,0:T(8,128)(2,1)S(1)}, bf16[20,8,128]{2,1,0:T(8,128)(2,1)S(1)}, u32[]{:S(2)}, u32[]{:S(2)}) collective-permute-start(bf16[20,8,128]{2,1,0:T(8,128)(2,1)S(1)} %collect_gains.1), channel_id=1, source_target_pairs={{0,1},{1,0},{2,3},{3,2},{4,5},{5,4},{6,7},{7,6},{8,9},{9,8},{10,11... | collective-permute-start | bytes 122888 | tf_op jit(solution)/shard_map/ppermute | solution.py:474
  39.5 0.9 %collective-permute-done.12.rest_13_ = bf16[20,8,128]{2,1,0:T(8,128)(2,1)S(1)} collective-permute-done((bf16[20,8,128]{2,1,0:T(8,128)(2,1)S(1)}, bf16[20,8,128]{2,1,0:T(8,128)(2,1)S(1)}, u32[]{:S(2)}, u32[]{:S(2)}) %collective-permute-start.12) | collective-permute-done | bytes 40992 | tf_op jit(solution)/shard_map/ppermute | solution.py:474
  40.3 0.9 %copy-done = bf16[53,8,128]{2,1,0:T(8,128)(2,1)S(1)} copy-done((bf16[53,8,128]{2,1,0:T(8,128)(2,1)S(1)}, bf16[53,8,128]{2,1,0:T(8,128)(2,1)}, u32[]{:S(2)}) %copy-start) | copy-done | bytes 108568
  41.2 0.7 %copy-done.1 = f32[8,384]{1,0:T(8,128)S(1)} copy-done((f32[8,384]{1,0:T(8,128)S(1)}, f32[8,384]{1,0:T(8,128)}, u32[]{:S(2)}) %copy-start.1) | copy-done | bytes 12312
  41.9 4.1 %gains_and_sums.1 = (f32[8,128,384]{2,1,0:T(8,128)S(1)}, f32[64,128]{1,0:T(8,128)S(1)}, s32[16,128]{1,0:T(8,128)S(1)}, f32[3,64,8,128]{3,2,1,0:T(8,128)S(1)}) custom-call(s32[1]{0:T(128)} %bitcast.me_s.turn_s, s32[1]{0:T(128)} %bitcast.me_s.turn_s, f32[8,384]{1,0:T(8,128)S(1)} %copy-done.1, bf16[53,8,128]{2,1,0:T(8,128)(2,1)S(1)} %copy-done, ...), custom_call_target="tpu_custom_call" | custom-call | tf_op jit(solution)/shard_map/gains_and_sums/pallas_call | solution.py:497
  46.1 0.9 %collective-permute-done.14.rest_1_ = bf16[48,8,128]{2,1,0:T(8,128)(2,1)S(1)} collective-permute-done((bf16[48,8,128]{2,1,0:T(8,128)(2,1)}, bf16[48,8,128]{2,1,0:T(8,128)(2,1)S(1)}, u32[]{:S(2)}, u32[]{:S(2)}) %collective-permute-start.14) | collective-permute-done | bytes 98336 | tf_op jit(solution)/shard_map/ppermute | solution.py:474
  47.0 2.6 %collective-permute-done.15.rest_2_ = bf16[48,8,128]{2,1,0:T(8,128)(2,1)S(1)} collective-permute-done((bf16[48,8,128]{2,1,0:T(8,128)(2,1)}, bf16[48,8,128]{2,1,0:T(8,128)(2,1)S(1)}, u32[]{:S(2)}, u32[]{:S(2)}) %collective-permute-start.15) | collective-permute-done | bytes 98336 | tf_op jit(solution)/shard_map/ppermute | solution.py:474
  49.6 2.1 %sum_and_apply.1 = bf16[64,8,384]{2,1,0:T(8,128)(2,1)} custom-call(s32[16,128]{1,0:T(8,128)S(1)} %get-tuple-element.40.slots_s, f32[8,128,384]{2,1,0:T(8,128)S(1)} %get-tuple-element.41.gains_ref, f32[64,128]{1,0:T(8,128)S(1)} %get-tuple-element.42.recip_ref, f32[3,64,8,128]{3,2,1,0:T(8,128)S(1)} %get-tuple-element.43.sums_ref, ...), custom_call_target="tpu_custom_call" | custom-call | tf_op jit(solution)/shard_map/sum_and_apply/pallas_call | solution.py:521
  (17 shorter events, 1.0 us)
Async XLA Ops:
  2.8 12.6 %collective-permute-start.11 = (bf16[48,8,128]{2,1,0:T(8,128)(2,1)}, bf16[48,8,128]{2,1,0:T(8,128)(2,1)S(1)}, u32[]{:S(2)}, u32[]{:S(2)}) collective-permute-start(bf16[48,8,128]{2,1,0:T(8,128)(2,1)} %get-tuple-element.39), channel_id=1, source_target_pairs={{0,9},{1,8},{2,11},{3,10},{4,13},{5,12},{6,15},{7,14},{8,1},{9,0},... | collective-permute-start | bytes 294920 | tf_op jit(solution)/shard_map/ppermute | solution.py:474
  5.8 11.9 %collective-permute-start = (bf16[53,8,128]{2,1,0:T(8,128)(2,1)}, bf16[53,8,128]{2,1,0:T(8,128)(2,1)S(1)}, u32[]{:S(2)}, u32[]{:S(2)}) collective-permute-start(bf16[53,8,128]{2,1,0:T(8,128)(2,1)} %get-tuple-element.28), channel_id=1, source_target_pairs={{0,8},{1,9},{2,10},{3,11},{4,12},{5,13},{6,14},{7,15},{8,0},{9,1},... | collective-permute-start | bytes 325640 | tf_op jit(solution)/shard_map/ppermute | solution.py:474
  5.8 14.7 %collective-permute-start.1 = (bf16[53,8,128]{2,1,0:T(8,128)(2,1)}, bf16[53,8,128]{2,1,0:T(8,128)(2,1)S(1)}, u32[]{:S(2)}, u32[]{:S(2)}) collective-permute-start(bf16[53,8,128]{2,1,0:T(8,128)(2,1)} %get-tuple-element.29), channel_id=1, source_target_pairs={{0,10},{1,11},{2,8},{3,9},{4,14},{5,15},{6,12},{7,13},{8,2},{9,3},... | collective-permute-start | bytes 325640 | tf_op jit(solution)/shard_map/ppermute | solution.py:474
  12.3 10.3 %collective-permute-start.2 = (bf16[53,8,128]{2,1,0:T(8,128)(2,1)}, bf16[53,8,128]{2,1,0:T(8,128)(2,1)S(1)}, u32[]{:S(2)}, u32[]{:S(2)}) collective-permute-start(bf16[53,8,128]{2,1,0:T(8,128)(2,1)} %get-tuple-element.30), channel_id=1, source_target_pairs={{0,4},{1,5},{2,6},{3,7},{4,0},{5,1},{6,2},{7,3},{8,12},{9,13},{10,... | collective-permute-start | bytes 325640 | tf_op jit(solution)/shard_map/ppermute | solution.py:474
  12.5 14.2 %collective-permute-start.3 = (bf16[53,8,128]{2,1,0:T(8,128)(2,1)}, bf16[53,8,128]{2,1,0:T(8,128)(2,1)S(1)}, u32[]{:S(2)}, u32[]{:S(2)}) collective-permute-start(bf16[53,8,128]{2,1,0:T(8,128)(2,1)} %get-tuple-element.31), channel_id=1, source_target_pairs={{0,5},{1,4},{2,7},{3,6},{4,1},{5,0},{6,3},{7,2},{8,13},{9,12},{10,... | collective-permute-start | bytes 325640 | tf_op jit(solution)/shard_map/ppermute | solution.py:474
  15.4 12.5 %collective-permute-start.4 = (bf16[53,8,128]{2,1,0:T(8,128)(2,1)}, bf16[53,8,128]{2,1,0:T(8,128)(2,1)S(1)}, u32[]{:S(2)}, u32[]{:S(2)}) collective-permute-start(bf16[53,8,128]{2,1,0:T(8,128)(2,1)} %get-tuple-element.32), channel_id=1, source_target_pairs={{0,12},{1,13},{2,14},{3,15},{4,8},{5,9},{6,10},{7,11},{8,4},{9,5},... | collective-permute-start | bytes 325640 | tf_op jit(solution)/shard_map/ppermute | solution.py:474
  17.7 11.9 %collective-permute-start.5 = (bf16[53,8,128]{2,1,0:T(8,128)(2,1)}, bf16[53,8,128]{2,1,0:T(8,128)(2,1)S(1)}, u32[]{:S(2)}, u32[]{:S(2)}) collective-permute-start(bf16[53,8,128]{2,1,0:T(8,128)(2,1)} %get-tuple-element.33), channel_id=1, source_target_pairs={{0,6},{1,7},{2,4},{3,5},{4,2},{5,3},{6,0},{7,1},{8,14},{9,15},{10,... | collective-permute-start | bytes 325640 | tf_op jit(solution)/shard_map/ppermute | solution.py:474
  20.5 10.6 %collective-permute-start.6 = (bf16[53,8,128]{2,1,0:T(8,128)(2,1)}, bf16[53,8,128]{2,1,0:T(8,128)(2,1)S(1)}, u32[]{:S(2)}, u32[]{:S(2)}) collective-permute-start(bf16[53,8,128]{2,1,0:T(8,128)(2,1)} %get-tuple-element.34), channel_id=1, source_target_pairs={{0,14},{1,15},{2,12},{3,13},{4,10},{5,11},{6,8},{7,9},{8,6},{9,7},... | collective-permute-start | bytes 325640 | tf_op jit(solution)/shard_map/ppermute | solution.py:474
  22.6 13.4 %collective-permute-start.7 = (bf16[53,8,128]{2,1,0:T(8,128)(2,1)}, bf16[53,8,128]{2,1,0:T(8,128)(2,1)S(1)}, u32[]{:S(2)}, u32[]{:S(2)}) collective-permute-start(bf16[53,8,128]{2,1,0:T(8,128)(2,1)} %get-tuple-element.35), channel_id=1, source_target_pairs={{0,7},{1,6},{2,5},{3,4},{4,3},{5,2},{6,1},{7,0},{8,15},{9,14},{10,... | collective-permute-start | bytes 325640 | tf_op jit(solution)/shard_map/ppermute | solution.py:474
  26.7 9.5 %collective-permute-start.8 = (bf16[53,8,128]{2,1,0:T(8,128)(2,1)}, bf16[53,8,128]{2,1,0:T(8,128)(2,1)S(1)}, u32[]{:S(2)}, u32[]{:S(2)}) collective-permute-start(bf16[53,8,128]{2,1,0:T(8,128)(2,1)} %get-tuple-element.36), channel_id=1, source_target_pairs={{0,1},{1,0},{2,3},{3,2},{4,5},{5,4},{6,7},{7,6},{8,9},{9,8},{10,11... | collective-permute-start | bytes 325640 | tf_op jit(solution)/shard_map/ppermute | solution.py:474
  27.9 9.7 %collective-permute-start.9 = (bf16[53,8,128]{2,1,0:T(8,128)(2,1)}, bf16[53,8,128]{2,1,0:T(8,128)(2,1)S(1)}, u32[]{:S(2)}, u32[]{:S(2)}) collective-permute-start(bf16[53,8,128]{2,1,0:T(8,128)(2,1)} %get-tuple-element.37), channel_id=1, source_target_pairs={{0,2},{1,3},{2,0},{3,1},{4,6},{5,7},{6,4},{7,5},{8,10},{9,11},{10,... | collective-permute-start | bytes 325640 | tf_op jit(solution)/shard_map/ppermute | solution.py:474
  29.6 9.9 %collective-permute-start.10 = (bf16[53,8,128]{2,1,0:T(8,128)(2,1)}, bf16[53,8,128]{2,1,0:T(8,128)(2,1)S(1)}, u32[]{:S(2)}, u32[]{:S(2)}) collective-permute-start(bf16[53,8,128]{2,1,0:T(8,128)(2,1)} %get-tuple-element.38), channel_id=1, source_target_pairs={{0,3},{1,2},{2,1},{3,0},{4,7},{5,6},{6,5},{7,4},{8,11},{9,10},{10,... | collective-permute-start | bytes 325640 | tf_op jit(solution)/shard_map/ppermute | solution.py:474
  31.2 14.9 %collective-permute-start.13 = (bf16[48,8,128]{2,1,0:T(8,128)(2,1)}, bf16[48,8,128]{2,1,0:T(8,128)(2,1)S(1)}, u32[]{:S(2)}, u32[]{:S(2)}) collective-permute-start(bf16[48,8,128]{2,1,0:T(8,128)(2,1)} %get-tuple-element.44), channel_id=1, source_target_pairs={{0,11},{1,10},{2,9},{3,8},{4,15},{5,14},{6,13},{7,12},{8,3},{9,2},... | collective-permute-start | bytes 294920 | tf_op jit(solution)/shard_map/ppermute | solution.py:474
  36.0 11.1 %collective-permute-start.14 = (bf16[48,8,128]{2,1,0:T(8,128)(2,1)}, bf16[48,8,128]{2,1,0:T(8,128)(2,1)S(1)}, u32[]{:S(2)}, u32[]{:S(2)}) collective-permute-start(bf16[48,8,128]{2,1,0:T(8,128)(2,1)} %get-tuple-element.45), channel_id=1, source_target_pairs={{0,13},{1,12},{2,15},{3,14},{4,9},{5,8},{6,11},{7,10},{8,5},{9,4},... | collective-permute-start | bytes 294920 | tf_op jit(solution)/shard_map/ppermute | solution.py:474
  36.2 13.4 %collective-permute-start.15 = (bf16[48,8,128]{2,1,0:T(8,128)(2,1)}, bf16[48,8,128]{2,1,0:T(8,128)(2,1)S(1)}, u32[]{:S(2)}, u32[]{:S(2)}) collective-permute-start(bf16[48,8,128]{2,1,0:T(8,128)(2,1)} %get-tuple-element.46), channel_id=1, source_target_pairs={{0,15},{1,14},{2,13},{3,12},{4,11},{5,10},{6,9},{7,8},{8,7},{9,6},... | collective-permute-start | bytes 294920 | tf_op jit(solution)/shard_map/ppermute | solution.py:474
  37.6 2.7 %collective-permute-start.12 = (bf16[20,8,128]{2,1,0:T(8,128)(2,1)S(1)}, bf16[20,8,128]{2,1,0:T(8,128)(2,1)S(1)}, u32[]{:S(2)}, u32[]{:S(2)}) collective-permute-start(bf16[20,8,128]{2,1,0:T(8,128)(2,1)S(1)} %collect_gains.1), channel_id=1, source_target_pairs={{0,1},{1,0},{2,3},{3,2},{4,5},{5,4},{6,7},{7,6},{8,9},{9,8},{10,11... | collective-permute-start | bytes 122888 | tf_op jit(solution)/shard_map/ppermute | solution.py:474
  40.3 0.9 %copy-start = (bf16[53,8,128]{2,1,0:T(8,128)(2,1)S(1)}, bf16[53,8,128]{2,1,0:T(8,128)(2,1)}, u32[]{:S(2)}) copy-start(bf16[53,8,128]{2,1,0:T(8,128)(2,1)} %get-tuple-element.27.rest_0_) | copy-start | bytes 325636
  41.2 0.7 %copy-start.1 = (f32[8,384]{1,0:T(8,128)S(1)}, f32[8,384]{1,0:T(8,128)}, u32[]{:S(2)}) copy-start(f32[8,384]{1,0:T(8,128)} %get-tuple-element.26.small_ref) | copy-start | bytes 36868

commit v3 on v1

--- a/solution.py
+++ b/solution.py
@@ -166,22 +166,24 @@
         send.wait()
 
 
-def interpolation(small):
+def ready_kernel(small_ref, own_ref, held_ref, own_out_ref, held_out_ref, high_ref, low_ref, pairs_ref, sems):
+    moves = start_all([(own_ref, own_out_ref), (held_ref, held_out_ref)], sems)
+    small = small_ref[...]
     channels = small.shape[1]
+    pairs_ref[...] = small[:, 0:LANES].astype(jnp.int32)
     index = lax.broadcasted_iota(jnp.int32, (LANES, channels), 0)
     knot = ((index & 63) >> 3).astype(jnp.float32)
     basis = jnp.zeros((LANES, channels), jnp.float32)
     for step in range(3):
         basis = basis + jnp.where(knot == small[3:4, :] + float(step), small[step : step + 1, :], 0.0)
     high = basis.astype(jnp.bfloat16).astype(jnp.float32)
+    low = basis - high
     part = index & 7
-    return [
-        (
-            jnp.where(part == j, high, 0.0).astype(jnp.bfloat16),
-            jnp.where(part == j, basis - high, 0.0).astype(jnp.bfloat16),
-        )
-        for j in range(8)
-    ]
+    for j in range(8):
+        high_ref[j] = jnp.where(part == j, high, 0.0).astype(jnp.bfloat16)
+        low_ref[j] = jnp.where(part == j, low, 0.0).astype(jnp.bfloat16)
+    for move in moves:
+        move.wait()
 
 
 def collect_kernel(at, depth, *rest):
@@ -248,19 +250,15 @@
     return hits
 
 
-def middle_kernel(capacity, near, stations, order, turn_s, me_s, small_ref, *rest):
-    arrived, passed = dict(zip(order, rest)), rest[len(order) : -13]
-    gains_ref, recip_ref, slots_ref, sums_ref = rest[-13:-9]
-    table_ref, pick_ref, owner_ref, slot_ref, slots_v, slots_s, pairs_v, pairs_s, sems = rest[-9:]
+def middle_kernel(capacity, near, stations, order, turn_s, me_s, pairs_s, high_ref, low_ref, *rest):
+    arrived, passed = dict(zip(order, rest)), rest[len(order) : -11]
+    gains_ref, recip_ref, slots_ref, sums_ref = rest[-11:-7]
+    table_ref, pick_ref, owner_ref, slot_ref, slots_v, slots_s, sem = rest[-7:]
     devices = table_ref.shape[0]
     owned = recip_ref.shape[0]
     chunks = sums_ref.shape[0]
     half = stations // 2
     depth = 2 * (table_ref.shape[1] // SUB) + 1
-    small = small_ref[...]
-    pairs_v[...] = small[0:SUB, 0:LANES].astype(jnp.int32)
-    scalars = [pltpu.make_async_copy(pairs_v, pairs_s, sems.at[0])]
-    scalars[0].start()
     for x in range(devices):
         if near == 1:
             code = add_table(table_ref, x, arrived[0].at[x], 0, depth)
@@ -274,13 +272,12 @@
     listing, mine = list_rows(owner_ref[...], slot, me_s[0].astype(jnp.float32), capacity)
     slots_ref[...] = listing
     slots_v[...] = listing
-    scalars.append(pltpu.make_async_copy(slots_v, slots_s, sems.at[1]))
-    scalars[1].start()
+    move = pltpu.make_async_copy(slots_v, slots_s, sem)
+    move.start()
     hits = count_rows(jnp.zeros((owned, LANES), jnp.float32), mine, slot)
     tally = jnp.sum(hits, axis=1, keepdims=True)
     recip_ref[...] = jnp.broadcast_to(1.0 / jnp.maximum(tally, 1.0), recip_ref.shape)
 
-    scalars[0].wait()
     turn = turn_s[0]
     column = lax.broadcasted_iota(jnp.int32, (1, LANES), 1)
     used = (column & 63) < USED
@@ -302,14 +299,15 @@
     both_high = both.astype(jnp.bfloat16)
     both_low = (both - both_high.astype(jnp.float32)).astype(jnp.bfloat16)
     both_two = jnp.concatenate([both_high, both_low], axis=1)
-    for j, (high, low) in enumerate(interpolation(small)):
+    for j in range(8):
+        high, low = high_ref[j], low_ref[j]
         fine = jnp.dot(
             both_two, jnp.concatenate([high, high], axis=0), preferred_element_type=jnp.float32
         ) + jnp.dot(both_high, low, preferred_element_type=jnp.float32)
         gains_ref[j] = fine.astype(jnp.bfloat16).astype(jnp.float32)
 
     sums_ref[...] = jnp.zeros_like(sums_ref)
-    scalars[1].wait()
+    move.wait()
     if near > 1:
         for x in order:
             add_rows(sums_ref, slots_s, x, capacity, arrived[x])
@@ -460,11 +458,31 @@
     )
 
 
+    def ready(own, held):
+        return pl.pallas_call(
+            ready_kernel,
+            out_shape=[
+                shape(own.shape, bf16),
+                shape(held.shape, bf16),
+                shape((parts, LANES, channels), bf16),
+                shape((parts, LANES, channels), bf16),
+                shape((SUB, LANES), i32),
+            ],
+            in_specs=[vmem, anywhere, anywhere],
+            out_specs=[vmem] * 5,
+            scratch_shapes=[dma((2,))],
+            compiler_params=some,
+            name="make_ready",
+        )(sent[-1], own, held)
+
     def swap(array, x):
         return lax.ppermute(array, "bl", [(d, d ^ x) for d in range(devices)])
 
     if halves:
-        arrived = {x: swap(sent[x], x) if x else sent[x] for x in range(devices)}
+        held = near + 2
+        own, through, high, low, ints = ready(sent[0], sent[held])
+        arrived = {0: own, held: swap(through, held)}
+        arrived.update({x: swap(sent[x], x) for x in range(1, devices) if x != held})
         order, late = schedule(near)
         even = list(range(near, devices, 2))
         collected = pl.pallas_call(
@@ -483,6 +501,7 @@
             1: lax.all_to_all(sent[0], "bl", split_axis=0, concat_axis=0, tiled=True),
         }
         order, late, passed = [0], [1], []
+        _, _, high, low, ints = ready(sent[1], sent[1])
 
     gains, recip, slots, sums = pl.pallas_call(
         functools.partial(middle_kernel, capacity, near, stations, order),
@@ -492,7 +511,7 @@
             shape((devices, LANES), i32),
             shape((chunks, owned, parts, LANES), f32),
         ),
-        in_specs=[smem] * 2 + [vmem] * (1 + len(order) + len(passed)),
+        in_specs=[smem] * 3 + [vmem] * (2 + len(order) + len(passed)),
         out_specs=(vmem,) * 4,
         scratch_shapes=[
             pltpu.VMEM((devices, gain_tiles * SUB, LANES), f32),
@@ -501,13 +520,11 @@
             pltpu.VMEM((devices, LANES), f32),
             pltpu.VMEM((devices, LANES), i32),
             pltpu.SMEM((devices, LANES), i32),
-            pltpu.VMEM((SUB, LANES), i32),
-            pltpu.SMEM((SUB, LANES), i32),
-            dma((2,)),
+            dma,
         ],
         compiler_params=some,
         name="gains_and_sums",
-    )(turn, me, sent[-1], *[arrived[x] for x in order], *passed)
+    )(turn, me, ints, high, low, *[arrived[x] for x in order], *passed)
     return pl.pallas_call(
         functools.partial(finish_kernel, capacity, late),
         out_shape=shape((owned, parts, channels), bf16),

time: 49.7 us -> 50.1 us (level)
  Pallas kernels: 9.06 us -> 10.8 us
  starting transfers between devices: 28.1 us -> 26.8 us
  waiting for transfers between devices: 10.6 us -> 9.68 us
  local copies, waits for them, and re-layouts: 1.6 us -> 2.5 us
    ppermute x16, starting transfers between devices: 28.1 us -> 26.8 us  [swap(): return lax.ppermute(array, 'bl', [(d, d ^ x) for d in range(devices)])]
    pallas_call x1, Pallas kernels: 3.77 us -> 4.84 us  [on_device(): pl.pallas_call(functools.partial(middle_kernel, capacity, near, stations,...]
    unnamed x4 -> x6, local copies, waits for them, and re-layouts: 1.6 us -> 2.5 us
    ppermute x16, waiting for transfers between devices: 10.6 us -> 9.68 us  [swap(): return lax.ppermute(array, 'bl', [(d, d ^ x) for d in range(devices)])]
    pallas_call x0 -> x1, Pallas kernels: none -> 0.55 us  [ready(): pl.pallas_call(ready_kernel, out_shape=[shape(own.shape, bf16), shape(hel...]
  transfers between devices with their start and end apart: 16 -> 16, of which waited for: 7 -> 5; matrix products, arithmetic and copies ran while one was open for 0% -> 0% of each run, Pallas kernels for 8% -> 11%
where the time goes in v3:
time: 50.1 us; the launch traced here: 49.9 us
  starting transfers between devices  26.8 us (53%)
  Pallas kernels  10.8 us (22%)
  waiting for transfers between devices  9.68 us (19%)
  local copies, waits for them, and re-layouts  2.5 us (5%)
    ppermute x16, starting transfers between devices, swap(): return lax.ppermute(array, 'bl', [(d, d ^ x) for d in range(devices)])  26.8 us
    ppermute x16, waiting for transfers between devices, swap(): return lax.ppermute(array, 'bl', [(d, d ^ x) for d in range(devices)])  9.68 us
    pallas_call x1, Pallas kernels, on_device(): pl.pallas_call(functools.partial(middle_kernel, capacity, near, stations,...  4.84 us
    pallas_call x1, Pallas kernels, on_device(): pl.pallas_call(functools.partial(pack_kernel, capacity, near), out_shape=...  3.21 us
    unnamed x6, local copies, waits for them, and re-layouts  2.5 us
    pallas_call x1, Pallas kernels, on_device(): pl.pallas_call(functools.partial(finish_kernel, capacity, late), out_shap...  2.17 us
  transfers between devices with their start and end apart: 16, of which 5 were waited for; matrix products, arithmetic and copies ran while one was open for 0% of the time, Pallas kernels for 11%

profile of v3, /device:TPU:0, one launch (start us, length us, event | category | flops | bytes accessed | tf_op | source)
XLA Modules:
  0.0 49.9 jit_solution(11831426030629160593)
XLA Ops:
  0.0 3.2 %pack_rows.1 = (bf16[53,8,128]{2,1,0:T(8,128)(2,1)}, bf16[53,8,128]{2,1,0:T(8,128)(2,1)}, bf16[53,8,128]{2,1,0:T(8,128)(2,1)}, bf16[53,8,128]{2,1,0:T(8,128)(2,1...) custom-call(s32[1]{0:T(128)} %bitcast.me_s.turn_s, ...), custom_call_target="tpu_custom_call" | custom-call | tf_op jit(solution)/shard_map/pack_rows/pallas_call | solution.py:424
  3.2 3.5 %collective-permute-start.12 = (bf16[48,8,128]{2,1,0:T(8,128)(2,1)}, bf16[48,8,128]{2,1,0:T(8,128)(2,1)S(1)}, u32[]{:S(2)}, u32[]{:S(2)}) collective-permute-start(bf16[48,8,128]{2,1,0:T(8,128)(2,1)} %get-tuple-element.50), channel_id=1, source_target_pairs={{0,9},{1,8},{2,11},{3,10},{4,13},{5,12},{6,15},{7,14},{8,1},{9,0},... | collective-permute-start | bytes 294920 | tf_op jit(solution)/shard_map/ppermute | solution.py:479
  6.8 0.6 %collective-permute-start = (bf16[53,8,128]{2,1,0:T(8,128)(2,1)}, bf16[53,8,128]{2,1,0:T(8,128)(2,1)S(1)}, u32[]{:S(2)}, u32[]{:S(2)}) collective-permute-start(bf16[53,8,128]{2,1,0:T(8,128)(2,1)} %get-tuple-element.38), channel_id=1, source_target_pairs={{0,8},{1,9},{2,10},{3,11},{4,12},{5,13},{6,14},{7,15},{8,0},{9,1},... | collective-permute-start | bytes 325640 | tf_op jit(solution)/shard_map/ppermute | solution.py:479
  7.4 1.6 %collective-permute-start.2 = (bf16[53,8,128]{2,1,0:T(8,128)(2,1)}, bf16[53,8,128]{2,1,0:T(8,128)(2,1)S(1)}, u32[]{:S(2)}, u32[]{:S(2)}) collective-permute-start(bf16[53,8,128]{2,1,0:T(8,128)(2,1)} %get-tuple-element.40), channel_id=1, source_target_pairs={{0,4},{1,5},{2,6},{3,7},{4,0},{5,1},{6,2},{7,3},{8,12},{9,13},{10,... | collective-permute-start | bytes 325640 | tf_op jit(solution)/shard_map/ppermute | solution.py:479
  9.0 3.5 %collective-permute-start.4 = (bf16[53,8,128]{2,1,0:T(8,128)(2,1)}, bf16[53,8,128]{2,1,0:T(8,128)(2,1)S(1)}, u32[]{:S(2)}, u32[]{:S(2)}) collective-permute-start(bf16[53,8,128]{2,1,0:T(8,128)(2,1)} %get-tuple-element.42), channel_id=1, source_target_pairs={{0,12},{1,13},{2,14},{3,15},{4,8},{5,9},{6,10},{7,11},{8,4},{9,5},... | collective-permute-start | bytes 325640 | tf_op jit(solution)/shard_map/ppermute | solution.py:479
  12.5 4.6 %collective-permute-start.5 = (bf16[53,8,128]{2,1,0:T(8,128)(2,1)}, bf16[53,8,128]{2,1,0:T(8,128)(2,1)S(1)}, u32[]{:S(2)}, u32[]{:S(2)}) collective-permute-start(bf16[53,8,128]{2,1,0:T(8,128)(2,1)} %get-tuple-element.43), channel_id=1, source_target_pairs={{0,6},{1,7},{2,4},{3,5},{4,2},{5,3},{6,0},{7,1},{8,14},{9,15},{10,... | collective-permute-start | bytes 325640 | tf_op jit(solution)/shard_map/ppermute | solution.py:479
  17.4 4.8 %collective-permute-start.6 = (bf16[53,8,128]{2,1,0:T(8,128)(2,1)}, bf16[53,8,128]{2,1,0:T(8,128)(2,1)S(1)}, u32[]{:S(2)}, u32[]{:S(2)}) collective-permute-start(bf16[53,8,128]{2,1,0:T(8,128)(2,1)} %get-tuple-element.44), channel_id=1, source_target_pairs={{0,14},{1,15},{2,12},{3,13},{4,10},{5,11},{6,8},{7,9},{8,6},{9,7},... | collective-permute-start | bytes 325640 | tf_op jit(solution)/shard_map/ppermute | solution.py:479
  22.2 0.9 %copy-done = bf16[53,8,128]{2,1,0:T(8,128)(2,1)S(1)} copy-done((bf16[53,8,128]{2,1,0:T(8,128)(2,1)S(1)}, bf16[53,8,128]{2,1,0:T(8,128)(2,1)}, u32[]{:S(2)}) %copy-start) | copy-done | bytes 108568
  23.1 0.9 %copy-done.1 = bf16[53,8,128]{2,1,0:T(8,128)(2,1)S(1)} copy-done((bf16[53,8,128]{2,1,0:T(8,128)(2,1)S(1)}, bf16[53,8,128]{2,1,0:T(8,128)(2,1)}, u32[]{:S(2)}) %copy-start.1) | copy-done | bytes 108568
  24.0 0.7 %copy-done.2 = f32[8,384]{1,0:T(8,128)S(1)} copy-done((f32[8,384]{1,0:T(8,128)S(1)}, f32[8,384]{1,0:T(8,128)}, u32[]{:S(2)}) %copy-start.2) | copy-done | bytes 12312
  24.7 0.5 %make_ready.1 = (bf16[53,8,128]{2,1,0:T(8,128)(2,1)S(1)}, bf16[53,8,128]{2,1,0:T(8,128)(2,1)S(1)}, bf16[8,128,384]{2,1,0:T(8,128)(2,1)S(1)}, bf16[8,128,384]{2,1,0:T(8,128)(2,1)S(1)}, s32[8,128]{1,0:T(8,128)S(1)}) custom-call(f32[8,384]{1,0:T(8,128)S(1)} %copy-done.2, bf16[53,8,128]{2,1,0:T(8,128)(2,1)S(1)} %copy-done, bf16[53,8,128]{2,1,0:T(8,128)(2,1)S(1)} %copy-done.1), custom_call_target="tpu_custom_call" | custom-call | tf_op jit(solution)/shard_map/make_ready/pallas_call | solution.py:462
  25.3 1.8 %collective-permute-start.8 = (bf16[53,8,128]{2,1,0:T(8,128)(2,1)}, bf16[53,8,128]{2,1,0:T(8,128)(2,1)S(1)}, u32[]{:S(2)}, u32[]{:S(2)}) collective-permute-start(bf16[53,8,128]{2,1,0:T(8,128)(2,1)} %get-tuple-element.46), channel_id=1, source_target_pairs={{0,11},{1,10},{2,9},{3,8},{4,15},{5,14},{6,13},{7,12},{8,3},{9,2},... | collective-permute-start | bytes 325640 | tf_op jit(solution)/shard_map/ppermute | solution.py:479
  27.1 1.5 %collective-permute-start.1 = (bf16[53,8,128]{2,1,0:T(8,128)(2,1)S(1)}, bf16[53,8,128]{2,1,0:T(8,128)(2,1)S(1)}, u32[]{:S(2)}, u32[]{:S(2)}) collective-permute-start(bf16[53,8,128]{2,1,0:T(8,128)(2,1)S(1)} %get-tuple-element.39), channel_id=1, source_target_pairs={{0,10},{1,11},{2,8},{3,9},{4,14},{5,15},{6,12},{7,13},{8,2},{9,3},... | collective-permute-start | bytes 325640 | tf_op jit(solution)/shard_map/ppermute | solution.py:479
  29.0 0.5 %collective-permute-start.10 = (bf16[53,8,128]{2,1,0:T(8,128)(2,1)}, bf16[53,8,128]{2,1,0:T(8,128)(2,1)S(1)}, u32[]{:S(2)}, u32[]{:S(2)}) collective-permute-start(bf16[53,8,128]{2,1,0:T(8,128)(2,1)} %get-tuple-element.48), channel_id=1, source_target_pairs={{0,2},{1,3},{2,0},{3,1},{4,6},{5,7},{6,4},{7,5},{8,10},{9,11},{10,... | collective-permute-start | bytes 325640 | tf_op jit(solution)/shard_map/ppermute | solution.py:479
  29.6 0.9 %collective-permute-start.11 = (bf16[53,8,128]{2,1,0:T(8,128)(2,1)}, bf16[53,8,128]{2,1,0:T(8,128)(2,1)S(1)}, u32[]{:S(2)}, u32[]{:S(2)}) collective-permute-start(bf16[53,8,128]{2,1,0:T(8,128)(2,1)} %get-tuple-element.49), channel_id=1, source_target_pairs={{0,3},{1,2},{2,1},{3,0},{4,7},{5,6},{6,5},{7,4},{8,11},{9,10},{10,... | collective-permute-start | bytes 325640 | tf_op jit(solution)/shard_map/ppermute | solution.py:479
  30.5 6.9 %collective-permute-done.8.rest_9_ = bf16[53,8,128]{2,1,0:T(8,128)(2,1)S(1)} collective-permute-done((bf16[53,8,128]{2,1,0:T(8,128)(2,1)}, bf16[53,8,128]{2,1,0:T(8,128)(2,1)S(1)}, u32[]{:S(2)}, u32[]{:S(2)}) %collective-permute-start.8) | collective-permute-done | bytes 108576 | tf_op jit(solution)/shard_map/ppermute | solution.py:479
  37.4 1.3 %collective-permute-start.14 = (bf16[48,8,128]{2,1,0:T(8,128)(2,1)}, bf16[48,8,128]{2,1,0:T(8,128)(2,1)S(1)}, u32[]{:S(2)}, u32[]{:S(2)}) collective-permute-start(bf16[48,8,128]{2,1,0:T(8,128)(2,1)} %get-tuple-element.55), channel_id=1, source_target_pairs={{0,13},{1,12},{2,15},{3,14},{4,9},{5,8},{6,11},{7,10},{8,5},{9,4},... | collective-permute-start | bytes 294920 | tf_op jit(solution)/shard_map/ppermute | solution.py:479
  38.8 1.0 %collective-permute-done.1.rest_1_.rest_2_ = bf16[53,8,128]{2,1,0:T(8,128)(2,1)S(1)} collective-permute-done((bf16[53,8,128]{2,1,0:T(8,128)(2,1)S(1)}, bf16[53,8,128]{2,1,0:T(8,128)(2,1)S(1)}, u32[]{:S(2)}, u32[]{:S(2)}) %collective-permute-start.1) | collective-permute-done | bytes 108576 | tf_op jit(solution)/shard_map/ppermute | solution.py:479
  39.8 1.1 %collective-permute-start.15 = (bf16[48,8,128]{2,1,0:T(8,128)(2,1)}, bf16[48,8,128]{2,1,0:T(8,128)(2,1)S(1)}, u32[]{:S(2)}, u32[]{:S(2)}) collective-permute-start(bf16[48,8,128]{2,1,0:T(8,128)(2,1)} %get-tuple-element.56), channel_id=1, source_target_pairs={{0,15},{1,14},{2,13},{3,12},{4,11},{5,10},{6,9},{7,8},{8,7},{9,6},... | collective-permute-start | bytes 294920 | tf_op jit(solution)/shard_map/ppermute | solution.py:479
  40.9 0.5 %collective-permute-start.13 = (bf16[20,8,128]{2,1,0:T(8,128)(2,1)S(1)}, bf16[20,8,128]{2,1,0:T(8,128)(2,1)S(1)}, u32[]{:S(2)}, u32[]{:S(2)}) collective-permute-start(bf16[20,8,128]{2,1,0:T(8,128)(2,1)S(1)} %collect_gains.1), channel_id=1, source_target_pairs={{0,1},{1,0},{2,3},{3,2},{4,5},{5,4},{6,7},{7,6},{8,9},{9,8},{10,11... | collective-permute-start | bytes 122888 | tf_op jit(solution)/shard_map/ppermute | solution.py:479
  41.5 0.9 %collective-permute-done.13.rest_14_ = bf16[20,8,128]{2,1,0:T(8,128)(2,1)S(1)} collective-permute-done((bf16[20,8,128]{2,1,0:T(8,128)(2,1)S(1)}, bf16[20,8,128]{2,1,0:T(8,128)(2,1)S(1)}, u32[]{:S(2)}, u32[]{:S(2)}) %collective-permute-start.13) | collective-permute-done | bytes 40992 | tf_op jit(solution)/shard_map/ppermute | solution.py:479
  42.3 4.8 %gains_and_sums.1 = (f32[8,128,384]{2,1,0:T(8,128)S(1)}, f32[64,128]{1,0:T(8,128)S(1)}, s32[16,128]{1,0:T(8,128)S(1)}, f32[3,64,8,128]{3,2,1,0:T(8,128)S(1)}) custom-call(s32[1]{0:T(128)} %bitcast.me_s.turn_s, s32[1]{0:T(128)} %bitcast.me_s.turn_s, s32[8,128]{1,0:T(8,128)S(1)} %get-tuple-element.34.pairs_s, ...), custom_call_target="tpu_custom_call" | custom-call | tf_op jit(solution)/shard_map/gains_and_sums/pallas_call | solution.py:506
  47.2 0.5 %collective-permute-done.15.rest_1_ = bf16[48,8,128]{2,1,0:T(8,128)(2,1)S(1)} collective-permute-done((bf16[48,8,128]{2,1,0:T(8,128)(2,1)}, bf16[48,8,128]{2,1,0:T(8,128)(2,1)S(1)}, u32[]{:S(2)}, u32[]{:S(2)}) %collective-permute-start.15) | collective-permute-done | bytes 98336 | tf_op jit(solution)/shard_map/ppermute | solution.py:479
  47.7 2.2 %sum_and_apply.1 = bf16[64,8,384]{2,1,0:T(8,128)(2,1)} custom-call(s32[16,128]{1,0:T(8,128)S(1)} %get-tuple-element.51.slots_s, f32[8,128,384]{2,1,0:T(8,128)S(1)} %get-tuple-element.52.gains_ref, f32[64,128]{1,0:T(8,128)S(1)} %get-tuple-element.53.recip_ref, f32[3,64,8,128]{3,2,1,0:T(8,128)S(1)} %get-tuple-element.54.sums_ref, ...), custom_call_target="tpu_custom_call" | custom-call | tf_op jit(solution)/shard_map/sum_and_apply/pallas_call | solution.py:528
  (19 shorter events, 0.8 us)
Async XLA Ops:
  3.2 9.3 %collective-permute-start.12 = (bf16[48,8,128]{2,1,0:T(8,128)(2,1)}, bf16[48,8,128]{2,1,0:T(8,128)(2,1)S(1)}, u32[]{:S(2)}, u32[]{:S(2)}) collective-permute-start(bf16[48,8,128]{2,1,0:T(8,128)(2,1)} %get-tuple-element.50), channel_id=1, source_target_pairs={{0,9},{1,8},{2,11},{3,10},{4,13},{5,12},{6,15},{7,14},{8,1},{9,0},... | collective-permute-start | bytes 294920 | tf_op jit(solution)/shard_map/ppermute | solution.py:479
  6.8 10.7 %collective-permute-start = (bf16[53,8,128]{2,1,0:T(8,128)(2,1)}, bf16[53,8,128]{2,1,0:T(8,128)(2,1)S(1)}, u32[]{:S(2)}, u32[]{:S(2)}) collective-permute-start(bf16[53,8,128]{2,1,0:T(8,128)(2,1)} %get-tuple-element.38), channel_id=1, source_target_pairs={{0,8},{1,9},{2,10},{3,11},{4,12},{5,13},{6,14},{7,15},{8,0},{9,1},... | collective-permute-start | bytes 325640 | tf_op jit(solution)/shard_map/ppermute | solution.py:479
  7.4 14.8 %collective-permute-start.2 = (bf16[53,8,128]{2,1,0:T(8,128)(2,1)}, bf16[53,8,128]{2,1,0:T(8,128)(2,1)S(1)}, u32[]{:S(2)}, u32[]{:S(2)}) collective-permute-start(bf16[53,8,128]{2,1,0:T(8,128)(2,1)} %get-tuple-element.40), channel_id=1, source_target_pairs={{0,4},{1,5},{2,6},{3,7},{4,0},{5,1},{6,2},{7,3},{8,12},{9,13},{10,... | collective-permute-start | bytes 325640 | tf_op jit(solution)/shard_map/ppermute | solution.py:479
  9.0 16.3 %collective-permute-start.3 = (bf16[53,8,128]{2,1,0:T(8,128)(2,1)}, bf16[53,8,128]{2,1,0:T(8,128)(2,1)S(1)}, u32[]{:S(2)}, u32[]{:S(2)}) collective-permute-start(bf16[53,8,128]{2,1,0:T(8,128)(2,1)} %get-tuple-element.41), channel_id=1, source_target_pairs={{0,5},{1,4},{2,7},{3,6},{4,1},{5,0},{6,3},{7,2},{8,13},{9,12},{10,... | collective-permute-start | bytes 325640 | tf_op jit(solution)/shard_map/ppermute | solution.py:479
  9.0 18.1 %collective-permute-start.4 = (bf16[53,8,128]{2,1,0:T(8,128)(2,1)}, bf16[53,8,128]{2,1,0:T(8,128)(2,1)S(1)}, u32[]{:S(2)}, u32[]{:S(2)}) collective-permute-start(bf16[53,8,128]{2,1,0:T(8,128)(2,1)} %get-tuple-element.42), channel_id=1, source_target_pairs={{0,12},{1,13},{2,14},{3,15},{4,8},{5,9},{6,10},{7,11},{8,4},{9,5},... | collective-permute-start | bytes 325640 | tf_op jit(solution)/shard_map/ppermute | solution.py:479
  12.5 16.1 %collective-permute-start.5 = (bf16[53,8,128]{2,1,0:T(8,128)(2,1)}, bf16[53,8,128]{2,1,0:T(8,128)(2,1)S(1)}, u32[]{:S(2)}, u32[]{:S(2)}) collective-permute-start(bf16[53,8,128]{2,1,0:T(8,128)(2,1)} %get-tuple-element.43), channel_id=1, source_target_pairs={{0,6},{1,7},{2,4},{3,5},{4,2},{5,3},{6,0},{7,1},{8,14},{9,15},{10,... | collective-permute-start | bytes 325640 | tf_op jit(solution)/shard_map/ppermute | solution.py:479
  17.4 11.6 %collective-permute-start.6 = (bf16[53,8,128]{2,1,0:T(8,128)(2,1)}, bf16[53,8,128]{2,1,0:T(8,128)(2,1)S(1)}, u32[]{:S(2)}, u32[]{:S(2)}) collective-permute-start(bf16[53,8,128]{2,1,0:T(8,128)(2,1)} %get-tuple-element.44), channel_id=1, source_target_pairs={{0,14},{1,15},{2,12},{3,13},{4,10},{5,11},{6,8},{7,9},{8,6},{9,7},... | collective-permute-start | bytes 325640 | tf_op jit(solution)/shard_map/ppermute | solution.py:479
  22.2 7.3 %collective-permute-start.7 = (bf16[53,8,128]{2,1,0:T(8,128)(2,1)}, bf16[53,8,128]{2,1,0:T(8,128)(2,1)S(1)}, u32[]{:S(2)}, u32[]{:S(2)}) collective-permute-start(bf16[53,8,128]{2,1,0:T(8,128)(2,1)} %get-tuple-element.45), channel_id=1, source_target_pairs={{0,7},{1,6},{2,5},{3,4},{4,3},{5,2},{6,1},{7,0},{8,15},{9,14},{10,... | collective-permute-start | bytes 325640 | tf_op jit(solution)/shard_map/ppermute | solution.py:479
  22.2 0.9 %copy-start = (bf16[53,8,128]{2,1,0:T(8,128)(2,1)S(1)}, bf16[53,8,128]{2,1,0:T(8,128)(2,1)}, u32[]{:S(2)}) copy-start(bf16[53,8,128]{2,1,0:T(8,128)(2,1)} %get-tuple-element.32.own_ref) | copy-start | bytes 325636
  23.1 0.9 %copy-start.1 = (bf16[53,8,128]{2,1,0:T(8,128)(2,1)S(1)}, bf16[53,8,128]{2,1,0:T(8,128)(2,1)}, u32[]{:S(2)}) copy-start(bf16[53,8,128]{2,1,0:T(8,128)(2,1)} %get-tuple-element.33.held_ref) | copy-start | bytes 325636
  24.0 0.7 %copy-start.2 = (f32[8,384]{1,0:T(8,128)S(1)}, f32[8,384]{1,0:T(8,128)}, u32[]{:S(2)}) copy-start(f32[8,384]{1,0:T(8,128)} %get-tuple-element.31.small_ref) | copy-start | bytes 36868
  25.3 12.1 %collective-permute-start.8 = (bf16[53,8,128]{2,1,0:T(8,128)(2,1)}, bf16[53,8,128]{2,1,0:T(8,128)(2,1)S(1)}, u32[]{:S(2)}, u32[]{:S(2)}) collective-permute-start(bf16[53,8,128]{2,1,0:T(8,128)(2,1)} %get-tuple-element.46), channel_id=1, source_target_pairs={{0,11},{1,10},{2,9},{3,8},{4,15},{5,14},{6,13},{7,12},{8,3},{9,2},... | collective-permute-start | bytes 325640 | tf_op jit(solution)/shard_map/ppermute | solution.py:479
  27.1 12.7 %collective-permute-start.1 = (bf16[53,8,128]{2,1,0:T(8,128)(2,1)S(1)}, bf16[53,8,128]{2,1,0:T(8,128)(2,1)S(1)}, u32[]{:S(2)}, u32[]{:S(2)}) collective-permute-start(bf16[53,8,128]{2,1,0:T(8,128)(2,1)S(1)} %get-tuple-element.39), channel_id=1, source_target_pairs={{0,10},{1,11},{2,8},{3,9},{4,14},{5,15},{6,12},{7,13},{8,2},{9,3},... | collective-permute-start | bytes 325640 | tf_op jit(solution)/shard_map/ppermute | solution.py:479
  28.6 12.3 %collective-permute-start.9 = (bf16[53,8,128]{2,1,0:T(8,128)(2,1)}, bf16[53,8,128]{2,1,0:T(8,128)(2,1)S(1)}, u32[]{:S(2)}, u32[]{:S(2)}) collective-permute-start(bf16[53,8,128]{2,1,0:T(8,128)(2,1)} %get-tuple-element.47), channel_id=1, source_target_pairs={{0,1},{1,0},{2,3},{3,2},{4,5},{5,4},{6,7},{7,6},{8,9},{9,8},{10,11... | collective-permute-start | bytes 325640 | tf_op jit(solution)/shard_map/ppermute | solution.py:479
  29.0 12.4 %collective-permute-start.10 = (bf16[53,8,128]{2,1,0:T(8,128)(2,1)}, bf16[53,8,128]{2,1,0:T(8,128)(2,1)S(1)}, u32[]{:S(2)}, u32[]{:S(2)}) collective-permute-start(bf16[53,8,128]{2,1,0:T(8,128)(2,1)} %get-tuple-element.48), channel_id=1, source_target_pairs={{0,2},{1,3},{2,0},{3,1},{4,6},{5,7},{6,4},{7,5},{8,10},{9,11},{10,... | collective-permute-start | bytes 325640 | tf_op jit(solution)/shard_map/ppermute | solution.py:479
  29.6 11.9 %collective-permute-start.11 = (bf16[53,8,128]{2,1,0:T(8,128)(2,1)}, bf16[53,8,128]{2,1,0:T(8,128)(2,1)S(1)}, u32[]{:S(2)}, u32[]{:S(2)}) collective-permute-start(bf16[53,8,128]{2,1,0:T(8,128)(2,1)} %get-tuple-element.49), channel_id=1, source_target_pairs={{0,3},{1,2},{2,1},{3,0},{4,7},{5,6},{6,5},{7,4},{8,11},{9,10},{10,... | collective-permute-start | bytes 325640 | tf_op jit(solution)/shard_map/ppermute | solution.py:479
  37.4 9.7 %collective-permute-start.14 = (bf16[48,8,128]{2,1,0:T(8,128)(2,1)}, bf16[48,8,128]{2,1,0:T(8,128)(2,1)S(1)}, u32[]{:S(2)}, u32[]{:S(2)}) collective-permute-start(bf16[48,8,128]{2,1,0:T(8,128)(2,1)} %get-tuple-element.55), channel_id=1, source_target_pairs={{0,13},{1,12},{2,15},{3,14},{4,9},{5,8},{6,11},{7,10},{8,5},{9,4},... | collective-permute-start | bytes 294920 | tf_op jit(solution)/shard_map/ppermute | solution.py:479
  39.8 7.9 %collective-permute-start.15 = (bf16[48,8,128]{2,1,0:T(8,128)(2,1)}, bf16[48,8,128]{2,1,0:T(8,128)(2,1)S(1)}, u32[]{:S(2)}, u32[]{:S(2)}) collective-permute-start(bf16[48,8,128]{2,1,0:T(8,128)(2,1)} %get-tuple-element.56), channel_id=1, source_target_pairs={{0,15},{1,14},{2,13},{3,12},{4,11},{5,10},{6,9},{7,8},{8,7},{9,6},... | collective-permute-start | bytes 294920 | tf_op jit(solution)/shard_map/ppermute | solution.py:479
  40.9 1.4 %collective-permute-start.13 = (bf16[20,8,128]{2,1,0:T(8,128)(2,1)S(1)}, bf16[20,8,128]{2,1,0:T(8,128)(2,1)S(1)}, u32[]{:S(2)}, u32[]{:S(2)}) collective-permute-start(bf16[20,8,128]{2,1,0:T(8,128)(2,1)S(1)} %collect_gains.1), channel_id=1, source_target_pairs={{0,1},{1,0},{2,3},{3,2},{4,5},{5,4},{6,7},{7,6},{8,9},{9,8},{10,11... | collective-permute-start | bytes 122888 | tf_op jit(solution)/shard_map/ppermute | solution.py:479

commit v4 on v3

--- a/solution.py
+++ b/solution.py
@@ -46,7 +46,6 @@
     capacity,
     near,
     me_s,
-    owner_hbm,
     owner_row_hbm,
     slot_row_hbm,
     vis_hbm,
@@ -56,15 +55,14 @@
     pairs_hbm,
     *rest,
 ):
-    outs = rest[:-15]
+    outs = rest[:-14]
     (
         weights_ref,
         offset_ref,
         pairs_ref,
         small_ref,
-        owner_s,
         place_s,
-        count_s,
+        place_ref,
         owner_ref,
         slot_ref,
         vis_ref,
@@ -73,7 +71,7 @@
         meta_ref,
         block_ref,
         sems,
-    ) = rest[-15:]
+    ) = rest[-14:]
     rows = vis_ref.shape[0]
     chunks = vis_ref.shape[2] // LANES
     devices = block_ref.shape[0]
@@ -84,9 +82,8 @@
     span = rows // PARTS
     moves = start_all(
         (
-            (owner_hbm, owner_s),
+            (owner_row_hbm, owner_ref),
             (coarse_hbm, coarse_ref),
-            (owner_row_hbm, owner_ref),
             (slot_row_hbm, slot_ref),
             (weights_hbm, weights_ref),
             (offset_hbm, offset_ref),
@@ -102,19 +99,21 @@
         sems.at[pl.ds(len(moves), PARTS)],
     )
     turn_ref[...] = jnp.zeros_like(turn_ref)
-    for d in range(devices):
-        count_s[d] = 0
-    me = me_s[0]
     moves[0].wait()
 
-    def rank(r, carry):
-        x = owner_s[r] ^ me
-        k = count_s[x]
-        count_s[x] = k + 1
-        place_s[r] = x * capacity + k
-        return carry
-
-    lax.fori_loop(0, rows, rank, 0, unroll=8)
+    owner = owner_ref[...]
+    each = lax.broadcasted_iota(jnp.int32, (devices, rows), 0)
+    member = owner == each
+    rank = jnp.dot(
+        member.astype(jnp.float32).astype(jnp.bfloat16),
+        earlier(rows),
+        preferred_element_type=jnp.float32,
+    )
+    base = ((each ^ me_s[0]) * capacity).astype(jnp.float32)
+    place = jnp.sum(jnp.where(member, base + rank, 0.0), axis=0, keepdims=True)
+    place_ref[...] = jnp.broadcast_to(place, place_ref.shape).astype(jnp.int32)
+    placing = pltpu.make_async_copy(place_ref, place_s, sems.at[0])
+    placing.start()
     for move in moves[1:]:
         move.wait()
 
@@ -127,7 +126,7 @@
         meta_ref[i] = high[i * SUB : (i + 1) * SUB, :]
         meta_ref[gain_tiles + i] = low[i * SUB : (i + 1) * SUB, :]
     sub = lax.broadcasted_iota(jnp.int32, (SUB, LANES), 0)
-    codes = jnp.where(sub == 0, owner_ref[...], slot_ref[...])
+    codes = jnp.where(sub == 0, owner, slot_ref[...])
     meta_ref[2 * gain_tiles] = codes.astype(jnp.float32).astype(jnp.bfloat16)
     steps = weights_ref.shape[0]
     small_ref[...] = jnp.zeros_like(small_ref)
@@ -148,12 +147,13 @@
     start += len(pairs)
 
     def place(r, carry):
-        p = place_s[r]
+        p = place_s[0, r]
         for c in range(chunks):
             flat_ref[p * chunks + c] = vis_ref[r, :, c * LANES : (c + 1) * LANES]
         return carry
 
     flat_ref = block_ref.reshape(devices * at, SUB, LANES)
+    placing.wait()
     for i in range(PARTS):
         fetches[i].wait()
         lax.fori_loop(i * span, (i + 1) * span, place, 0, unroll=8)
@@ -199,17 +199,18 @@
         move.wait()
 
 
+def earlier(width):
+    first = lax.broadcasted_iota(jnp.int32, (width, width), 0)
+    second = lax.broadcasted_iota(jnp.int32, (width, width), 1)
+    return (first < second).astype(jnp.float32).astype(jnp.bfloat16)
+
+
 def list_rows(owner, slot, target, capacity):
     senders = owner.shape[0]
     mine = owner == target
     counted = mine.astype(jnp.float32)
-    before = lax.broadcasted_iota(jnp.int32, (LANES, LANES), 0) < lax.broadcasted_iota(
-        jnp.int32, (LANES, LANES), 1
-    )
     rank = jnp.dot(
-        counted.astype(jnp.bfloat16),
-        before.astype(jnp.float32).astype(jnp.bfloat16),
-        preferred_element_type=jnp.float32,
+        counted.astype(jnp.bfloat16), earlier(LANES), preferred_element_type=jnp.float32
     )
     lane = lax.broadcasted_iota(jnp.int32, (senders, LANES), 1)
     count = jnp.sum(counted, axis=1, keepdims=True)
@@ -405,12 +406,11 @@
 
     me = lax.axis_index("bl").astype(i32).reshape(1)
     turn = me if halves else jnp.zeros_like(me)
-    owner = row_owner.reshape(rows)
     coarse = gains_coarse.transpose(2, 1, 0).reshape(knots * parts, stations)
     block = (chunks * capacity, parts, LANES)
     rows_at = chunks * capacity
     if halves:
-        long = with_gains(near) + [near + 3]
+        long = with_gains(near)
         outs = [
             shape((rows_at + (depth if x in long else 0), parts, LANES), bf16)
             for x in range(devices)
@@ -424,16 +424,15 @@
     sent = pl.pallas_call(
         functools.partial(pack_kernel, capacity, near),
         out_shape=outs,
-        in_specs=[smem] + [hbm] * 8,
+        in_specs=[smem] + [hbm] * 7,
         out_specs=[hbm] * len(outs),
         scratch_shapes=[
             pltpu.VMEM(weights.shape, f32),
             pltpu.VMEM(offset.shape, i32),
             pltpu.VMEM(pairs.shape, i32),
             pltpu.VMEM((SUB, channels), f32),
-            pltpu.SMEM((rows,), i32),
-            pltpu.SMEM((rows,), i32),
-            pltpu.SMEM((devices,), i32),
+            pltpu.SMEM((SUB, rows), i32),
+            pltpu.VMEM((SUB, rows), i32),
             pltpu.VMEM((1, rows), i32),
             pltpu.VMEM((1, rows), i32),
             pltpu.VMEM((rows, parts, channels), bf16),
@@ -447,7 +446,6 @@
         name="pack_rows",
     )(
         turn,
-        owner,
         row_owner.reshape(1, rows),
         row_slot.reshape(1, rows),
         visibilities,
@@ -479,7 +477,7 @@
         return lax.ppermute(array, "bl", [(d, d ^ x) for d in range(devices)])
 
     if halves:
-        held = near + 2
+        held = near + 4
         own, through, high, low, ints = ready(sent[0], sent[held])
         arrived = {0: own, held: swap(through, held)}
         arrived.update({x: swap(sent[x], x) for x in range(1, devices) if x != held})

time: 50.1 us -> 51.6 us (1.030)
  starting transfers between devices: 26.8 us -> 30.3 us
  waiting for transfers between devices: 9.68 us -> 8.32 us
  Pallas kernels: 10.8 us -> 9.83 us
    ppermute x16, starting transfers between devices: 26.8 us -> 30.3 us  [swap(): return lax.ppermute(array, 'bl', [(d, d ^ x) for d in range(devices)])]
    ppermute x16, waiting for transfers between devices: 9.68 us -> 8.32 us  [swap(): return lax.ppermute(array, 'bl', [(d, d ^ x) for d in range(devices)])]
    pallas_call x1, Pallas kernels: 4.84 us -> 4.02 us  [on_device(): pl.pallas_call(functools.partial(middle_kernel, capacity, near, stations,...]
  transfers between devices with their start and end apart: 16 -> 16, of which waited for: 5 -> 4; matrix products, arithmetic and copies ran while one was open for 0% -> 0% of each run, Pallas kernels for 11% -> 9%
where the time goes in v4:
time: 51.6 us; the launch traced here: 51 us
  starting transfers between devices  30.3 us (59%)
  Pallas kernels  9.83 us (19%)
  waiting for transfers between devices  8.32 us (16%)
  local copies, waits for them, and re-layouts  2.5 us (5%)
    ppermute x16, starting transfers between devices, swap(): return lax.ppermute(array, 'bl', [(d, d ^ x) for d in range(devices)])  30.3 us
    ppermute x16, waiting for transfers between devices, swap(): return lax.ppermute(array, 'bl', [(d, d ^ x) for d in range(devices)])  8.32 us
    pallas_call x1, Pallas kernels, on_device(): pl.pallas_call(functools.partial(middle_kernel, capacity, near, stations,...  4.02 us
    pallas_call x1, Pallas kernels, on_device(): pl.pallas_call(functools.partial(pack_kernel, capacity, near), out_shape=...  3.15 us
    unnamed x6, local copies, waits for them, and re-layouts  2.5 us
    pallas_call x1, Pallas kernels, on_device(): pl.pallas_call(functools.partial(finish_kernel, capacity, late), out_shap...  2.04 us
  transfers between devices with their start and end apart: 16, of which 4 were waited for; matrix products, arithmetic and copies ran while one was open for 0% of the time, Pallas kernels for 9%

profile of v4, /device:TPU:0, one launch (start us, length us, event | category | flops | bytes accessed | tf_op | source)
XLA Modules:
  0.0 51.0 jit_solution(9251043588261518117)
XLA Ops:
  0.0 3.1 %pack_rows.1 = (bf16[53,8,128]{2,1,0:T(8,128)(2,1)}, bf16[53,8,128]{2,1,0:T(8,128)(2,1)}, bf16[53,8,128]{2,1,0:T(8,128)(2,1)}, bf16[53,8,128]{2,1,0:T(8,128)(2,1...) custom-call(s32[1]{0:T(128)} %bitcast.me_s.turn_s, ...), custom_call_target="tpu_custom_call" | custom-call | tf_op jit(solution)/shard_map/pack_rows/pallas_call | solution.py:424
  3.2 4.5 %collective-permute-start.8 = (bf16[48,8,128]{2,1,0:T(8,128)(2,1)}, bf16[48,8,128]{2,1,0:T(8,128)(2,1)S(1)}, u32[]{:S(2)}, u32[]{:S(2)}) collective-permute-start(bf16[48,8,128]{2,1,0:T(8,128)(2,1)} %get-tuple-element.46), channel_id=1, source_target_pairs={{0,11},{1,10},{2,9},{3,8},{4,15},{5,14},{6,13},{7,12},{8,3},{9,2},... | collective-permute-start | bytes 294920 | tf_op jit(solution)/shard_map/ppermute | solution.py:477
  8.0 2.6 %collective-permute-start.12 = (bf16[48,8,128]{2,1,0:T(8,128)(2,1)}, bf16[48,8,128]{2,1,0:T(8,128)(2,1)S(1)}, u32[]{:S(2)}, u32[]{:S(2)}) collective-permute-start(bf16[48,8,128]{2,1,0:T(8,128)(2,1)} %get-tuple-element.50), channel_id=1, source_target_pairs={{0,9},{1,8},{2,11},{3,10},{4,13},{5,12},{6,15},{7,14},{8,1},{9,0},... | collective-permute-start | bytes 294920 | tf_op jit(solution)/shard_map/ppermute | solution.py:477
  10.8 1.6 %collective-permute-start.2 = (bf16[53,8,128]{2,1,0:T(8,128)(2,1)}, bf16[53,8,128]{2,1,0:T(8,128)(2,1)S(1)}, u32[]{:S(2)}, u32[]{:S(2)}) collective-permute-start(bf16[53,8,128]{2,1,0:T(8,128)(2,1)} %get-tuple-element.40), channel_id=1, source_target_pairs={{0,4},{1,5},{2,6},{3,7},{4,0},{5,1},{6,2},{7,3},{8,12},{9,13},{10,... | collective-permute-start | bytes 325640 | tf_op jit(solution)/shard_map/ppermute | solution.py:477
  12.4 8.8 %collective-permute-start.3 = (bf16[53,8,128]{2,1,0:T(8,128)(2,1)}, bf16[53,8,128]{2,1,0:T(8,128)(2,1)S(1)}, u32[]{:S(2)}, u32[]{:S(2)}) collective-permute-start(bf16[53,8,128]{2,1,0:T(8,128)(2,1)} %get-tuple-element.41), channel_id=1, source_target_pairs={{0,5},{1,4},{2,7},{3,6},{4,1},{5,0},{6,3},{7,2},{8,13},{9,12},{10,... | collective-permute-start | bytes 325640 | tf_op jit(solution)/shard_map/ppermute | solution.py:477
  21.2 4.0 %collective-permute-done.12.rest_13_ = bf16[48,8,128]{2,1,0:T(8,128)(2,1)S(1)} collective-permute-done((bf16[48,8,128]{2,1,0:T(8,128)(2,1)}, bf16[48,8,128]{2,1,0:T(8,128)(2,1)S(1)}, u32[]{:S(2)}, u32[]{:S(2)}) %collective-permute-start.12) | collective-permute-done | bytes 98336 | tf_op jit(solution)/shard_map/ppermute | solution.py:477
  25.2 0.6 %collective-permute-start.5 = (bf16[53,8,128]{2,1,0:T(8,128)(2,1)}, bf16[53,8,128]{2,1,0:T(8,128)(2,1)S(1)}, u32[]{:S(2)}, u32[]{:S(2)}) collective-permute-start(bf16[53,8,128]{2,1,0:T(8,128)(2,1)} %get-tuple-element.43), channel_id=1, source_target_pairs={{0,6},{1,7},{2,4},{3,5},{4,2},{5,3},{6,0},{7,1},{8,14},{9,15},{10,... | collective-permute-start | bytes 325640 | tf_op jit(solution)/shard_map/ppermute | solution.py:477
  25.8 2.7 %collective-permute-start.6 = (bf16[53,8,128]{2,1,0:T(8,128)(2,1)}, bf16[53,8,128]{2,1,0:T(8,128)(2,1)S(1)}, u32[]{:S(2)}, u32[]{:S(2)}) collective-permute-start(bf16[53,8,128]{2,1,0:T(8,128)(2,1)} %get-tuple-element.44), channel_id=1, source_target_pairs={{0,14},{1,15},{2,12},{3,13},{4,10},{5,11},{6,8},{7,9},{8,6},{9,7},... | collective-permute-start | bytes 325640 | tf_op jit(solution)/shard_map/ppermute | solution.py:477
  28.6 0.9 %copy-done = bf16[53,8,128]{2,1,0:T(8,128)(2,1)S(1)} copy-done((bf16[53,8,128]{2,1,0:T(8,128)(2,1)S(1)}, bf16[53,8,128]{2,1,0:T(8,128)(2,1)}, u32[]{:S(2)}) %copy-start) | copy-done | bytes 108568
  29.5 0.9 %copy-done.1 = bf16[53,8,128]{2,1,0:T(8,128)(2,1)S(1)} copy-done((bf16[53,8,128]{2,1,0:T(8,128)(2,1)S(1)}, bf16[53,8,128]{2,1,0:T(8,128)(2,1)}, u32[]{:S(2)}) %copy-start.1) | copy-done | bytes 108568
  30.4 0.7 %copy-done.2 = f32[8,384]{1,0:T(8,128)S(1)} copy-done((f32[8,384]{1,0:T(8,128)S(1)}, f32[8,384]{1,0:T(8,128)}, u32[]{:S(2)}) %copy-start.2) | copy-done | bytes 12312
  31.1 0.5 %make_ready.1 = (bf16[53,8,128]{2,1,0:T(8,128)(2,1)S(1)}, bf16[53,8,128]{2,1,0:T(8,128)(2,1)S(1)}, bf16[8,128,384]{2,1,0:T(8,128)(2,1)S(1)}, bf16[8,128,384]{2,1,0:T(8,128)(2,1)S(1)}, s32[8,128]{1,0:T(8,128)S(1)}) custom-call(f32[8,384]{1,0:T(8,128)S(1)} %copy-done.2, bf16[53,8,128]{2,1,0:T(8,128)(2,1)S(1)} %copy-done, bf16[53,8,128]{2,1,0:T(8,128)(2,1)S(1)} %copy-done.1), custom_call_target="tpu_custom_call" | custom-call | tf_op jit(solution)/shard_map/make_ready/pallas_call | solution.py:460
  31.7 1.2 %collective-permute-start.7 = (bf16[53,8,128]{2,1,0:T(8,128)(2,1)}, bf16[53,8,128]{2,1,0:T(8,128)(2,1)S(1)}, u32[]{:S(2)}, u32[]{:S(2)}) collective-permute-start(bf16[53,8,128]{2,1,0:T(8,128)(2,1)} %get-tuple-element.45), channel_id=1, source_target_pairs={{0,7},{1,6},{2,5},{3,4},{4,3},{5,2},{6,1},{7,0},{8,15},{9,14},{10,... | collective-permute-start | bytes 325640 | tf_op jit(solution)/shard_map/ppermute | solution.py:477
  32.9 1.2 %collective-permute-start.4 = (bf16[53,8,128]{2,1,0:T(8,128)(2,1)S(1)}, bf16[53,8,128]{2,1,0:T(8,128)(2,1)S(1)}, u32[]{:S(2)}, u32[]{:S(2)}) collective-permute-start(bf16[53,8,128]{2,1,0:T(8,128)(2,1)S(1)} %get-tuple-element.42), channel_id=1, source_target_pairs={{0,12},{1,13},{2,14},{3,15},{4,8},{5,9},{6,10},{7,11},{8,4},{9,5},... | collective-permute-start | bytes 325640 | tf_op jit(solution)/shard_map/ppermute | solution.py:477
  34.1 0.5 collective-permute-start.9
  34.6 0.9 %collective-permute-start.10 = (bf16[53,8,128]{2,1,0:T(8,128)(2,1)}, bf16[53,8,128]{2,1,0:T(8,128)(2,1)S(1)}, u32[]{:S(2)}, u32[]{:S(2)}) collective-permute-start(bf16[53,8,128]{2,1,0:T(8,128)(2,1)} %get-tuple-element.48), channel_id=1, source_target_pairs={{0,2},{1,3},{2,0},{3,1},{4,6},{5,7},{6,4},{7,5},{8,10},{9,11},{10,... | collective-permute-start | bytes 325640 | tf_op jit(solution)/shard_map/ppermute | solution.py:477
  35.5 0.5 %collective-permute-start.11 = (bf16[53,8,128]{2,1,0:T(8,128)(2,1)}, bf16[53,8,128]{2,1,0:T(8,128)(2,1)S(1)}, u32[]{:S(2)}, u32[]{:S(2)}) collective-permute-start(bf16[53,8,128]{2,1,0:T(8,128)(2,1)} %get-tuple-element.49), channel_id=1, source_target_pairs={{0,3},{1,2},{2,1},{3,0},{4,7},{5,6},{6,5},{7,4},{8,11},{9,10},{10,... | collective-permute-start | bytes 325640 | tf_op jit(solution)/shard_map/ppermute | solution.py:477
  36.1 2.1 %collective-permute-done.7.rest_8_ = bf16[53,8,128]{2,1,0:T(8,128)(2,1)S(1)} collective-permute-done((bf16[53,8,128]{2,1,0:T(8,128)(2,1)}, bf16[53,8,128]{2,1,0:T(8,128)(2,1)S(1)}, u32[]{:S(2)}, u32[]{:S(2)}) %collective-permute-start.7) | collective-permute-done | bytes 108576 | tf_op jit(solution)/shard_map/ppermute | solution.py:477
  38.2 1.6 %collective-permute-start.14 = (bf16[48,8,128]{2,1,0:T(8,128)(2,1)}, bf16[48,8,128]{2,1,0:T(8,128)(2,1)S(1)}, u32[]{:S(2)}, u32[]{:S(2)}) collective-permute-start(bf16[48,8,128]{2,1,0:T(8,128)(2,1)} %get-tuple-element.55), channel_id=1, source_target_pairs={{0,13},{1,12},{2,15},{3,14},{4,9},{5,8},{6,11},{7,10},{8,5},{9,4},... | collective-permute-start | bytes 294920 | tf_op jit(solution)/shard_map/ppermute | solution.py:477
  39.8 1.3 %collective-permute-done.4.rest_2_.rest_5_ = bf16[53,8,128]{2,1,0:T(8,128)(2,1)S(1)} collective-permute-done((bf16[53,8,128]{2,1,0:T(8,128)(2,1)S(1)}, bf16[53,8,128]{2,1,0:T(8,128)(2,1)S(1)}, u32[]{:S(2)}, u32[]{:S(2)}) %collective-permute-start.4) | collective-permute-done | bytes 108576 | tf_op jit(solution)/shard_map/ppermute | solution.py:477
  41.1 2.4 %collective-permute-start.15 = (bf16[48,8,128]{2,1,0:T(8,128)(2,1)}, bf16[48,8,128]{2,1,0:T(8,128)(2,1)S(1)}, u32[]{:S(2)}, u32[]{:S(2)}) collective-permute-start(bf16[48,8,128]{2,1,0:T(8,128)(2,1)} %get-tuple-element.56), channel_id=1, source_target_pairs={{0,15},{1,14},{2,13},{3,12},{4,11},{5,10},{6,9},{7,8},{8,7},{9,6},... | collective-permute-start | bytes 294920 | tf_op jit(solution)/shard_map/ppermute | solution.py:477
  44.1 0.9 %collective-permute-done.13.rest_14_ = bf16[20,8,128]{2,1,0:T(8,128)(2,1)S(1)} collective-permute-done((bf16[20,8,128]{2,1,0:T(8,128)(2,1)S(1)}, bf16[20,8,128]{2,1,0:T(8,128)(2,1)S(1)}, u32[]{:S(2)}, u32[]{:S(2)}) %collective-permute-start.13) | collective-permute-done | bytes 40992 | tf_op jit(solution)/shard_map/ppermute | solution.py:477
  44.9 4.0 %gains_and_sums.1 = (f32[8,128,384]{2,1,0:T(8,128)S(1)}, f32[64,128]{1,0:T(8,128)S(1)}, s32[16,128]{1,0:T(8,128)S(1)}, f32[3,64,8,128]{3,2,1,0:T(8,128)S(1)}) custom-call(s32[1]{0:T(128)} %bitcast.me_s.turn_s, s32[1]{0:T(128)} %bitcast.me_s.turn_s, s32[8,128]{1,0:T(8,128)S(1)} %get-tuple-element.34.pairs_s, ...), custom_call_target="tpu_custom_call" | custom-call | tf_op jit(solution)/shard_map/gains_and_sums/pallas_call | solution.py:504
  49.0 2.0 %sum_and_apply.1 = bf16[64,8,384]{2,1,0:T(8,128)(2,1)} custom-call(s32[16,128]{1,0:T(8,128)S(1)} %get-tuple-element.51.slots_s, f32[8,128,384]{2,1,0:T(8,128)S(1)} %get-tuple-element.52.gains_ref, f32[64,128]{1,0:T(8,128)S(1)} %get-tuple-element.53.recip_ref, f32[3,64,8,128]{3,2,1,0:T(8,128)S(1)} %get-tuple-element.54.sums_ref, ...), custom_call_target="tpu_custom_call" | custom-call | tf_op jit(solution)/shard_map/sum_and_apply/pallas_call | solution.py:526
  (19 shorter events, 1.1 us)
Async XLA Ops:
  3.2 9.3 %collective-permute-start.8 = (bf16[48,8,128]{2,1,0:T(8,128)(2,1)}, bf16[48,8,128]{2,1,0:T(8,128)(2,1)S(1)}, u32[]{:S(2)}, u32[]{:S(2)}) collective-permute-start(bf16[48,8,128]{2,1,0:T(8,128)(2,1)} %get-tuple-element.46), channel_id=1, source_target_pairs={{0,11},{1,10},{2,9},{3,8},{4,15},{5,14},{6,13},{7,12},{8,3},{9,2},... | collective-permute-start | bytes 294920 | tf_op jit(solution)/shard_map/ppermute | solution.py:477
  7.7 18.2 %collective-permute-start = (bf16[53,8,128]{2,1,0:T(8,128)(2,1)}, bf16[53,8,128]{2,1,0:T(8,128)(2,1)S(1)}, u32[]{:S(2)}, u32[]{:S(2)}) collective-permute-start(bf16[53,8,128]{2,1,0:T(8,128)(2,1)} %get-tuple-element.38), channel_id=1, source_target_pairs={{0,8},{1,9},{2,10},{3,11},{4,12},{5,13},{6,14},{7,15},{8,0},{9,1},... | collective-permute-start | bytes 325640 | tf_op jit(solution)/shard_map/ppermute | solution.py:477
  8.0 17.2 %collective-permute-start.12 = (bf16[48,8,128]{2,1,0:T(8,128)(2,1)}, bf16[48,8,128]{2,1,0:T(8,128)(2,1)S(1)}, u32[]{:S(2)}, u32[]{:S(2)}) collective-permute-start(bf16[48,8,128]{2,1,0:T(8,128)(2,1)} %get-tuple-element.50), channel_id=1, source_target_pairs={{0,9},{1,8},{2,11},{3,10},{4,13},{5,12},{6,15},{7,14},{8,1},{9,0},... | collective-permute-start | bytes 294920 | tf_op jit(solution)/shard_map/ppermute | solution.py:477
  10.6 21.0 %collective-permute-start.1 = (bf16[53,8,128]{2,1,0:T(8,128)(2,1)}, bf16[53,8,128]{2,1,0:T(8,128)(2,1)S(1)}, u32[]{:S(2)}, u32[]{:S(2)}) collective-permute-start(bf16[53,8,128]{2,1,0:T(8,128)(2,1)} %get-tuple-element.39), channel_id=1, source_target_pairs={{0,10},{1,11},{2,8},{3,9},{4,14},{5,15},{6,12},{7,13},{8,2},{9,3},... | collective-permute-start | bytes 325640 | tf_op jit(solution)/shard_map/ppermute | solution.py:477
  10.8 22.0 %collective-permute-start.2 = (bf16[53,8,128]{2,1,0:T(8,128)(2,1)}, bf16[53,8,128]{2,1,0:T(8,128)(2,1)S(1)}, u32[]{:S(2)}, u32[]{:S(2)}) collective-permute-start(bf16[53,8,128]{2,1,0:T(8,128)(2,1)} %get-tuple-element.40), channel_id=1, source_target_pairs={{0,4},{1,5},{2,6},{3,7},{4,0},{5,1},{6,2},{7,3},{8,12},{9,13},{10,... | collective-permute-start | bytes 325640 | tf_op jit(solution)/shard_map/ppermute | solution.py:477
  12.4 21.7 %collective-permute-start.3 = (bf16[53,8,128]{2,1,0:T(8,128)(2,1)}, bf16[53,8,128]{2,1,0:T(8,128)(2,1)S(1)}, u32[]{:S(2)}, u32[]{:S(2)}) collective-permute-start(bf16[53,8,128]{2,1,0:T(8,128)(2,1)} %get-tuple-element.41), channel_id=1, source_target_pairs={{0,5},{1,4},{2,7},{3,6},{4,1},{5,0},{6,3},{7,2},{8,13},{9,12},{10,... | collective-permute-start | bytes 325640 | tf_op jit(solution)/shard_map/ppermute | solution.py:477
  25.2 9.4 %collective-permute-start.5 = (bf16[53,8,128]{2,1,0:T(8,128)(2,1)}, bf16[53,8,128]{2,1,0:T(8,128)(2,1)S(1)}, u32[]{:S(2)}, u32[]{:S(2)}) collective-permute-start(bf16[53,8,128]{2,1,0:T(8,128)(2,1)} %get-tuple-element.43), channel_id=1, source_target_pairs={{0,6},{1,7},{2,4},{3,5},{4,2},{5,3},{6,0},{7,1},{8,14},{9,15},{10,... | collective-permute-start | bytes 325640 | tf_op jit(solution)/shard_map/ppermute | solution.py:477
  25.8 9.7 %collective-permute-start.6 = (bf16[53,8,128]{2,1,0:T(8,128)(2,1)}, bf16[53,8,128]{2,1,0:T(8,128)(2,1)S(1)}, u32[]{:S(2)}, u32[]{:S(2)}) collective-permute-start(bf16[53,8,128]{2,1,0:T(8,128)(2,1)} %get-tuple-element.44), channel_id=1, source_target_pairs={{0,14},{1,15},{2,12},{3,13},{4,10},{5,11},{6,8},{7,9},{8,6},{9,7},... | collective-permute-start | bytes 325640 | tf_op jit(solution)/shard_map/ppermute | solution.py:477
  28.6 0.9 %copy-start = (bf16[53,8,128]{2,1,0:T(8,128)(2,1)S(1)}, bf16[53,8,128]{2,1,0:T(8,128)(2,1)}, u32[]{:S(2)}) copy-start(bf16[53,8,128]{2,1,0:T(8,128)(2,1)} %get-tuple-element.32.own_ref) | copy-start | bytes 325636
  29.5 0.9 %copy-start.1 = (bf16[53,8,128]{2,1,0:T(8,128)(2,1)S(1)}, bf16[53,8,128]{2,1,0:T(8,128)(2,1)}, u32[]{:S(2)}) copy-start(bf16[53,8,128]{2,1,0:T(8,128)(2,1)} %get-tuple-element.33.held_ref) | copy-start | bytes 325636
  30.4 0.7 %copy-start.2 = (f32[8,384]{1,0:T(8,128)S(1)}, f32[8,384]{1,0:T(8,128)}, u32[]{:S(2)}) copy-start(f32[8,384]{1,0:T(8,128)} %get-tuple-element.31.small_ref) | copy-start | bytes 36868
  31.7 6.5 %collective-permute-start.7 = (bf16[53,8,128]{2,1,0:T(8,128)(2,1)}, bf16[53,8,128]{2,1,0:T(8,128)(2,1)S(1)}, u32[]{:S(2)}, u32[]{:S(2)}) collective-permute-start(bf16[53,8,128]{2,1,0:T(8,128)(2,1)} %get-tuple-element.45), channel_id=1, source_target_pairs={{0,7},{1,6},{2,5},{3,4},{4,3},{5,2},{6,1},{7,0},{8,15},{9,14},{10,... | collective-permute-start | bytes 325640 | tf_op jit(solution)/shard_map/ppermute | solution.py:477
  32.9 8.2 %collective-permute-start.4 = (bf16[53,8,128]{2,1,0:T(8,128)(2,1)S(1)}, bf16[53,8,128]{2,1,0:T(8,128)(2,1)S(1)}, u32[]{:S(2)}, u32[]{:S(2)}) collective-permute-start(bf16[53,8,128]{2,1,0:T(8,128)(2,1)S(1)} %get-tuple-element.42), channel_id=1, source_target_pairs={{0,12},{1,13},{2,14},{3,15},{4,8},{5,9},{6,10},{7,11},{8,4},{9,5},... | collective-permute-start | bytes 325640 | tf_op jit(solution)/shard_map/ppermute | solution.py:477
  34.1 9.5 %collective-permute-start.9 = (bf16[53,8,128]{2,1,0:T(8,128)(2,1)}, bf16[53,8,128]{2,1,0:T(8,128)(2,1)S(1)}, u32[]{:S(2)}, u32[]{:S(2)}) collective-permute-start(bf16[53,8,128]{2,1,0:T(8,128)(2,1)} %get-tuple-element.47), channel_id=1, source_target_pairs={{0,1},{1,0},{2,3},{3,2},{4,5},{5,4},{6,7},{7,6},{8,9},{9,8},{10,11... | collective-permute-start | bytes 325640 | tf_op jit(solution)/shard_map/ppermute | solution.py:477
  34.6 9.5 %collective-permute-start.10 = (bf16[53,8,128]{2,1,0:T(8,128)(2,1)}, bf16[53,8,128]{2,1,0:T(8,128)(2,1)S(1)}, u32[]{:S(2)}, u32[]{:S(2)}) collective-permute-start(bf16[53,8,128]{2,1,0:T(8,128)(2,1)} %get-tuple-element.48), channel_id=1, source_target_pairs={{0,2},{1,3},{2,0},{3,1},{4,6},{5,7},{6,4},{7,5},{8,10},{9,11},{10,... | collective-permute-start | bytes 325640 | tf_op jit(solution)/shard_map/ppermute | solution.py:477
  35.5 8.5 %collective-permute-start.11 = (bf16[53,8,128]{2,1,0:T(8,128)(2,1)}, bf16[53,8,128]{2,1,0:T(8,128)(2,1)S(1)}, u32[]{:S(2)}, u32[]{:S(2)}) collective-permute-start(bf16[53,8,128]{2,1,0:T(8,128)(2,1)} %get-tuple-element.49), channel_id=1, source_target_pairs={{0,3},{1,2},{2,1},{3,0},{4,7},{5,6},{6,5},{7,4},{8,11},{9,10},{10,... | collective-permute-start | bytes 325640 | tf_op jit(solution)/shard_map/ppermute | solution.py:477
  38.2 10.8 %collective-permute-start.14 = (bf16[48,8,128]{2,1,0:T(8,128)(2,1)}, bf16[48,8,128]{2,1,0:T(8,128)(2,1)S(1)}, u32[]{:S(2)}, u32[]{:S(2)}) collective-permute-start(bf16[48,8,128]{2,1,0:T(8,128)(2,1)} %get-tuple-element.55), channel_id=1, source_target_pairs={{0,13},{1,12},{2,15},{3,14},{4,9},{5,8},{6,11},{7,10},{8,5},{9,4},... | collective-permute-start | bytes 294920 | tf_op jit(solution)/shard_map/ppermute | solution.py:477
  41.1 7.9 %collective-permute-start.15 = (bf16[48,8,128]{2,1,0:T(8,128)(2,1)}, bf16[48,8,128]{2,1,0:T(8,128)(2,1)S(1)}, u32[]{:S(2)}, u32[]{:S(2)}) collective-permute-start(bf16[48,8,128]{2,1,0:T(8,128)(2,1)} %get-tuple-element.56), channel_id=1, source_target_pairs={{0,15},{1,14},{2,13},{3,12},{4,11},{5,10},{6,9},{7,8},{8,7},{9,6},... | collective-permute-start | bytes 294920 | tf_op jit(solution)/shard_map/ppermute | solution.py:477
  43.6 1.3 %collective-permute-start.13 = (bf16[20,8,128]{2,1,0:T(8,128)(2,1)S(1)}, bf16[20,8,128]{2,1,0:T(8,128)(2,1)S(1)}, u32[]{:S(2)}, u32[]{:S(2)}) collective-permute-start(bf16[20,8,128]{2,1,0:T(8,128)(2,1)S(1)} %collect_gains.1), channel_id=1, source_target_pairs={{0,1},{1,0},{2,3},{3,2},{4,5},{5,4},{6,7},{7,6},{8,9},{9,8},{10,11... | collective-permute-start | bytes 122888 | tf_op jit(solution)/shard_map/ppermute | solution.py:477

commit v5 on v3

--- a/solution.py
+++ b/solution.py
@@ -166,8 +166,9 @@
         send.wait()
 
 
-def ready_kernel(small_ref, own_ref, held_ref, own_out_ref, held_out_ref, high_ref, low_ref, pairs_ref, sems):
-    moves = start_all([(own_ref, own_out_ref), (held_ref, held_out_ref)], sems)
+def ready_kernel(small_ref, own_ref, own_out_ref, high_ref, low_ref, pairs_ref, sem):
+    move = pltpu.make_async_copy(own_ref, own_out_ref, sem)
+    move.start()
     small = small_ref[...]
     channels = small.shape[1]
     pairs_ref[...] = small[:, 0:LANES].astype(jnp.int32)
@@ -182,8 +183,7 @@
     for j in range(8):
         high_ref[j] = jnp.where(part == j, high, 0.0).astype(jnp.bfloat16)
         low_ref[j] = jnp.where(part == j, low, 0.0).astype(jnp.bfloat16)
-    for move in moves:
-        move.wait()
+    move.wait()
 
 
 def collect_kernel(at, depth, *rest):
@@ -199,7 +199,7 @@
         move.wait()
 
 
-def list_rows(owner, slot, target, capacity):
+def list_rows(owner, slot, target, capacity, spare):
     senders = owner.shape[0]
     mine = owner == target
     counted = mine.astype(jnp.float32)
@@ -217,20 +217,23 @@
     for k in range(capacity):
         here = jnp.logical_and(mine, rank == float(k))
         kth = jnp.sum(jnp.where(here, slot, 0.0), axis=1, keepdims=True)
+        kth = jnp.where(count > float(k), kth, float(spare))
         listing = jnp.where(lane == k, kth, listing)
     return listing.astype(jnp.int32), mine
 
 
-def add_rows(acc_ref, slots_s, line, capacity, rows_ref):
-    chunks = acc_ref.shape[0]
-
-    def add(k, carry):
-        b = slots_s[line, k]
-        for c in range(chunks):
-            acc_ref[c, b] += rows_ref[chunks * k + c].astype(jnp.float32)
+def add_rows(acc_refs, slots_s, line, capacity, rows_ref):
+    chunks, several = acc_refs[0].shape[0], len(acc_refs)
+
+    def add(i, carry):
+        for u, acc_ref in enumerate(acc_refs):
+            k = several * i + u
+            b = slots_s[line, k]
+            for c in range(chunks):
+                acc_ref[c, b] += rows_ref[chunks * k + c].astype(jnp.float32)
         return carry
 
-    lax.fori_loop(0, slots_s[line, capacity], add, 0)
+    lax.fori_loop(0, (slots_s[line, capacity] + several - 1) // several, add, 0)
 
 
 def add_table(table_ref, x, block, at, depth):
@@ -251,9 +254,9 @@
 
 
 def middle_kernel(capacity, near, stations, order, turn_s, me_s, pairs_s, high_ref, low_ref, *rest):
-    arrived, passed = dict(zip(order, rest)), rest[len(order) : -11]
-    gains_ref, recip_ref, slots_ref, sums_ref = rest[-11:-7]
-    table_ref, pick_ref, owner_ref, slot_ref, slots_v, slots_s, sem = rest[-7:]
+    arrived, passed = dict(zip(order, rest)), rest[len(order) : -13]
+    gains_ref, recip_ref, slots_ref, sums_ref = rest[-13:-9]
+    table_ref, pick_ref, owner_ref, slot_ref, slots_v, slots_s, one_ref, two_ref, sem = rest[-9:]
     devices = table_ref.shape[0]
     owned = recip_ref.shape[0]
     chunks = sums_ref.shape[0]
@@ -269,7 +272,9 @@
         owner_ref[x : x + 1, :] = code[0:1, :]
         slot_ref[x : x + 1, :] = code[1:2, :]
     slot = slot_ref[...]
-    listing, mine = list_rows(owner_ref[...], slot, me_s[0].astype(jnp.float32), capacity)
+    listing, mine = list_rows(
+        owner_ref[...], slot, me_s[0].astype(jnp.float32), capacity, owned
+    )
     slots_ref[...] = listing
     slots_v[...] = listing
     move = pltpu.make_async_copy(slots_v, slots_s, sem)
@@ -306,11 +311,13 @@
         ) + jnp.dot(both_high, low, preferred_element_type=jnp.float32)
         gains_ref[j] = fine.astype(jnp.bfloat16).astype(jnp.float32)
 
-    sums_ref[...] = jnp.zeros_like(sums_ref)
+    one_ref[...] = jnp.zeros_like(one_ref)
+    two_ref[...] = jnp.zeros_like(two_ref)
     move.wait()
     if near > 1:
         for x in order:
-            add_rows(sums_ref, slots_s, x, capacity, arrived[x])
+            add_rows((one_ref, two_ref), slots_s, x, capacity, arrived[x])
+    sums_ref[...] = one_ref[:, 0:owned] + two_ref[:, 0:owned]
 
 
 def finish_kernel(capacity, late, slots_s, gains_ref, recip_ref, sums_ref, *rest):
@@ -321,11 +328,11 @@
     acc_ref[...] = sums_ref[...]
     if len(late) > 1:
         for x, rows_ref in zip(late, far):
-            add_rows(acc_ref, slots_s, x, capacity, rows_ref)
+            add_rows((acc_ref,), slots_s, x, capacity, rows_ref)
     else:
 
         def from_device(d, carry):
-            add_rows(acc_ref, slots_s, d, capacity, far[0].at[d])
+            add_rows((acc_ref,), slots_s, d, capacity, far[0].at[d])
             return carry
 
         lax.fori_loop(0, far[0].shape[0], from_device, 0)
@@ -458,31 +465,28 @@
     )
 
 
-    def ready(own, held):
+    def ready(own):
         return pl.pallas_call(
             ready_kernel,
             out_shape=[
                 shape(own.shape, bf16),
-                shape(held.shape, bf16),
                 shape((parts, LANES, channels), bf16),
                 shape((parts, LANES, channels), bf16),
                 shape((SUB, LANES), i32),
             ],
-            in_specs=[vmem, anywhere, anywhere],
-            out_specs=[vmem] * 5,
-            scratch_shapes=[dma((2,))],
+            in_specs=[vmem, anywhere],
+            out_specs=[vmem] * 4,
+            scratch_shapes=[dma],
             compiler_params=some,
             name="make_ready",
-        )(sent[-1], own, held)
+        )(sent[-1], own)
 
     def swap(array, x):
         return lax.ppermute(array, "bl", [(d, d ^ x) for d in range(devices)])
 
     if halves:
-        held = near + 2
-        own, through, high, low, ints = ready(sent[0], sent[held])
-        arrived = {0: own, held: swap(through, held)}
-        arrived.update({x: swap(sent[x], x) for x in range(1, devices) if x != held})
+        own, high, low, ints = ready(sent[0])
+        arrived = {x: swap(sent[x], x) if x else own for x in range(devices)}
         order, late = schedule(near)
         even = list(range(near, devices, 2))
         collected = pl.pallas_call(
@@ -501,7 +505,7 @@
             1: lax.all_to_all(sent[0], "bl", split_axis=0, concat_axis=0, tiled=True),
         }
         order, late, passed = [0], [1], []
-        _, _, high, low, ints = ready(sent[1], sent[1])
+        _, high, low, ints = ready(sent[1])
 
     gains, recip, slots, sums = pl.pallas_call(
         functools.partial(middle_kernel, capacity, near, stations, order),
@@ -520,6 +524,8 @@
             pltpu.VMEM((devices, LANES), f32),
             pltpu.VMEM((devices, LANES), i32),
             pltpu.SMEM((devices, LANES), i32),
+            pltpu.VMEM((chunks, owned + 1, parts, LANES), f32),
+            pltpu.VMEM((chunks, owned + 1, parts, LANES), f32),
             dma,
         ],
         compiler_params=some,

time: 50.1 us -> 49.1 us (0.980)
  Pallas kernels: 10.8 us -> 9.26 us
  starting transfers between devices: 26.8 us -> 28.1 us
  local copies, waits for them, and re-layouts: 2.5 us -> 1.6 us
    ppermute x16, starting transfers between devices: 26.8 us -> 28.1 us  [swap(): return lax.ppermute(array, 'bl', [(d, d ^ x) for d in range(devices)])]
    pallas_call x1, Pallas kernels: 4.84 us -> 3.57 us  [on_device(): pl.pallas_call(functools.partial(middle_kernel, capacity, near, stations,...]
    unnamed x6 -> x4, local copies, waits for them, and re-layouts: 2.5 us -> 1.6 us
  transfers between devices with their start and end apart: 16 -> 16, of which waited for: 5 -> 5; matrix products, arithmetic and copies ran while one was open for 0% -> 0% of each run, Pallas kernels for 11% -> 8%
where the time goes in v5:
time: 49.1 us; the launch traced here: 48.8 us
  starting transfers between devices  28.1 us (57%)
  waiting for transfers between devices  9.7 us (20%)
  Pallas kernels  9.26 us (19%)
  local copies, waits for them, and re-layouts  1.6 us (3%)
    ppermute x16, starting transfers between devices, swap(): return lax.ppermute(array, 'bl', [(d, d ^ x) for d in range(devices)])  28.1 us
    ppermute x16, waiting for transfers between devices, swap(): return lax.ppermute(array, 'bl', [(d, d ^ x) for d in range(devices)])  9.7 us
    pallas_call x1, Pallas kernels, on_device(): pl.pallas_call(functools.partial(middle_kernel, capacity, near, stations,...  3.57 us
    pallas_call x1, Pallas kernels, on_device(): pl.pallas_call(functools.partial(pack_kernel, capacity, near), out_shape=...  3.22 us
    pallas_call x1, Pallas kernels, on_device(): pl.pallas_call(functools.partial(finish_kernel, capacity, late), out_shap...  2.01 us
    unnamed x4, local copies, waits for them, and re-layouts  1.6 us
  transfers between devices with their start and end apart: 16, of which 5 were waited for; matrix products, arithmetic and copies ran while one was open for 0% of the time, Pallas kernels for 8%

profile of v5, /device:TPU:0, one launch (start us, length us, event | category | flops | bytes accessed | tf_op | source)
XLA Modules:
  0.0 48.8 jit_solution(29482099182991601)
XLA Ops:
  0.0 3.2 %pack_rows.1 = (bf16[53,8,128]{2,1,0:T(8,128)(2,1)}, bf16[53,8,128]{2,1,0:T(8,128)(2,1)}, bf16[53,8,128]{2,1,0:T(8,128)(2,1)}, bf16[53,8,128]{2,1,0:T(8,128)(2,1...) custom-call(s32[1]{0:T(128)} %bitcast.me_s.turn_s, ...), custom_call_target="tpu_custom_call" | custom-call | tf_op jit(solution)/shard_map/pack_rows/pallas_call | solution.py:431
  3.2 3.5 %collective-permute-start.12 = (bf16[48,8,128]{2,1,0:T(8,128)(2,1)}, bf16[48,8,128]{2,1,0:T(8,128)(2,1)S(1)}, u32[]{:S(2)}, u32[]{:S(2)}) collective-permute-start(bf16[48,8,128]{2,1,0:T(8,128)(2,1)} %get-tuple-element.48), channel_id=1, source_target_pairs={{0,9},{1,8},{2,11},{3,10},{4,13},{5,12},{6,15},{7,14},{8,1},{9,0},... | collective-permute-start | bytes 294920 | tf_op jit(solution)/shard_map/ppermute | solution.py:485
  6.8 0.6 %collective-permute-start = (bf16[53,8,128]{2,1,0:T(8,128)(2,1)}, bf16[53,8,128]{2,1,0:T(8,128)(2,1)S(1)}, u32[]{:S(2)}, u32[]{:S(2)}) collective-permute-start(bf16[53,8,128]{2,1,0:T(8,128)(2,1)} %get-tuple-element.36), channel_id=1, source_target_pairs={{0,8},{1,9},{2,10},{3,11},{4,12},{5,13},{6,14},{7,15},{8,0},{9,1},... | collective-permute-start | bytes 325640 | tf_op jit(solution)/shard_map/ppermute | solution.py:485
  7.4 3.2 %collective-permute-start.1 = (bf16[53,8,128]{2,1,0:T(8,128)(2,1)}, bf16[53,8,128]{2,1,0:T(8,128)(2,1)S(1)}, u32[]{:S(2)}, u32[]{:S(2)}) collective-permute-start(bf16[53,8,128]{2,1,0:T(8,128)(2,1)} %get-tuple-element.37), channel_id=1, source_target_pairs={{0,10},{1,11},{2,8},{3,9},{4,14},{5,15},{6,12},{7,13},{8,2},{9,3},... | collective-permute-start | bytes 325640 | tf_op jit(solution)/shard_map/ppermute | solution.py:485
  10.7 1.6 %collective-permute-start.2 = (bf16[53,8,128]{2,1,0:T(8,128)(2,1)}, bf16[53,8,128]{2,1,0:T(8,128)(2,1)S(1)}, u32[]{:S(2)}, u32[]{:S(2)}) collective-permute-start(bf16[53,8,128]{2,1,0:T(8,128)(2,1)} %get-tuple-element.38), channel_id=1, source_target_pairs={{0,4},{1,5},{2,6},{3,7},{4,0},{5,1},{6,2},{7,3},{8,12},{9,13},{10,... | collective-permute-start | bytes 325640 | tf_op jit(solution)/shard_map/ppermute | solution.py:485
  12.2 9.1 %collective-permute-start.4 = (bf16[53,8,128]{2,1,0:T(8,128)(2,1)}, bf16[53,8,128]{2,1,0:T(8,128)(2,1)S(1)}, u32[]{:S(2)}, u32[]{:S(2)}) collective-permute-start(bf16[53,8,128]{2,1,0:T(8,128)(2,1)} %get-tuple-element.40), channel_id=1, source_target_pairs={{0,12},{1,13},{2,14},{3,15},{4,8},{5,9},{6,10},{7,11},{8,4},{9,5},... | collective-permute-start | bytes 325640 | tf_op jit(solution)/shard_map/ppermute | solution.py:485
  21.3 0.5 collective-permute-start.5
  21.8 4.2 %collective-permute-done.1.rest_1_.rest_2_ = bf16[53,8,128]{2,1,0:T(8,128)(2,1)S(1)} collective-permute-done((bf16[53,8,128]{2,1,0:T(8,128)(2,1)}, bf16[53,8,128]{2,1,0:T(8,128)(2,1)S(1)}, u32[]{:S(2)}, u32[]{:S(2)}) %collective-permute-start.1) | collective-permute-done | bytes 108576 | tf_op jit(solution)/shard_map/ppermute | solution.py:485
  25.9 0.9 %collective-permute-start.6 = (bf16[53,8,128]{2,1,0:T(8,128)(2,1)}, bf16[53,8,128]{2,1,0:T(8,128)(2,1)S(1)}, u32[]{:S(2)}, u32[]{:S(2)}) collective-permute-start(bf16[53,8,128]{2,1,0:T(8,128)(2,1)} %get-tuple-element.42), channel_id=1, source_target_pairs={{0,14},{1,15},{2,12},{3,13},{4,10},{5,11},{6,8},{7,9},{8,6},{9,7},... | collective-permute-start | bytes 325640 | tf_op jit(solution)/shard_map/ppermute | solution.py:485
  26.9 1.2 %collective-permute-start.8 = (bf16[53,8,128]{2,1,0:T(8,128)(2,1)}, bf16[53,8,128]{2,1,0:T(8,128)(2,1)S(1)}, u32[]{:S(2)}, u32[]{:S(2)}) collective-permute-start(bf16[53,8,128]{2,1,0:T(8,128)(2,1)} %get-tuple-element.44), channel_id=1, source_target_pairs={{0,11},{1,10},{2,9},{3,8},{4,15},{5,14},{6,13},{7,12},{8,3},{9,2},... | collective-permute-start | bytes 325640 | tf_op jit(solution)/shard_map/ppermute | solution.py:485
  28.0 0.1 collective-permute-start.9
  28.1 0.3 collective-permute-done.5.rest_6_
  28.4 4.1 %collective-permute-start.10 = (bf16[53,8,128]{2,1,0:T(8,128)(2,1)}, bf16[53,8,128]{2,1,0:T(8,128)(2,1)S(1)}, u32[]{:S(2)}, u32[]{:S(2)}) collective-permute-start(bf16[53,8,128]{2,1,0:T(8,128)(2,1)} %get-tuple-element.46), channel_id=1, source_target_pairs={{0,2},{1,3},{2,0},{3,1},{4,6},{5,7},{6,4},{7,5},{8,10},{9,11},{10,... | collective-permute-start | bytes 325640 | tf_op jit(solution)/shard_map/ppermute | solution.py:485
  32.5 1.3 %collective-permute-done.6.rest_3_.rest_7_ = bf16[53,8,128]{2,1,0:T(8,128)(2,1)S(1)} collective-permute-done((bf16[53,8,128]{2,1,0:T(8,128)(2,1)}, bf16[53,8,128]{2,1,0:T(8,128)(2,1)S(1)}, u32[]{:S(2)}, u32[]{:S(2)}) %collective-permute-start.6) | collective-permute-done | bytes 108576 | tf_op jit(solution)/shard_map/ppermute | solution.py:485
  33.8 2.4 %collective-permute-done.7.rest_8_ = bf16[53,8,128]{2,1,0:T(8,128)(2,1)S(1)} collective-permute-done((bf16[53,8,128]{2,1,0:T(8,128)(2,1)}, bf16[53,8,128]{2,1,0:T(8,128)(2,1)S(1)}, u32[]{:S(2)}, u32[]{:S(2)}) %collective-permute-start.7) | collective-permute-done | bytes 108576 | tf_op jit(solution)/shard_map/ppermute | solution.py:485
  36.2 0.1 collective-permute-start.14
  36.3 1.5 %collective-permute-done.8.rest_9_ = bf16[53,8,128]{2,1,0:T(8,128)(2,1)S(1)} collective-permute-done((bf16[53,8,128]{2,1,0:T(8,128)(2,1)}, bf16[53,8,128]{2,1,0:T(8,128)(2,1)S(1)}, u32[]{:S(2)}, u32[]{:S(2)}) %collective-permute-start.8) | collective-permute-done | bytes 108576 | tf_op jit(solution)/shard_map/ppermute | solution.py:485
  37.8 2.6 %collective-permute-start.15 = (bf16[48,8,128]{2,1,0:T(8,128)(2,1)}, bf16[48,8,128]{2,1,0:T(8,128)(2,1)S(1)}, u32[]{:S(2)}, u32[]{:S(2)}) collective-permute-start(bf16[48,8,128]{2,1,0:T(8,128)(2,1)} %get-tuple-element.54), channel_id=1, source_target_pairs={{0,15},{1,14},{2,13},{3,12},{4,11},{5,10},{6,9},{7,8},{8,7},{9,6},... | collective-permute-start | bytes 294920 | tf_op jit(solution)/shard_map/ppermute | solution.py:485
  40.5 0.6 %collective-permute-start.13 = (bf16[20,8,128]{2,1,0:T(8,128)(2,1)S(1)}, bf16[20,8,128]{2,1,0:T(8,128)(2,1)S(1)}, u32[]{:S(2)}, u32[]{:S(2)}) collective-permute-start(bf16[20,8,128]{2,1,0:T(8,128)(2,1)S(1)} %collect_gains.1), channel_id=1, source_target_pairs={{0,1},{1,0},{2,3},{3,2},{4,5},{5,4},{6,7},{7,6},{8,9},{9,8},{10,11... | collective-permute-start | bytes 122888 | tf_op jit(solution)/shard_map/ppermute | solution.py:485
  41.1 0.9 %copy-done = bf16[53,8,128]{2,1,0:T(8,128)(2,1)S(1)} copy-done((bf16[53,8,128]{2,1,0:T(8,128)(2,1)S(1)}, bf16[53,8,128]{2,1,0:T(8,128)(2,1)}, u32[]{:S(2)}) %copy-start) | copy-done | bytes 108568
  42.0 0.7 %copy-done.1 = f32[8,384]{1,0:T(8,128)S(1)} copy-done((f32[8,384]{1,0:T(8,128)S(1)}, f32[8,384]{1,0:T(8,128)}, u32[]{:S(2)}) %copy-start.1) | copy-done | bytes 12312
  42.7 0.4 make_ready.1
  43.2 3.6 %gains_and_sums.1 = (f32[8,128,384]{2,1,0:T(8,128)S(1)}, f32[64,128]{1,0:T(8,128)S(1)}, s32[16,128]{1,0:T(8,128)S(1)}, f32[3,64,8,128]{3,2,1,0:T(8,128)S(1)}) custom-call(s32[1]{0:T(128)} %bitcast.me_s.turn_s, s32[1]{0:T(128)} %bitcast.me_s.turn_s, s32[8,128]{1,0:T(8,128)S(1)} %get-tuple-element.32.pairs_s, ...), custom_call_target="tpu_custom_call" | custom-call | tf_op jit(solution)/shard_map/gains_and_sums/pallas_call | solution.py:510
  46.8 2.0 %sum_and_apply.1 = bf16[64,8,384]{2,1,0:T(8,128)(2,1)} custom-call(s32[16,128]{1,0:T(8,128)S(1)} %get-tuple-element.49.slots_s, f32[8,128,384]{2,1,0:T(8,128)S(1)} %get-tuple-element.50.gains_ref, f32[64,128]{1,0:T(8,128)S(1)} %get-tuple-element.51.recip_ref, f32[3,64,8,128]{3,2,1,0:T(8,128)S(1)} %get-tuple-element.52.sums_ref, ...), custom_call_target="tpu_custom_call" | custom-call | tf_op jit(solution)/shard_map/sum_and_apply/pallas_call | solution.py:534
  (17 shorter events, 0.1 us)
Async XLA Ops:
  3.2 9.0 %collective-permute-start.12 = (bf16[48,8,128]{2,1,0:T(8,128)(2,1)}, bf16[48,8,128]{2,1,0:T(8,128)(2,1)S(1)}, u32[]{:S(2)}, u32[]{:S(2)}) collective-permute-start(bf16[48,8,128]{2,1,0:T(8,128)(2,1)} %get-tuple-element.48), channel_id=1, source_target_pairs={{0,9},{1,8},{2,11},{3,10},{4,13},{5,12},{6,15},{7,14},{8,1},{9,0},... | collective-permute-start | bytes 294920 | tf_op jit(solution)/shard_map/ppermute | solution.py:485
  6.8 14.5 %collective-permute-start = (bf16[53,8,128]{2,1,0:T(8,128)(2,1)}, bf16[53,8,128]{2,1,0:T(8,128)(2,1)S(1)}, u32[]{:S(2)}, u32[]{:S(2)}) collective-permute-start(bf16[53,8,128]{2,1,0:T(8,128)(2,1)} %get-tuple-element.36), channel_id=1, source_target_pairs={{0,8},{1,9},{2,10},{3,11},{4,12},{5,13},{6,14},{7,15},{8,0},{9,1},... | collective-permute-start | bytes 325640 | tf_op jit(solution)/shard_map/ppermute | solution.py:485
  7.4 18.5 %collective-permute-start.1 = (bf16[53,8,128]{2,1,0:T(8,128)(2,1)}, bf16[53,8,128]{2,1,0:T(8,128)(2,1)S(1)}, u32[]{:S(2)}, u32[]{:S(2)}) collective-permute-start(bf16[53,8,128]{2,1,0:T(8,128)(2,1)} %get-tuple-element.37), channel_id=1, source_target_pairs={{0,10},{1,11},{2,8},{3,9},{4,14},{5,15},{6,12},{7,13},{8,2},{9,3},... | collective-permute-start | bytes 325640 | tf_op jit(solution)/shard_map/ppermute | solution.py:485
  10.7 16.2 %collective-permute-start.2 = (bf16[53,8,128]{2,1,0:T(8,128)(2,1)}, bf16[53,8,128]{2,1,0:T(8,128)(2,1)S(1)}, u32[]{:S(2)}, u32[]{:S(2)}) collective-permute-start(bf16[53,8,128]{2,1,0:T(8,128)(2,1)} %get-tuple-element.38), channel_id=1, source_target_pairs={{0,4},{1,5},{2,6},{3,7},{4,0},{5,1},{6,2},{7,3},{8,12},{9,13},{10,... | collective-permute-start | bytes 325640 | tf_op jit(solution)/shard_map/ppermute | solution.py:485
  12.2 14.6 %collective-permute-start.3 = (bf16[53,8,128]{2,1,0:T(8,128)(2,1)}, bf16[53,8,128]{2,1,0:T(8,128)(2,1)S(1)}, u32[]{:S(2)}, u32[]{:S(2)}) collective-permute-start(bf16[53,8,128]{2,1,0:T(8,128)(2,1)} %get-tuple-element.39), channel_id=1, source_target_pairs={{0,5},{1,4},{2,7},{3,6},{4,1},{5,0},{6,3},{7,2},{8,13},{9,12},{10,... | collective-permute-start | bytes 325640 | tf_op jit(solution)/shard_map/ppermute | solution.py:485
  12.2 15.8 %collective-permute-start.4 = (bf16[53,8,128]{2,1,0:T(8,128)(2,1)}, bf16[53,8,128]{2,1,0:T(8,128)(2,1)S(1)}, u32[]{:S(2)}, u32[]{:S(2)}) collective-permute-start(bf16[53,8,128]{2,1,0:T(8,128)(2,1)} %get-tuple-element.40), channel_id=1, source_target_pairs={{0,12},{1,13},{2,14},{3,15},{4,8},{5,9},{6,10},{7,11},{8,4},{9,5},... | collective-permute-start | bytes 325640 | tf_op jit(solution)/shard_map/ppermute | solution.py:485
  21.3 7.1 %collective-permute-start.5 = (bf16[53,8,128]{2,1,0:T(8,128)(2,1)}, bf16[53,8,128]{2,1,0:T(8,128)(2,1)S(1)}, u32[]{:S(2)}, u32[]{:S(2)}) collective-permute-start(bf16[53,8,128]{2,1,0:T(8,128)(2,1)} %get-tuple-element.41), channel_id=1, source_target_pairs={{0,6},{1,7},{2,4},{3,5},{4,2},{5,3},{6,0},{7,1},{8,14},{9,15},{10,... | collective-permute-start | bytes 325640 | tf_op jit(solution)/shard_map/ppermute | solution.py:485
  25.9 7.8 %collective-permute-start.6 = (bf16[53,8,128]{2,1,0:T(8,128)(2,1)}, bf16[53,8,128]{2,1,0:T(8,128)(2,1)S(1)}, u32[]{:S(2)}, u32[]{:S(2)}) collective-permute-start(bf16[53,8,128]{2,1,0:T(8,128)(2,1)} %get-tuple-element.42), channel_id=1, source_target_pairs={{0,14},{1,15},{2,12},{3,13},{4,10},{5,11},{6,8},{7,9},{8,6},{9,7},... | collective-permute-start | bytes 325640 | tf_op jit(solution)/shard_map/ppermute | solution.py:485
  26.8 9.4 %collective-permute-start.7 = (bf16[53,8,128]{2,1,0:T(8,128)(2,1)}, bf16[53,8,128]{2,1,0:T(8,128)(2,1)S(1)}, u32[]{:S(2)}, u32[]{:S(2)}) collective-permute-start(bf16[53,8,128]{2,1,0:T(8,128)(2,1)} %get-tuple-element.43), channel_id=1, source_target_pairs={{0,7},{1,6},{2,5},{3,4},{4,3},{5,2},{6,1},{7,0},{8,15},{9,14},{10,... | collective-permute-start | bytes 325640 | tf_op jit(solution)/shard_map/ppermute | solution.py:485
  26.9 11.0 %collective-permute-start.8 = (bf16[53,8,128]{2,1,0:T(8,128)(2,1)}, bf16[53,8,128]{2,1,0:T(8,128)(2,1)S(1)}, u32[]{:S(2)}, u32[]{:S(2)}) collective-permute-start(bf16[53,8,128]{2,1,0:T(8,128)(2,1)} %get-tuple-element.44), channel_id=1, source_target_pairs={{0,11},{1,10},{2,9},{3,8},{4,15},{5,14},{6,13},{7,12},{8,3},{9,2},... | collective-permute-start | bytes 325640 | tf_op jit(solution)/shard_map/ppermute | solution.py:485
  28.0 12.5 %collective-permute-start.9 = (bf16[53,8,128]{2,1,0:T(8,128)(2,1)}, bf16[53,8,128]{2,1,0:T(8,128)(2,1)S(1)}, u32[]{:S(2)}, u32[]{:S(2)}) collective-permute-start(bf16[53,8,128]{2,1,0:T(8,128)(2,1)} %get-tuple-element.45), channel_id=1, source_target_pairs={{0,1},{1,0},{2,3},{3,2},{4,5},{5,4},{6,7},{7,6},{8,9},{9,8},{10,11... | collective-permute-start | bytes 325640 | tf_op jit(solution)/shard_map/ppermute | solution.py:485
  28.4 14.7 %collective-permute-start.10 = (bf16[53,8,128]{2,1,0:T(8,128)(2,1)}, bf16[53,8,128]{2,1,0:T(8,128)(2,1)S(1)}, u32[]{:S(2)}, u32[]{:S(2)}) collective-permute-start(bf16[53,8,128]{2,1,0:T(8,128)(2,1)} %get-tuple-element.46), channel_id=1, source_target_pairs={{0,2},{1,3},{2,0},{3,1},{4,6},{5,7},{6,4},{7,5},{8,10},{9,11},{10,... | collective-permute-start | bytes 325640 | tf_op jit(solution)/shard_map/ppermute | solution.py:485
  33.8 9.4 %collective-permute-start.11 = (bf16[53,8,128]{2,1,0:T(8,128)(2,1)}, bf16[53,8,128]{2,1,0:T(8,128)(2,1)S(1)}, u32[]{:S(2)}, u32[]{:S(2)}) collective-permute-start(bf16[53,8,128]{2,1,0:T(8,128)(2,1)} %get-tuple-element.47), channel_id=1, source_target_pairs={{0,3},{1,2},{2,1},{3,0},{4,7},{5,6},{6,5},{7,4},{8,11},{9,10},{10,... | collective-permute-start | bytes 325640 | tf_op jit(solution)/shard_map/ppermute | solution.py:485
  36.2 10.5 %collective-permute-start.14 = (bf16[48,8,128]{2,1,0:T(8,128)(2,1)}, bf16[48,8,128]{2,1,0:T(8,128)(2,1)S(1)}, u32[]{:S(2)}, u32[]{:S(2)}) collective-permute-start(bf16[48,8,128]{2,1,0:T(8,128)(2,1)} %get-tuple-element.53), channel_id=1, source_target_pairs={{0,13},{1,12},{2,15},{3,14},{4,9},{5,8},{6,11},{7,10},{8,5},{9,4},... | collective-permute-start | bytes 294920 | tf_op jit(solution)/shard_map/ppermute | solution.py:485
  37.8 8.9 %collective-permute-start.15 = (bf16[48,8,128]{2,1,0:T(8,128)(2,1)}, bf16[48,8,128]{2,1,0:T(8,128)(2,1)S(1)}, u32[]{:S(2)}, u32[]{:S(2)}) collective-permute-start(bf16[48,8,128]{2,1,0:T(8,128)(2,1)} %get-tuple-element.54), channel_id=1, source_target_pairs={{0,15},{1,14},{2,13},{3,12},{4,11},{5,10},{6,9},{7,8},{8,7},{9,6},... | collective-permute-start | bytes 294920 | tf_op jit(solution)/shard_map/ppermute | solution.py:485
  40.5 2.6 %collective-permute-start.13 = (bf16[20,8,128]{2,1,0:T(8,128)(2,1)S(1)}, bf16[20,8,128]{2,1,0:T(8,128)(2,1)S(1)}, u32[]{:S(2)}, u32[]{:S(2)}) collective-permute-start(bf16[20,8,128]{2,1,0:T(8,128)(2,1)S(1)} %collect_gains.1), channel_id=1, source_target_pairs={{0,1},{1,0},{2,3},{3,2},{4,5},{5,4},{6,7},{7,6},{8,9},{9,8},{10,11... | collective-permute-start | bytes 122888 | tf_op jit(solution)/shard_map/ppermute | solution.py:485
  41.1 0.9 %copy-start = (bf16[53,8,128]{2,1,0:T(8,128)(2,1)S(1)}, bf16[53,8,128]{2,1,0:T(8,128)(2,1)}, u32[]{:S(2)}) copy-start(bf16[53,8,128]{2,1,0:T(8,128)(2,1)} %get-tuple-element.31.own_ref) | copy-start | bytes 325636
  42.0 0.7 %copy-start.1 = (f32[8,384]{1,0:T(8,128)S(1)}, f32[8,384]{1,0:T(8,128)}, u32[]{:S(2)}) copy-start(f32[8,384]{1,0:T(8,128)} %get-tuple-element.30.small_ref) | copy-start | bytes 36868

commit v6 on v5

--- a/solution.py
+++ b/solution.py
@@ -56,12 +56,13 @@
     pairs_hbm,
     *rest,
 ):
-    outs = rest[:-15]
+    outs = rest[:-16]
     (
         weights_ref,
         offset_ref,
         pairs_ref,
         small_ref,
+        parts_ref,
         owner_s,
         place_s,
         count_s,
@@ -73,7 +74,7 @@
         meta_ref,
         block_ref,
         sems,
-    ) = rest[-15:]
+    ) = rest[-16:]
     rows = vis_ref.shape[0]
     chunks = vis_ref.shape[2] // LANES
     devices = block_ref.shape[0]
@@ -136,13 +137,20 @@
         lanes = slice(c * LANES, (c + 1) * LANES)
         small_ref[steps : steps + 1, lanes] = offset_ref[c : c + 1, :].astype(jnp.float32)
     small_ref[4:6, 0 : pairs_ref.shape[1]] = pairs_ref[...].astype(jnp.float32)
+    left = small_ref[...]
+    for p in range(3):
+        piece = left.astype(jnp.bfloat16)
+        left = left - piece.astype(jnp.float32)
+        for c in range(chunks):
+            parts_ref[p * chunks + c] = piece[:, c * LANES : (c + 1) * LANES]
 
     at = chunks * capacity
     if near > 1:
         pairs = [(meta_ref, outs[x].at[pl.ds(at, depth)]) for x in with_gains(near)]
     else:
         pairs = [(meta_ref, outs[1])]
-    pairs += [(small_ref, outs[-1])]
+    at_small = at + depth if near > 1 else 0
+    pairs += [(parts_ref, outs[0 if near > 1 else -1].at[pl.ds(at_small, 3 * chunks)])]
     start = len(moves) + PARTS
     sends = start_all(pairs, sems.at[pl.ds(start, len(pairs))])
     start += len(pairs)
@@ -166,23 +174,57 @@
         send.wait()
 
 
-def ready_kernel(small_ref, own_ref, own_out_ref, high_ref, low_ref, pairs_ref, sem):
+def ready_kernel(
+    at, chunks, owned, stations, trows, turn_s, own_ref, own_out_ref, choice_ref, basis_ref, sem
+):
     move = pltpu.make_async_copy(own_ref, own_out_ref, sem)
     move.start()
-    small = small_ref[...]
+    pieces = [
+        jnp.concatenate(
+            [own_ref[at + p * chunks + c].astype(jnp.float32) for c in range(chunks)], axis=1
+        )
+        for p in range(3)
+    ]
+    small = pieces[0] + pieces[1] + pieces[2]
     channels = small.shape[1]
-    pairs_ref[...] = small[:, 0:LANES].astype(jnp.int32)
-    index = lax.broadcasted_iota(jnp.int32, (LANES, channels), 0)
-    knot = ((index & 63) >> 3).astype(jnp.float32)
-    basis = jnp.zeros((LANES, channels), jnp.float32)
+    half = stations // 2
+
+    station = small[4:6, 0:LANES]
+    sender = jnp.floor((station + 0.5) * (1.0 / stations))
+    within = station - sender * stations
+    second = (within >= float(half)).astype(jnp.float32)
+    line = (sender.astype(jnp.int32) ^ turn_s[0]).astype(jnp.float32) * trows + within - second * half
+    diagonal = lax.broadcasted_iota(jnp.int32, (owned, LANES), 0) == lax.broadcasted_iota(
+        jnp.int32, (owned, LANES), 1
+    )
+
+    def upright(row):
+        return jnp.sum(jnp.where(diagonal, row, 0.0), axis=1, keepdims=True)
+
+    lines = jnp.concatenate([upright(line[side : side + 1]) for side in range(2)], axis=0)
+    seconds = jnp.concatenate([upright(second[side : side + 1]) for side in range(2)], axis=0)
+    table = choice_ref.shape[1]
+    same = lines == lax.broadcasted_iota(jnp.int32, (2 * owned, table), 1).astype(jnp.float32)
+    for h in range(2):
+        choice_ref[2 * owned * h : 2 * owned * (h + 1), :] = (
+            jnp.where(jnp.logical_and(same, seconds == float(h)), 1.0, 0.0).astype(jnp.bfloat16)
+        )
+
+    index = lax.broadcasted_iota(jnp.int32, (64, channels), 0)
+    knot = (index >> 3).astype(jnp.float32)
+    basis = jnp.zeros((64, channels), jnp.float32)
     for step in range(3):
         basis = basis + jnp.where(knot == small[3:4, :] + float(step), small[step : step + 1, :], 0.0)
     high = basis.astype(jnp.bfloat16).astype(jnp.float32)
-    low = basis - high
-    part = index & 7
+    component = index & 7
     for j in range(8):
-        high_ref[j] = jnp.where(part == j, high, 0.0).astype(jnp.bfloat16)
-        low_ref[j] = jnp.where(part == j, low, 0.0).astype(jnp.bfloat16)
+        cols = slice(j * channels, (j + 1) * channels)
+        main = jnp.where(component == j, high, 0.0).astype(jnp.bfloat16)
+        rest = jnp.where(component == j, basis - high, 0.0).astype(jnp.bfloat16)
+        basis_ref[0:64, cols] = main
+        basis_ref[64:128, cols] = main
+        basis_ref[128:192, cols] = rest
+        basis_ref[192:256, cols] = jnp.zeros_like(rest)
     move.wait()
 
 
@@ -239,9 +281,9 @@
 def add_table(table_ref, x, block, at, depth):
     gain_tiles = (depth - 1) // 2
     for i in range(gain_tiles):
-        table_ref[x, i * SUB : (i + 1) * SUB, :] = block[at + i].astype(jnp.float32) + block[
-            at + gain_tiles + i
-        ].astype(jnp.float32)
+        rows = slice((x * gain_tiles + i) * SUB, (x * gain_tiles + i + 1) * SUB)
+        table_ref[rows, 0:LANES] = block[at + i].astype(jnp.float32)
+        table_ref[rows, LANES : 2 * LANES] = block[at + gain_tiles + i].astype(jnp.float32)
     return block[at + 2 * gain_tiles].astype(jnp.float32)
 
 
@@ -253,15 +295,13 @@
     return hits
 
 
-def middle_kernel(capacity, near, stations, order, turn_s, me_s, pairs_s, high_ref, low_ref, *rest):
-    arrived, passed = dict(zip(order, rest)), rest[len(order) : -13]
-    gains_ref, recip_ref, slots_ref, sums_ref = rest[-13:-9]
-    table_ref, pick_ref, owner_ref, slot_ref, slots_v, slots_s, one_ref, two_ref, sem = rest[-9:]
-    devices = table_ref.shape[0]
+def middle_kernel(capacity, near, depth, order, me_s, choice_ref, basis_ref, *rest):
+    arrived, passed = dict(zip(order, rest)), rest[len(order) : -12]
+    gains_ref, recip_ref, slots_ref, sums_ref = rest[-12:-8]
+    table_ref, owner_ref, slot_ref, slots_v, slots_s, one_ref, two_ref, sem = rest[-8:]
+    devices = owner_ref.shape[0]
     owned = recip_ref.shape[0]
     chunks = sums_ref.shape[0]
-    half = stations // 2
-    depth = 2 * (table_ref.shape[1] // SUB) + 1
     for x in range(devices):
         if near == 1:
             code = add_table(table_ref, x, arrived[0].at[x], 0, depth)
@@ -283,33 +323,19 @@
     tally = jnp.sum(hits, axis=1, keepdims=True)
     recip_ref[...] = jnp.broadcast_to(1.0 / jnp.maximum(tally, 1.0), recip_ref.shape)
 
-    turn = turn_s[0]
-    column = lax.broadcasted_iota(jnp.int32, (1, LANES), 1)
-    used = (column & 63) < USED
-    upper = column >> 6
-
-    def pick(b, carry):
-        for side in range(2):
-            s = pairs_s[4 + side, b]
-            d = s // stations
-            within = s - d * stations
-            second = jnp.where(within >= half, 1, 0)
-            row = table_ref[d ^ turn, pl.ds(within - second * half, 1), :]
-            keep = jnp.logical_and(used, upper == second)
-            pick_ref[pl.ds(side * owned + b, 1), :] = jnp.where(keep, row, 0.0)
-        return carry
-
-    lax.fori_loop(0, owned, pick, 0, unroll=8)
-    both = pick_ref[...]
-    both_high = both.astype(jnp.bfloat16)
-    both_low = (both - both_high.astype(jnp.float32)).astype(jnp.bfloat16)
-    both_two = jnp.concatenate([both_high, both_low], axis=1)
-    for j in range(8):
-        high, low = high_ref[j], low_ref[j]
-        fine = jnp.dot(
-            both_two, jnp.concatenate([high, high], axis=0), preferred_element_type=jnp.float32
-        ) + jnp.dot(both_high, low, preferred_element_type=jnp.float32)
-        gains_ref[j] = fine.astype(jnp.bfloat16).astype(jnp.float32)
+    picked = jnp.dot(
+        choice_ref[...], table_ref[...].astype(jnp.bfloat16), preferred_element_type=jnp.float32
+    )
+    front, back = picked[0 : 2 * owned], picked[2 * owned : 4 * owned]
+    lower = lax.broadcasted_iota(jnp.int32, (2 * owned, LANES), 1) < 64
+    high = front[:, 0:LANES] + pltpu.roll(back[:, 0:LANES], 64, 1)
+    low = pltpu.roll(front[:, LANES:], 64, 1) + back[:, LANES:]
+    coarse = jnp.concatenate([jnp.where(lower, high, low), jnp.where(lower, high, 0.0)], axis=1)
+    coarse = coarse.astype(jnp.bfloat16)
+    width = 2 * LANES * chunks
+    for n in range(0, basis_ref.shape[1], width):
+        fine = jnp.dot(coarse, basis_ref[:, n : n + width], preferred_element_type=jnp.float32)
+        gains_ref[:, n : n + width] = fine.astype(jnp.bfloat16).astype(jnp.float32)
 
     one_ref[...] = jnp.zeros_like(one_ref)
     two_ref[...] = jnp.zeros_like(two_ref)
@@ -341,13 +367,13 @@
     done = res_ref.reshape(chunks * owned * parts, LANES)
     sends = []
     for c in range(chunks):
-        cols = slice(c * LANES, (c + 1) * LANES)
         for b0 in range(0, owned, SUB):
             scale = recip_ref[b0 : b0 + SUB, :]
             row = (c * owned + b0) * parts
             vis = [flat[pl.ds(row + j, SUB, stride=parts), :] for j in range(parts)]
-            lhs = [gains_ref[j, b0 : b0 + SUB, cols] for j in range(parts)]
-            rhs = [gains_ref[j, owned + b0 : owned + b0 + SUB, cols] for j in range(parts)]
+            planes = [slice(j * channels + c * LANES, j * channels + (c + 1) * LANES) for j in range(parts)]
+            lhs = [gains_ref[b0 : b0 + SUB, plane] for plane in planes]
+            rhs = [gains_ref[owned + b0 : owned + b0 + SUB, plane] for plane in planes]
             mid_re, mid_im = [], []
             for row_a in range(2):
                 for col_b in range(2):
@@ -422,9 +448,13 @@
             shape((rows_at + (depth if x in long else 0), parts, LANES), bf16)
             for x in range(devices)
         ]
+        outs[0] = shape((rows_at + depth + 3 * chunks, parts, LANES), bf16)
     else:
-        outs = [shape((devices,) + block, bf16), shape((depth, SUB, LANES), bf16)]
-    outs += [shape((SUB, channels), f32)]
+        outs = [
+            shape((devices,) + block, bf16),
+            shape((depth, SUB, LANES), bf16),
+            shape((3 * chunks, SUB, LANES), bf16),
+        ]
     pairs = baseline_station_pairs.T
     weights = band_weights.T
     offset = band_offset.reshape(chunks, LANES)
@@ -438,6 +468,7 @@
             pltpu.VMEM(offset.shape, i32),
             pltpu.VMEM(pairs.shape, i32),
             pltpu.VMEM((SUB, channels), f32),
+            pltpu.VMEM((3 * chunks, SUB, LANES), bf16),
             pltpu.SMEM((rows,), i32),
             pltpu.SMEM((rows,), i32),
             pltpu.SMEM((devices,), i32),
@@ -465,27 +496,28 @@
     )
 
 
-    def ready(own):
+    trows = gain_tiles * SUB
+
+    def ready(own, at):
         return pl.pallas_call(
-            ready_kernel,
+            functools.partial(ready_kernel, at, chunks, owned, stations, trows),
             out_shape=[
                 shape(own.shape, bf16),
-                shape((parts, LANES, channels), bf16),
-                shape((parts, LANES, channels), bf16),
-                shape((SUB, LANES), i32),
+                shape((4 * owned, devices * trows), bf16),
+                shape((2 * LANES, parts * channels), bf16),
             ],
-            in_specs=[vmem, anywhere],
-            out_specs=[vmem] * 4,
+            in_specs=[smem, vmem],
+            out_specs=[vmem] * 3,
             scratch_shapes=[dma],
             compiler_params=some,
             name="make_ready",
-        )(sent[-1], own)
+        )(turn, own)
 
     def swap(array, x):
         return lax.ppermute(array, "bl", [(d, d ^ x) for d in range(devices)])
 
     if halves:
-        own, high, low, ints = ready(sent[0])
+        own, choice, basis = ready(sent[0], rows_at + depth)
         arrived = {x: swap(sent[x], x) if x else own for x in range(devices)}
         order, late = schedule(near)
         even = list(range(near, devices, 2))
@@ -505,21 +537,20 @@
             1: lax.all_to_all(sent[0], "bl", split_axis=0, concat_axis=0, tiled=True),
         }
         order, late, passed = [0], [1], []
-        _, high, low, ints = ready(sent[1])
+        _, choice, basis = ready(sent[2], 0)
 
     gains, recip, slots, sums = pl.pallas_call(
-        functools.partial(middle_kernel, capacity, near, stations, order),
+        functools.partial(middle_kernel, capacity, near, depth, order),
         out_shape=(
-            shape((parts, 2 * owned, channels), f32),
+            shape((2 * owned, parts * channels), f32),
             shape((owned, LANES), f32),
             shape((devices, LANES), i32),
             shape((chunks, owned, parts, LANES), f32),
         ),
-        in_specs=[smem] * 3 + [vmem] * (2 + len(order) + len(passed)),
+        in_specs=[smem] + [vmem] * (2 + len(order) + len(passed)),
         out_specs=(vmem,) * 4,
         scratch_shapes=[
-            pltpu.VMEM((devices, gain_tiles * SUB, LANES), f32),
-            pltpu.VMEM((2 * owned, LANES), f32),
+            pltpu.VMEM((devices * trows, 2 * LANES), f32),
             pltpu.VMEM((devices, LANES), f32),
             pltpu.VMEM((devices, LANES), f32),
             pltpu.VMEM((devices, LANES), i32),
@@ -530,7 +561,7 @@
         ],
         compiler_params=some,
         name="gains_and_sums",
-    )(turn, me, ints, high, low, *[arrived[x] for x in order], *passed)
+    )(me, choice, basis, *[arrived[x] for x in order], *passed)
     return pl.pallas_call(
         functools.partial(finish_kernel, capacity, late),
         out_shape=shape((owned, parts, channels), bf16),

time: 49.1 us -> 48 us (0.978)
  Pallas kernels: 9.26 us -> 7.72 us
  waiting for transfers between devices: 9.7 us -> 11 us
  local copies, waits for them, and re-layouts: 1.6 us -> 0.9 us
    pallas_call x2, Pallas kernels: 3.97 us -> 2.45 us  [the longest x1 1.92 us: on_device(): pl.pallas_call(functools.partial(middle_kernel, capacity, near, depth, or...]
    ppermute x16, waiting for transfers between devices: 9.7 us -> 11 us  [swap(): return lax.ppermute(array, 'bl', [(d, d ^ x) for d in range(devices)])]
    unnamed x4 -> x2, local copies, waits for them, and re-layouts: 1.6 us -> 0.9 us
  transfers between devices with their start and end apart: 16 -> 16, of which waited for: 5 -> 6; matrix products, arithmetic and copies ran while one was open for 0% -> 0% of each run, Pallas kernels for 8% -> 5%
where the time goes in v6:
time: 48 us; the launch traced here: 47.8 us
  starting transfers between devices  28.1 us (59%)
  waiting for transfers between devices  11 us (23%)
  Pallas kernels  7.72 us (16%)
  local copies, waits for them, and re-layouts  0.9 us (2%)
    ppermute x16, starting transfers between devices, swap(): return lax.ppermute(array, 'bl', [(d, d ^ x) for d in range(devices)])  28.1 us
    ppermute x16, waiting for transfers between devices, swap(): return lax.ppermute(array, 'bl', [(d, d ^ x) for d in range(devices)])  11 us
    pallas_call x1, Pallas kernels, on_device(): pl.pallas_call(functools.partial(pack_kernel, capacity, near), out_shape=...  3.23 us
    pallas_call x1, Pallas kernels, on_device(): pl.pallas_call(functools.partial(finish_kernel, capacity, late), out_shap...  1.97 us
    pallas_call x1, Pallas kernels, on_device(): pl.pallas_call(functools.partial(middle_kernel, capacity, near, depth, or...  1.92 us
  transfers between devices with their start and end apart: 16, of which 6 were waited for; matrix products, arithmetic and copies ran while one was open for 0% of the time, Pallas kernels for 5%

profile of v6, /device:TPU:0, one launch (start us, length us, event | category | flops | bytes accessed | tf_op | source)
XLA Modules:
  0.0 47.8 jit_solution(10559478967759152168)
XLA Ops:
  0.0 3.2 %pack_rows.1 = (bf16[62,8,128]{2,1,0:T(8,128)(2,1)}, bf16[53,8,128]{2,1,0:T(8,128)(2,1)}, bf16[53,8,128]{2,1,0:T(8,128)(2,1)}, bf16[53,8,128]{2,1,0:T(8,128)(2,1...) custom-call(s32[1]{0:T(128)} %bitcast.me_s.turn_s, ...), custom_call_target="tpu_custom_call" | custom-call | tf_op jit(solution)/shard_map/pack_rows/pallas_call | solution.py:461
  3.2 3.5 %collective-permute-start.12 = (bf16[48,8,128]{2,1,0:T(8,128)(2,1)}, bf16[48,8,128]{2,1,0:T(8,128)(2,1)S(1)}, u32[]{:S(2)}, u32[]{:S(2)}) collective-permute-start(bf16[48,8,128]{2,1,0:T(8,128)(2,1)} %get-tuple-element.44), channel_id=1, source_target_pairs={{0,9},{1,8},{2,11},{3,10},{4,13},{5,12},{6,15},{7,14},{8,1},{9,0},... | collective-permute-start | bytes 294920 | tf_op jit(solution)/shard_map/ppermute | solution.py:517
  6.8 0.6 %collective-permute-start = (bf16[53,8,128]{2,1,0:T(8,128)(2,1)}, bf16[53,8,128]{2,1,0:T(8,128)(2,1)S(1)}, u32[]{:S(2)}, u32[]{:S(2)}) collective-permute-start(bf16[53,8,128]{2,1,0:T(8,128)(2,1)} %get-tuple-element.32), channel_id=1, source_target_pairs={{0,8},{1,9},{2,10},{3,11},{4,12},{5,13},{6,14},{7,15},{8,0},{9,1},... | collective-permute-start | bytes 325640 | tf_op jit(solution)/shard_map/ppermute | solution.py:517
  7.4 3.2 %collective-permute-start.1 = (bf16[53,8,128]{2,1,0:T(8,128)(2,1)}, bf16[53,8,128]{2,1,0:T(8,128)(2,1)S(1)}, u32[]{:S(2)}, u32[]{:S(2)}) collective-permute-start(bf16[53,8,128]{2,1,0:T(8,128)(2,1)} %get-tuple-element.33), channel_id=1, source_target_pairs={{0,10},{1,11},{2,8},{3,9},{4,14},{5,15},{6,12},{7,13},{8,2},{9,3},... | collective-permute-start | bytes 325640 | tf_op jit(solution)/shard_map/ppermute | solution.py:517
  10.7 1.6 %collective-permute-start.2 = (bf16[53,8,128]{2,1,0:T(8,128)(2,1)}, bf16[53,8,128]{2,1,0:T(8,128)(2,1)S(1)}, u32[]{:S(2)}, u32[]{:S(2)}) collective-permute-start(bf16[53,8,128]{2,1,0:T(8,128)(2,1)} %get-tuple-element.34), channel_id=1, source_target_pairs={{0,4},{1,5},{2,6},{3,7},{4,0},{5,1},{6,2},{7,3},{8,12},{9,13},{10,... | collective-permute-start | bytes 325640 | tf_op jit(solution)/shard_map/ppermute | solution.py:517
  12.2 9.1 %collective-permute-start.4 = (bf16[53,8,128]{2,1,0:T(8,128)(2,1)}, bf16[53,8,128]{2,1,0:T(8,128)(2,1)S(1)}, u32[]{:S(2)}, u32[]{:S(2)}) collective-permute-start(bf16[53,8,128]{2,1,0:T(8,128)(2,1)} %get-tuple-element.36), channel_id=1, source_target_pairs={{0,12},{1,13},{2,14},{3,15},{4,8},{5,9},{6,10},{7,11},{8,4},{9,5},... | collective-permute-start | bytes 325640 | tf_op jit(solution)/shard_map/ppermute | solution.py:517
  21.3 0.5 collective-permute-start.5
  21.8 4.2 %collective-permute-done.1.rest_1_.rest_2_ = bf16[53,8,128]{2,1,0:T(8,128)(2,1)S(1)} collective-permute-done((bf16[53,8,128]{2,1,0:T(8,128)(2,1)}, bf16[53,8,128]{2,1,0:T(8,128)(2,1)S(1)}, u32[]{:S(2)}, u32[]{:S(2)}) %collective-permute-start.1) | collective-permute-done | bytes 108576 | tf_op jit(solution)/shard_map/ppermute | solution.py:517
  26.0 0.9 %collective-permute-start.6 = (bf16[53,8,128]{2,1,0:T(8,128)(2,1)}, bf16[53,8,128]{2,1,0:T(8,128)(2,1)S(1)}, u32[]{:S(2)}, u32[]{:S(2)}) collective-permute-start(bf16[53,8,128]{2,1,0:T(8,128)(2,1)} %get-tuple-element.38), channel_id=1, source_target_pairs={{0,14},{1,15},{2,12},{3,13},{4,10},{5,11},{6,8},{7,9},{8,6},{9,7},... | collective-permute-start | bytes 325640 | tf_op jit(solution)/shard_map/ppermute | solution.py:517
  26.9 1.2 %collective-permute-start.8 = (bf16[53,8,128]{2,1,0:T(8,128)(2,1)}, bf16[53,8,128]{2,1,0:T(8,128)(2,1)S(1)}, u32[]{:S(2)}, u32[]{:S(2)}) collective-permute-start(bf16[53,8,128]{2,1,0:T(8,128)(2,1)} %get-tuple-element.40), channel_id=1, source_target_pairs={{0,11},{1,10},{2,9},{3,8},{4,15},{5,14},{6,13},{7,12},{8,3},{9,2},... | collective-permute-start | bytes 325640 | tf_op jit(solution)/shard_map/ppermute | solution.py:517
  28.1 0.1 collective-permute-start.9
  28.1 0.3 collective-permute-done.5.rest_6_
  28.4 4.1 %collective-permute-start.10 = (bf16[53,8,128]{2,1,0:T(8,128)(2,1)}, bf16[53,8,128]{2,1,0:T(8,128)(2,1)S(1)}, u32[]{:S(2)}, u32[]{:S(2)}) collective-permute-start(bf16[53,8,128]{2,1,0:T(8,128)(2,1)} %get-tuple-element.42), channel_id=1, source_target_pairs={{0,2},{1,3},{2,0},{3,1},{4,6},{5,7},{6,4},{7,5},{8,10},{9,11},{10,... | collective-permute-start | bytes 325640 | tf_op jit(solution)/shard_map/ppermute | solution.py:517
  32.5 1.3 %collective-permute-done.6.rest_3_.rest_7_ = bf16[53,8,128]{2,1,0:T(8,128)(2,1)S(1)} collective-permute-done((bf16[53,8,128]{2,1,0:T(8,128)(2,1)}, bf16[53,8,128]{2,1,0:T(8,128)(2,1)S(1)}, u32[]{:S(2)}, u32[]{:S(2)}) %collective-permute-start.6) | collective-permute-done | bytes 108576 | tf_op jit(solution)/shard_map/ppermute | solution.py:517
  33.8 2.4 %collective-permute-done.7.rest_8_ = bf16[53,8,128]{2,1,0:T(8,128)(2,1)S(1)} collective-permute-done((bf16[53,8,128]{2,1,0:T(8,128)(2,1)}, bf16[53,8,128]{2,1,0:T(8,128)(2,1)S(1)}, u32[]{:S(2)}, u32[]{:S(2)}) %collective-permute-start.7) | collective-permute-done | bytes 108576 | tf_op jit(solution)/shard_map/ppermute | solution.py:517
  36.2 0.1 collective-permute-start.14
  36.3 1.5 %collective-permute-done.8.rest_9_ = bf16[53,8,128]{2,1,0:T(8,128)(2,1)S(1)} collective-permute-done((bf16[53,8,128]{2,1,0:T(8,128)(2,1)}, bf16[53,8,128]{2,1,0:T(8,128)(2,1)S(1)}, u32[]{:S(2)}, u32[]{:S(2)}) %collective-permute-start.8) | collective-permute-done | bytes 108576 | tf_op jit(solution)/shard_map/ppermute | solution.py:517
  37.9 2.6 %collective-permute-start.15 = (bf16[48,8,128]{2,1,0:T(8,128)(2,1)}, bf16[48,8,128]{2,1,0:T(8,128)(2,1)S(1)}, u32[]{:S(2)}, u32[]{:S(2)}) collective-permute-start(bf16[48,8,128]{2,1,0:T(8,128)(2,1)} %get-tuple-element.50), channel_id=1, source_target_pairs={{0,15},{1,14},{2,13},{3,12},{4,11},{5,10},{6,9},{7,8},{8,7},{9,6},... | collective-permute-start | bytes 294920 | tf_op jit(solution)/shard_map/ppermute | solution.py:517
  40.6 0.6 %collective-permute-start.13 = (bf16[20,8,128]{2,1,0:T(8,128)(2,1)S(1)}, bf16[20,8,128]{2,1,0:T(8,128)(2,1)S(1)}, u32[]{:S(2)}, u32[]{:S(2)}) collective-permute-start(bf16[20,8,128]{2,1,0:T(8,128)(2,1)S(1)} %collect_gains.1), channel_id=1, source_target_pairs={{0,1},{1,0},{2,3},{3,2},{4,5},{5,4},{6,7},{7,6},{8,9},{9,8},{10,11... | collective-permute-start | bytes 122888 | tf_op jit(solution)/shard_map/ppermute | solution.py:517
  41.1 0.9 %copy-done = bf16[62,8,128]{2,1,0:T(8,128)(2,1)S(1)} copy-done((bf16[62,8,128]{2,1,0:T(8,128)(2,1)S(1)}, bf16[62,8,128]{2,1,0:T(8,128)(2,1)}, u32[]{:S(2)}) %copy-start) | copy-done | bytes 127000
  42.0 0.5 %make_ready.1 = (bf16[62,8,128]{2,1,0:T(8,128)(2,1)S(1)}, bf16[256,256]{1,0:T(8,128)(2,1)S(1)}, bf16[256,3072]{1,0:T(8,128)(2,1)S(1)}) custom-call(s32[1]{0:T(128)} %bitcast.me_s.turn_s, bf16[62,8,128]{2,1,0:T(8,128)(2,1)S(1)} %copy-done), custom_call_target="tpu_custom_call" | custom-call | tf_op jit(solution)/shard_map/make_ready/pallas_call | solution.py:502
  42.6 1.9 %gains_and_sums.1 = (f32[128,3072]{1,0:T(8,128)S(1)}, f32[64,128]{1,0:T(8,128)S(1)}, s32[16,128]{1,0:T(8,128)S(1)}, f32[3,64,8,128]{3,2,1,0:T(8,128)S(1)}) custom-call(s32[1]{0:T(128)} %bitcast.me_s.turn_s, bf16[256,256]{1,0:T(8,128)(2,1)S(1)} %get-tuple-element.29.choice_ref, bf16[256,3072]{1,0:T(8,128)(2,1)S(1)} %get-tuple-element.30.basis_ref, ...), custom_call_target="tpu_custom_call" | custom-call | tf_op jit(solution)/shard_map/gains_and_sums/pallas_call | solution.py:542
  44.5 1.3 %collective-permute-done.15.rest_1_ = bf16[48,8,128]{2,1,0:T(8,128)(2,1)S(1)} collective-permute-done((bf16[48,8,128]{2,1,0:T(8,128)(2,1)}, bf16[48,8,128]{2,1,0:T(8,128)(2,1)S(1)}, u32[]{:S(2)}, u32[]{:S(2)}) %collective-permute-start.15) | collective-permute-done | bytes 98336 | tf_op jit(solution)/shard_map/ppermute | solution.py:517
  45.8 2.0 %sum_and_apply.1 = bf16[64,8,384]{2,1,0:T(8,128)(2,1)} custom-call(s32[16,128]{1,0:T(8,128)S(1)} %get-tuple-element.45.slots_s, f32[128,3072]{1,0:T(8,128)S(1)} %get-tuple-element.46.gains_ref, f32[64,128]{1,0:T(8,128)S(1)} %get-tuple-element.47.recip_ref, f32[3,64,8,128]{3,2,1,0:T(8,128)S(1)} %get-tuple-element.48.sums_ref, ...), custom_call_target="tpu_custom_call" | custom-call | tf_op jit(solution)/shard_map/sum_and_apply/pallas_call | solution.py:565
  (15 shorter events, 0.1 us)
Async XLA Ops:
  3.2 9.0 %collective-permute-start.12 = (bf16[48,8,128]{2,1,0:T(8,128)(2,1)}, bf16[48,8,128]{2,1,0:T(8,128)(2,1)S(1)}, u32[]{:S(2)}, u32[]{:S(2)}) collective-permute-start(bf16[48,8,128]{2,1,0:T(8,128)(2,1)} %get-tuple-element.44), channel_id=1, source_target_pairs={{0,9},{1,8},{2,11},{3,10},{4,13},{5,12},{6,15},{7,14},{8,1},{9,0},... | collective-permute-start | bytes 294920 | tf_op jit(solution)/shard_map/ppermute | solution.py:517
  6.8 14.5 %collective-permute-start = (bf16[53,8,128]{2,1,0:T(8,128)(2,1)}, bf16[53,8,128]{2,1,0:T(8,128)(2,1)S(1)}, u32[]{:S(2)}, u32[]{:S(2)}) collective-permute-start(bf16[53,8,128]{2,1,0:T(8,128)(2,1)} %get-tuple-element.32), channel_id=1, source_target_pairs={{0,8},{1,9},{2,10},{3,11},{4,12},{5,13},{6,14},{7,15},{8,0},{9,1},... | collective-permute-start | bytes 325640 | tf_op jit(solution)/shard_map/ppermute | solution.py:517
  7.4 18.5 %collective-permute-start.1 = (bf16[53,8,128]{2,1,0:T(8,128)(2,1)}, bf16[53,8,128]{2,1,0:T(8,128)(2,1)S(1)}, u32[]{:S(2)}, u32[]{:S(2)}) collective-permute-start(bf16[53,8,128]{2,1,0:T(8,128)(2,1)} %get-tuple-element.33), channel_id=1, source_target_pairs={{0,10},{1,11},{2,8},{3,9},{4,14},{5,15},{6,12},{7,13},{8,2},{9,3},... | collective-permute-start | bytes 325640 | tf_op jit(solution)/shard_map/ppermute | solution.py:517
  10.7 16.2 %collective-permute-start.2 = (bf16[53,8,128]{2,1,0:T(8,128)(2,1)}, bf16[53,8,128]{2,1,0:T(8,128)(2,1)S(1)}, u32[]{:S(2)}, u32[]{:S(2)}) collective-permute-start(bf16[53,8,128]{2,1,0:T(8,128)(2,1)} %get-tuple-element.34), channel_id=1, source_target_pairs={{0,4},{1,5},{2,6},{3,7},{4,0},{5,1},{6,2},{7,3},{8,12},{9,13},{10,... | collective-permute-start | bytes 325640 | tf_op jit(solution)/shard_map/ppermute | solution.py:517
  12.2 14.6 %collective-permute-start.3 = (bf16[53,8,128]{2,1,0:T(8,128)(2,1)}, bf16[53,8,128]{2,1,0:T(8,128)(2,1)S(1)}, u32[]{:S(2)}, u32[]{:S(2)}) collective-permute-start(bf16[53,8,128]{2,1,0:T(8,128)(2,1)} %get-tuple-element.35), channel_id=1, source_target_pairs={{0,5},{1,4},{2,7},{3,6},{4,1},{5,0},{6,3},{7,2},{8,13},{9,12},{10,... | collective-permute-start | bytes 325640 | tf_op jit(solution)/shard_map/ppermute | solution.py:517
  12.2 15.8 %collective-permute-start.4 = (bf16[53,8,128]{2,1,0:T(8,128)(2,1)}, bf16[53,8,128]{2,1,0:T(8,128)(2,1)S(1)}, u32[]{:S(2)}, u32[]{:S(2)}) collective-permute-start(bf16[53,8,128]{2,1,0:T(8,128)(2,1)} %get-tuple-element.36), channel_id=1, source_target_pairs={{0,12},{1,13},{2,14},{3,15},{4,8},{5,9},{6,10},{7,11},{8,4},{9,5},... | collective-permute-start | bytes 325640 | tf_op jit(solution)/shard_map/ppermute | solution.py:517
  21.3 7.1 %collective-permute-start.5 = (bf16[53,8,128]{2,1,0:T(8,128)(2,1)}, bf16[53,8,128]{2,1,0:T(8,128)(2,1)S(1)}, u32[]{:S(2)}, u32[]{:S(2)}) collective-permute-start(bf16[53,8,128]{2,1,0:T(8,128)(2,1)} %get-tuple-element.37), channel_id=1, source_target_pairs={{0,6},{1,7},{2,4},{3,5},{4,2},{5,3},{6,0},{7,1},{8,14},{9,15},{10,... | collective-permute-start | bytes 325640 | tf_op jit(solution)/shard_map/ppermute | solution.py:517
  26.0 7.8 %collective-permute-start.6 = (bf16[53,8,128]{2,1,0:T(8,128)(2,1)}, bf16[53,8,128]{2,1,0:T(8,128)(2,1)S(1)}, u32[]{:S(2)}, u32[]{:S(2)}) collective-permute-start(bf16[53,8,128]{2,1,0:T(8,128)(2,1)} %get-tuple-element.38), channel_id=1, source_target_pairs={{0,14},{1,15},{2,12},{3,13},{4,10},{5,11},{6,8},{7,9},{8,6},{9,7},... | collective-permute-start | bytes 325640 | tf_op jit(solution)/shard_map/ppermute | solution.py:517
  26.9 9.4 %collective-permute-start.7 = (bf16[53,8,128]{2,1,0:T(8,128)(2,1)}, bf16[53,8,128]{2,1,0:T(8,128)(2,1)S(1)}, u32[]{:S(2)}, u32[]{:S(2)}) collective-permute-start(bf16[53,8,128]{2,1,0:T(8,128)(2,1)} %get-tuple-element.39), channel_id=1, source_target_pairs={{0,7},{1,6},{2,5},{3,4},{4,3},{5,2},{6,1},{7,0},{8,15},{9,14},{10,... | collective-permute-start | bytes 325640 | tf_op jit(solution)/shard_map/ppermute | solution.py:517
  26.9 11.0 %collective-permute-start.8 = (bf16[53,8,128]{2,1,0:T(8,128)(2,1)}, bf16[53,8,128]{2,1,0:T(8,128)(2,1)S(1)}, u32[]{:S(2)}, u32[]{:S(2)}) collective-permute-start(bf16[53,8,128]{2,1,0:T(8,128)(2,1)} %get-tuple-element.40), channel_id=1, source_target_pairs={{0,11},{1,10},{2,9},{3,8},{4,15},{5,14},{6,13},{7,12},{8,3},{9,2},... | collective-permute-start | bytes 325640 | tf_op jit(solution)/shard_map/ppermute | solution.py:517
  28.1 12.5 %collective-permute-start.9 = (bf16[53,8,128]{2,1,0:T(8,128)(2,1)}, bf16[53,8,128]{2,1,0:T(8,128)(2,1)S(1)}, u32[]{:S(2)}, u32[]{:S(2)}) collective-permute-start(bf16[53,8,128]{2,1,0:T(8,128)(2,1)} %get-tuple-element.41), channel_id=1, source_target_pairs={{0,1},{1,0},{2,3},{3,2},{4,5},{5,4},{6,7},{7,6},{8,9},{9,8},{10,11... | collective-permute-start | bytes 325640 | tf_op jit(solution)/shard_map/ppermute | solution.py:517
  28.4 14.2 %collective-permute-start.10 = (bf16[53,8,128]{2,1,0:T(8,128)(2,1)}, bf16[53,8,128]{2,1,0:T(8,128)(2,1)S(1)}, u32[]{:S(2)}, u32[]{:S(2)}) collective-permute-start(bf16[53,8,128]{2,1,0:T(8,128)(2,1)} %get-tuple-element.42), channel_id=1, source_target_pairs={{0,2},{1,3},{2,0},{3,1},{4,6},{5,7},{6,4},{7,5},{8,10},{9,11},{10,... | collective-permute-start | bytes 325640 | tf_op jit(solution)/shard_map/ppermute | solution.py:517
  33.8 8.8 %collective-permute-start.11 = (bf16[53,8,128]{2,1,0:T(8,128)(2,1)}, bf16[53,8,128]{2,1,0:T(8,128)(2,1)S(1)}, u32[]{:S(2)}, u32[]{:S(2)}) collective-permute-start(bf16[53,8,128]{2,1,0:T(8,128)(2,1)} %get-tuple-element.43), channel_id=1, source_target_pairs={{0,3},{1,2},{2,1},{3,0},{4,7},{5,6},{6,5},{7,4},{8,11},{9,10},{10,... | collective-permute-start | bytes 325640 | tf_op jit(solution)/shard_map/ppermute | solution.py:517
  36.2 8.3 %collective-permute-start.14 = (bf16[48,8,128]{2,1,0:T(8,128)(2,1)}, bf16[48,8,128]{2,1,0:T(8,128)(2,1)S(1)}, u32[]{:S(2)}, u32[]{:S(2)}) collective-permute-start(bf16[48,8,128]{2,1,0:T(8,128)(2,1)} %get-tuple-element.49), channel_id=1, source_target_pairs={{0,13},{1,12},{2,15},{3,14},{4,9},{5,8},{6,11},{7,10},{8,5},{9,4},... | collective-permute-start | bytes 294920 | tf_op jit(solution)/shard_map/ppermute | solution.py:517
  37.9 8.0 %collective-permute-start.15 = (bf16[48,8,128]{2,1,0:T(8,128)(2,1)}, bf16[48,8,128]{2,1,0:T(8,128)(2,1)S(1)}, u32[]{:S(2)}, u32[]{:S(2)}) collective-permute-start(bf16[48,8,128]{2,1,0:T(8,128)(2,1)} %get-tuple-element.50), channel_id=1, source_target_pairs={{0,15},{1,14},{2,13},{3,12},{4,11},{5,10},{6,9},{7,8},{8,7},{9,6},... | collective-permute-start | bytes 294920 | tf_op jit(solution)/shard_map/ppermute | solution.py:517
  40.6 2.0 %collective-permute-start.13 = (bf16[20,8,128]{2,1,0:T(8,128)(2,1)S(1)}, bf16[20,8,128]{2,1,0:T(8,128)(2,1)S(1)}, u32[]{:S(2)}, u32[]{:S(2)}) collective-permute-start(bf16[20,8,128]{2,1,0:T(8,128)(2,1)S(1)} %collect_gains.1), channel_id=1, source_target_pairs={{0,1},{1,0},{2,3},{3,2},{4,5},{5,4},{6,7},{7,6},{8,9},{9,8},{10,11... | collective-permute-start | bytes 122888 | tf_op jit(solution)/shard_map/ppermute | solution.py:517
  41.1 0.9 %copy-start = (bf16[62,8,128]{2,1,0:T(8,128)(2,1)S(1)}, bf16[62,8,128]{2,1,0:T(8,128)(2,1)}, u32[]{:S(2)}) copy-start(bf16[62,8,128]{2,1,0:T(8,128)(2,1)} %get-tuple-element.28.own_ref) | copy-start | bytes 380932

commit v7 on v6

--- a/solution.py
+++ b/solution.py
@@ -22,13 +22,8 @@
 def schedule(near):
     even, odd = list(range(near, 2 * near, 2)), list(range(near + 1, 2 * near, 2))
     close = list(range(near // 2, near)) + list(range(1, near // 2))
-    cross, late = even[2:] + odd[1:-2], odd[-2:]
-    order = [0] + even[:2] + close[:2]
-    close = close[2:]
-    while cross:
-        order += cross[:1] + close[:1]
-        cross, close = cross[1:], close[1:]
-    return order + close + odd[:1], late
+    order = [0] + even[:3] + close[:2] + even[3:] + close[2:4] + odd[1:-2] + close[4:] + odd[:1]
+    return order, odd[-2:]
 
 
 def with_gains(near):

time: 48 us -> 50.4 us (1.050)
  starting transfers between devices: 28.1 us -> 34.6 us
  waiting for transfers between devices: 11 us -> 6.71 us
    ppermute x16, starting transfers between devices: 28.1 us -> 34.6 us  [swap(): return lax.ppermute(array, 'bl', [(d, d ^ x) for d in range(devices)])]
    ppermute x16, waiting for transfers between devices: 11 us -> 6.71 us  [swap(): return lax.ppermute(array, 'bl', [(d, d ^ x) for d in range(devices)])]
  transfers between devices with their start and end apart: 16 -> 16, of which waited for: 6 -> 4; matrix products, arithmetic and copies ran while one was open for 0% -> 0% of each run, Pallas kernels for 5% -> 5%
where the time goes in v7:
time: 50.4 us; the launch traced here: 50.2 us
  starting transfers between devices  34.6 us (69%)
  Pallas kernels  7.87 us (16%)
  waiting for transfers between devices  6.71 us (13%)
  local copies, waits for them, and re-layouts  0.9 us (2%)
    ppermute x16, starting transfers between devices, swap(): return lax.ppermute(array, 'bl', [(d, d ^ x) for d in range(devices)])  34.6 us
    ppermute x16, waiting for transfers between devices, swap(): return lax.ppermute(array, 'bl', [(d, d ^ x) for d in range(devices)])  6.71 us
    pallas_call x1, Pallas kernels, on_device(): pl.pallas_call(functools.partial(pack_kernel, capacity, near), out_shape=...  3.23 us
    pallas_call x1, Pallas kernels, on_device(): pl.pallas_call(functools.partial(middle_kernel, capacity, near, depth, or...  2.03 us
    pallas_call x1, Pallas kernels, on_device(): pl.pallas_call(functools.partial(finish_kernel, capacity, late), out_shap...  2.02 us
  transfers between devices with their start and end apart: 16, of which 4 were waited for; matrix products, arithmetic and copies ran while one was open for 0% of the time, Pallas kernels for 5%

profile of v7, /device:TPU:0, one launch (start us, length us, event | category | flops | bytes accessed | tf_op | source)
XLA Modules:
  0.0 50.2 jit_solution(18073348774425052829)
XLA Ops:
  0.0 3.2 %pack_rows.1 = (bf16[62,8,128]{2,1,0:T(8,128)(2,1)}, bf16[53,8,128]{2,1,0:T(8,128)(2,1)}, bf16[53,8,128]{2,1,0:T(8,128)(2,1)}, bf16[53,8,128]{2,1,0:T(8,128)(2,1...) custom-call(s32[1]{0:T(128)} %bitcast.me_s.turn_s, ...), custom_call_target="tpu_custom_call" | custom-call | tf_op jit(solution)/shard_map/pack_rows/pallas_call | solution.py:456
  3.2 3.5 %collective-permute-start.12 = (bf16[48,8,128]{2,1,0:T(8,128)(2,1)}, bf16[48,8,128]{2,1,0:T(8,128)(2,1)S(1)}, u32[]{:S(2)}, u32[]{:S(2)}) collective-permute-start(bf16[48,8,128]{2,1,0:T(8,128)(2,1)} %get-tuple-element.44), channel_id=1, source_target_pairs={{0,9},{1,8},{2,11},{3,10},{4,13},{5,12},{6,15},{7,14},{8,1},{9,0},... | collective-permute-start | bytes 294920 | tf_op jit(solution)/shard_map/ppermute | solution.py:512
  6.8 0.6 %collective-permute-start = (bf16[53,8,128]{2,1,0:T(8,128)(2,1)}, bf16[53,8,128]{2,1,0:T(8,128)(2,1)S(1)}, u32[]{:S(2)}, u32[]{:S(2)}) collective-permute-start(bf16[53,8,128]{2,1,0:T(8,128)(2,1)} %get-tuple-element.32), channel_id=1, source_target_pairs={{0,8},{1,9},{2,10},{3,11},{4,12},{5,13},{6,14},{7,15},{8,0},{9,1},... | collective-permute-start | bytes 325640 | tf_op jit(solution)/shard_map/ppermute | solution.py:512
  7.4 3.2 %collective-permute-start.1 = (bf16[53,8,128]{2,1,0:T(8,128)(2,1)}, bf16[53,8,128]{2,1,0:T(8,128)(2,1)S(1)}, u32[]{:S(2)}, u32[]{:S(2)}) collective-permute-start(bf16[53,8,128]{2,1,0:T(8,128)(2,1)} %get-tuple-element.33), channel_id=1, source_target_pairs={{0,10},{1,11},{2,8},{3,9},{4,14},{5,15},{6,12},{7,13},{8,2},{9,3},... | collective-permute-start | bytes 325640 | tf_op jit(solution)/shard_map/ppermute | solution.py:512
  10.7 1.7 %collective-permute-start.2 = (bf16[53,8,128]{2,1,0:T(8,128)(2,1)}, bf16[53,8,128]{2,1,0:T(8,128)(2,1)S(1)}, u32[]{:S(2)}, u32[]{:S(2)}) collective-permute-start(bf16[53,8,128]{2,1,0:T(8,128)(2,1)} %get-tuple-element.34), channel_id=1, source_target_pairs={{0,12},{1,13},{2,14},{3,15},{4,8},{5,9},{6,10},{7,11},{8,4},{9,5},... | collective-permute-start | bytes 325640 | tf_op jit(solution)/shard_map/ppermute | solution.py:512
  12.3 0.0 collective-permute-start.3
  12.3 8.3 %collective-permute-start.4 = (bf16[53,8,128]{2,1,0:T(8,128)(2,1)}, bf16[53,8,128]{2,1,0:T(8,128)(2,1)S(1)}, u32[]{:S(2)}, u32[]{:S(2)}) collective-permute-start(bf16[53,8,128]{2,1,0:T(8,128)(2,1)} %get-tuple-element.36), channel_id=1, source_target_pairs={{0,5},{1,4},{2,7},{3,6},{4,1},{5,0},{6,3},{7,2},{8,13},{9,12},{10,... | collective-permute-start | bytes 325640 | tf_op jit(solution)/shard_map/ppermute | solution.py:512
  20.6 1.6 %collective-permute-done.rest_0_.rest_1_ = bf16[53,8,128]{2,1,0:T(8,128)(2,1)S(1)} collective-permute-done((bf16[53,8,128]{2,1,0:T(8,128)(2,1)}, bf16[53,8,128]{2,1,0:T(8,128)(2,1)S(1)}, u32[]{:S(2)}, u32[]{:S(2)}) %collective-permute-start) | collective-permute-done | bytes 108576 | tf_op jit(solution)/shard_map/ppermute | solution.py:512
  22.2 4.6 %collective-permute-start.5 = (bf16[53,8,128]{2,1,0:T(8,128)(2,1)}, bf16[53,8,128]{2,1,0:T(8,128)(2,1)S(1)}, u32[]{:S(2)}, u32[]{:S(2)}) collective-permute-start(bf16[53,8,128]{2,1,0:T(8,128)(2,1)} %get-tuple-element.37), channel_id=1, source_target_pairs={{0,14},{1,15},{2,12},{3,13},{4,10},{5,11},{6,8},{7,9},{8,6},{9,7},... | collective-permute-start | bytes 325640 | tf_op jit(solution)/shard_map/ppermute | solution.py:512
  26.8 2.1 %collective-permute-start.7 = (bf16[53,8,128]{2,1,0:T(8,128)(2,1)}, bf16[53,8,128]{2,1,0:T(8,128)(2,1)S(1)}, u32[]{:S(2)}, u32[]{:S(2)}) collective-permute-start(bf16[53,8,128]{2,1,0:T(8,128)(2,1)} %get-tuple-element.39), channel_id=1, source_target_pairs={{0,7},{1,6},{2,5},{3,4},{4,3},{5,2},{6,1},{7,0},{8,15},{9,14},{10,... | collective-permute-start | bytes 325640 | tf_op jit(solution)/shard_map/ppermute | solution.py:512
  28.9 1.5 %collective-permute-start.8 = (bf16[53,8,128]{2,1,0:T(8,128)(2,1)}, bf16[53,8,128]{2,1,0:T(8,128)(2,1)S(1)}, u32[]{:S(2)}, u32[]{:S(2)}) collective-permute-start(bf16[53,8,128]{2,1,0:T(8,128)(2,1)} %get-tuple-element.40), channel_id=1, source_target_pairs={{0,11},{1,10},{2,9},{3,8},{4,15},{5,14},{6,13},{7,12},{8,3},{9,2},... | collective-permute-start | bytes 325640 | tf_op jit(solution)/shard_map/ppermute | solution.py:512
  30.5 0.8 %collective-permute-start.9 = (bf16[53,8,128]{2,1,0:T(8,128)(2,1)}, bf16[53,8,128]{2,1,0:T(8,128)(2,1)S(1)}, u32[]{:S(2)}, u32[]{:S(2)}) collective-permute-start(bf16[53,8,128]{2,1,0:T(8,128)(2,1)} %get-tuple-element.41), channel_id=1, source_target_pairs={{0,1},{1,0},{2,3},{3,2},{4,5},{5,4},{6,7},{7,6},{8,9},{9,8},{10,11... | collective-permute-start | bytes 325640 | tf_op jit(solution)/shard_map/ppermute | solution.py:512
  31.3 0.6 %collective-permute-start.10 = (bf16[53,8,128]{2,1,0:T(8,128)(2,1)}, bf16[53,8,128]{2,1,0:T(8,128)(2,1)S(1)}, u32[]{:S(2)}, u32[]{:S(2)}) collective-permute-start(bf16[53,8,128]{2,1,0:T(8,128)(2,1)} %get-tuple-element.42), channel_id=1, source_target_pairs={{0,2},{1,3},{2,0},{3,1},{4,6},{5,7},{6,4},{7,5},{8,10},{9,11},{10,... | collective-permute-start | bytes 325640 | tf_op jit(solution)/shard_map/ppermute | solution.py:512
  31.9 2.0 %collective-permute-done.6.rest_7_ = bf16[53,8,128]{2,1,0:T(8,128)(2,1)S(1)} collective-permute-done((bf16[53,8,128]{2,1,0:T(8,128)(2,1)}, bf16[53,8,128]{2,1,0:T(8,128)(2,1)S(1)}, u32[]{:S(2)}, u32[]{:S(2)}) %collective-permute-start.6) | collective-permute-done | bytes 108576 | tf_op jit(solution)/shard_map/ppermute | solution.py:512
  33.8 0.6 %collective-permute-done.7.rest_8_ = bf16[53,8,128]{2,1,0:T(8,128)(2,1)S(1)} collective-permute-done((bf16[53,8,128]{2,1,0:T(8,128)(2,1)}, bf16[53,8,128]{2,1,0:T(8,128)(2,1)S(1)}, u32[]{:S(2)}, u32[]{:S(2)}) %collective-permute-start.7) | collective-permute-done | bytes 108576 | tf_op jit(solution)/shard_map/ppermute | solution.py:512
  34.4 6.0 %collective-permute-start.14 = (bf16[48,8,128]{2,1,0:T(8,128)(2,1)}, bf16[48,8,128]{2,1,0:T(8,128)(2,1)S(1)}, u32[]{:S(2)}, u32[]{:S(2)}) collective-permute-start(bf16[48,8,128]{2,1,0:T(8,128)(2,1)} %get-tuple-element.49), channel_id=1, source_target_pairs={{0,13},{1,12},{2,15},{3,14},{4,9},{5,8},{6,11},{7,10},{8,5},{9,4},... | collective-permute-start | bytes 294920 | tf_op jit(solution)/shard_map/ppermute | solution.py:512
  40.5 1.1 %collective-permute-start.15 = (bf16[48,8,128]{2,1,0:T(8,128)(2,1)}, bf16[48,8,128]{2,1,0:T(8,128)(2,1)S(1)}, u32[]{:S(2)}, u32[]{:S(2)}) collective-permute-start(bf16[48,8,128]{2,1,0:T(8,128)(2,1)} %get-tuple-element.50), channel_id=1, source_target_pairs={{0,15},{1,14},{2,13},{3,12},{4,11},{5,10},{6,9},{7,8},{8,7},{9,6},... | collective-permute-start | bytes 294920 | tf_op jit(solution)/shard_map/ppermute | solution.py:512
  41.5 0.1 collect_gains.1
  41.6 0.5 %collective-permute-start.13 = (bf16[20,8,128]{2,1,0:T(8,128)(2,1)S(1)}, bf16[20,8,128]{2,1,0:T(8,128)(2,1)S(1)}, u32[]{:S(2)}, u32[]{:S(2)}) collective-permute-start(bf16[20,8,128]{2,1,0:T(8,128)(2,1)S(1)} %collect_gains.1), channel_id=1, source_target_pairs={{0,1},{1,0},{2,3},{3,2},{4,5},{5,4},{6,7},{7,6},{8,9},{9,8},{10,11... | collective-permute-start | bytes 122888 | tf_op jit(solution)/shard_map/ppermute | solution.py:512
  42.1 0.9 %copy-done = bf16[62,8,128]{2,1,0:T(8,128)(2,1)S(1)} copy-done((bf16[62,8,128]{2,1,0:T(8,128)(2,1)S(1)}, bf16[62,8,128]{2,1,0:T(8,128)(2,1)}, u32[]{:S(2)}) %copy-start) | copy-done | bytes 127000
  43.0 0.5 %make_ready.1 = (bf16[62,8,128]{2,1,0:T(8,128)(2,1)S(1)}, bf16[256,256]{1,0:T(8,128)(2,1)S(1)}, bf16[256,3072]{1,0:T(8,128)(2,1)S(1)}) custom-call(s32[1]{0:T(128)} %bitcast.me_s.turn_s, bf16[62,8,128]{2,1,0:T(8,128)(2,1)S(1)} %copy-done), custom_call_target="tpu_custom_call" | custom-call | tf_op jit(solution)/shard_map/make_ready/pallas_call | solution.py:497
  43.6 2.0 %gains_and_sums.1 = (f32[128,3072]{1,0:T(8,128)S(1)}, f32[64,128]{1,0:T(8,128)S(1)}, s32[16,128]{1,0:T(8,128)S(1)}, f32[3,64,8,128]{3,2,1,0:T(8,128)S(1)}) custom-call(s32[1]{0:T(128)} %bitcast.me_s.turn_s, bf16[256,256]{1,0:T(8,128)(2,1)S(1)} %get-tuple-element.29.choice_ref, bf16[256,3072]{1,0:T(8,128)(2,1)S(1)} %get-tuple-element.30.basis_ref, ...), custom_call_target="tpu_custom_call" | custom-call | tf_op jit(solution)/shard_map/gains_and_sums/pallas_call | solution.py:537
  45.6 2.5 %collective-permute-done.15.rest_1_ = bf16[48,8,128]{2,1,0:T(8,128)(2,1)S(1)} collective-permute-done((bf16[48,8,128]{2,1,0:T(8,128)(2,1)}, bf16[48,8,128]{2,1,0:T(8,128)(2,1)S(1)}, u32[]{:S(2)}, u32[]{:S(2)}) %collective-permute-start.15) | collective-permute-done | bytes 98336 | tf_op jit(solution)/shard_map/ppermute | solution.py:512
  48.2 2.0 %sum_and_apply.1 = bf16[64,8,384]{2,1,0:T(8,128)(2,1)} custom-call(s32[16,128]{1,0:T(8,128)S(1)} %get-tuple-element.45.slots_s, f32[128,3072]{1,0:T(8,128)S(1)} %get-tuple-element.46.gains_ref, f32[64,128]{1,0:T(8,128)S(1)} %get-tuple-element.47.recip_ref, f32[3,64,8,128]{3,2,1,0:T(8,128)S(1)} %get-tuple-element.48.sums_ref, ...), custom_call_target="tpu_custom_call" | custom-call | tf_op jit(solution)/shard_map/sum_and_apply/pallas_call | solution.py:560
  (15 shorter events, 0.0 us)
Async XLA Ops:
  3.2 9.1 %collective-permute-start.12 = (bf16[48,8,128]{2,1,0:T(8,128)(2,1)}, bf16[48,8,128]{2,1,0:T(8,128)(2,1)S(1)}, u32[]{:S(2)}, u32[]{:S(2)}) collective-permute-start(bf16[48,8,128]{2,1,0:T(8,128)(2,1)} %get-tuple-element.44), channel_id=1, source_target_pairs={{0,9},{1,8},{2,11},{3,10},{4,13},{5,12},{6,15},{7,14},{8,1},{9,0},... | collective-permute-start | bytes 294920 | tf_op jit(solution)/shard_map/ppermute | solution.py:512
  6.8 15.4 %collective-permute-start = (bf16[53,8,128]{2,1,0:T(8,128)(2,1)}, bf16[53,8,128]{2,1,0:T(8,128)(2,1)S(1)}, u32[]{:S(2)}, u32[]{:S(2)}) collective-permute-start(bf16[53,8,128]{2,1,0:T(8,128)(2,1)} %get-tuple-element.32), channel_id=1, source_target_pairs={{0,8},{1,9},{2,10},{3,11},{4,12},{5,13},{6,14},{7,15},{8,0},{9,1},... | collective-permute-start | bytes 325640 | tf_op jit(solution)/shard_map/ppermute | solution.py:512
  7.4 19.4 %collective-permute-start.1 = (bf16[53,8,128]{2,1,0:T(8,128)(2,1)}, bf16[53,8,128]{2,1,0:T(8,128)(2,1)S(1)}, u32[]{:S(2)}, u32[]{:S(2)}) collective-permute-start(bf16[53,8,128]{2,1,0:T(8,128)(2,1)} %get-tuple-element.33), channel_id=1, source_target_pairs={{0,10},{1,11},{2,8},{3,9},{4,14},{5,15},{6,12},{7,13},{8,2},{9,3},... | collective-permute-start | bytes 325640 | tf_op jit(solution)/shard_map/ppermute | solution.py:512
  10.7 16.2 %collective-permute-start.2 = (bf16[53,8,128]{2,1,0:T(8,128)(2,1)}, bf16[53,8,128]{2,1,0:T(8,128)(2,1)S(1)}, u32[]{:S(2)}, u32[]{:S(2)}) collective-permute-start(bf16[53,8,128]{2,1,0:T(8,128)(2,1)} %get-tuple-element.34), channel_id=1, source_target_pairs={{0,12},{1,13},{2,14},{3,15},{4,8},{5,9},{6,10},{7,11},{8,4},{9,5},... | collective-permute-start | bytes 325640 | tf_op jit(solution)/shard_map/ppermute | solution.py:512
  12.3 16.6 %collective-permute-start.3 = (bf16[53,8,128]{2,1,0:T(8,128)(2,1)}, bf16[53,8,128]{2,1,0:T(8,128)(2,1)S(1)}, u32[]{:S(2)}, u32[]{:S(2)}) collective-permute-start(bf16[53,8,128]{2,1,0:T(8,128)(2,1)} %get-tuple-element.35), channel_id=1, source_target_pairs={{0,4},{1,5},{2,6},{3,7},{4,0},{5,1},{6,2},{7,3},{8,12},{9,13},{10,... | collective-permute-start | bytes 325640 | tf_op jit(solution)/shard_map/ppermute | solution.py:512
  12.3 18.1 %collective-permute-start.4 = (bf16[53,8,128]{2,1,0:T(8,128)(2,1)}, bf16[53,8,128]{2,1,0:T(8,128)(2,1)S(1)}, u32[]{:S(2)}, u32[]{:S(2)}) collective-permute-start(bf16[53,8,128]{2,1,0:T(8,128)(2,1)} %get-tuple-element.36), channel_id=1, source_target_pairs={{0,5},{1,4},{2,7},{3,6},{4,1},{5,0},{6,3},{7,2},{8,13},{9,12},{10,... | collective-permute-start | bytes 325640 | tf_op jit(solution)/shard_map/ppermute | solution.py:512
  22.2 9.1 %collective-permute-start.5 = (bf16[53,8,128]{2,1,0:T(8,128)(2,1)}, bf16[53,8,128]{2,1,0:T(8,128)(2,1)S(1)}, u32[]{:S(2)}, u32[]{:S(2)}) collective-permute-start(bf16[53,8,128]{2,1,0:T(8,128)(2,1)} %get-tuple-element.37), channel_id=1, source_target_pairs={{0,14},{1,15},{2,12},{3,13},{4,10},{5,11},{6,8},{7,9},{8,6},{9,7},... | collective-permute-start | bytes 325640 | tf_op jit(solution)/shard_map/ppermute | solution.py:512
  26.8 7.0 %collective-permute-start.6 = (bf16[53,8,128]{2,1,0:T(8,128)(2,1)}, bf16[53,8,128]{2,1,0:T(8,128)(2,1)S(1)}, u32[]{:S(2)}, u32[]{:S(2)}) collective-permute-start(bf16[53,8,128]{2,1,0:T(8,128)(2,1)} %get-tuple-element.38), channel_id=1, source_target_pairs={{0,6},{1,7},{2,4},{3,5},{4,2},{5,3},{6,0},{7,1},{8,14},{9,15},{10,... | collective-permute-start | bytes 325640 | tf_op jit(solution)/shard_map/ppermute | solution.py:512
  26.8 7.6 %collective-permute-start.7 = (bf16[53,8,128]{2,1,0:T(8,128)(2,1)}, bf16[53,8,128]{2,1,0:T(8,128)(2,1)S(1)}, u32[]{:S(2)}, u32[]{:S(2)}) collective-permute-start(bf16[53,8,128]{2,1,0:T(8,128)(2,1)} %get-tuple-element.39), channel_id=1, source_target_pairs={{0,7},{1,6},{2,5},{3,4},{4,3},{5,2},{6,1},{7,0},{8,15},{9,14},{10,... | collective-permute-start | bytes 325640 | tf_op jit(solution)/shard_map/ppermute | solution.py:512
  28.9 11.5 %collective-permute-start.8 = (bf16[53,8,128]{2,1,0:T(8,128)(2,1)}, bf16[53,8,128]{2,1,0:T(8,128)(2,1)S(1)}, u32[]{:S(2)}, u32[]{:S(2)}) collective-permute-start(bf16[53,8,128]{2,1,0:T(8,128)(2,1)} %get-tuple-element.40), channel_id=1, source_target_pairs={{0,11},{1,10},{2,9},{3,8},{4,15},{5,14},{6,13},{7,12},{8,3},{9,2},... | collective-permute-start | bytes 325640 | tf_op jit(solution)/shard_map/ppermute | solution.py:512
  30.5 11.1 %collective-permute-start.9 = (bf16[53,8,128]{2,1,0:T(8,128)(2,1)}, bf16[53,8,128]{2,1,0:T(8,128)(2,1)S(1)}, u32[]{:S(2)}, u32[]{:S(2)}) collective-permute-start(bf16[53,8,128]{2,1,0:T(8,128)(2,1)} %get-tuple-element.41), channel_id=1, source_target_pairs={{0,1},{1,0},{2,3},{3,2},{4,5},{5,4},{6,7},{7,6},{8,9},{9,8},{10,11... | collective-permute-start | bytes 325640 | tf_op jit(solution)/shard_map/ppermute | solution.py:512
  31.3 12.3 %collective-permute-start.10 = (bf16[53,8,128]{2,1,0:T(8,128)(2,1)}, bf16[53,8,128]{2,1,0:T(8,128)(2,1)S(1)}, u32[]{:S(2)}, u32[]{:S(2)}) collective-permute-start(bf16[53,8,128]{2,1,0:T(8,128)(2,1)} %get-tuple-element.42), channel_id=1, source_target_pairs={{0,2},{1,3},{2,0},{3,1},{4,6},{5,7},{6,4},{7,5},{8,10},{9,11},{10,... | collective-permute-start | bytes 325640 | tf_op jit(solution)/shard_map/ppermute | solution.py:512
  33.8 9.7 %collective-permute-start.11 = (bf16[53,8,128]{2,1,0:T(8,128)(2,1)}, bf16[53,8,128]{2,1,0:T(8,128)(2,1)S(1)}, u32[]{:S(2)}, u32[]{:S(2)}) collective-permute-start(bf16[53,8,128]{2,1,0:T(8,128)(2,1)} %get-tuple-element.43), channel_id=1, source_target_pairs={{0,3},{1,2},{2,1},{3,0},{4,7},{5,6},{6,5},{7,4},{8,11},{9,10},{10,... | collective-permute-start | bytes 325640 | tf_op jit(solution)/shard_map/ppermute | solution.py:512
  34.4 11.2 %collective-permute-start.14 = (bf16[48,8,128]{2,1,0:T(8,128)(2,1)}, bf16[48,8,128]{2,1,0:T(8,128)(2,1)S(1)}, u32[]{:S(2)}, u32[]{:S(2)}) collective-permute-start(bf16[48,8,128]{2,1,0:T(8,128)(2,1)} %get-tuple-element.49), channel_id=1, source_target_pairs={{0,13},{1,12},{2,15},{3,14},{4,9},{5,8},{6,11},{7,10},{8,5},{9,4},... | collective-permute-start | bytes 294920 | tf_op jit(solution)/shard_map/ppermute | solution.py:512
  40.5 7.7 %collective-permute-start.15 = (bf16[48,8,128]{2,1,0:T(8,128)(2,1)}, bf16[48,8,128]{2,1,0:T(8,128)(2,1)S(1)}, u32[]{:S(2)}, u32[]{:S(2)}) collective-permute-start(bf16[48,8,128]{2,1,0:T(8,128)(2,1)} %get-tuple-element.50), channel_id=1, source_target_pairs={{0,15},{1,14},{2,13},{3,12},{4,11},{5,10},{6,9},{7,8},{8,7},{9,6},... | collective-permute-start | bytes 294920 | tf_op jit(solution)/shard_map/ppermute | solution.py:512
  41.6 2.0 %collective-permute-start.13 = (bf16[20,8,128]{2,1,0:T(8,128)(2,1)S(1)}, bf16[20,8,128]{2,1,0:T(8,128)(2,1)S(1)}, u32[]{:S(2)}, u32[]{:S(2)}) collective-permute-start(bf16[20,8,128]{2,1,0:T(8,128)(2,1)S(1)} %collect_gains.1), channel_id=1, source_target_pairs={{0,1},{1,0},{2,3},{3,2},{4,5},{5,4},{6,7},{7,6},{8,9},{9,8},{10,11... | collective-permute-start | bytes 122888 | tf_op jit(solution)/shard_map/ppermute | solution.py:512
  42.1 0.9 %copy-start = (bf16[62,8,128]{2,1,0:T(8,128)(2,1)S(1)}, bf16[62,8,128]{2,1,0:T(8,128)(2,1)}, u32[]{:S(2)}) copy-start(bf16[62,8,128]{2,1,0:T(8,128)(2,1)} %get-tuple-element.28.own_ref) | copy-start | bytes 380932

commit v8 on v7

--- a/solution.py
+++ b/solution.py
@@ -22,8 +22,8 @@
 def schedule(near):
     even, odd = list(range(near, 2 * near, 2)), list(range(near + 1, 2 * near, 2))
     close = list(range(near // 2, near)) + list(range(1, near // 2))
-    order = [0] + even[:3] + close[:2] + even[3:] + close[2:4] + odd[1:-2] + close[4:] + odd[:1]
-    return order, odd[-2:]
+    order = [0] + even[:1] + close[:3] + even[1:3] + close[3:6] + even[3:] + odd[1:-2] + close[6:]
+    return order + odd[:1], odd[-2:]
 
 
 def with_gains(near):

time: 50.4 us -> 50.6 us (level)
  starting transfers between devices: 34.6 us -> 32.6 us
  waiting for transfers between devices: 6.71 us -> 8.63 us
    ppermute x16, starting transfers between devices: 34.6 us -> 32.6 us  [swap(): return lax.ppermute(array, 'bl', [(d, d ^ x) for d in range(devices)])]
    ppermute x16, waiting for transfers between devices: 6.71 us -> 8.63 us  [swap(): return lax.ppermute(array, 'bl', [(d, d ^ x) for d in range(devices)])]
  transfers between devices with their start and end apart: 16 -> 16, of which waited for: 4 -> 3; matrix products, arithmetic and copies ran while one was open for 0% -> 0% of each run, Pallas kernels for 5% -> 5%
where the time goes in v8:
time: 50.6 us; the launch traced here: 49.9 us
  starting transfers between devices  32.6 us (64%)
  waiting for transfers between devices  8.63 us (17%)
  Pallas kernels  7.68 us (15%)
  local copies, waits for them, and re-layouts  0.9 us (2%)
    ppermute x16, starting transfers between devices, swap(): return lax.ppermute(array, 'bl', [(d, d ^ x) for d in range(devices)])  32.6 us
    ppermute x16, waiting for transfers between devices, swap(): return lax.ppermute(array, 'bl', [(d, d ^ x) for d in range(devices)])  8.63 us
    pallas_call x1, Pallas kernels, on_device(): pl.pallas_call(functools.partial(pack_kernel, capacity, near), out_shape=...  3.23 us
    pallas_call x1, Pallas kernels, on_device(): pl.pallas_call(functools.partial(finish_kernel, capacity, late), out_shap...  1.94 us
    pallas_call x1, Pallas kernels, on_device(): pl.pallas_call(functools.partial(middle_kernel, capacity, near, depth, or...  1.91 us
  transfers between devices with their start and end apart: 16, of which 3 were waited for; matrix products, arithmetic and copies ran while one was open for 0% of the time, Pallas kernels for 5%

profile of v8, /device:TPU:0, one launch (start us, length us, event | category | flops | bytes accessed | tf_op | source)
XLA Modules:
  0.0 49.9 jit_solution(14713696009447139159)
XLA Ops:
  0.0 3.2 %pack_rows.1 = (bf16[62,8,128]{2,1,0:T(8,128)(2,1)}, bf16[53,8,128]{2,1,0:T(8,128)(2,1)}, bf16[53,8,128]{2,1,0:T(8,128)(2,1)}, bf16[53,8,128]{2,1,0:T(8,128)(2,1...) custom-call(s32[1]{0:T(128)} %bitcast.me_s.turn_s, ...), custom_call_target="tpu_custom_call" | custom-call | tf_op jit(solution)/shard_map/pack_rows/pallas_call | solution.py:456
  3.2 3.5 %collective-permute-start.12 = (bf16[48,8,128]{2,1,0:T(8,128)(2,1)}, bf16[48,8,128]{2,1,0:T(8,128)(2,1)S(1)}, u32[]{:S(2)}, u32[]{:S(2)}) collective-permute-start(bf16[48,8,128]{2,1,0:T(8,128)(2,1)} %get-tuple-element.44), channel_id=1, source_target_pairs={{0,9},{1,8},{2,11},{3,10},{4,13},{5,12},{6,15},{7,14},{8,1},{9,0},... | collective-permute-start | bytes 294920 | tf_op jit(solution)/shard_map/ppermute | solution.py:512
  6.8 0.6 %collective-permute-start = (bf16[53,8,128]{2,1,0:T(8,128)(2,1)}, bf16[53,8,128]{2,1,0:T(8,128)(2,1)S(1)}, u32[]{:S(2)}, u32[]{:S(2)}) collective-permute-start(bf16[53,8,128]{2,1,0:T(8,128)(2,1)} %get-tuple-element.32), channel_id=1, source_target_pairs={{0,8},{1,9},{2,10},{3,11},{4,12},{5,13},{6,14},{7,15},{8,0},{9,1},... | collective-permute-start | bytes 325640 | tf_op jit(solution)/shard_map/ppermute | solution.py:512
  7.4 1.6 %collective-permute-start.1 = (bf16[53,8,128]{2,1,0:T(8,128)(2,1)}, bf16[53,8,128]{2,1,0:T(8,128)(2,1)S(1)}, u32[]{:S(2)}, u32[]{:S(2)}) collective-permute-start(bf16[53,8,128]{2,1,0:T(8,128)(2,1)} %get-tuple-element.33), channel_id=1, source_target_pairs={{0,4},{1,5},{2,6},{3,7},{4,0},{5,1},{6,2},{7,3},{8,12},{9,13},{10,... | collective-permute-start | bytes 325640 | tf_op jit(solution)/shard_map/ppermute | solution.py:512
  9.0 0.0 collective-permute-start.2
  9.0 2.4 %collective-permute-start.3 = (bf16[53,8,128]{2,1,0:T(8,128)(2,1)}, bf16[53,8,128]{2,1,0:T(8,128)(2,1)S(1)}, u32[]{:S(2)}, u32[]{:S(2)}) collective-permute-start(bf16[53,8,128]{2,1,0:T(8,128)(2,1)} %get-tuple-element.35), channel_id=1, source_target_pairs={{0,6},{1,7},{2,4},{3,5},{4,2},{5,3},{6,0},{7,1},{8,14},{9,15},{10,... | collective-permute-start | bytes 325640 | tf_op jit(solution)/shard_map/ppermute | solution.py:512
  11.4 4.8 %collective-permute-start.4 = (bf16[53,8,128]{2,1,0:T(8,128)(2,1)}, bf16[53,8,128]{2,1,0:T(8,128)(2,1)S(1)}, u32[]{:S(2)}, u32[]{:S(2)}) collective-permute-start(bf16[53,8,128]{2,1,0:T(8,128)(2,1)} %get-tuple-element.36), channel_id=1, source_target_pairs={{0,10},{1,11},{2,8},{3,9},{4,14},{5,15},{6,12},{7,13},{8,2},{9,3},... | collective-permute-start | bytes 325640 | tf_op jit(solution)/shard_map/ppermute | solution.py:512
  16.2 1.0 %collective-permute-done.rest_0_.rest_1_ = bf16[53,8,128]{2,1,0:T(8,128)(2,1)S(1)} collective-permute-done((bf16[53,8,128]{2,1,0:T(8,128)(2,1)}, bf16[53,8,128]{2,1,0:T(8,128)(2,1)S(1)}, u32[]{:S(2)}, u32[]{:S(2)}) %collective-permute-start) | collective-permute-done | bytes 108576 | tf_op jit(solution)/shard_map/ppermute | solution.py:512
  17.2 4.1 %collective-permute-start.5 = (bf16[53,8,128]{2,1,0:T(8,128)(2,1)}, bf16[53,8,128]{2,1,0:T(8,128)(2,1)S(1)}, u32[]{:S(2)}, u32[]{:S(2)}) collective-permute-start(bf16[53,8,128]{2,1,0:T(8,128)(2,1)} %get-tuple-element.37), channel_id=1, source_target_pairs={{0,12},{1,13},{2,14},{3,15},{4,8},{5,9},{6,10},{7,11},{8,4},{9,5},... | collective-permute-start | bytes 325640 | tf_op jit(solution)/shard_map/ppermute | solution.py:512
  21.3 0.0 collective-permute-done.2.rest_3_
  21.3 0.1 collective-permute-start.7
  21.4 2.5 %collective-permute-done.3.rest_4_ = bf16[53,8,128]{2,1,0:T(8,128)(2,1)S(1)} collective-permute-done((bf16[53,8,128]{2,1,0:T(8,128)(2,1)}, bf16[53,8,128]{2,1,0:T(8,128)(2,1)S(1)}, u32[]{:S(2)}, u32[]{:S(2)}) %collective-permute-start.3) | collective-permute-done | bytes 108576 | tf_op jit(solution)/shard_map/ppermute | solution.py:512
  23.9 2.5 %collective-permute-start.9 = (bf16[53,8,128]{2,1,0:T(8,128)(2,1)}, bf16[53,8,128]{2,1,0:T(8,128)(2,1)S(1)}, u32[]{:S(2)}, u32[]{:S(2)}) collective-permute-start(bf16[53,8,128]{2,1,0:T(8,128)(2,1)} %get-tuple-element.41), channel_id=1, source_target_pairs={{0,14},{1,15},{2,12},{3,13},{4,10},{5,11},{6,8},{7,9},{8,6},{9,7},... | collective-permute-start | bytes 325640 | tf_op jit(solution)/shard_map/ppermute | solution.py:512
  26.4 6.2 %collective-permute-start.8 = (bf16[53,8,128]{2,1,0:T(8,128)(2,1)}, bf16[53,8,128]{2,1,0:T(8,128)(2,1)S(1)}, u32[]{:S(2)}, u32[]{:S(2)}) collective-permute-start(bf16[53,8,128]{2,1,0:T(8,128)(2,1)} %get-tuple-element.40), channel_id=1, source_target_pairs={{0,2},{1,3},{2,0},{3,1},{4,6},{5,7},{6,4},{7,5},{8,10},{9,11},{10,... | collective-permute-start | bytes 325640 | tf_op jit(solution)/shard_map/ppermute | solution.py:512
  32.6 3.3 %collective-permute-start.11 = (bf16[53,8,128]{2,1,0:T(8,128)(2,1)}, bf16[53,8,128]{2,1,0:T(8,128)(2,1)S(1)}, u32[]{:S(2)}, u32[]{:S(2)}) collective-permute-start(bf16[53,8,128]{2,1,0:T(8,128)(2,1)} %get-tuple-element.43), channel_id=1, source_target_pairs={{0,3},{1,2},{2,1},{3,0},{4,7},{5,6},{6,5},{7,4},{8,11},{9,10},{10,... | collective-permute-start | bytes 325640 | tf_op jit(solution)/shard_map/ppermute | solution.py:512
  35.9 0.2 collective-permute-start.14
  36.1 2.8 %collective-permute-start.15 = (bf16[48,8,128]{2,1,0:T(8,128)(2,1)}, bf16[48,8,128]{2,1,0:T(8,128)(2,1)S(1)}, u32[]{:S(2)}, u32[]{:S(2)}) collective-permute-start(bf16[48,8,128]{2,1,0:T(8,128)(2,1)} %get-tuple-element.50), channel_id=1, source_target_pairs={{0,15},{1,14},{2,13},{3,12},{4,11},{5,10},{6,9},{7,8},{8,7},{9,6},... | collective-permute-start | bytes 294920 | tf_op jit(solution)/shard_map/ppermute | solution.py:512
  38.9 0.1 collect_gains.1
  39.0 0.4 collective-permute-start.13
  39.5 0.9 %copy-done = bf16[62,8,128]{2,1,0:T(8,128)(2,1)S(1)} copy-done((bf16[62,8,128]{2,1,0:T(8,128)(2,1)S(1)}, bf16[62,8,128]{2,1,0:T(8,128)(2,1)}, u32[]{:S(2)}) %copy-start) | copy-done | bytes 127000
  40.4 0.5 %make_ready.1 = (bf16[62,8,128]{2,1,0:T(8,128)(2,1)S(1)}, bf16[256,256]{1,0:T(8,128)(2,1)S(1)}, bf16[256,3072]{1,0:T(8,128)(2,1)S(1)}) custom-call(s32[1]{0:T(128)} %bitcast.me_s.turn_s, bf16[62,8,128]{2,1,0:T(8,128)(2,1)S(1)} %copy-done), custom_call_target="tpu_custom_call" | custom-call | tf_op jit(solution)/shard_map/make_ready/pallas_call | solution.py:497
  40.9 5.1 %collective-permute-done.10.rest_11_ = bf16[53,8,128]{2,1,0:T(8,128)(2,1)S(1)} collective-permute-done((bf16[53,8,128]{2,1,0:T(8,128)(2,1)}, bf16[53,8,128]{2,1,0:T(8,128)(2,1)S(1)}, u32[]{:S(2)}, u32[]{:S(2)}) %collective-permute-start.10) | collective-permute-done | bytes 108576 | tf_op jit(solution)/shard_map/ppermute | solution.py:512
  46.0 1.9 %gains_and_sums.1 = (f32[128,3072]{1,0:T(8,128)S(1)}, f32[64,128]{1,0:T(8,128)S(1)}, s32[16,128]{1,0:T(8,128)S(1)}, f32[3,64,8,128]{3,2,1,0:T(8,128)S(1)}) custom-call(s32[1]{0:T(128)} %bitcast.me_s.turn_s, bf16[256,256]{1,0:T(8,128)(2,1)S(1)} %get-tuple-element.29.choice_ref, bf16[256,3072]{1,0:T(8,128)(2,1)S(1)} %get-tuple-element.30.basis_ref, ...), custom_call_target="tpu_custom_call" | custom-call | tf_op jit(solution)/shard_map/gains_and_sums/pallas_call | solution.py:537
  48.0 1.9 %sum_and_apply.1 = bf16[64,8,384]{2,1,0:T(8,128)(2,1)} custom-call(s32[16,128]{1,0:T(8,128)S(1)} %get-tuple-element.45.slots_s, f32[128,3072]{1,0:T(8,128)S(1)} %get-tuple-element.46.gains_ref, f32[64,128]{1,0:T(8,128)S(1)} %get-tuple-element.47.recip_ref, f32[3,64,8,128]{3,2,1,0:T(8,128)S(1)} %get-tuple-element.48.sums_ref, ...), custom_call_target="tpu_custom_call" | custom-call | tf_op jit(solution)/shard_map/sum_and_apply/pallas_call | solution.py:560
  (15 shorter events, 0.0 us)
Async XLA Ops:
  3.2 8.2 %collective-permute-start.12 = (bf16[48,8,128]{2,1,0:T(8,128)(2,1)}, bf16[48,8,128]{2,1,0:T(8,128)(2,1)S(1)}, u32[]{:S(2)}, u32[]{:S(2)}) collective-permute-start(bf16[48,8,128]{2,1,0:T(8,128)(2,1)} %get-tuple-element.44), channel_id=1, source_target_pairs={{0,9},{1,8},{2,11},{3,10},{4,13},{5,12},{6,15},{7,14},{8,1},{9,0},... | collective-permute-start | bytes 294920 | tf_op jit(solution)/shard_map/ppermute | solution.py:512
  6.8 10.4 %collective-permute-start = (bf16[53,8,128]{2,1,0:T(8,128)(2,1)}, bf16[53,8,128]{2,1,0:T(8,128)(2,1)S(1)}, u32[]{:S(2)}, u32[]{:S(2)}) collective-permute-start(bf16[53,8,128]{2,1,0:T(8,128)(2,1)} %get-tuple-element.32), channel_id=1, source_target_pairs={{0,8},{1,9},{2,10},{3,11},{4,12},{5,13},{6,14},{7,15},{8,0},{9,1},... | collective-permute-start | bytes 325640 | tf_op jit(solution)/shard_map/ppermute | solution.py:512
  7.4 13.9 %collective-permute-start.1 = (bf16[53,8,128]{2,1,0:T(8,128)(2,1)}, bf16[53,8,128]{2,1,0:T(8,128)(2,1)S(1)}, u32[]{:S(2)}, u32[]{:S(2)}) collective-permute-start(bf16[53,8,128]{2,1,0:T(8,128)(2,1)} %get-tuple-element.33), channel_id=1, source_target_pairs={{0,4},{1,5},{2,6},{3,7},{4,0},{5,1},{6,2},{7,3},{8,12},{9,13},{10,... | collective-permute-start | bytes 325640 | tf_op jit(solution)/shard_map/ppermute | solution.py:512
  9.0 12.3 %collective-permute-start.2 = (bf16[53,8,128]{2,1,0:T(8,128)(2,1)}, bf16[53,8,128]{2,1,0:T(8,128)(2,1)S(1)}, u32[]{:S(2)}, u32[]{:S(2)}) collective-permute-start(bf16[53,8,128]{2,1,0:T(8,128)(2,1)} %get-tuple-element.34), channel_id=1, source_target_pairs={{0,5},{1,4},{2,7},{3,6},{4,1},{5,0},{6,3},{7,2},{8,13},{9,12},{10,... | collective-permute-start | bytes 325640 | tf_op jit(solution)/shard_map/ppermute | solution.py:512
  9.0 14.9 %collective-permute-start.3 = (bf16[53,8,128]{2,1,0:T(8,128)(2,1)}, bf16[53,8,128]{2,1,0:T(8,128)(2,1)S(1)}, u32[]{:S(2)}, u32[]{:S(2)}) collective-permute-start(bf16[53,8,128]{2,1,0:T(8,128)(2,1)} %get-tuple-element.35), channel_id=1, source_target_pairs={{0,6},{1,7},{2,4},{3,5},{4,2},{5,3},{6,0},{7,1},{8,14},{9,15},{10,... | collective-permute-start | bytes 325640 | tf_op jit(solution)/shard_map/ppermute | solution.py:512
  11.4 15.0 %collective-permute-start.4 = (bf16[53,8,128]{2,1,0:T(8,128)(2,1)}, bf16[53,8,128]{2,1,0:T(8,128)(2,1)S(1)}, u32[]{:S(2)}, u32[]{:S(2)}) collective-permute-start(bf16[53,8,128]{2,1,0:T(8,128)(2,1)} %get-tuple-element.36), channel_id=1, source_target_pairs={{0,10},{1,11},{2,8},{3,9},{4,14},{5,15},{6,12},{7,13},{8,2},{9,3},... | collective-permute-start | bytes 325640 | tf_op jit(solution)/shard_map/ppermute | solution.py:512
  17.2 15.4 %collective-permute-start.5 = (bf16[53,8,128]{2,1,0:T(8,128)(2,1)}, bf16[53,8,128]{2,1,0:T(8,128)(2,1)S(1)}, u32[]{:S(2)}, u32[]{:S(2)}) collective-permute-start(bf16[53,8,128]{2,1,0:T(8,128)(2,1)} %get-tuple-element.37), channel_id=1, source_target_pairs={{0,12},{1,13},{2,14},{3,15},{4,8},{5,9},{6,10},{7,11},{8,4},{9,5},... | collective-permute-start | bytes 325640 | tf_op jit(solution)/shard_map/ppermute | solution.py:512
  21.3 11.3 %collective-permute-start.6 = (bf16[53,8,128]{2,1,0:T(8,128)(2,1)}, bf16[53,8,128]{2,1,0:T(8,128)(2,1)S(1)}, u32[]{:S(2)}, u32[]{:S(2)}) collective-permute-start(bf16[53,8,128]{2,1,0:T(8,128)(2,1)} %get-tuple-element.38), channel_id=1, source_target_pairs={{0,7},{1,6},{2,5},{3,4},{4,3},{5,2},{6,1},{7,0},{8,15},{9,14},{10,... | collective-permute-start | bytes 325640 | tf_op jit(solution)/shard_map/ppermute | solution.py:512
  21.3 14.5 %collective-permute-start.7 = (bf16[53,8,128]{2,1,0:T(8,128)(2,1)}, bf16[53,8,128]{2,1,0:T(8,128)(2,1)S(1)}, u32[]{:S(2)}, u32[]{:S(2)}) collective-permute-start(bf16[53,8,128]{2,1,0:T(8,128)(2,1)} %get-tuple-element.39), channel_id=1, source_target_pairs={{0,1},{1,0},{2,3},{3,2},{4,5},{5,4},{6,7},{7,6},{8,9},{9,8},{10,11... | collective-permute-start | bytes 325640 | tf_op jit(solution)/shard_map/ppermute | solution.py:512
  23.9 12.2 %collective-permute-start.9 = (bf16[53,8,128]{2,1,0:T(8,128)(2,1)}, bf16[53,8,128]{2,1,0:T(8,128)(2,1)S(1)}, u32[]{:S(2)}, u32[]{:S(2)}) collective-permute-start(bf16[53,8,128]{2,1,0:T(8,128)(2,1)} %get-tuple-element.41), channel_id=1, source_target_pairs={{0,14},{1,15},{2,12},{3,13},{4,10},{5,11},{6,8},{7,9},{8,6},{9,7},... | collective-permute-start | bytes 325640 | tf_op jit(solution)/shard_map/ppermute | solution.py:512
  26.4 12.7 %collective-permute-start.8 = (bf16[53,8,128]{2,1,0:T(8,128)(2,1)}, bf16[53,8,128]{2,1,0:T(8,128)(2,1)S(1)}, u32[]{:S(2)}, u32[]{:S(2)}) collective-permute-start(bf16[53,8,128]{2,1,0:T(8,128)(2,1)} %get-tuple-element.40), channel_id=1, source_target_pairs={{0,2},{1,3},{2,0},{3,1},{4,6},{5,7},{6,4},{7,5},{8,10},{9,11},{10,... | collective-permute-start | bytes 325640 | tf_op jit(solution)/shard_map/ppermute | solution.py:512
  32.6 13.5 %collective-permute-start.10 = (bf16[53,8,128]{2,1,0:T(8,128)(2,1)}, bf16[53,8,128]{2,1,0:T(8,128)(2,1)S(1)}, u32[]{:S(2)}, u32[]{:S(2)}) collective-permute-start(bf16[53,8,128]{2,1,0:T(8,128)(2,1)} %get-tuple-element.42), channel_id=1, source_target_pairs={{0,11},{1,10},{2,9},{3,8},{4,15},{5,14},{6,13},{7,12},{8,3},{9,2},... | collective-permute-start | bytes 325640 | tf_op jit(solution)/shard_map/ppermute | solution.py:512
  32.6 13.5 %collective-permute-start.11 = (bf16[53,8,128]{2,1,0:T(8,128)(2,1)}, bf16[53,8,128]{2,1,0:T(8,128)(2,1)S(1)}, u32[]{:S(2)}, u32[]{:S(2)}) collective-permute-start(bf16[53,8,128]{2,1,0:T(8,128)(2,1)} %get-tuple-element.43), channel_id=1, source_target_pairs={{0,3},{1,2},{2,1},{3,0},{4,7},{5,6},{6,5},{7,4},{8,11},{9,10},{10,... | collective-permute-start | bytes 325640 | tf_op jit(solution)/shard_map/ppermute | solution.py:512
  35.9 12.1 %collective-permute-start.14 = (bf16[48,8,128]{2,1,0:T(8,128)(2,1)}, bf16[48,8,128]{2,1,0:T(8,128)(2,1)S(1)}, u32[]{:S(2)}, u32[]{:S(2)}) collective-permute-start(bf16[48,8,128]{2,1,0:T(8,128)(2,1)} %get-tuple-element.49), channel_id=1, source_target_pairs={{0,13},{1,12},{2,15},{3,14},{4,9},{5,8},{6,11},{7,10},{8,5},{9,4},... | collective-permute-start | bytes 294920 | tf_op jit(solution)/shard_map/ppermute | solution.py:512
  36.1 11.9 %collective-permute-start.15 = (bf16[48,8,128]{2,1,0:T(8,128)(2,1)}, bf16[48,8,128]{2,1,0:T(8,128)(2,1)S(1)}, u32[]{:S(2)}, u32[]{:S(2)}) collective-permute-start(bf16[48,8,128]{2,1,0:T(8,128)(2,1)} %get-tuple-element.50), channel_id=1, source_target_pairs={{0,15},{1,14},{2,13},{3,12},{4,11},{5,10},{6,9},{7,8},{8,7},{9,6},... | collective-permute-start | bytes 294920 | tf_op jit(solution)/shard_map/ppermute | solution.py:512
  39.0 7.0 %collective-permute-start.13 = (bf16[20,8,128]{2,1,0:T(8,128)(2,1)S(1)}, bf16[20,8,128]{2,1,0:T(8,128)(2,1)S(1)}, u32[]{:S(2)}, u32[]{:S(2)}) collective-permute-start(bf16[20,8,128]{2,1,0:T(8,128)(2,1)S(1)} %collect_gains.1), channel_id=1, source_target_pairs={{0,1},{1,0},{2,3},{3,2},{4,5},{5,4},{6,7},{7,6},{8,9},{9,8},{10,11... | collective-permute-start | bytes 122888 | tf_op jit(solution)/shard_map/ppermute | solution.py:512
  39.5 0.9 %copy-start = (bf16[62,8,128]{2,1,0:T(8,128)(2,1)S(1)}, bf16[62,8,128]{2,1,0:T(8,128)(2,1)}, u32[]{:S(2)}) copy-start(bf16[62,8,128]{2,1,0:T(8,128)(2,1)} %get-tuple-element.28.own_ref) | copy-start | bytes 380932

commit v9 on v6

--- a/solution.py
+++ b/solution.py
@@ -146,6 +146,7 @@
 
     at = chunks * capacity
     if near > 1:
+        outs = list(outs[: near + 1]) + [None] + list(outs[near + 1 :])
         pairs = [(meta_ref, outs[x].at[pl.ds(at, depth)]) for x in with_gains(near)]
     else:
         pairs = [(meta_ref, outs[1])]
@@ -166,12 +167,39 @@
         fetches[i].wait()
         lax.fori_loop(i * span, (i + 1) * span, place, 0, unroll=8)
     if near > 1:
-        pairs = [(block_ref.at[x], outs[x].at[pl.ds(0, at)]) for x in range(devices)]
+        pairs = [
+            (block_ref.at[x], outs[x].at[pl.ds(0, at)]) for x in range(devices) if x != near + 1
+        ]
     else:
         pairs = [(block_ref, outs[0])]
     sends += start_all(pairs, sems.at[pl.ds(start, len(pairs))])
     for send in sends:
         send.wait()
+
+
+def first_kernel(capacity, target, me_s, owner_hbm, vis_hbm, out_hbm, owner_s, list_s, vis_ref, block_ref, sems):
+    rows = vis_ref.shape[0]
+    chunks = vis_ref.shape[2] // LANES
+    moves = start_all(((owner_hbm, owner_s), (vis_hbm, vis_ref)), sems)
+    wanted = me_s[0] ^ target
+    moves[0].wait()
+
+    def note(r, k):
+        list_s[k] = r
+        return k + jnp.where(owner_s[r] == wanted, 1, 0)
+
+    count = lax.fori_loop(0, rows, note, 0, unroll=8)
+    moves[1].wait()
+
+    def place(k, carry):
+        r = list_s[k]
+        for c in range(chunks):
+            block_ref[chunks * k + c] = vis_ref[r, :, c * LANES : (c + 1) * LANES]
+        return carry
+
+    lax.fori_loop(0, count, place, 0)
+    send = start_all([(block_ref, out_hbm)], sems)[0]
+    send.wait()
 
 
 def ready_kernel(
@@ -458,6 +486,24 @@
     pairs = baseline_station_pairs.T
     weights = band_weights.T
     offset = band_offset.reshape(chunks, LANES)
+    me_owner = row_owner.reshape(rows)
+    if halves:
+        first = outs.pop(near + 1)
+        alone = pl.pallas_call(
+            functools.partial(first_kernel, capacity, near + 1),
+            out_shape=first,
+            in_specs=[smem, hbm, hbm],
+            out_specs=hbm,
+            scratch_shapes=[
+                pltpu.SMEM((rows,), i32),
+                pltpu.SMEM((rows + 8,), i32),
+                pltpu.VMEM((rows, parts, channels), bf16),
+                pltpu.VMEM(first.shape, bf16),
+                dma((2,)),
+            ],
+            compiler_params=most,
+            name="pack_first",
+        )(me, me_owner, visibilities)
     sent = pl.pallas_call(
         functools.partial(pack_kernel, capacity, near),
         out_shape=outs,
@@ -512,6 +558,10 @@
             compiler_params=some,
             name="make_ready",
         )(turn, own)
+
+    if halves:
+        sent = list(sent)
+        sent.insert(near + 1, alone)
 
     def swap(array, x):
         return lax.ppermute(array, "bl", [(d, d ^ x) for d in range(devices)])

time: 48 us -> 47 us (0.979)
  starting transfers between devices: 28.1 us -> 24.3 us
  Pallas kernels: 7.72 us -> 9.58 us
  waiting for transfers between devices: 11 us -> 11.9 us
    ppermute x16, starting transfers between devices: 28.1 us -> 24.3 us  [swap(): return lax.ppermute(array, 'bl', [(d, d ^ x) for d in range(devices)])]
    pallas_call x0 -> x1, Pallas kernels: none -> 1.79 us  [on_device(): pl.pallas_call(functools.partial(first_kernel, capacity, near + 1), out_s...]
    ppermute x16, waiting for transfers between devices: 11 us -> 11.9 us  [swap(): return lax.ppermute(array, 'bl', [(d, d ^ x) for d in range(devices)])]
  transfers between devices with their start and end apart: 16 -> 16, of which waited for: 6 -> 6; matrix products, arithmetic and copies ran while one was open for 0% -> 0% of each run, Pallas kernels for 5% -> 12%
where the time goes in v9:
time: 47 us; the launch traced here: 46.8 us
  starting transfers between devices  24.3 us (52%)
  waiting for transfers between devices  11.9 us (25%)
  Pallas kernels  9.58 us (20%)
  local copies, waits for them, and re-layouts  0.9 us (2%)
    ppermute x16, starting transfers between devices, swap(): return lax.ppermute(array, 'bl', [(d, d ^ x) for d in range(devices)])  24.3 us
    ppermute x16, waiting for transfers between devices, swap(): return lax.ppermute(array, 'bl', [(d, d ^ x) for d in range(devices)])  11.9 us
    pallas_call x1, Pallas kernels, on_device(): pl.pallas_call(functools.partial(pack_kernel, capacity, near), out_shape=...  3.2 us
    pallas_call x1, Pallas kernels, on_device(): pl.pallas_call(functools.partial(finish_kernel, capacity, late), out_shap...  2.04 us
    pallas_call x1, Pallas kernels, on_device(): pl.pallas_call(functools.partial(middle_kernel, capacity, near, depth, or...  1.95 us
    pallas_call x1, Pallas kernels, on_device(): pl.pallas_call(functools.partial(first_kernel, capacity, near + 1), out_s...  1.79 us
  transfers between devices with their start and end apart: 16, of which 6 were waited for; matrix products, arithmetic and copies ran while one was open for 0% of the time, Pallas kernels for 12%

profile of v9, /device:TPU:0, one launch (start us, length us, event | category | flops | bytes accessed | tf_op | source)
XLA Modules:
  0.0 46.8 jit_solution(5623794875404702565)
XLA Ops:
  0.0 1.8 %pack_first.1 = bf16[48,8,128]{2,1,0:T(8,128)(2,1)} custom-call(s32[1]{0:T(128)} %bitcast.me_s.turn_s, s32[128]{0:T(128)} %bitcast.12, bf16[128,8,384]{2,1,0:T(8,128)(2,1)} %vis_hbm.3), custom_call_target="tpu_custom_call" | custom-call | tf_op jit(solution)/shard_map/pack_first/pallas_call | solution.py:492
  1.8 3.5 %collective-permute-start.12 = (bf16[48,8,128]{2,1,0:T(8,128)(2,1)}, bf16[48,8,128]{2,1,0:T(8,128)(2,1)S(1)}, u32[]{:S(2)}, u32[]{:S(2)}) collective-permute-start(bf16[48,8,128]{2,1,0:T(8,128)(2,1)} %pack_first.1), channel_id=1, source_target_pairs={{0,9},{1,8},{2,11},{3,10},{4,13},{5,12},{6,15},{7,14},{8,1},{9,0},... | collective-permute-start | bytes 294920 | tf_op jit(solution)/shard_map/ppermute | solution.py:567
  5.3 3.2 %pack_rows.1 = (bf16[62,8,128]{2,1,0:T(8,128)(2,1)}, bf16[53,8,128]{2,1,0:T(8,128)(2,1)}, bf16[53,8,128]{2,1,0:T(8,128)(2,1)}, bf16[53,8,128]{2,1,0:T(8,128)(2,1...) custom-call(s32[1]{0:T(128)} %bitcast.me_s.turn_s, ...), custom_call_target="tpu_custom_call" | custom-call | tf_op jit(solution)/shard_map/pack_rows/pallas_call | solution.py:507
  8.5 0.7 %collective-permute-start = (bf16[53,8,128]{2,1,0:T(8,128)(2,1)}, bf16[53,8,128]{2,1,0:T(8,128)(2,1)S(1)}, u32[]{:S(2)}, u32[]{:S(2)}) collective-permute-start(bf16[53,8,128]{2,1,0:T(8,128)(2,1)} %get-tuple-element.31), channel_id=1, source_target_pairs={{0,8},{1,9},{2,10},{3,11},{4,12},{5,13},{6,14},{7,15},{8,0},{9,1},... | collective-permute-start | bytes 325640 | tf_op jit(solution)/shard_map/ppermute | solution.py:567
  9.2 3.3 %collective-permute-start.1 = (bf16[53,8,128]{2,1,0:T(8,128)(2,1)}, bf16[53,8,128]{2,1,0:T(8,128)(2,1)S(1)}, u32[]{:S(2)}, u32[]{:S(2)}) collective-permute-start(bf16[53,8,128]{2,1,0:T(8,128)(2,1)} %get-tuple-element.32), channel_id=1, source_target_pairs={{0,10},{1,11},{2,8},{3,9},{4,14},{5,15},{6,12},{7,13},{8,2},{9,3},... | collective-permute-start | bytes 325640 | tf_op jit(solution)/shard_map/ppermute | solution.py:567
  12.5 1.5 %collective-permute-start.2 = (bf16[53,8,128]{2,1,0:T(8,128)(2,1)}, bf16[53,8,128]{2,1,0:T(8,128)(2,1)S(1)}, u32[]{:S(2)}, u32[]{:S(2)}) collective-permute-start(bf16[53,8,128]{2,1,0:T(8,128)(2,1)} %get-tuple-element.33), channel_id=1, source_target_pairs={{0,4},{1,5},{2,6},{3,7},{4,0},{5,1},{6,2},{7,3},{8,12},{9,13},{10,... | collective-permute-start | bytes 325640 | tf_op jit(solution)/shard_map/ppermute | solution.py:567
  14.1 3.4 %collective-permute-start.4 = (bf16[53,8,128]{2,1,0:T(8,128)(2,1)}, bf16[53,8,128]{2,1,0:T(8,128)(2,1)S(1)}, u32[]{:S(2)}, u32[]{:S(2)}) collective-permute-start(bf16[53,8,128]{2,1,0:T(8,128)(2,1)} %get-tuple-element.35), channel_id=1, source_target_pairs={{0,12},{1,13},{2,14},{3,15},{4,8},{5,9},{6,10},{7,11},{8,4},{9,5},... | collective-permute-start | bytes 325640 | tf_op jit(solution)/shard_map/ppermute | solution.py:567
  17.5 2.9 %collective-permute-done.rest_0_.rest_1_ = bf16[53,8,128]{2,1,0:T(8,128)(2,1)S(1)} collective-permute-done((bf16[53,8,128]{2,1,0:T(8,128)(2,1)}, bf16[53,8,128]{2,1,0:T(8,128)(2,1)S(1)}, u32[]{:S(2)}, u32[]{:S(2)}) %collective-permute-start) | collective-permute-done | bytes 108576 | tf_op jit(solution)/shard_map/ppermute | solution.py:567
  20.4 3.2 %collective-permute-done.1.rest_1_.rest_2_ = bf16[53,8,128]{2,1,0:T(8,128)(2,1)S(1)} collective-permute-done((bf16[53,8,128]{2,1,0:T(8,128)(2,1)}, bf16[53,8,128]{2,1,0:T(8,128)(2,1)S(1)}, u32[]{:S(2)}, u32[]{:S(2)}) %collective-permute-start.1) | collective-permute-done | bytes 108576 | tf_op jit(solution)/shard_map/ppermute | solution.py:567
  23.6 2.3 %collective-permute-start.6 = (bf16[53,8,128]{2,1,0:T(8,128)(2,1)}, bf16[53,8,128]{2,1,0:T(8,128)(2,1)S(1)}, u32[]{:S(2)}, u32[]{:S(2)}) collective-permute-start(bf16[53,8,128]{2,1,0:T(8,128)(2,1)} %get-tuple-element.37), channel_id=1, source_target_pairs={{0,14},{1,15},{2,12},{3,13},{4,10},{5,11},{6,8},{7,9},{8,6},{9,7},... | collective-permute-start | bytes 325640 | tf_op jit(solution)/shard_map/ppermute | solution.py:567
  25.9 2.6 %collective-permute-start.8 = (bf16[53,8,128]{2,1,0:T(8,128)(2,1)}, bf16[53,8,128]{2,1,0:T(8,128)(2,1)S(1)}, u32[]{:S(2)}, u32[]{:S(2)}) collective-permute-start(bf16[53,8,128]{2,1,0:T(8,128)(2,1)} %get-tuple-element.39), channel_id=1, source_target_pairs={{0,11},{1,10},{2,9},{3,8},{4,15},{5,14},{6,13},{7,12},{8,3},{9,2},... | collective-permute-start | bytes 325640 | tf_op jit(solution)/shard_map/ppermute | solution.py:567
  28.6 2.6 %collective-permute-start.10 = (bf16[53,8,128]{2,1,0:T(8,128)(2,1)}, bf16[53,8,128]{2,1,0:T(8,128)(2,1)S(1)}, u32[]{:S(2)}, u32[]{:S(2)}) collective-permute-start(bf16[53,8,128]{2,1,0:T(8,128)(2,1)} %get-tuple-element.41), channel_id=1, source_target_pairs={{0,2},{1,3},{2,0},{3,1},{4,6},{5,7},{6,4},{7,5},{8,10},{9,11},{10,... | collective-permute-start | bytes 325640 | tf_op jit(solution)/shard_map/ppermute | solution.py:567
  31.1 1.4 %collective-permute-done.6.rest_3_.rest_7_ = bf16[53,8,128]{2,1,0:T(8,128)(2,1)S(1)} collective-permute-done((bf16[53,8,128]{2,1,0:T(8,128)(2,1)}, bf16[53,8,128]{2,1,0:T(8,128)(2,1)S(1)}, u32[]{:S(2)}, u32[]{:S(2)}) %collective-permute-start.6) | collective-permute-done | bytes 108576 | tf_op jit(solution)/shard_map/ppermute | solution.py:567
  32.5 2.4 %collective-permute-done.7.rest_8_ = bf16[53,8,128]{2,1,0:T(8,128)(2,1)S(1)} collective-permute-done((bf16[53,8,128]{2,1,0:T(8,128)(2,1)}, bf16[53,8,128]{2,1,0:T(8,128)(2,1)S(1)}, u32[]{:S(2)}, u32[]{:S(2)}) %collective-permute-start.7) | collective-permute-done | bytes 108576 | tf_op jit(solution)/shard_map/ppermute | solution.py:567
  34.9 2.0 %collective-permute-start.14 = (bf16[48,8,128]{2,1,0:T(8,128)(2,1)}, bf16[48,8,128]{2,1,0:T(8,128)(2,1)S(1)}, u32[]{:S(2)}, u32[]{:S(2)}) collective-permute-start(bf16[48,8,128]{2,1,0:T(8,128)(2,1)} %get-tuple-element.47), channel_id=1, source_target_pairs={{0,13},{1,12},{2,15},{3,14},{4,9},{5,8},{6,11},{7,10},{8,5},{9,4},... | collective-permute-start | bytes 294920 | tf_op jit(solution)/shard_map/ppermute | solution.py:567
  37.0 0.1 collective-permute-done.8.rest_9_
  37.0 1.9 %collective-permute-start.15 = (bf16[48,8,128]{2,1,0:T(8,128)(2,1)}, bf16[48,8,128]{2,1,0:T(8,128)(2,1)S(1)}, u32[]{:S(2)}, u32[]{:S(2)}) collective-permute-start(bf16[48,8,128]{2,1,0:T(8,128)(2,1)} %get-tuple-element.48), channel_id=1, source_target_pairs={{0,15},{1,14},{2,13},{3,12},{4,11},{5,10},{6,9},{7,8},{8,7},{9,6},... | collective-permute-start | bytes 294920 | tf_op jit(solution)/shard_map/ppermute | solution.py:567
  39.0 0.1 collect_gains.1
  39.0 0.3 collective-permute-start.13
  39.3 0.9 %copy-done = bf16[62,8,128]{2,1,0:T(8,128)(2,1)S(1)} copy-done((bf16[62,8,128]{2,1,0:T(8,128)(2,1)S(1)}, bf16[62,8,128]{2,1,0:T(8,128)(2,1)}, u32[]{:S(2)}) %copy-start) | copy-done | bytes 127000
  40.2 0.5 %make_ready.1 = (bf16[62,8,128]{2,1,0:T(8,128)(2,1)S(1)}, bf16[256,256]{1,0:T(8,128)(2,1)S(1)}, bf16[256,3072]{1,0:T(8,128)(2,1)S(1)}) custom-call(s32[1]{0:T(128)} %bitcast.me_s.turn_s, bf16[62,8,128]{2,1,0:T(8,128)(2,1)S(1)} %copy-done), custom_call_target="tpu_custom_call" | custom-call | tf_op jit(solution)/shard_map/make_ready/pallas_call | solution.py:548
  40.8 2.0 %gains_and_sums.1 = (f32[128,3072]{1,0:T(8,128)S(1)}, f32[64,128]{1,0:T(8,128)S(1)}, s32[16,128]{1,0:T(8,128)S(1)}, f32[3,64,8,128]{3,2,1,0:T(8,128)S(1)}) custom-call(s32[1]{0:T(128)} %bitcast.me_s.turn_s, bf16[256,256]{1,0:T(8,128)(2,1)S(1)} %get-tuple-element.28.choice_ref, bf16[256,3072]{1,0:T(8,128)(2,1)S(1)} %get-tuple-element.29.basis_ref, ...), custom_call_target="tpu_custom_call" | custom-call | tf_op jit(solution)/shard_map/gains_and_sums/pallas_call | solution.py:592
  42.8 1.9 %collective-permute-done.15.rest_1_ = bf16[48,8,128]{2,1,0:T(8,128)(2,1)S(1)} collective-permute-done((bf16[48,8,128]{2,1,0:T(8,128)(2,1)}, bf16[48,8,128]{2,1,0:T(8,128)(2,1)S(1)}, u32[]{:S(2)}, u32[]{:S(2)}) %collective-permute-start.15) | collective-permute-done | bytes 98336 | tf_op jit(solution)/shard_map/ppermute | solution.py:567
  44.7 2.0 %sum_and_apply.1 = bf16[64,8,384]{2,1,0:T(8,128)(2,1)} custom-call(s32[16,128]{1,0:T(8,128)S(1)} %get-tuple-element.43.slots_s, f32[128,3072]{1,0:T(8,128)S(1)} %get-tuple-element.44.gains_ref, f32[64,128]{1,0:T(8,128)S(1)} %get-tuple-element.45.recip_ref, f32[3,64,8,128]{3,2,1,0:T(8,128)S(1)} %get-tuple-element.46.sums_ref, ...), custom_call_target="tpu_custom_call" | custom-call | tf_op jit(solution)/shard_map/sum_and_apply/pallas_call | solution.py:615
  (16 shorter events, 0.0 us)
Async XLA Ops:
  1.8 12.3 %collective-permute-start.12 = (bf16[48,8,128]{2,1,0:T(8,128)(2,1)}, bf16[48,8,128]{2,1,0:T(8,128)(2,1)S(1)}, u32[]{:S(2)}, u32[]{:S(2)}) collective-permute-start(bf16[48,8,128]{2,1,0:T(8,128)(2,1)} %pack_first.1), channel_id=1, source_target_pairs={{0,9},{1,8},{2,11},{3,10},{4,13},{5,12},{6,15},{7,14},{8,1},{9,0},... | collective-permute-start | bytes 294920 | tf_op jit(solution)/shard_map/ppermute | solution.py:567
  8.5 11.8 %collective-permute-start = (bf16[53,8,128]{2,1,0:T(8,128)(2,1)}, bf16[53,8,128]{2,1,0:T(8,128)(2,1)S(1)}, u32[]{:S(2)}, u32[]{:S(2)}) collective-permute-start(bf16[53,8,128]{2,1,0:T(8,128)(2,1)} %get-tuple-element.31), channel_id=1, source_target_pairs={{0,8},{1,9},{2,10},{3,11},{4,12},{5,13},{6,14},{7,15},{8,0},{9,1},... | collective-permute-start | bytes 325640 | tf_op jit(solution)/shard_map/ppermute | solution.py:567
  9.2 14.4 %collective-permute-start.1 = (bf16[53,8,128]{2,1,0:T(8,128)(2,1)}, bf16[53,8,128]{2,1,0:T(8,128)(2,1)S(1)}, u32[]{:S(2)}, u32[]{:S(2)}) collective-permute-start(bf16[53,8,128]{2,1,0:T(8,128)(2,1)} %get-tuple-element.32), channel_id=1, source_target_pairs={{0,10},{1,11},{2,8},{3,9},{4,14},{5,15},{6,12},{7,13},{8,2},{9,3},... | collective-permute-start | bytes 325640 | tf_op jit(solution)/shard_map/ppermute | solution.py:567
  12.5 13.4 %collective-permute-start.2 = (bf16[53,8,128]{2,1,0:T(8,128)(2,1)}, bf16[53,8,128]{2,1,0:T(8,128)(2,1)S(1)}, u32[]{:S(2)}, u32[]{:S(2)}) collective-permute-start(bf16[53,8,128]{2,1,0:T(8,128)(2,1)} %get-tuple-element.33), channel_id=1, source_target_pairs={{0,4},{1,5},{2,6},{3,7},{4,0},{5,1},{6,2},{7,3},{8,12},{9,13},{10,... | collective-permute-start | bytes 325640 | tf_op jit(solution)/shard_map/ppermute | solution.py:567
  14.1 11.8 %collective-permute-start.3 = (bf16[53,8,128]{2,1,0:T(8,128)(2,1)}, bf16[53,8,128]{2,1,0:T(8,128)(2,1)S(1)}, u32[]{:S(2)}, u32[]{:S(2)}) collective-permute-start(bf16[53,8,128]{2,1,0:T(8,128)(2,1)} %get-tuple-element.34), channel_id=1, source_target_pairs={{0,5},{1,4},{2,7},{3,6},{4,1},{5,0},{6,3},{7,2},{8,13},{9,12},{10,... | collective-permute-start | bytes 325640 | tf_op jit(solution)/shard_map/ppermute | solution.py:567
  14.1 14.5 %collective-permute-start.4 = (bf16[53,8,128]{2,1,0:T(8,128)(2,1)}, bf16[53,8,128]{2,1,0:T(8,128)(2,1)S(1)}, u32[]{:S(2)}, u32[]{:S(2)}) collective-permute-start(bf16[53,8,128]{2,1,0:T(8,128)(2,1)} %get-tuple-element.35), channel_id=1, source_target_pairs={{0,12},{1,13},{2,14},{3,15},{4,8},{5,9},{6,10},{7,11},{8,4},{9,5},... | collective-permute-start | bytes 325640 | tf_op jit(solution)/shard_map/ppermute | solution.py:567
  20.4 8.2 %collective-permute-start.5 = (bf16[53,8,128]{2,1,0:T(8,128)(2,1)}, bf16[53,8,128]{2,1,0:T(8,128)(2,1)S(1)}, u32[]{:S(2)}, u32[]{:S(2)}) collective-permute-start(bf16[53,8,128]{2,1,0:T(8,128)(2,1)} %get-tuple-element.36), channel_id=1, source_target_pairs={{0,6},{1,7},{2,4},{3,5},{4,2},{5,3},{6,0},{7,1},{8,14},{9,15},{10,... | collective-permute-start | bytes 325640 | tf_op jit(solution)/shard_map/ppermute | solution.py:567
  23.6 8.9 %collective-permute-start.6 = (bf16[53,8,128]{2,1,0:T(8,128)(2,1)}, bf16[53,8,128]{2,1,0:T(8,128)(2,1)S(1)}, u32[]{:S(2)}, u32[]{:S(2)}) collective-permute-start(bf16[53,8,128]{2,1,0:T(8,128)(2,1)} %get-tuple-element.37), channel_id=1, source_target_pairs={{0,14},{1,15},{2,12},{3,13},{4,10},{5,11},{6,8},{7,9},{8,6},{9,7},... | collective-permute-start | bytes 325640 | tf_op jit(solution)/shard_map/ppermute | solution.py:567
  25.9 9.0 %collective-permute-start.7 = (bf16[53,8,128]{2,1,0:T(8,128)(2,1)}, bf16[53,8,128]{2,1,0:T(8,128)(2,1)S(1)}, u32[]{:S(2)}, u32[]{:S(2)}) collective-permute-start(bf16[53,8,128]{2,1,0:T(8,128)(2,1)} %get-tuple-element.38), channel_id=1, source_target_pairs={{0,7},{1,6},{2,5},{3,4},{4,3},{5,2},{6,1},{7,0},{8,15},{9,14},{10,... | collective-permute-start | bytes 325640 | tf_op jit(solution)/shard_map/ppermute | solution.py:567
  25.9 11.1 %collective-permute-start.8 = (bf16[53,8,128]{2,1,0:T(8,128)(2,1)}, bf16[53,8,128]{2,1,0:T(8,128)(2,1)S(1)}, u32[]{:S(2)}, u32[]{:S(2)}) collective-permute-start(bf16[53,8,128]{2,1,0:T(8,128)(2,1)} %get-tuple-element.39), channel_id=1, source_target_pairs={{0,11},{1,10},{2,9},{3,8},{4,15},{5,14},{6,13},{7,12},{8,3},{9,2},... | collective-permute-start | bytes 325640 | tf_op jit(solution)/shard_map/ppermute | solution.py:567
  28.5 10.5 %collective-permute-start.9 = (bf16[53,8,128]{2,1,0:T(8,128)(2,1)}, bf16[53,8,128]{2,1,0:T(8,128)(2,1)S(1)}, u32[]{:S(2)}, u32[]{:S(2)}) collective-permute-start(bf16[53,8,128]{2,1,0:T(8,128)(2,1)} %get-tuple-element.40), channel_id=1, source_target_pairs={{0,1},{1,0},{2,3},{3,2},{4,5},{5,4},{6,7},{7,6},{8,9},{9,8},{10,11... | collective-permute-start | bytes 325640 | tf_op jit(solution)/shard_map/ppermute | solution.py:567
  28.6 12.2 %collective-permute-start.10 = (bf16[53,8,128]{2,1,0:T(8,128)(2,1)}, bf16[53,8,128]{2,1,0:T(8,128)(2,1)S(1)}, u32[]{:S(2)}, u32[]{:S(2)}) collective-permute-start(bf16[53,8,128]{2,1,0:T(8,128)(2,1)} %get-tuple-element.41), channel_id=1, source_target_pairs={{0,2},{1,3},{2,0},{3,1},{4,6},{5,7},{6,4},{7,5},{8,10},{9,11},{10,... | collective-permute-start | bytes 325640 | tf_op jit(solution)/shard_map/ppermute | solution.py:567
  32.5 8.3 %collective-permute-start.11 = (bf16[53,8,128]{2,1,0:T(8,128)(2,1)}, bf16[53,8,128]{2,1,0:T(8,128)(2,1)S(1)}, u32[]{:S(2)}, u32[]{:S(2)}) collective-permute-start(bf16[53,8,128]{2,1,0:T(8,128)(2,1)} %get-tuple-element.42), channel_id=1, source_target_pairs={{0,3},{1,2},{2,1},{3,0},{4,7},{5,6},{6,5},{7,4},{8,11},{9,10},{10,... | collective-permute-start | bytes 325640 | tf_op jit(solution)/shard_map/ppermute | solution.py:567
  34.9 7.9 %collective-permute-start.14 = (bf16[48,8,128]{2,1,0:T(8,128)(2,1)}, bf16[48,8,128]{2,1,0:T(8,128)(2,1)S(1)}, u32[]{:S(2)}, u32[]{:S(2)}) collective-permute-start(bf16[48,8,128]{2,1,0:T(8,128)(2,1)} %get-tuple-element.47), channel_id=1, source_target_pairs={{0,13},{1,12},{2,15},{3,14},{4,9},{5,8},{6,11},{7,10},{8,5},{9,4},... | collective-permute-start | bytes 294920 | tf_op jit(solution)/shard_map/ppermute | solution.py:567
  37.0 7.7 %collective-permute-start.15 = (bf16[48,8,128]{2,1,0:T(8,128)(2,1)}, bf16[48,8,128]{2,1,0:T(8,128)(2,1)S(1)}, u32[]{:S(2)}, u32[]{:S(2)}) collective-permute-start(bf16[48,8,128]{2,1,0:T(8,128)(2,1)} %get-tuple-element.48), channel_id=1, source_target_pairs={{0,15},{1,14},{2,13},{3,12},{4,11},{5,10},{6,9},{7,8},{8,7},{9,6},... | collective-permute-start | bytes 294920 | tf_op jit(solution)/shard_map/ppermute | solution.py:567
  39.0 1.8 %collective-permute-start.13 = (bf16[20,8,128]{2,1,0:T(8,128)(2,1)S(1)}, bf16[20,8,128]{2,1,0:T(8,128)(2,1)S(1)}, u32[]{:S(2)}, u32[]{:S(2)}) collective-permute-start(bf16[20,8,128]{2,1,0:T(8,128)(2,1)S(1)} %collect_gains.1), channel_id=1, source_target_pairs={{0,1},{1,0},{2,3},{3,2},{4,5},{5,4},{6,7},{7,6},{8,9},{9,8},{10,11... | collective-permute-start | bytes 122888 | tf_op jit(solution)/shard_map/ppermute | solution.py:567
  39.3 0.9 %copy-start = (bf16[62,8,128]{2,1,0:T(8,128)(2,1)S(1)}, bf16[62,8,128]{2,1,0:T(8,128)(2,1)}, u32[]{:S(2)}) copy-start(bf16[62,8,128]{2,1,0:T(8,128)(2,1)} %get-tuple-element.27.own_ref) | copy-start | bytes 380932

commit v10 on v9

--- a/solution.py
+++ b/solution.py
@@ -20,15 +20,19 @@
 
 
 def schedule(near):
-    even, odd = list(range(near, 2 * near, 2)), list(range(near + 1, 2 * near, 2))
+    even, odd = far(near)
     close = list(range(near // 2, near)) + list(range(1, near // 2))
-    cross, late = even[2:] + odd[1:-2], odd[-2:]
     order = [0] + even[:2] + close[:2]
-    close = close[2:]
+    cross, close = even[2:] + odd[1:-2], close[2:]
     while cross:
         order += cross[:1] + close[:1]
         cross, close = cross[1:], close[1:]
-    return order + close + odd[:1], late
+    return order + close + odd[:1], odd[-2:]
+
+
+def far(near):
+    spans = list(range(near + near // 2, 2 * near)) + list(range(near, near + near // 2))
+    return [x for x in spans if x % 2 == 0], [x for x in spans if x % 2]
 
 
 def with_gains(near):
@@ -146,7 +150,8 @@
 
     at = chunks * capacity
     if near > 1:
-        outs = list(outs[: near + 1]) + [None] + list(outs[near + 1 :])
+        target = far(near)[1][0]
+        outs = list(outs[:target]) + [None] + list(outs[target:])
         pairs = [(meta_ref, outs[x].at[pl.ds(at, depth)]) for x in with_gains(near)]
     else:
         pairs = [(meta_ref, outs[1])]
@@ -168,7 +173,7 @@
         lax.fori_loop(i * span, (i + 1) * span, place, 0, unroll=8)
     if near > 1:
         pairs = [
-            (block_ref.at[x], outs[x].at[pl.ds(0, at)]) for x in range(devices) if x != near + 1
+            (block_ref.at[x], outs[x].at[pl.ds(0, at)]) for x in range(devices) if x != target
         ]
     else:
         pairs = [(block_ref, outs[0])]
@@ -471,7 +476,8 @@
     block = (chunks * capacity, parts, LANES)
     rows_at = chunks * capacity
     if halves:
-        long = with_gains(near) + [near + 3]
+        even, odd = far(near)
+        long = with_gains(near) + odd[1:-2]
         outs = [
             shape((rows_at + (depth if x in long else 0), parts, LANES), bf16)
             for x in range(devices)
@@ -488,9 +494,10 @@
     offset = band_offset.reshape(chunks, LANES)
     me_owner = row_owner.reshape(rows)
     if halves:
-        first = outs.pop(near + 1)
+        target = odd[0]
+        first = outs.pop(target)
         alone = pl.pallas_call(
-            functools.partial(first_kernel, capacity, near + 1),
+            functools.partial(first_kernel, capacity, target),
             out_shape=first,
             in_specs=[smem, hbm, hbm],
             out_specs=hbm,
@@ -561,7 +568,7 @@
 
     if halves:
         sent = list(sent)
-        sent.insert(near + 1, alone)
+        sent.insert(target, alone)
 
     def swap(array, x):
         return lax.ppermute(array, "bl", [(d, d ^ x) for d in range(devices)])

time: 47 us -> 49 us (1.043)
  waiting for transfers between devices: 11.9 us -> 15.7 us
  starting transfers between devices: 24.3 us -> 22.6 us
    ppermute x16, waiting for transfers between devices: 11.9 us -> 15.7 us  [swap(): return lax.ppermute(array, 'bl', [(d, d ^ x) for d in range(devices)])]
    ppermute x16, starting transfers between devices: 24.3 us -> 22.6 us  [swap(): return lax.ppermute(array, 'bl', [(d, d ^ x) for d in range(devices)])]
  transfers between devices with their start and end apart: 16 -> 16, of which waited for: 6 -> 10; matrix products, arithmetic and copies ran while one was open for 0% -> 0% of each run, Pallas kernels for 12% -> 12%
where the time goes in v10:
time: 49 us; the launch traced here: 48.9 us
  starting transfers between devices  22.6 us (46%)
  waiting for transfers between devices  15.7 us (32%)
  Pallas kernels  9.61 us (20%)
  local copies, waits for them, and re-layouts  0.9 us (2%)
    ppermute x16, starting transfers between devices, swap(): return lax.ppermute(array, 'bl', [(d, d ^ x) for d in range(devices)])  22.6 us
    ppermute x16, waiting for transfers between devices, swap(): return lax.ppermute(array, 'bl', [(d, d ^ x) for d in range(devices)])  15.7 us
    pallas_call x1, Pallas kernels, on_device(): pl.pallas_call(functools.partial(pack_kernel, capacity, near), out_shape=...  3.2 us
    pallas_call x1, Pallas kernels, on_device(): pl.pallas_call(functools.partial(middle_kernel, capacity, near, depth, or...  2.04 us
    pallas_call x1, Pallas kernels, on_device(): pl.pallas_call(functools.partial(finish_kernel, capacity, late), out_shap...  1.98 us
    pallas_call x1, Pallas kernels, on_device(): pl.pallas_call(functools.partial(first_kernel, capacity, target), out_sha...  1.79 us
  transfers between devices with their start and end apart: 16, of which 10 were waited for; matrix products, arithmetic and copies ran while one was open for 0% of the time, Pallas kernels for 12%

profile of v10, /device:TPU:0, one launch (start us, length us, event | category | flops | bytes accessed | tf_op | source)
XLA Modules:
  0.0 48.9 jit_solution(10599331832982442166)
XLA Ops:
  0.0 1.8 %pack_first.1 = bf16[48,8,128]{2,1,0:T(8,128)(2,1)} custom-call(s32[1]{0:T(128)} %bitcast.me_s.turn_s, s32[128]{0:T(128)} %bitcast.12, bf16[128,8,384]{2,1,0:T(8,128)(2,1)} %vis_hbm.3), custom_call_target="tpu_custom_call" | custom-call | tf_op jit(solution)/shard_map/pack_first/pallas_call | solution.py:499
  1.8 4.6 %collective-permute-start.12 = (bf16[48,8,128]{2,1,0:T(8,128)(2,1)}, bf16[48,8,128]{2,1,0:T(8,128)(2,1)S(1)}, u32[]{:S(2)}, u32[]{:S(2)}) collective-permute-start(bf16[48,8,128]{2,1,0:T(8,128)(2,1)} %pack_first.1), channel_id=1, source_target_pairs={{0,13},{1,12},{2,15},{3,14},{4,9},{5,8},{6,11},{7,10},{8,5},{9,4},... | collective-permute-start | bytes 294920 | tf_op jit(solution)/shard_map/ppermute | solution.py:574
  6.3 3.2 %pack_rows.1 = (bf16[62,8,128]{2,1,0:T(8,128)(2,1)}, bf16[53,8,128]{2,1,0:T(8,128)(2,1)}, bf16[53,8,128]{2,1,0:T(8,128)(2,1)}, bf16[53,8,128]{2,1,0:T(8,128)(2,1...) custom-call(s32[1]{0:T(128)} %bitcast.me_s.turn_s, ...), custom_call_target="tpu_custom_call" | custom-call | tf_op jit(solution)/shard_map/pack_rows/pallas_call | solution.py:514
  9.6 0.7 %collective-permute-start = (bf16[53,8,128]{2,1,0:T(8,128)(2,1)}, bf16[53,8,128]{2,1,0:T(8,128)(2,1)S(1)}, u32[]{:S(2)}, u32[]{:S(2)}) collective-permute-start(bf16[53,8,128]{2,1,0:T(8,128)(2,1)} %get-tuple-element.31), channel_id=1, source_target_pairs={{0,12},{1,13},{2,14},{3,15},{4,8},{5,9},{6,10},{7,11},{8,4},{9,5},... | collective-permute-start | bytes 325640 | tf_op jit(solution)/shard_map/ppermute | solution.py:574
  10.2 4.2 %collective-permute-start.1 = (bf16[53,8,128]{2,1,0:T(8,128)(2,1)}, bf16[53,8,128]{2,1,0:T(8,128)(2,1)S(1)}, u32[]{:S(2)}, u32[]{:S(2)}) collective-permute-start(bf16[53,8,128]{2,1,0:T(8,128)(2,1)} %get-tuple-element.32), channel_id=1, source_target_pairs={{0,14},{1,15},{2,12},{3,13},{4,10},{5,11},{6,8},{7,9},{8,6},{9,7},... | collective-permute-start | bytes 325640 | tf_op jit(solution)/shard_map/ppermute | solution.py:574
  14.4 1.5 %collective-permute-start.3 = (bf16[53,8,128]{2,1,0:T(8,128)(2,1)}, bf16[53,8,128]{2,1,0:T(8,128)(2,1)S(1)}, u32[]{:S(2)}, u32[]{:S(2)}) collective-permute-start(bf16[53,8,128]{2,1,0:T(8,128)(2,1)} %get-tuple-element.34), channel_id=1, source_target_pairs={{0,5},{1,4},{2,7},{3,6},{4,1},{5,0},{6,3},{7,2},{8,13},{9,12},{10,... | collective-permute-start | bytes 325640 | tf_op jit(solution)/shard_map/ppermute | solution.py:574
  15.9 1.7 %collective-permute-done.rest_2_.rest_1_ = bf16[53,8,128]{2,1,0:T(8,128)(2,1)S(1)} collective-permute-done((bf16[53,8,128]{2,1,0:T(8,128)(2,1)}, bf16[53,8,128]{2,1,0:T(8,128)(2,1)S(1)}, u32[]{:S(2)}, u32[]{:S(2)}) %collective-permute-start) | collective-permute-done | bytes 108576 | tf_op jit(solution)/shard_map/ppermute | solution.py:574
  17.6 1.5 %collective-permute-start.5 = (bf16[53,8,128]{2,1,0:T(8,128)(2,1)}, bf16[53,8,128]{2,1,0:T(8,128)(2,1)S(1)}, u32[]{:S(2)}, u32[]{:S(2)}) collective-permute-start(bf16[53,8,128]{2,1,0:T(8,128)(2,1)} %get-tuple-element.36), channel_id=1, source_target_pairs={{0,6},{1,7},{2,4},{3,5},{4,2},{5,3},{6,0},{7,1},{8,14},{9,15},{10,... | collective-permute-start | bytes 325640 | tf_op jit(solution)/shard_map/ppermute | solution.py:574
  19.2 1.8 %collective-permute-done.1.rest_3_.rest_2_ = bf16[53,8,128]{2,1,0:T(8,128)(2,1)S(1)} collective-permute-done((bf16[53,8,128]{2,1,0:T(8,128)(2,1)}, bf16[53,8,128]{2,1,0:T(8,128)(2,1)S(1)}, u32[]{:S(2)}, u32[]{:S(2)}) %collective-permute-start.1) | collective-permute-done | bytes 108576 | tf_op jit(solution)/shard_map/ppermute | solution.py:574
  20.9 2.6 %collective-permute-start.6 = (bf16[53,8,128]{2,1,0:T(8,128)(2,1)}, bf16[53,8,128]{2,1,0:T(8,128)(2,1)S(1)}, u32[]{:S(2)}, u32[]{:S(2)}) collective-permute-start(bf16[53,8,128]{2,1,0:T(8,128)(2,1)} %get-tuple-element.37), channel_id=1, source_target_pairs={{0,10},{1,11},{2,8},{3,9},{4,14},{5,15},{6,12},{7,13},{8,2},{9,3},... | collective-permute-start | bytes 325640 | tf_op jit(solution)/shard_map/ppermute | solution.py:574
  23.6 0.8 %collective-permute-done.2.rest_3_ = bf16[53,8,128]{2,1,0:T(8,128)(2,1)S(1)} collective-permute-done((bf16[53,8,128]{2,1,0:T(8,128)(2,1)}, bf16[53,8,128]{2,1,0:T(8,128)(2,1)S(1)}, u32[]{:S(2)}, u32[]{:S(2)}) %collective-permute-start.2) | collective-permute-done | bytes 108576 | tf_op jit(solution)/shard_map/ppermute | solution.py:574
  24.4 2.4 %collective-permute-done.3.rest_4_ = bf16[53,8,128]{2,1,0:T(8,128)(2,1)S(1)} collective-permute-done((bf16[53,8,128]{2,1,0:T(8,128)(2,1)}, bf16[53,8,128]{2,1,0:T(8,128)(2,1)S(1)}, u32[]{:S(2)}, u32[]{:S(2)}) %collective-permute-start.3) | collective-permute-done | bytes 108576 | tf_op jit(solution)/shard_map/ppermute | solution.py:574
  27.4 1.5 %collective-permute-start.9 = (bf16[53,8,128]{2,1,0:T(8,128)(2,1)}, bf16[53,8,128]{2,1,0:T(8,128)(2,1)S(1)}, u32[]{:S(2)}, u32[]{:S(2)}) collective-permute-start(bf16[53,8,128]{2,1,0:T(8,128)(2,1)} %get-tuple-element.40), channel_id=1, source_target_pairs={{0,1},{1,0},{2,3},{3,2},{4,5},{5,4},{6,7},{7,6},{8,9},{9,8},{10,11... | collective-permute-start | bytes 325640 | tf_op jit(solution)/shard_map/ppermute | solution.py:574
  28.9 3.5 %collective-permute-done.5.rest_6_ = bf16[53,8,128]{2,1,0:T(8,128)(2,1)S(1)} collective-permute-done((bf16[53,8,128]{2,1,0:T(8,128)(2,1)}, bf16[53,8,128]{2,1,0:T(8,128)(2,1)S(1)}, u32[]{:S(2)}, u32[]{:S(2)}) %collective-permute-start.5) | collective-permute-done | bytes 108576 | tf_op jit(solution)/shard_map/ppermute | solution.py:574
  32.8 0.8 %collective-permute-start.11 = (bf16[53,8,128]{2,1,0:T(8,128)(2,1)}, bf16[53,8,128]{2,1,0:T(8,128)(2,1)S(1)}, u32[]{:S(2)}, u32[]{:S(2)}) collective-permute-start(bf16[53,8,128]{2,1,0:T(8,128)(2,1)} %get-tuple-element.42), channel_id=1, source_target_pairs={{0,3},{1,2},{2,1},{3,0},{4,7},{5,6},{6,5},{7,4},{8,11},{9,10},{10,... | collective-permute-start | bytes 325640 | tf_op jit(solution)/shard_map/ppermute | solution.py:574
  33.7 0.9 %collective-permute-done.7.rest_8_ = bf16[53,8,128]{2,1,0:T(8,128)(2,1)S(1)} collective-permute-done((bf16[53,8,128]{2,1,0:T(8,128)(2,1)}, bf16[53,8,128]{2,1,0:T(8,128)(2,1)S(1)}, u32[]{:S(2)}, u32[]{:S(2)}) %collective-permute-start.7) | collective-permute-done | bytes 108576 | tf_op jit(solution)/shard_map/ppermute | solution.py:574
  34.5 2.3 %collective-permute-start.14 = (bf16[48,8,128]{2,1,0:T(8,128)(2,1)}, bf16[48,8,128]{2,1,0:T(8,128)(2,1)S(1)}, u32[]{:S(2)}, u32[]{:S(2)}) collective-permute-start(bf16[48,8,128]{2,1,0:T(8,128)(2,1)} %get-tuple-element.47), channel_id=1, source_target_pairs={{0,9},{1,8},{2,11},{3,10},{4,13},{5,12},{6,15},{7,14},{8,1},{9,0},... | collective-permute-start | bytes 294920 | tf_op jit(solution)/shard_map/ppermute | solution.py:574
  36.8 1.0 %collective-permute-done.8.rest_9_ = bf16[53,8,128]{2,1,0:T(8,128)(2,1)S(1)} collective-permute-done((bf16[53,8,128]{2,1,0:T(8,128)(2,1)}, bf16[53,8,128]{2,1,0:T(8,128)(2,1)S(1)}, u32[]{:S(2)}, u32[]{:S(2)}) %collective-permute-start.8) | collective-permute-done | bytes 108576 | tf_op jit(solution)/shard_map/ppermute | solution.py:574
  37.8 1.3 %collective-permute-start.15 = (bf16[48,8,128]{2,1,0:T(8,128)(2,1)}, bf16[48,8,128]{2,1,0:T(8,128)(2,1)S(1)}, u32[]{:S(2)}, u32[]{:S(2)}) collective-permute-start(bf16[48,8,128]{2,1,0:T(8,128)(2,1)} %get-tuple-element.48), channel_id=1, source_target_pairs={{0,11},{1,10},{2,9},{3,8},{4,15},{5,14},{6,13},{7,12},{8,3},{9,2},... | collective-permute-start | bytes 294920 | tf_op jit(solution)/shard_map/ppermute | solution.py:574
  39.7 0.9 %copy-done = bf16[62,8,128]{2,1,0:T(8,128)(2,1)S(1)} copy-done((bf16[62,8,128]{2,1,0:T(8,128)(2,1)S(1)}, bf16[62,8,128]{2,1,0:T(8,128)(2,1)}, u32[]{:S(2)}) %copy-start) | copy-done | bytes 127000
  41.5 2.0 %gains_and_sums.1 = (f32[128,3072]{1,0:T(8,128)S(1)}, f32[64,128]{1,0:T(8,128)S(1)}, s32[16,128]{1,0:T(8,128)S(1)}, f32[3,64,8,128]{3,2,1,0:T(8,128)S(1)}) custom-call(s32[1]{0:T(128)} %bitcast.me_s.turn_s, bf16[256,256]{1,0:T(8,128)(2,1)S(1)} %get-tuple-element.28.choice_ref, bf16[256,3072]{1,0:T(8,128)(2,1)S(1)} %get-tuple-element.29.basis_ref, ...), custom_call_target="tpu_custom_call" | custom-call | tf_op jit(solution)/shard_map/gains_and_sums/pallas_call | solution.py:599
  43.6 1.1 %collective-permute-done.14.rest_0_ = bf16[48,8,128]{2,1,0:T(8,128)(2,1)S(1)} collective-permute-done((bf16[48,8,128]{2,1,0:T(8,128)(2,1)}, bf16[48,8,128]{2,1,0:T(8,128)(2,1)S(1)}, u32[]{:S(2)}, u32[]{:S(2)}) %collective-permute-start.14) | collective-permute-done | bytes 98336 | tf_op jit(solution)/shard_map/ppermute | solution.py:574
  44.7 2.3 %collective-permute-done.15.rest_1_ = bf16[48,8,128]{2,1,0:T(8,128)(2,1)S(1)} collective-permute-done((bf16[48,8,128]{2,1,0:T(8,128)(2,1)}, bf16[48,8,128]{2,1,0:T(8,128)(2,1)S(1)}, u32[]{:S(2)}, u32[]{:S(2)}) %collective-permute-start.15) | collective-permute-done | bytes 98336 | tf_op jit(solution)/shard_map/ppermute | solution.py:574
  46.9 2.0 %sum_and_apply.1 = bf16[64,8,384]{2,1,0:T(8,128)(2,1)} custom-call(s32[16,128]{1,0:T(8,128)S(1)} %get-tuple-element.43.slots_s, f32[128,3072]{1,0:T(8,128)S(1)} %get-tuple-element.44.gains_ref, f32[64,128]{1,0:T(8,128)S(1)} %get-tuple-element.45.recip_ref, f32[3,64,8,128]{3,2,1,0:T(8,128)S(1)} %get-tuple-element.46.sums_ref, ...), custom_call_target="tpu_custom_call" | custom-call | tf_op jit(solution)/shard_map/sum_and_apply/pallas_call | solution.py:622
  (16 shorter events, 2.6 us)
Async XLA Ops:
  1.8 14.2 %collective-permute-start.12 = (bf16[48,8,128]{2,1,0:T(8,128)(2,1)}, bf16[48,8,128]{2,1,0:T(8,128)(2,1)S(1)}, u32[]{:S(2)}, u32[]{:S(2)}) collective-permute-start(bf16[48,8,128]{2,1,0:T(8,128)(2,1)} %pack_first.1), channel_id=1, source_target_pairs={{0,13},{1,12},{2,15},{3,14},{4,9},{5,8},{6,11},{7,10},{8,5},{9,4},... | collective-permute-start | bytes 294920 | tf_op jit(solution)/shard_map/ppermute | solution.py:574
  9.6 8.1 %collective-permute-start = (bf16[53,8,128]{2,1,0:T(8,128)(2,1)}, bf16[53,8,128]{2,1,0:T(8,128)(2,1)S(1)}, u32[]{:S(2)}, u32[]{:S(2)}) collective-permute-start(bf16[53,8,128]{2,1,0:T(8,128)(2,1)} %get-tuple-element.31), channel_id=1, source_target_pairs={{0,12},{1,13},{2,14},{3,15},{4,8},{5,9},{6,10},{7,11},{8,4},{9,5},... | collective-permute-start | bytes 325640 | tf_op jit(solution)/shard_map/ppermute | solution.py:574
  10.2 10.7 %collective-permute-start.1 = (bf16[53,8,128]{2,1,0:T(8,128)(2,1)}, bf16[53,8,128]{2,1,0:T(8,128)(2,1)S(1)}, u32[]{:S(2)}, u32[]{:S(2)}) collective-permute-start(bf16[53,8,128]{2,1,0:T(8,128)(2,1)} %get-tuple-element.32), channel_id=1, source_target_pairs={{0,14},{1,15},{2,12},{3,13},{4,10},{5,11},{6,8},{7,9},{8,6},{9,7},... | collective-permute-start | bytes 325640 | tf_op jit(solution)/shard_map/ppermute | solution.py:574
  14.4 9.9 %collective-permute-start.2 = (bf16[53,8,128]{2,1,0:T(8,128)(2,1)}, bf16[53,8,128]{2,1,0:T(8,128)(2,1)S(1)}, u32[]{:S(2)}, u32[]{:S(2)}) collective-permute-start(bf16[53,8,128]{2,1,0:T(8,128)(2,1)} %get-tuple-element.33), channel_id=1, source_target_pairs={{0,4},{1,5},{2,6},{3,7},{4,0},{5,1},{6,2},{7,3},{8,12},{9,13},{10,... | collective-permute-start | bytes 325640 | tf_op jit(solution)/shard_map/ppermute | solution.py:574
  14.4 12.4 %collective-permute-start.3 = (bf16[53,8,128]{2,1,0:T(8,128)(2,1)}, bf16[53,8,128]{2,1,0:T(8,128)(2,1)S(1)}, u32[]{:S(2)}, u32[]{:S(2)}) collective-permute-start(bf16[53,8,128]{2,1,0:T(8,128)(2,1)} %get-tuple-element.34), channel_id=1, source_target_pairs={{0,5},{1,4},{2,7},{3,6},{4,1},{5,0},{6,3},{7,2},{8,13},{9,12},{10,... | collective-permute-start | bytes 325640 | tf_op jit(solution)/shard_map/ppermute | solution.py:574
  15.9 11.4 %collective-permute-start.4 = (bf16[53,8,128]{2,1,0:T(8,128)(2,1)}, bf16[53,8,128]{2,1,0:T(8,128)(2,1)S(1)}, u32[]{:S(2)}, u32[]{:S(2)}) collective-permute-start(bf16[53,8,128]{2,1,0:T(8,128)(2,1)} %get-tuple-element.35), channel_id=1, source_target_pairs={{0,8},{1,9},{2,10},{3,11},{4,12},{5,13},{6,14},{7,15},{8,0},{9,1},... | collective-permute-start | bytes 325640 | tf_op jit(solution)/shard_map/ppermute | solution.py:574
  17.6 14.7 %collective-permute-start.5 = (bf16[53,8,128]{2,1,0:T(8,128)(2,1)}, bf16[53,8,128]{2,1,0:T(8,128)(2,1)S(1)}, u32[]{:S(2)}, u32[]{:S(2)}) collective-permute-start(bf16[53,8,128]{2,1,0:T(8,128)(2,1)} %get-tuple-element.36), channel_id=1, source_target_pairs={{0,6},{1,7},{2,4},{3,5},{4,2},{5,3},{6,0},{7,1},{8,14},{9,15},{10,... | collective-permute-start | bytes 325640 | tf_op jit(solution)/shard_map/ppermute | solution.py:574
  20.9 11.9 %collective-permute-start.6 = (bf16[53,8,128]{2,1,0:T(8,128)(2,1)}, bf16[53,8,128]{2,1,0:T(8,128)(2,1)S(1)}, u32[]{:S(2)}, u32[]{:S(2)}) collective-permute-start(bf16[53,8,128]{2,1,0:T(8,128)(2,1)} %get-tuple-element.37), channel_id=1, source_target_pairs={{0,10},{1,11},{2,8},{3,9},{4,14},{5,15},{6,12},{7,13},{8,2},{9,3},... | collective-permute-start | bytes 325640 | tf_op jit(solution)/shard_map/ppermute | solution.py:574
  24.4 10.1 %collective-permute-start.7 = (bf16[53,8,128]{2,1,0:T(8,128)(2,1)}, bf16[53,8,128]{2,1,0:T(8,128)(2,1)S(1)}, u32[]{:S(2)}, u32[]{:S(2)}) collective-permute-start(bf16[53,8,128]{2,1,0:T(8,128)(2,1)} %get-tuple-element.38), channel_id=1, source_target_pairs={{0,7},{1,6},{2,5},{3,4},{4,3},{5,2},{6,1},{7,0},{8,15},{9,14},{10,... | collective-permute-start | bytes 325640 | tf_op jit(solution)/shard_map/ppermute | solution.py:574
  26.8 10.9 %collective-permute-start.8 = (bf16[53,8,128]{2,1,0:T(8,128)(2,1)}, bf16[53,8,128]{2,1,0:T(8,128)(2,1)S(1)}, u32[]{:S(2)}, u32[]{:S(2)}) collective-permute-start(bf16[53,8,128]{2,1,0:T(8,128)(2,1)} %get-tuple-element.39), channel_id=1, source_target_pairs={{0,15},{1,14},{2,13},{3,12},{4,11},{5,10},{6,9},{7,8},{8,7},{9,6},... | collective-permute-start | bytes 325640 | tf_op jit(solution)/shard_map/ppermute | solution.py:574
  27.4 11.7 %collective-permute-start.9 = (bf16[53,8,128]{2,1,0:T(8,128)(2,1)}, bf16[53,8,128]{2,1,0:T(8,128)(2,1)S(1)}, u32[]{:S(2)}, u32[]{:S(2)}) collective-permute-start(bf16[53,8,128]{2,1,0:T(8,128)(2,1)} %get-tuple-element.40), channel_id=1, source_target_pairs={{0,1},{1,0},{2,3},{3,2},{4,5},{5,4},{6,7},{7,6},{8,9},{9,8},{10,11... | collective-permute-start | bytes 325640 | tf_op jit(solution)/shard_map/ppermute | solution.py:574
  32.4 8.7 %collective-permute-start.10 = (bf16[53,8,128]{2,1,0:T(8,128)(2,1)}, bf16[53,8,128]{2,1,0:T(8,128)(2,1)S(1)}, u32[]{:S(2)}, u32[]{:S(2)}) collective-permute-start(bf16[53,8,128]{2,1,0:T(8,128)(2,1)} %get-tuple-element.41), channel_id=1, source_target_pairs={{0,2},{1,3},{2,0},{3,1},{4,6},{5,7},{6,4},{7,5},{8,10},{9,11},{10,... | collective-permute-start | bytes 325640 | tf_op jit(solution)/shard_map/ppermute | solution.py:574
  32.8 8.7 %collective-permute-start.11 = (bf16[53,8,128]{2,1,0:T(8,128)(2,1)}, bf16[53,8,128]{2,1,0:T(8,128)(2,1)S(1)}, u32[]{:S(2)}, u32[]{:S(2)}) collective-permute-start(bf16[53,8,128]{2,1,0:T(8,128)(2,1)} %get-tuple-element.42), channel_id=1, source_target_pairs={{0,3},{1,2},{2,1},{3,0},{4,7},{5,6},{6,5},{7,4},{8,11},{9,10},{10,... | collective-permute-start | bytes 325640 | tf_op jit(solution)/shard_map/ppermute | solution.py:574
  34.5 10.1 %collective-permute-start.14 = (bf16[48,8,128]{2,1,0:T(8,128)(2,1)}, bf16[48,8,128]{2,1,0:T(8,128)(2,1)S(1)}, u32[]{:S(2)}, u32[]{:S(2)}) collective-permute-start(bf16[48,8,128]{2,1,0:T(8,128)(2,1)} %get-tuple-element.47), channel_id=1, source_target_pairs={{0,9},{1,8},{2,11},{3,10},{4,13},{5,12},{6,15},{7,14},{8,1},{9,0},... | collective-permute-start | bytes 294920 | tf_op jit(solution)/shard_map/ppermute | solution.py:574
  37.8 9.2 %collective-permute-start.15 = (bf16[48,8,128]{2,1,0:T(8,128)(2,1)}, bf16[48,8,128]{2,1,0:T(8,128)(2,1)S(1)}, u32[]{:S(2)}, u32[]{:S(2)}) collective-permute-start(bf16[48,8,128]{2,1,0:T(8,128)(2,1)} %get-tuple-element.48), channel_id=1, source_target_pairs={{0,11},{1,10},{2,9},{3,8},{4,15},{5,14},{6,13},{7,12},{8,3},{9,2},... | collective-permute-start | bytes 294920 | tf_op jit(solution)/shard_map/ppermute | solution.py:574
  39.1 2.4 %collective-permute-start.13 = (bf16[20,8,128]{2,1,0:T(8,128)(2,1)S(1)}, bf16[20,8,128]{2,1,0:T(8,128)(2,1)S(1)}, u32[]{:S(2)}, u32[]{:S(2)}) collective-permute-start(bf16[20,8,128]{2,1,0:T(8,128)(2,1)S(1)} %collect_gains.1), channel_id=1, source_target_pairs={{0,1},{1,0},{2,3},{3,2},{4,5},{5,4},{6,7},{7,6},{8,9},{9,8},{10,11... | collective-permute-start | bytes 122888 | tf_op jit(solution)/shard_map/ppermute | solution.py:574
  39.7 0.9 %copy-start = (bf16[62,8,128]{2,1,0:T(8,128)(2,1)S(1)}, bf16[62,8,128]{2,1,0:T(8,128)(2,1)}, u32[]{:S(2)}) copy-start(bf16[62,8,128]{2,1,0:T(8,128)(2,1)} %get-tuple-element.27.own_ref) | copy-start | bytes 380932

commit v11 on v9

--- a/solution.py
+++ b/solution.py
@@ -22,13 +22,12 @@
 def schedule(near):
     even, odd = list(range(near, 2 * near, 2)), list(range(near + 1, 2 * near, 2))
     close = list(range(near // 2, near)) + list(range(1, near // 2))
-    cross, late = even[2:] + odd[1:-2], odd[-2:]
-    order = [0] + even[:2] + close[:2]
-    close = close[2:]
+    order = [0] + even[:1] + close[:2]
+    cross, close = even[1:], close[2:]
     while cross:
         order += cross[:1] + close[:1]
         cross, close = cross[1:], close[1:]
-    return order + close + odd[:1], late
+    return order + close + odd[:-2], odd[-2:]
 
 
 def with_gains(near):
@@ -45,6 +44,7 @@
 def pack_kernel(
     capacity,
     near,
+    targets,
     me_s,
     owner_hbm,
     owner_row_hbm,
@@ -146,12 +146,14 @@
 
     at = chunks * capacity
     if near > 1:
-        outs = list(outs[: near + 1]) + [None] + list(outs[near + 1 :])
-        pairs = [(meta_ref, outs[x].at[pl.ds(at, depth)]) for x in with_gains(near)]
+        outs = dict(zip(targets, outs))
+        pairs = [(meta_ref, outs[x].at[pl.ds(at, depth)]) for x in targets if x in with_gains(near)]
     else:
         pairs = [(meta_ref, outs[1])]
-    at_small = at + depth if near > 1 else 0
-    pairs += [(parts_ref, outs[0 if near > 1 else -1].at[pl.ds(at_small, 3 * chunks)])]
+    if near == 1:
+        pairs += [(parts_ref, outs[2])]
+    elif 0 in targets:
+        pairs += [(parts_ref, outs[0].at[pl.ds(at + depth, 3 * chunks)])]
     start = len(moves) + PARTS
     sends = start_all(pairs, sems.at[pl.ds(start, len(pairs))])
     start += len(pairs)
@@ -167,9 +169,7 @@
         fetches[i].wait()
         lax.fori_loop(i * span, (i + 1) * span, place, 0, unroll=8)
     if near > 1:
-        pairs = [
-            (block_ref.at[x], outs[x].at[pl.ds(0, at)]) for x in range(devices) if x != near + 1
-        ]
+        pairs = [(block_ref.at[x], outs[x].at[pl.ds(0, at)]) for x in targets]
     else:
         pairs = [(block_ref, outs[0])]
     sends += start_all(pairs, sems.at[pl.ds(start, len(pairs))])
@@ -471,7 +471,7 @@
     block = (chunks * capacity, parts, LANES)
     rows_at = chunks * capacity
     if halves:
-        long = with_gains(near) + [near + 3]
+        long = with_gains(near)
         outs = [
             shape((rows_at + (depth if x in long else 0), parts, LANES), bf16)
             for x in range(devices)
@@ -488,59 +488,70 @@
     offset = band_offset.reshape(chunks, LANES)
     me_owner = row_owner.reshape(rows)
     if halves:
-        first = outs.pop(near + 1)
+        target = near + 1
         alone = pl.pallas_call(
-            functools.partial(first_kernel, capacity, near + 1),
-            out_shape=first,
+            functools.partial(first_kernel, capacity, target),
+            out_shape=outs[target],
             in_specs=[smem, hbm, hbm],
             out_specs=hbm,
             scratch_shapes=[
                 pltpu.SMEM((rows,), i32),
                 pltpu.SMEM((rows + 8,), i32),
                 pltpu.VMEM((rows, parts, channels), bf16),
-                pltpu.VMEM(first.shape, bf16),
+                pltpu.VMEM(outs[target].shape, bf16),
                 dma((2,)),
             ],
             compiler_params=most,
             name="pack_first",
         )(me, me_owner, visibilities)
-    sent = pl.pallas_call(
-        functools.partial(pack_kernel, capacity, near),
-        out_shape=outs,
-        in_specs=[smem] + [hbm] * 8,
-        out_specs=[hbm] * len(outs),
-        scratch_shapes=[
-            pltpu.VMEM(weights.shape, f32),
-            pltpu.VMEM(offset.shape, i32),
-            pltpu.VMEM(pairs.shape, i32),
-            pltpu.VMEM((SUB, channels), f32),
-            pltpu.VMEM((3 * chunks, SUB, LANES), bf16),
-            pltpu.SMEM((rows,), i32),
-            pltpu.SMEM((rows,), i32),
-            pltpu.SMEM((devices,), i32),
-            pltpu.VMEM((1, rows), i32),
-            pltpu.VMEM((1, rows), i32),
-            pltpu.VMEM((rows, parts, channels), bf16),
-            pltpu.VMEM((knots * parts, stations), f32),
-            pltpu.VMEM((LANES, LANES), f32),
-            pltpu.VMEM((depth, SUB, LANES), bf16),
-            pltpu.VMEM((devices,) + block, bf16),
-            dma((9 + PARTS + 2 * devices,)),
-        ],
-        compiler_params=most,
-        name="pack_rows",
-    )(
-        turn,
-        owner,
-        row_owner.reshape(1, rows),
-        row_slot.reshape(1, rows),
-        visibilities,
-        coarse,
-        weights,
-        offset,
-        pairs,
-    )
-
+    def pack(targets, outs):
+        return pl.pallas_call(
+            functools.partial(pack_kernel, capacity, near, targets),
+            out_shape=outs,
+            in_specs=[smem] + [hbm] * 8,
+            out_specs=[hbm] * len(outs),
+            scratch_shapes=[
+                pltpu.VMEM(weights.shape, f32),
+                pltpu.VMEM(offset.shape, i32),
+                pltpu.VMEM(pairs.shape, i32),
+                pltpu.VMEM((SUB, channels), f32),
+                pltpu.VMEM((3 * chunks, SUB, LANES), bf16),
+                pltpu.SMEM((rows,), i32),
+                pltpu.SMEM((rows,), i32),
+                pltpu.SMEM((devices,), i32),
+                pltpu.VMEM((1, rows), i32),
+                pltpu.VMEM((1, rows), i32),
+                pltpu.VMEM((rows, parts, channels), bf16),
+                pltpu.VMEM((knots * parts, stations), f32),
+                pltpu.VMEM((LANES, LANES), f32),
+                pltpu.VMEM((depth, SUB, LANES), bf16),
+                pltpu.VMEM((devices,) + block, bf16),
+                dma((9 + PARTS + 2 * devices,)),
+            ],
+            compiler_params=most,
+            name="pack_rows",
+        )(
+            turn,
+            owner,
+            row_owner.reshape(1, rows),
+            row_slot.reshape(1, rows),
+            visibilities,
+            coarse,
+            weights,
+            offset,
+            pairs,
+        )
+
+
+    if halves:
+        order, _ = schedule(near)
+        soon = order[1:4] + [near + 3]
+        later = [x for x in range(devices) if x not in soon + [target]]
+        sent = {target: alone}
+        for some_of in (soon, later):
+            sent.update(zip(some_of, pack(some_of, [outs[x] for x in some_of])))
+    else:
+        sent = pack([0, 1, 2], outs)
 
     trows = gain_tiles * SUB
 
@@ -558,10 +569,6 @@
             compiler_params=some,
             name="make_ready",
         )(turn, own)
-
-    if halves:
-        sent = list(sent)
-        sent.insert(near + 1, alone)
 
     def swap(array, x):
         return lax.ppermute(array, "bl", [(d, d ^ x) for d in range(devices)])

time: 47 us -> 49.3 us (1.049)
  Pallas kernels: 9.58 us -> 12.1 us
  starting transfers between devices: 24.3 us -> 23.2 us
  waiting for transfers between devices: 11.9 us -> 12.9 us
    pallas_call x2 -> x3, Pallas kernels: 4.99 us -> 7.71 us  [the longest x2 5.92 us: pack(): pl.pallas_call(functools.partial(pack_kernel, capacity, near, targets), o...]
    ppermute x16, starting transfers between devices: 24.3 us -> 23.2 us  [swap(): return lax.ppermute(array, 'bl', [(d, d ^ x) for d in range(devices)])]
    ppermute x16, waiting for transfers between devices: 11.9 us -> 12.9 us  [swap(): return lax.ppermute(array, 'bl', [(d, d ^ x) for d in range(devices)])]
  transfers between devices with their start and end apart: 16 -> 16, of which waited for: 6 -> 5; matrix products, arithmetic and copies ran while one was open for 0% -> 0% of each run, Pallas kernels for 12% -> 17%
where the time goes in v11:
time: 49.3 us; the launch traced here: 49.2 us
  starting transfers between devices  23.2 us (47%)
  waiting for transfers between devices  12.9 us (26%)
  Pallas kernels  12.1 us (25%)
  local copies, waits for them, and re-layouts  0.9 us (2%)
    ppermute x16, starting transfers between devices, swap(): return lax.ppermute(array, 'bl', [(d, d ^ x) for d in range(devices)])  23.2 us
    ppermute x16, waiting for transfers between devices, swap(): return lax.ppermute(array, 'bl', [(d, d ^ x) for d in range(devices)])  12.9 us
    pallas_call x2, Pallas kernels, pack(): pl.pallas_call(functools.partial(pack_kernel, capacity, near, targets), o...  5.92 us
    pallas_call x1, Pallas kernels, on_device(): pl.pallas_call(functools.partial(finish_kernel, capacity, late), out_shap...  2 us
    pallas_call x1, Pallas kernels, on_device(): pl.pallas_call(functools.partial(first_kernel, capacity, target), out_sha...  1.79 us
    pallas_call x1, Pallas kernels, on_device(): pl.pallas_call(functools.partial(middle_kernel, capacity, near, depth, or...  1.76 us
  transfers between devices with their start and end apart: 16, of which 5 were waited for; matrix products, arithmetic and copies ran while one was open for 0% of the time, Pallas kernels for 17%

profile of v11, /device:TPU:0, one launch (start us, length us, event | category | flops | bytes accessed | tf_op | source)
XLA Modules:
  0.0 49.2 jit_solution(1769822125290511970)
XLA Ops:
  0.0 1.8 %pack_first.1 = bf16[48,8,128]{2,1,0:T(8,128)(2,1)} custom-call(s32[1]{0:T(128)} %bitcast.me_s.turn_s, s32[128]{0:T(128)} %bitcast.14, bf16[128,8,384]{2,1,0:T(8,128)(2,1)} %vis_hbm.5), custom_call_target="tpu_custom_call" | custom-call | tf_op jit(solution)/shard_map/pack_first/pallas_call | solution.py:492
  1.8 3.5 %collective-permute-start.11 = (bf16[48,8,128]{2,1,0:T(8,128)(2,1)}, bf16[48,8,128]{2,1,0:T(8,128)(2,1)S(1)}, u32[]{:S(2)}, u32[]{:S(2)}) collective-permute-start(bf16[48,8,128]{2,1,0:T(8,128)(2,1)} %pack_first.1), channel_id=1, source_target_pairs={{0,9},{1,8},{2,11},{3,10},{4,13},{5,12},{6,15},{7,14},{8,1},{9,0},... | collective-permute-start | bytes 294920 | tf_op jit(solution)/shard_map/ppermute | solution.py:574
  5.3 2.9 %pack_rows.3 = (bf16[53,8,128]{2,1,0:T(8,128)(2,1)}, bf16[53,8,128]{2,1,0:T(8,128)(2,1)}, bf16[53,8,128]{2,1,0:T(8,128)(2,1)}, bf16[48,8,128]{2,1,0:T(8,128)(2,1)}) custom-call(s32[1]{0:T(128)} %bitcast.me_s.turn_s, s32[128]{0:T(128)} %bitcast.15, s32[1,128]{1,0:T(1,128)} %bitcast.16, s32[1,128]{1,0:T(1,128)} %bitcast.23, bf16[128,8,384]{2,1,0:T(8,128)(2,1)} %vis_hbm.5, ...), custom_call_target="tpu_custom_call" | custom-call | tf_op jit(solution)/shard_map/pack_rows/pallas_call | solution.py:508
  8.2 0.6 %collective-permute-start = (bf16[53,8,128]{2,1,0:T(8,128)(2,1)}, bf16[53,8,128]{2,1,0:T(8,128)(2,1)S(1)}, u32[]{:S(2)}, u32[]{:S(2)}) collective-permute-start(bf16[53,8,128]{2,1,0:T(8,128)(2,1)} %get-tuple-element.31), channel_id=1, source_target_pairs={{0,8},{1,9},{2,10},{3,11},{4,12},{5,13},{6,14},{7,15},{8,0},{9,1},... | collective-permute-start | bytes 325640 | tf_op jit(solution)/shard_map/ppermute | solution.py:574
  8.9 3.3 %collective-permute-start.12 = (bf16[48,8,128]{2,1,0:T(8,128)(2,1)}, bf16[48,8,128]{2,1,0:T(8,128)(2,1)S(1)}, u32[]{:S(2)}, u32[]{:S(2)}) collective-permute-start(bf16[48,8,128]{2,1,0:T(8,128)(2,1)} %get-tuple-element.42), channel_id=1, source_target_pairs={{0,11},{1,10},{2,9},{3,8},{4,15},{5,14},{6,13},{7,12},{8,3},{9,2},... | collective-permute-start | bytes 294920 | tf_op jit(solution)/shard_map/ppermute | solution.py:574
  12.2 1.5 %collective-permute-start.1 = (bf16[53,8,128]{2,1,0:T(8,128)(2,1)}, bf16[53,8,128]{2,1,0:T(8,128)(2,1)S(1)}, u32[]{:S(2)}, u32[]{:S(2)}) collective-permute-start(bf16[53,8,128]{2,1,0:T(8,128)(2,1)} %get-tuple-element.32), channel_id=1, source_target_pairs={{0,4},{1,5},{2,6},{3,7},{4,0},{5,1},{6,2},{7,3},{8,12},{9,13},{10,... | collective-permute-start | bytes 325640 | tf_op jit(solution)/shard_map/ppermute | solution.py:574
  13.7 3.1 %pack_rows.2 = (bf16[62,8,128]{2,1,0:T(8,128)(2,1)}, bf16[53,8,128]{2,1,0:T(8,128)(2,1)}, bf16[53,8,128]{2,1,0:T(8,128)(2,1)}, bf16[53,8,128]{2,1,0:T(8,128)(2,1...) custom-call(s32[1]{0:T(128)} %bitcast.me_s.turn_s, ...), custom_call_target="tpu_custom_call" | custom-call | tf_op jit(solution)/shard_map/pack_rows/pallas_call | solution.py:508
  16.8 0.5 collective-permute-start.3
  17.3 5.0 %collective-permute-done.12.rest_13_ = bf16[48,8,128]{2,1,0:T(8,128)(2,1)S(1)} collective-permute-done((bf16[48,8,128]{2,1,0:T(8,128)(2,1)}, bf16[48,8,128]{2,1,0:T(8,128)(2,1)S(1)}, u32[]{:S(2)}, u32[]{:S(2)}) %collective-permute-start.12) | collective-permute-done | bytes 98336 | tf_op jit(solution)/shard_map/ppermute | solution.py:574
  22.3 2.3 %collective-permute-start.4 = (bf16[53,8,128]{2,1,0:T(8,128)(2,1)}, bf16[53,8,128]{2,1,0:T(8,128)(2,1)S(1)}, u32[]{:S(2)}, u32[]{:S(2)}) collective-permute-start(bf16[53,8,128]{2,1,0:T(8,128)(2,1)} %get-tuple-element.35), channel_id=1, source_target_pairs={{0,6},{1,7},{2,4},{3,5},{4,2},{5,3},{6,0},{7,1},{8,14},{9,15},{10,... | collective-permute-start | bytes 325640 | tf_op jit(solution)/shard_map/ppermute | solution.py:574
  24.6 2.7 %collective-permute-start.5 = (bf16[53,8,128]{2,1,0:T(8,128)(2,1)}, bf16[53,8,128]{2,1,0:T(8,128)(2,1)S(1)}, u32[]{:S(2)}, u32[]{:S(2)}) collective-permute-start(bf16[53,8,128]{2,1,0:T(8,128)(2,1)} %get-tuple-element.36), channel_id=1, source_target_pairs={{0,12},{1,13},{2,14},{3,15},{4,8},{5,9},{6,10},{7,11},{8,4},{9,5},... | collective-permute-start | bytes 325640 | tf_op jit(solution)/shard_map/ppermute | solution.py:574
  27.3 1.2 %collective-permute-start.6 = (bf16[53,8,128]{2,1,0:T(8,128)(2,1)}, bf16[53,8,128]{2,1,0:T(8,128)(2,1)S(1)}, u32[]{:S(2)}, u32[]{:S(2)}) collective-permute-start(bf16[53,8,128]{2,1,0:T(8,128)(2,1)} %get-tuple-element.37), channel_id=1, source_target_pairs={{0,7},{1,6},{2,5},{3,4},{4,3},{5,2},{6,1},{7,0},{8,15},{9,14},{10,... | collective-permute-start | bytes 325640 | tf_op jit(solution)/shard_map/ppermute | solution.py:574
  28.5 1.0 %collective-permute-start.8 = (bf16[53,8,128]{2,1,0:T(8,128)(2,1)}, bf16[53,8,128]{2,1,0:T(8,128)(2,1)S(1)}, u32[]{:S(2)}, u32[]{:S(2)}) collective-permute-start(bf16[53,8,128]{2,1,0:T(8,128)(2,1)} %get-tuple-element.39), channel_id=1, source_target_pairs={{0,1},{1,0},{2,3},{3,2},{4,5},{5,4},{6,7},{7,6},{8,9},{9,8},{10,11... | collective-permute-start | bytes 325640 | tf_op jit(solution)/shard_map/ppermute | solution.py:574
  29.5 2.3 %collective-permute-done.4.rest_5_ = bf16[53,8,128]{2,1,0:T(8,128)(2,1)S(1)} collective-permute-done((bf16[53,8,128]{2,1,0:T(8,128)(2,1)}, bf16[53,8,128]{2,1,0:T(8,128)(2,1)S(1)}, u32[]{:S(2)}, u32[]{:S(2)}) %collective-permute-start.4) | collective-permute-done | bytes 108576 | tf_op jit(solution)/shard_map/ppermute | solution.py:574
  31.9 1.8 %collective-permute-done.5.rest_2_.rest_6_ = bf16[53,8,128]{2,1,0:T(8,128)(2,1)S(1)} collective-permute-done((bf16[53,8,128]{2,1,0:T(8,128)(2,1)}, bf16[53,8,128]{2,1,0:T(8,128)(2,1)S(1)}, u32[]{:S(2)}, u32[]{:S(2)}) %collective-permute-start.5) | collective-permute-done | bytes 108576 | tf_op jit(solution)/shard_map/ppermute | solution.py:574
  33.6 0.5 collective-permute-done.6.rest_7_
  34.1 5.7 %collective-permute-start.14 = (bf16[48,8,128]{2,1,0:T(8,128)(2,1)}, bf16[48,8,128]{2,1,0:T(8,128)(2,1)S(1)}, u32[]{:S(2)}, u32[]{:S(2)}) collective-permute-start(bf16[48,8,128]{2,1,0:T(8,128)(2,1)} %get-tuple-element.47), channel_id=1, source_target_pairs={{0,13},{1,12},{2,15},{3,14},{4,9},{5,8},{6,11},{7,10},{8,5},{9,4},... | collective-permute-start | bytes 294920 | tf_op jit(solution)/shard_map/ppermute | solution.py:574
  39.8 0.2 collective-permute-start.15
  40.1 0.6 %collective-permute-start.13 = (bf16[20,8,128]{2,1,0:T(8,128)(2,1)S(1)}, bf16[20,8,128]{2,1,0:T(8,128)(2,1)S(1)}, u32[]{:S(2)}, u32[]{:S(2)}) collective-permute-start(bf16[20,8,128]{2,1,0:T(8,128)(2,1)S(1)} %collect_gains.1), channel_id=1, source_target_pairs={{0,1},{1,0},{2,3},{3,2},{4,5},{5,4},{6,7},{7,6},{8,9},{9,8},{10,11... | collective-permute-start | bytes 122888 | tf_op jit(solution)/shard_map/ppermute | solution.py:574
  40.6 0.9 %copy-done = bf16[62,8,128]{2,1,0:T(8,128)(2,1)S(1)} copy-done((bf16[62,8,128]{2,1,0:T(8,128)(2,1)S(1)}, bf16[62,8,128]{2,1,0:T(8,128)(2,1)}, u32[]{:S(2)}) %copy-start) | copy-done | bytes 127000
  41.5 0.5 %make_ready.1 = (bf16[62,8,128]{2,1,0:T(8,128)(2,1)S(1)}, bf16[256,256]{1,0:T(8,128)(2,1)S(1)}, bf16[256,3072]{1,0:T(8,128)(2,1)S(1)}) custom-call(s32[1]{0:T(128)} %bitcast.me_s.turn_s, bf16[62,8,128]{2,1,0:T(8,128)(2,1)S(1)} %copy-done), custom_call_target="tpu_custom_call" | custom-call | tf_op jit(solution)/shard_map/make_ready/pallas_call | solution.py:559
  42.1 1.8 %gains_and_sums.1 = (f32[128,3072]{1,0:T(8,128)S(1)}, f32[64,128]{1,0:T(8,128)S(1)}, s32[16,128]{1,0:T(8,128)S(1)}, f32[3,64,8,128]{3,2,1,0:T(8,128)S(1)}) custom-call(s32[1]{0:T(128)} %bitcast.me_s.turn_s, bf16[256,256]{1,0:T(8,128)(2,1)S(1)} %get-tuple-element.28.choice_ref, bf16[256,3072]{1,0:T(8,128)(2,1)S(1)} %get-tuple-element.29.basis_ref, ...), custom_call_target="tpu_custom_call" | custom-call | tf_op jit(solution)/shard_map/gains_and_sums/pallas_call | solution.py:599
  43.9 3.3 %collective-permute-done.15.rest_1_ = bf16[48,8,128]{2,1,0:T(8,128)(2,1)S(1)} collective-permute-done((bf16[48,8,128]{2,1,0:T(8,128)(2,1)}, bf16[48,8,128]{2,1,0:T(8,128)(2,1)S(1)}, u32[]{:S(2)}, u32[]{:S(2)}) %collective-permute-start.15) | collective-permute-done | bytes 98336 | tf_op jit(solution)/shard_map/ppermute | solution.py:574
  47.2 2.0 %sum_and_apply.1 = bf16[64,8,384]{2,1,0:T(8,128)(2,1)} custom-call(s32[16,128]{1,0:T(8,128)S(1)} %get-tuple-element.43.slots_s, f32[128,3072]{1,0:T(8,128)S(1)} %get-tuple-element.44.gains_ref, f32[64,128]{1,0:T(8,128)S(1)} %get-tuple-element.45.recip_ref, f32[3,64,8,128]{3,2,1,0:T(8,128)S(1)} %get-tuple-element.46.sums_ref, ...), custom_call_target="tpu_custom_call" | custom-call | tf_op jit(solution)/shard_map/sum_and_apply/pallas_call | solution.py:622
  (17 shorter events, 0.1 us)
Async XLA Ops:
  1.8 15.0 %collective-permute-start.11 = (bf16[48,8,128]{2,1,0:T(8,128)(2,1)}, bf16[48,8,128]{2,1,0:T(8,128)(2,1)S(1)}, u32[]{:S(2)}, u32[]{:S(2)}) collective-permute-start(bf16[48,8,128]{2,1,0:T(8,128)(2,1)} %pack_first.1), channel_id=1, source_target_pairs={{0,9},{1,8},{2,11},{3,10},{4,13},{5,12},{6,15},{7,14},{8,1},{9,0},... | collective-permute-start | bytes 294920 | tf_op jit(solution)/shard_map/ppermute | solution.py:574
  8.2 16.4 %collective-permute-start = (bf16[53,8,128]{2,1,0:T(8,128)(2,1)}, bf16[53,8,128]{2,1,0:T(8,128)(2,1)S(1)}, u32[]{:S(2)}, u32[]{:S(2)}) collective-permute-start(bf16[53,8,128]{2,1,0:T(8,128)(2,1)} %get-tuple-element.31), channel_id=1, source_target_pairs={{0,8},{1,9},{2,10},{3,11},{4,12},{5,13},{6,14},{7,15},{8,0},{9,1},... | collective-permute-start | bytes 325640 | tf_op jit(solution)/shard_map/ppermute | solution.py:574
  8.9 13.4 %collective-permute-start.12 = (bf16[48,8,128]{2,1,0:T(8,128)(2,1)}, bf16[48,8,128]{2,1,0:T(8,128)(2,1)S(1)}, u32[]{:S(2)}, u32[]{:S(2)}) collective-permute-start(bf16[48,8,128]{2,1,0:T(8,128)(2,1)} %get-tuple-element.42), channel_id=1, source_target_pairs={{0,11},{1,10},{2,9},{3,8},{4,15},{5,14},{6,13},{7,12},{8,3},{9,2},... | collective-permute-start | bytes 294920 | tf_op jit(solution)/shard_map/ppermute | solution.py:574
  12.2 15.1 %collective-permute-start.1 = (bf16[53,8,128]{2,1,0:T(8,128)(2,1)}, bf16[53,8,128]{2,1,0:T(8,128)(2,1)S(1)}, u32[]{:S(2)}, u32[]{:S(2)}) collective-permute-start(bf16[53,8,128]{2,1,0:T(8,128)(2,1)} %get-tuple-element.32), channel_id=1, source_target_pairs={{0,4},{1,5},{2,6},{3,7},{4,0},{5,1},{6,2},{7,3},{8,12},{9,13},{10,... | collective-permute-start | bytes 325640 | tf_op jit(solution)/shard_map/ppermute | solution.py:574
  13.7 14.8 %collective-permute-start.2 = (bf16[53,8,128]{2,1,0:T(8,128)(2,1)}, bf16[53,8,128]{2,1,0:T(8,128)(2,1)S(1)}, u32[]{:S(2)}, u32[]{:S(2)}) collective-permute-start(bf16[53,8,128]{2,1,0:T(8,128)(2,1)} %get-tuple-element.33), channel_id=1, source_target_pairs={{0,5},{1,4},{2,7},{3,6},{4,1},{5,0},{6,3},{7,2},{8,13},{9,12},{10,... | collective-permute-start | bytes 325640 | tf_op jit(solution)/shard_map/ppermute | solution.py:574
  16.8 11.7 %collective-permute-start.3 = (bf16[53,8,128]{2,1,0:T(8,128)(2,1)}, bf16[53,8,128]{2,1,0:T(8,128)(2,1)S(1)}, u32[]{:S(2)}, u32[]{:S(2)}) collective-permute-start(bf16[53,8,128]{2,1,0:T(8,128)(2,1)} %get-tuple-element.34), channel_id=1, source_target_pairs={{0,10},{1,11},{2,8},{3,9},{4,14},{5,15},{6,12},{7,13},{8,2},{9,3},... | collective-permute-start | bytes 325640 | tf_op jit(solution)/shard_map/ppermute | solution.py:574
  22.3 9.6 %collective-permute-start.4 = (bf16[53,8,128]{2,1,0:T(8,128)(2,1)}, bf16[53,8,128]{2,1,0:T(8,128)(2,1)S(1)}, u32[]{:S(2)}, u32[]{:S(2)}) collective-permute-start(bf16[53,8,128]{2,1,0:T(8,128)(2,1)} %get-tuple-element.35), channel_id=1, source_target_pairs={{0,6},{1,7},{2,4},{3,5},{4,2},{5,3},{6,0},{7,1},{8,14},{9,15},{10,... | collective-permute-start | bytes 325640 | tf_op jit(solution)/shard_map/ppermute | solution.py:574
  24.6 9.1 %collective-permute-start.5 = (bf16[53,8,128]{2,1,0:T(8,128)(2,1)}, bf16[53,8,128]{2,1,0:T(8,128)(2,1)S(1)}, u32[]{:S(2)}, u32[]{:S(2)}) collective-permute-start(bf16[53,8,128]{2,1,0:T(8,128)(2,1)} %get-tuple-element.36), channel_id=1, source_target_pairs={{0,12},{1,13},{2,14},{3,15},{4,8},{5,9},{6,10},{7,11},{8,4},{9,5},... | collective-permute-start | bytes 325640 | tf_op jit(solution)/shard_map/ppermute | solution.py:574
  27.3 6.8 %collective-permute-start.6 = (bf16[53,8,128]{2,1,0:T(8,128)(2,1)}, bf16[53,8,128]{2,1,0:T(8,128)(2,1)S(1)}, u32[]{:S(2)}, u32[]{:S(2)}) collective-permute-start(bf16[53,8,128]{2,1,0:T(8,128)(2,1)} %get-tuple-element.37), channel_id=1, source_target_pairs={{0,7},{1,6},{2,5},{3,4},{4,3},{5,2},{6,1},{7,0},{8,15},{9,14},{10,... | collective-permute-start | bytes 325640 | tf_op jit(solution)/shard_map/ppermute | solution.py:574
  28.5 11.3 %collective-permute-start.7 = (bf16[53,8,128]{2,1,0:T(8,128)(2,1)}, bf16[53,8,128]{2,1,0:T(8,128)(2,1)S(1)}, u32[]{:S(2)}, u32[]{:S(2)}) collective-permute-start(bf16[53,8,128]{2,1,0:T(8,128)(2,1)} %get-tuple-element.38), channel_id=1, source_target_pairs={{0,14},{1,15},{2,12},{3,13},{4,10},{5,11},{6,8},{7,9},{8,6},{9,7},... | collective-permute-start | bytes 325640 | tf_op jit(solution)/shard_map/ppermute | solution.py:574
  28.5 11.5 %collective-permute-start.8 = (bf16[53,8,128]{2,1,0:T(8,128)(2,1)}, bf16[53,8,128]{2,1,0:T(8,128)(2,1)S(1)}, u32[]{:S(2)}, u32[]{:S(2)}) collective-permute-start(bf16[53,8,128]{2,1,0:T(8,128)(2,1)} %get-tuple-element.39), channel_id=1, source_target_pairs={{0,1},{1,0},{2,3},{3,2},{4,5},{5,4},{6,7},{7,6},{8,9},{9,8},{10,11... | collective-permute-start | bytes 325640 | tf_op jit(solution)/shard_map/ppermute | solution.py:574
  31.9 10.2 %collective-permute-start.9 = (bf16[53,8,128]{2,1,0:T(8,128)(2,1)}, bf16[53,8,128]{2,1,0:T(8,128)(2,1)S(1)}, u32[]{:S(2)}, u32[]{:S(2)}) collective-permute-start(bf16[53,8,128]{2,1,0:T(8,128)(2,1)} %get-tuple-element.40), channel_id=1, source_target_pairs={{0,2},{1,3},{2,0},{3,1},{4,6},{5,7},{6,4},{7,5},{8,10},{9,11},{10,... | collective-permute-start | bytes 325640 | tf_op jit(solution)/shard_map/ppermute | solution.py:574
  33.6 8.4 %collective-permute-start.10 = (bf16[53,8,128]{2,1,0:T(8,128)(2,1)}, bf16[53,8,128]{2,1,0:T(8,128)(2,1)S(1)}, u32[]{:S(2)}, u32[]{:S(2)}) collective-permute-start(bf16[53,8,128]{2,1,0:T(8,128)(2,1)} %get-tuple-element.41), channel_id=1, source_target_pairs={{0,3},{1,2},{2,1},{3,0},{4,7},{5,6},{6,5},{7,4},{8,11},{9,10},{10,... | collective-permute-start | bytes 325640 | tf_op jit(solution)/shard_map/ppermute | solution.py:574
  34.1 9.8 %collective-permute-start.14 = (bf16[48,8,128]{2,1,0:T(8,128)(2,1)}, bf16[48,8,128]{2,1,0:T(8,128)(2,1)S(1)}, u32[]{:S(2)}, u32[]{:S(2)}) collective-permute-start(bf16[48,8,128]{2,1,0:T(8,128)(2,1)} %get-tuple-element.47), channel_id=1, source_target_pairs={{0,13},{1,12},{2,15},{3,14},{4,9},{5,8},{6,11},{7,10},{8,5},{9,4},... | collective-permute-start | bytes 294920 | tf_op jit(solution)/shard_map/ppermute | solution.py:574
  39.8 7.4 %collective-permute-start.15 = (bf16[48,8,128]{2,1,0:T(8,128)(2,1)}, bf16[48,8,128]{2,1,0:T(8,128)(2,1)S(1)}, u32[]{:S(2)}, u32[]{:S(2)}) collective-permute-start(bf16[48,8,128]{2,1,0:T(8,128)(2,1)} %get-tuple-element.48), channel_id=1, source_target_pairs={{0,15},{1,14},{2,13},{3,12},{4,11},{5,10},{6,9},{7,8},{8,7},{9,6},... | collective-permute-start | bytes 294920 | tf_op jit(solution)/shard_map/ppermute | solution.py:574
  40.1 2.0 %collective-permute-start.13 = (bf16[20,8,128]{2,1,0:T(8,128)(2,1)S(1)}, bf16[20,8,128]{2,1,0:T(8,128)(2,1)S(1)}, u32[]{:S(2)}, u32[]{:S(2)}) collective-permute-start(bf16[20,8,128]{2,1,0:T(8,128)(2,1)S(1)} %collect_gains.1), channel_id=1, source_target_pairs={{0,1},{1,0},{2,3},{3,2},{4,5},{5,4},{6,7},{7,6},{8,9},{9,8},{10,11... | collective-permute-start | bytes 122888 | tf_op jit(solution)/shard_map/ppermute | solution.py:574
  40.6 0.9 %copy-start = (bf16[62,8,128]{2,1,0:T(8,128)(2,1)S(1)}, bf16[62,8,128]{2,1,0:T(8,128)(2,1)}, u32[]{:S(2)}) copy-start(bf16[62,8,128]{2,1,0:T(8,128)(2,1)} %get-tuple-element.27.own_ref) | copy-start | bytes 380932

commit v12 on v9

--- a/solution.py
+++ b/solution.py
@@ -22,13 +22,12 @@
 def schedule(near):
     even, odd = list(range(near, 2 * near, 2)), list(range(near + 1, 2 * near, 2))
     close = list(range(near // 2, near)) + list(range(1, near // 2))
-    cross, late = even[2:] + odd[1:-2], odd[-2:]
     order = [0] + even[:2] + close[:2]
-    close = close[2:]
+    cross, close = even[2:], close[2:]
     while cross:
         order += cross[:1] + close[:1]
         cross, close = cross[1:], close[1:]
-    return order + close + odd[:1], late
+    return order + close[:1] + odd[1:-2] + close[1:] + odd[:1], odd[-2:]
 
 
 def with_gains(near):

time: 47 us -> 46.9 us (level)
  waiting for transfers between devices: 11.9 us -> 12.5 us
    ppermute x16, waiting for transfers between devices: 11.9 us -> 12.5 us  [swap(): return lax.ppermute(array, 'bl', [(d, d ^ x) for d in range(devices)])]
where the time goes in v12:
time: 46.9 us; the launch traced here: 46.7 us
  starting transfers between devices  23.9 us (51%)
  waiting for transfers between devices  12.5 us (27%)
  Pallas kernels  9.27 us (20%)
  local copies, waits for them, and re-layouts  0.9 us (2%)
    ppermute x16, starting transfers between devices, swap(): return lax.ppermute(array, 'bl', [(d, d ^ x) for d in range(devices)])  23.9 us
    ppermute x16, waiting for transfers between devices, swap(): return lax.ppermute(array, 'bl', [(d, d ^ x) for d in range(devices)])  12.5 us
    pallas_call x1, Pallas kernels, on_device(): pl.pallas_call(functools.partial(pack_kernel, capacity, near), out_shape=...  3.2 us
    pallas_call x1, Pallas kernels, on_device(): pl.pallas_call(functools.partial(finish_kernel, capacity, late), out_shap...  1.94 us
    pallas_call x1, Pallas kernels, on_device(): pl.pallas_call(functools.partial(first_kernel, capacity, near + 1), out_s...  1.79 us
    pallas_call x1, Pallas kernels, on_device(): pl.pallas_call(functools.partial(middle_kernel, capacity, near, depth, or...  1.75 us
  transfers between devices with their start and end apart: 16, of which 6 were waited for; matrix products, arithmetic and copies ran while one was open for 0% of the time, Pallas kernels for 12%

profile of v12, /device:TPU:0, one launch (start us, length us, event | category | flops | bytes accessed | tf_op | source)
XLA Modules:
  0.0 46.7 jit_solution(17464409173536327216)
XLA Ops:
  0.0 1.8 %pack_first.1 = bf16[48,8,128]{2,1,0:T(8,128)(2,1)} custom-call(s32[1]{0:T(128)} %bitcast.me_s.turn_s, s32[128]{0:T(128)} %bitcast.12, bf16[128,8,384]{2,1,0:T(8,128)(2,1)} %vis_hbm.3), custom_call_target="tpu_custom_call" | custom-call | tf_op jit(solution)/shard_map/pack_first/pallas_call | solution.py:491
  1.8 3.5 %collective-permute-start.12 = (bf16[48,8,128]{2,1,0:T(8,128)(2,1)}, bf16[48,8,128]{2,1,0:T(8,128)(2,1)S(1)}, u32[]{:S(2)}, u32[]{:S(2)}) collective-permute-start(bf16[48,8,128]{2,1,0:T(8,128)(2,1)} %pack_first.1), channel_id=1, source_target_pairs={{0,9},{1,8},{2,11},{3,10},{4,13},{5,12},{6,15},{7,14},{8,1},{9,0},... | collective-permute-start | bytes 294920 | tf_op jit(solution)/shard_map/ppermute | solution.py:566
  5.3 3.2 %pack_rows.1 = (bf16[62,8,128]{2,1,0:T(8,128)(2,1)}, bf16[53,8,128]{2,1,0:T(8,128)(2,1)}, bf16[53,8,128]{2,1,0:T(8,128)(2,1)}, bf16[53,8,128]{2,1,0:T(8,128)(2,1...) custom-call(s32[1]{0:T(128)} %bitcast.me_s.turn_s, ...), custom_call_target="tpu_custom_call" | custom-call | tf_op jit(solution)/shard_map/pack_rows/pallas_call | solution.py:506
  8.5 0.7 %collective-permute-start = (bf16[53,8,128]{2,1,0:T(8,128)(2,1)}, bf16[53,8,128]{2,1,0:T(8,128)(2,1)S(1)}, u32[]{:S(2)}, u32[]{:S(2)}) collective-permute-start(bf16[53,8,128]{2,1,0:T(8,128)(2,1)} %get-tuple-element.31), channel_id=1, source_target_pairs={{0,8},{1,9},{2,10},{3,11},{4,12},{5,13},{6,14},{7,15},{8,0},{9,1},... | collective-permute-start | bytes 325640 | tf_op jit(solution)/shard_map/ppermute | solution.py:566
  9.2 3.3 %collective-permute-start.1 = (bf16[53,8,128]{2,1,0:T(8,128)(2,1)}, bf16[53,8,128]{2,1,0:T(8,128)(2,1)S(1)}, u32[]{:S(2)}, u32[]{:S(2)}) collective-permute-start(bf16[53,8,128]{2,1,0:T(8,128)(2,1)} %get-tuple-element.32), channel_id=1, source_target_pairs={{0,10},{1,11},{2,8},{3,9},{4,14},{5,15},{6,12},{7,13},{8,2},{9,3},... | collective-permute-start | bytes 325640 | tf_op jit(solution)/shard_map/ppermute | solution.py:566
  12.5 1.6 %collective-permute-start.2 = (bf16[53,8,128]{2,1,0:T(8,128)(2,1)}, bf16[53,8,128]{2,1,0:T(8,128)(2,1)S(1)}, u32[]{:S(2)}, u32[]{:S(2)}) collective-permute-start(bf16[53,8,128]{2,1,0:T(8,128)(2,1)} %get-tuple-element.33), channel_id=1, source_target_pairs={{0,4},{1,5},{2,6},{3,7},{4,0},{5,1},{6,2},{7,3},{8,12},{9,13},{10,... | collective-permute-start | bytes 325640 | tf_op jit(solution)/shard_map/ppermute | solution.py:566
  14.1 3.4 %collective-permute-start.4 = (bf16[53,8,128]{2,1,0:T(8,128)(2,1)}, bf16[53,8,128]{2,1,0:T(8,128)(2,1)S(1)}, u32[]{:S(2)}, u32[]{:S(2)}) collective-permute-start(bf16[53,8,128]{2,1,0:T(8,128)(2,1)} %get-tuple-element.35), channel_id=1, source_target_pairs={{0,12},{1,13},{2,14},{3,15},{4,8},{5,9},{6,10},{7,11},{8,4},{9,5},... | collective-permute-start | bytes 325640 | tf_op jit(solution)/shard_map/ppermute | solution.py:566
  17.5 2.9 %collective-permute-done.rest_0_.rest_1_ = bf16[53,8,128]{2,1,0:T(8,128)(2,1)S(1)} collective-permute-done((bf16[53,8,128]{2,1,0:T(8,128)(2,1)}, bf16[53,8,128]{2,1,0:T(8,128)(2,1)S(1)}, u32[]{:S(2)}, u32[]{:S(2)}) %collective-permute-start) | collective-permute-done | bytes 108576 | tf_op jit(solution)/shard_map/ppermute | solution.py:566
  20.4 3.2 %collective-permute-done.1.rest_1_.rest_2_ = bf16[53,8,128]{2,1,0:T(8,128)(2,1)S(1)} collective-permute-done((bf16[53,8,128]{2,1,0:T(8,128)(2,1)}, bf16[53,8,128]{2,1,0:T(8,128)(2,1)S(1)}, u32[]{:S(2)}, u32[]{:S(2)}) %collective-permute-start.1) | collective-permute-done | bytes 108576 | tf_op jit(solution)/shard_map/ppermute | solution.py:566
  23.6 2.2 %collective-permute-start.6 = (bf16[53,8,128]{2,1,0:T(8,128)(2,1)}, bf16[53,8,128]{2,1,0:T(8,128)(2,1)S(1)}, u32[]{:S(2)}, u32[]{:S(2)}) collective-permute-start(bf16[53,8,128]{2,1,0:T(8,128)(2,1)} %get-tuple-element.37), channel_id=1, source_target_pairs={{0,14},{1,15},{2,12},{3,13},{4,10},{5,11},{6,8},{7,9},{8,6},{9,7},... | collective-permute-start | bytes 325640 | tf_op jit(solution)/shard_map/ppermute | solution.py:566
  25.8 0.4 collective-permute-start.8
  26.2 2.7 %collective-permute-start.9 = (bf16[53,8,128]{2,1,0:T(8,128)(2,1)}, bf16[53,8,128]{2,1,0:T(8,128)(2,1)S(1)}, u32[]{:S(2)}, u32[]{:S(2)}) collective-permute-start(bf16[53,8,128]{2,1,0:T(8,128)(2,1)} %get-tuple-element.40), channel_id=1, source_target_pairs={{0,11},{1,10},{2,9},{3,8},{4,15},{5,14},{6,13},{7,12},{8,3},{9,2},... | collective-permute-start | bytes 325640 | tf_op jit(solution)/shard_map/ppermute | solution.py:566
  28.9 2.3 %collective-permute-start.10 = (bf16[53,8,128]{2,1,0:T(8,128)(2,1)}, bf16[53,8,128]{2,1,0:T(8,128)(2,1)S(1)}, u32[]{:S(2)}, u32[]{:S(2)}) collective-permute-start(bf16[53,8,128]{2,1,0:T(8,128)(2,1)} %get-tuple-element.41), channel_id=1, source_target_pairs={{0,2},{1,3},{2,0},{3,1},{4,6},{5,7},{6,4},{7,5},{8,10},{9,11},{10,... | collective-permute-start | bytes 325640 | tf_op jit(solution)/shard_map/ppermute | solution.py:566
  31.2 1.2 %collective-permute-done.6.rest_3_.rest_7_ = bf16[53,8,128]{2,1,0:T(8,128)(2,1)S(1)} collective-permute-done((bf16[53,8,128]{2,1,0:T(8,128)(2,1)}, bf16[53,8,128]{2,1,0:T(8,128)(2,1)S(1)}, u32[]{:S(2)}, u32[]{:S(2)}) %collective-permute-start.6) | collective-permute-done | bytes 108576 | tf_op jit(solution)/shard_map/ppermute | solution.py:566
  32.5 2.5 %collective-permute-done.7.rest_8_ = bf16[53,8,128]{2,1,0:T(8,128)(2,1)S(1)} collective-permute-done((bf16[53,8,128]{2,1,0:T(8,128)(2,1)}, bf16[53,8,128]{2,1,0:T(8,128)(2,1)S(1)}, u32[]{:S(2)}, u32[]{:S(2)}) %collective-permute-start.7) | collective-permute-done | bytes 108576 | tf_op jit(solution)/shard_map/ppermute | solution.py:566
  35.0 2.0 %collective-permute-start.14 = (bf16[48,8,128]{2,1,0:T(8,128)(2,1)}, bf16[48,8,128]{2,1,0:T(8,128)(2,1)S(1)}, u32[]{:S(2)}, u32[]{:S(2)}) collective-permute-start(bf16[48,8,128]{2,1,0:T(8,128)(2,1)} %get-tuple-element.47), channel_id=1, source_target_pairs={{0,13},{1,12},{2,15},{3,14},{4,9},{5,8},{6,11},{7,10},{8,5},{9,4},... | collective-permute-start | bytes 294920 | tf_op jit(solution)/shard_map/ppermute | solution.py:566
  37.0 1.7 %collective-permute-start.15 = (bf16[48,8,128]{2,1,0:T(8,128)(2,1)}, bf16[48,8,128]{2,1,0:T(8,128)(2,1)S(1)}, u32[]{:S(2)}, u32[]{:S(2)}) collective-permute-start(bf16[48,8,128]{2,1,0:T(8,128)(2,1)} %get-tuple-element.48), channel_id=1, source_target_pairs={{0,15},{1,14},{2,13},{3,12},{4,11},{5,10},{6,9},{7,8},{8,7},{9,6},... | collective-permute-start | bytes 294920 | tf_op jit(solution)/shard_map/ppermute | solution.py:566
  38.7 0.1 collective-permute-start.13
  38.9 0.9 %copy-done = bf16[62,8,128]{2,1,0:T(8,128)(2,1)S(1)} copy-done((bf16[62,8,128]{2,1,0:T(8,128)(2,1)S(1)}, bf16[62,8,128]{2,1,0:T(8,128)(2,1)}, u32[]{:S(2)}) %copy-start) | copy-done | bytes 127000
  39.8 0.5 %make_ready.1 = (bf16[62,8,128]{2,1,0:T(8,128)(2,1)S(1)}, bf16[256,256]{1,0:T(8,128)(2,1)S(1)}, bf16[256,3072]{1,0:T(8,128)(2,1)S(1)}) custom-call(s32[1]{0:T(128)} %bitcast.me_s.turn_s, bf16[62,8,128]{2,1,0:T(8,128)(2,1)S(1)} %copy-done), custom_call_target="tpu_custom_call" | custom-call | tf_op jit(solution)/shard_map/make_ready/pallas_call | solution.py:547
  40.3 0.3 collective-permute-done.11.rest_12_
  40.7 1.8 %gains_and_sums.1 = (f32[128,3072]{1,0:T(8,128)S(1)}, f32[64,128]{1,0:T(8,128)S(1)}, s32[16,128]{1,0:T(8,128)S(1)}, f32[3,64,8,128]{3,2,1,0:T(8,128)S(1)}) custom-call(s32[1]{0:T(128)} %bitcast.me_s.turn_s, bf16[256,256]{1,0:T(8,128)(2,1)S(1)} %get-tuple-element.28.choice_ref, bf16[256,3072]{1,0:T(8,128)(2,1)S(1)} %get-tuple-element.29.basis_ref, ...), custom_call_target="tpu_custom_call" | custom-call | tf_op jit(solution)/shard_map/gains_and_sums/pallas_call | solution.py:591
  42.4 2.3 %collective-permute-done.15.rest_1_ = bf16[48,8,128]{2,1,0:T(8,128)(2,1)S(1)} collective-permute-done((bf16[48,8,128]{2,1,0:T(8,128)(2,1)}, bf16[48,8,128]{2,1,0:T(8,128)(2,1)S(1)}, u32[]{:S(2)}, u32[]{:S(2)}) %collective-permute-start.15) | collective-permute-done | bytes 98336 | tf_op jit(solution)/shard_map/ppermute | solution.py:566
  44.8 1.9 %sum_and_apply.1 = bf16[64,8,384]{2,1,0:T(8,128)(2,1)} custom-call(s32[16,128]{1,0:T(8,128)S(1)} %get-tuple-element.43.slots_s, f32[128,3072]{1,0:T(8,128)S(1)} %get-tuple-element.44.gains_ref, f32[64,128]{1,0:T(8,128)S(1)} %get-tuple-element.45.recip_ref, f32[3,64,8,128]{3,2,1,0:T(8,128)S(1)} %get-tuple-element.46.sums_ref, ...), custom_call_target="tpu_custom_call" | custom-call | tf_op jit(solution)/shard_map/sum_and_apply/pallas_call | solution.py:614
  (16 shorter events, 0.1 us)
Async XLA Ops:
  1.8 12.3 %collective-permute-start.12 = (bf16[48,8,128]{2,1,0:T(8,128)(2,1)}, bf16[48,8,128]{2,1,0:T(8,128)(2,1)S(1)}, u32[]{:S(2)}, u32[]{:S(2)}) collective-permute-start(bf16[48,8,128]{2,1,0:T(8,128)(2,1)} %pack_first.1), channel_id=1, source_target_pairs={{0,9},{1,8},{2,11},{3,10},{4,13},{5,12},{6,15},{7,14},{8,1},{9,0},... | collective-permute-start | bytes 294920 | tf_op jit(solution)/shard_map/ppermute | solution.py:566
  8.5 11.8 %collective-permute-start = (bf16[53,8,128]{2,1,0:T(8,128)(2,1)}, bf16[53,8,128]{2,1,0:T(8,128)(2,1)S(1)}, u32[]{:S(2)}, u32[]{:S(2)}) collective-permute-start(bf16[53,8,128]{2,1,0:T(8,128)(2,1)} %get-tuple-element.31), channel_id=1, source_target_pairs={{0,8},{1,9},{2,10},{3,11},{4,12},{5,13},{6,14},{7,15},{8,0},{9,1},... | collective-permute-start | bytes 325640 | tf_op jit(solution)/shard_map/ppermute | solution.py:566
  9.2 14.4 %collective-permute-start.1 = (bf16[53,8,128]{2,1,0:T(8,128)(2,1)}, bf16[53,8,128]{2,1,0:T(8,128)(2,1)S(1)}, u32[]{:S(2)}, u32[]{:S(2)}) collective-permute-start(bf16[53,8,128]{2,1,0:T(8,128)(2,1)} %get-tuple-element.32), channel_id=1, source_target_pairs={{0,10},{1,11},{2,8},{3,9},{4,14},{5,15},{6,12},{7,13},{8,2},{9,3},... | collective-permute-start | bytes 325640 | tf_op jit(solution)/shard_map/ppermute | solution.py:566
  12.5 13.3 %collective-permute-start.2 = (bf16[53,8,128]{2,1,0:T(8,128)(2,1)}, bf16[53,8,128]{2,1,0:T(8,128)(2,1)S(1)}, u32[]{:S(2)}, u32[]{:S(2)}) collective-permute-start(bf16[53,8,128]{2,1,0:T(8,128)(2,1)} %get-tuple-element.33), channel_id=1, source_target_pairs={{0,4},{1,5},{2,6},{3,7},{4,0},{5,1},{6,2},{7,3},{8,12},{9,13},{10,... | collective-permute-start | bytes 325640 | tf_op jit(solution)/shard_map/ppermute | solution.py:566
  14.1 11.7 %collective-permute-start.3 = (bf16[53,8,128]{2,1,0:T(8,128)(2,1)}, bf16[53,8,128]{2,1,0:T(8,128)(2,1)S(1)}, u32[]{:S(2)}, u32[]{:S(2)}) collective-permute-start(bf16[53,8,128]{2,1,0:T(8,128)(2,1)} %get-tuple-element.34), channel_id=1, source_target_pairs={{0,5},{1,4},{2,7},{3,6},{4,1},{5,0},{6,3},{7,2},{8,13},{9,12},{10,... | collective-permute-start | bytes 325640 | tf_op jit(solution)/shard_map/ppermute | solution.py:566
  14.1 12.1 %collective-permute-start.4 = (bf16[53,8,128]{2,1,0:T(8,128)(2,1)}, bf16[53,8,128]{2,1,0:T(8,128)(2,1)S(1)}, u32[]{:S(2)}, u32[]{:S(2)}) collective-permute-start(bf16[53,8,128]{2,1,0:T(8,128)(2,1)} %get-tuple-element.35), channel_id=1, source_target_pairs={{0,12},{1,13},{2,14},{3,15},{4,8},{5,9},{6,10},{7,11},{8,4},{9,5},... | collective-permute-start | bytes 325640 | tf_op jit(solution)/shard_map/ppermute | solution.py:566
  20.4 8.5 %collective-permute-start.5 = (bf16[53,8,128]{2,1,0:T(8,128)(2,1)}, bf16[53,8,128]{2,1,0:T(8,128)(2,1)S(1)}, u32[]{:S(2)}, u32[]{:S(2)}) collective-permute-start(bf16[53,8,128]{2,1,0:T(8,128)(2,1)} %get-tuple-element.36), channel_id=1, source_target_pairs={{0,6},{1,7},{2,4},{3,5},{4,2},{5,3},{6,0},{7,1},{8,14},{9,15},{10,... | collective-permute-start | bytes 325640 | tf_op jit(solution)/shard_map/ppermute | solution.py:566
  23.6 8.9 %collective-permute-start.6 = (bf16[53,8,128]{2,1,0:T(8,128)(2,1)}, bf16[53,8,128]{2,1,0:T(8,128)(2,1)S(1)}, u32[]{:S(2)}, u32[]{:S(2)}) collective-permute-start(bf16[53,8,128]{2,1,0:T(8,128)(2,1)} %get-tuple-element.37), channel_id=1, source_target_pairs={{0,14},{1,15},{2,12},{3,13},{4,10},{5,11},{6,8},{7,9},{8,6},{9,7},... | collective-permute-start | bytes 325640 | tf_op jit(solution)/shard_map/ppermute | solution.py:566
  25.8 9.2 %collective-permute-start.7 = (bf16[53,8,128]{2,1,0:T(8,128)(2,1)}, bf16[53,8,128]{2,1,0:T(8,128)(2,1)S(1)}, u32[]{:S(2)}, u32[]{:S(2)}) collective-permute-start(bf16[53,8,128]{2,1,0:T(8,128)(2,1)} %get-tuple-element.38), channel_id=1, source_target_pairs={{0,7},{1,6},{2,5},{3,4},{4,3},{5,2},{6,1},{7,0},{8,15},{9,14},{10,... | collective-permute-start | bytes 325640 | tf_op jit(solution)/shard_map/ppermute | solution.py:566
  25.8 11.2 %collective-permute-start.8 = (bf16[53,8,128]{2,1,0:T(8,128)(2,1)}, bf16[53,8,128]{2,1,0:T(8,128)(2,1)S(1)}, u32[]{:S(2)}, u32[]{:S(2)}) collective-permute-start(bf16[53,8,128]{2,1,0:T(8,128)(2,1)} %get-tuple-element.39), channel_id=1, source_target_pairs={{0,1},{1,0},{2,3},{3,2},{4,5},{5,4},{6,7},{7,6},{8,9},{9,8},{10,11... | collective-permute-start | bytes 325640 | tf_op jit(solution)/shard_map/ppermute | solution.py:566
  26.2 12.6 %collective-permute-start.9 = (bf16[53,8,128]{2,1,0:T(8,128)(2,1)}, bf16[53,8,128]{2,1,0:T(8,128)(2,1)S(1)}, u32[]{:S(2)}, u32[]{:S(2)}) collective-permute-start(bf16[53,8,128]{2,1,0:T(8,128)(2,1)} %get-tuple-element.40), channel_id=1, source_target_pairs={{0,11},{1,10},{2,9},{3,8},{4,15},{5,14},{6,13},{7,12},{8,3},{9,2},... | collective-permute-start | bytes 325640 | tf_op jit(solution)/shard_map/ppermute | solution.py:566
  28.9 11.4 %collective-permute-start.10 = (bf16[53,8,128]{2,1,0:T(8,128)(2,1)}, bf16[53,8,128]{2,1,0:T(8,128)(2,1)S(1)}, u32[]{:S(2)}, u32[]{:S(2)}) collective-permute-start(bf16[53,8,128]{2,1,0:T(8,128)(2,1)} %get-tuple-element.41), channel_id=1, source_target_pairs={{0,2},{1,3},{2,0},{3,1},{4,6},{5,7},{6,4},{7,5},{8,10},{9,11},{10,... | collective-permute-start | bytes 325640 | tf_op jit(solution)/shard_map/ppermute | solution.py:566
  32.5 8.2 %collective-permute-start.11 = (bf16[53,8,128]{2,1,0:T(8,128)(2,1)}, bf16[53,8,128]{2,1,0:T(8,128)(2,1)S(1)}, u32[]{:S(2)}, u32[]{:S(2)}) collective-permute-start(bf16[53,8,128]{2,1,0:T(8,128)(2,1)} %get-tuple-element.42), channel_id=1, source_target_pairs={{0,3},{1,2},{2,1},{3,0},{4,7},{5,6},{6,5},{7,4},{8,11},{9,10},{10,... | collective-permute-start | bytes 325640 | tf_op jit(solution)/shard_map/ppermute | solution.py:566
  35.0 7.4 %collective-permute-start.14 = (bf16[48,8,128]{2,1,0:T(8,128)(2,1)}, bf16[48,8,128]{2,1,0:T(8,128)(2,1)S(1)}, u32[]{:S(2)}, u32[]{:S(2)}) collective-permute-start(bf16[48,8,128]{2,1,0:T(8,128)(2,1)} %get-tuple-element.47), channel_id=1, source_target_pairs={{0,13},{1,12},{2,15},{3,14},{4,9},{5,8},{6,11},{7,10},{8,5},{9,4},... | collective-permute-start | bytes 294920 | tf_op jit(solution)/shard_map/ppermute | solution.py:566
  37.0 7.8 %collective-permute-start.15 = (bf16[48,8,128]{2,1,0:T(8,128)(2,1)}, bf16[48,8,128]{2,1,0:T(8,128)(2,1)S(1)}, u32[]{:S(2)}, u32[]{:S(2)}) collective-permute-start(bf16[48,8,128]{2,1,0:T(8,128)(2,1)} %get-tuple-element.48), channel_id=1, source_target_pairs={{0,15},{1,14},{2,13},{3,12},{4,11},{5,10},{6,9},{7,8},{8,7},{9,6},... | collective-permute-start | bytes 294920 | tf_op jit(solution)/shard_map/ppermute | solution.py:566
  38.7 1.9 %collective-permute-start.13 = (bf16[20,8,128]{2,1,0:T(8,128)(2,1)S(1)}, bf16[20,8,128]{2,1,0:T(8,128)(2,1)S(1)}, u32[]{:S(2)}, u32[]{:S(2)}) collective-permute-start(bf16[20,8,128]{2,1,0:T(8,128)(2,1)S(1)} %collect_gains.1), channel_id=1, source_target_pairs={{0,1},{1,0},{2,3},{3,2},{4,5},{5,4},{6,7},{7,6},{8,9},{9,8},{10,11... | collective-permute-start | bytes 122888 | tf_op jit(solution)/shard_map/ppermute | solution.py:566
  38.9 0.9 %copy-start = (bf16[62,8,128]{2,1,0:T(8,128)(2,1)S(1)}, bf16[62,8,128]{2,1,0:T(8,128)(2,1)}, u32[]{:S(2)}) copy-start(bf16[62,8,128]{2,1,0:T(8,128)(2,1)} %get-tuple-element.27.own_ref) | copy-start | bytes 380932

commit v13 on v11

--- a/solution.py
+++ b/solution.py
@@ -22,12 +22,13 @@
 def schedule(near):
     even, odd = list(range(near, 2 * near, 2)), list(range(near + 1, 2 * near, 2))
     close = list(range(near // 2, near)) + list(range(1, near // 2))
-    order = [0] + even[:1] + close[:2]
-    cross, close = even[1:], close[2:]
+    cross, late = even[2:] + odd[1:-2], odd[-2:]
+    order = [0] + even[:2] + close[:2]
+    close = close[2:]
     while cross:
         order += cross[:1] + close[:1]
         cross, close = cross[1:], close[1:]
-    return order + close + odd[:-2], odd[-2:]
+    return order + close + odd[:1], late
 
 
 def with_gains(near):
@@ -471,7 +472,7 @@
     block = (chunks * capacity, parts, LANES)
     rows_at = chunks * capacity
     if halves:
-        long = with_gains(near)
+        long = with_gains(near) + [near + 3]
         outs = [
             shape((rows_at + (depth if x in long else 0), parts, LANES), bf16)
             for x in range(devices)
@@ -545,7 +546,7 @@
 
     if halves:
         order, _ = schedule(near)
-        soon = order[1:4] + [near + 3]
+        soon = order[1:5]
         later = [x for x in range(devices) if x not in soon + [target]]
         sent = {target: alone}
         for some_of in (soon, later):

time: 49.3 us -> 47.1 us (0.955)
  waiting for transfers between devices: 12.9 us -> 10.1 us
    ppermute x16, waiting for transfers between devices: 12.9 us -> 10.1 us  [swap(): return lax.ppermute(array, 'bl', [(d, d ^ x) for d in range(devices)])]
  transfers between devices with their start and end apart: 16 -> 16, of which waited for: 5 -> 5; matrix products, arithmetic and copies ran while one was open for 0% -> 0% of each run, Pallas kernels for 17% -> 18%
where the time goes in v13:
time: 47.1 us; the launch traced here: 46.8 us
  starting transfers between devices  23.6 us (50%)
  Pallas kernels  12 us (25%)
  waiting for transfers between devices  10.1 us (21%)
  local copies, waits for them, and re-layouts  0.9 us (2%)
    ppermute x16, starting transfers between devices, swap(): return lax.ppermute(array, 'bl', [(d, d ^ x) for d in range(devices)])  23.6 us
    ppermute x16, waiting for transfers between devices, swap(): return lax.ppermute(array, 'bl', [(d, d ^ x) for d in range(devices)])  10.1 us
    pallas_call x2, Pallas kernels, pack(): pl.pallas_call(functools.partial(pack_kernel, capacity, near, targets), o...  5.9 us
    pallas_call x1, Pallas kernels, on_device(): pl.pallas_call(functools.partial(finish_kernel, capacity, late), out_shap...  1.95 us
    pallas_call x1, Pallas kernels, on_device(): pl.pallas_call(functools.partial(first_kernel, capacity, target), out_sha...  1.83 us
    pallas_call x1, Pallas kernels, on_device(): pl.pallas_call(functools.partial(middle_kernel, capacity, near, depth, or...  1.78 us
  transfers between devices with their start and end apart: 16, of which 5 were waited for; matrix products, arithmetic and copies ran while one was open for 0% of the time, Pallas kernels for 18%

profile of v13, /device:TPU:0, one launch (start us, length us, event | category | flops | bytes accessed | tf_op | source)
XLA Modules:
  0.0 46.8 jit_solution(1586356321270831704)
XLA Ops:
  0.0 1.8 %pack_first.1 = bf16[48,8,128]{2,1,0:T(8,128)(2,1)} custom-call(s32[1]{0:T(128)} %bitcast.me_s.turn_s, s32[128]{0:T(128)} %bitcast.14, bf16[128,8,384]{2,1,0:T(8,128)(2,1)} %vis_hbm.5), custom_call_target="tpu_custom_call" | custom-call | tf_op jit(solution)/shard_map/pack_first/pallas_call | solution.py:493
  1.8 3.5 %collective-permute-start.12 = (bf16[48,8,128]{2,1,0:T(8,128)(2,1)}, bf16[48,8,128]{2,1,0:T(8,128)(2,1)S(1)}, u32[]{:S(2)}, u32[]{:S(2)}) collective-permute-start(bf16[48,8,128]{2,1,0:T(8,128)(2,1)} %pack_first.1), channel_id=1, source_target_pairs={{0,9},{1,8},{2,11},{3,10},{4,13},{5,12},{6,15},{7,14},{8,1},{9,0},... | collective-permute-start | bytes 294920 | tf_op jit(solution)/shard_map/ppermute | solution.py:575
  5.3 2.8 %pack_rows.3 = (bf16[53,8,128]{2,1,0:T(8,128)(2,1)}, bf16[53,8,128]{2,1,0:T(8,128)(2,1)}, bf16[53,8,128]{2,1,0:T(8,128)(2,1)}, bf16[53,8,128]{2,1,0:T(8,128)(2,1)}) custom-call(s32[1]{0:T(128)} %bitcast.me_s.turn_s, s32[128]{0:T(128)} %bitcast.15, s32[1,128]{1,0:T(1,128)} %bitcast.16, s32[1,128]{1,0:T(1,128)} %bitcast.23, bf16[128,8,384]{2,1,0:T(8,128)(2,1)} %vis_hbm.5, ...), custom_call_target="tpu_custom_call" | custom-call | tf_op jit(solution)/shard_map/pack_rows/pallas_call | solution.py:509
  8.2 0.7 %collective-permute-start = (bf16[53,8,128]{2,1,0:T(8,128)(2,1)}, bf16[53,8,128]{2,1,0:T(8,128)(2,1)S(1)}, u32[]{:S(2)}, u32[]{:S(2)}) collective-permute-start(bf16[53,8,128]{2,1,0:T(8,128)(2,1)} %get-tuple-element.31), channel_id=1, source_target_pairs={{0,8},{1,9},{2,10},{3,11},{4,12},{5,13},{6,14},{7,15},{8,0},{9,1},... | collective-permute-start | bytes 325640 | tf_op jit(solution)/shard_map/ppermute | solution.py:575
  8.8 3.4 %collective-permute-start.1 = (bf16[53,8,128]{2,1,0:T(8,128)(2,1)}, bf16[53,8,128]{2,1,0:T(8,128)(2,1)S(1)}, u32[]{:S(2)}, u32[]{:S(2)}) collective-permute-start(bf16[53,8,128]{2,1,0:T(8,128)(2,1)} %get-tuple-element.32), channel_id=1, source_target_pairs={{0,10},{1,11},{2,8},{3,9},{4,14},{5,15},{6,12},{7,13},{8,2},{9,3},... | collective-permute-start | bytes 325640 | tf_op jit(solution)/shard_map/ppermute | solution.py:575
  12.2 1.5 %collective-permute-start.2 = (bf16[53,8,128]{2,1,0:T(8,128)(2,1)}, bf16[53,8,128]{2,1,0:T(8,128)(2,1)S(1)}, u32[]{:S(2)}, u32[]{:S(2)}) collective-permute-start(bf16[53,8,128]{2,1,0:T(8,128)(2,1)} %get-tuple-element.33), channel_id=1, source_target_pairs={{0,4},{1,5},{2,6},{3,7},{4,0},{5,1},{6,2},{7,3},{8,12},{9,13},{10,... | collective-permute-start | bytes 325640 | tf_op jit(solution)/shard_map/ppermute | solution.py:575
  13.7 3.1 %pack_rows.2 = (bf16[62,8,128]{2,1,0:T(8,128)(2,1)}, bf16[53,8,128]{2,1,0:T(8,128)(2,1)}, bf16[53,8,128]{2,1,0:T(8,128)(2,1)}, bf16[53,8,128]{2,1,0:T(8,128)(2,1...) custom-call(s32[1]{0:T(128)} %bitcast.me_s.turn_s, ...), custom_call_target="tpu_custom_call" | custom-call | tf_op jit(solution)/shard_map/pack_rows/pallas_call | solution.py:509
  16.8 2.7 %collective-permute-start.4 = (bf16[53,8,128]{2,1,0:T(8,128)(2,1)}, bf16[53,8,128]{2,1,0:T(8,128)(2,1)S(1)}, u32[]{:S(2)}, u32[]{:S(2)}) collective-permute-start(bf16[53,8,128]{2,1,0:T(8,128)(2,1)} %get-tuple-element.35), channel_id=1, source_target_pairs={{0,12},{1,13},{2,14},{3,15},{4,8},{5,9},{6,10},{7,11},{8,4},{9,5},... | collective-permute-start | bytes 325640 | tf_op jit(solution)/shard_map/ppermute | solution.py:575
  19.4 0.6 %collective-permute-done.rest_0_.rest_1_ = bf16[53,8,128]{2,1,0:T(8,128)(2,1)S(1)} collective-permute-done((bf16[53,8,128]{2,1,0:T(8,128)(2,1)}, bf16[53,8,128]{2,1,0:T(8,128)(2,1)S(1)}, u32[]{:S(2)}, u32[]{:S(2)}) %collective-permute-start) | collective-permute-done | bytes 108576 | tf_op jit(solution)/shard_map/ppermute | solution.py:575
  20.0 0.4 collective-permute-start.5
  20.4 2.9 %collective-permute-done.1.rest_1_.rest_2_ = bf16[53,8,128]{2,1,0:T(8,128)(2,1)S(1)} collective-permute-done((bf16[53,8,128]{2,1,0:T(8,128)(2,1)}, bf16[53,8,128]{2,1,0:T(8,128)(2,1)S(1)}, u32[]{:S(2)}, u32[]{:S(2)}) %collective-permute-start.1) | collective-permute-done | bytes 108576 | tf_op jit(solution)/shard_map/ppermute | solution.py:575
  23.3 3.9 %collective-permute-start.6 = (bf16[53,8,128]{2,1,0:T(8,128)(2,1)}, bf16[53,8,128]{2,1,0:T(8,128)(2,1)S(1)}, u32[]{:S(2)}, u32[]{:S(2)}) collective-permute-start(bf16[53,8,128]{2,1,0:T(8,128)(2,1)} %get-tuple-element.37), channel_id=1, source_target_pairs={{0,14},{1,15},{2,12},{3,13},{4,10},{5,11},{6,8},{7,9},{8,6},{9,7},... | collective-permute-start | bytes 325640 | tf_op jit(solution)/shard_map/ppermute | solution.py:575
  27.2 1.0 %collective-permute-start.8 = (bf16[53,8,128]{2,1,0:T(8,128)(2,1)}, bf16[53,8,128]{2,1,0:T(8,128)(2,1)S(1)}, u32[]{:S(2)}, u32[]{:S(2)}) collective-permute-start(bf16[53,8,128]{2,1,0:T(8,128)(2,1)} %get-tuple-element.39), channel_id=1, source_target_pairs={{0,11},{1,10},{2,9},{3,8},{4,15},{5,14},{6,13},{7,12},{8,3},{9,2},... | collective-permute-start | bytes 325640 | tf_op jit(solution)/shard_map/ppermute | solution.py:575
  28.2 0.3 collective-permute-start.9
  28.5 2.2 %collective-permute-start.10 = (bf16[53,8,128]{2,1,0:T(8,128)(2,1)}, bf16[53,8,128]{2,1,0:T(8,128)(2,1)S(1)}, u32[]{:S(2)}, u32[]{:S(2)}) collective-permute-start(bf16[53,8,128]{2,1,0:T(8,128)(2,1)} %get-tuple-element.41), channel_id=1, source_target_pairs={{0,2},{1,3},{2,0},{3,1},{4,6},{5,7},{6,4},{7,5},{8,10},{9,11},{10,... | collective-permute-start | bytes 325640 | tf_op jit(solution)/shard_map/ppermute | solution.py:575
  30.8 1.4 %collective-permute-done.6.rest_3_.rest_7_ = bf16[53,8,128]{2,1,0:T(8,128)(2,1)S(1)} collective-permute-done((bf16[53,8,128]{2,1,0:T(8,128)(2,1)}, bf16[53,8,128]{2,1,0:T(8,128)(2,1)S(1)}, u32[]{:S(2)}, u32[]{:S(2)}) %collective-permute-start.6) | collective-permute-done | bytes 108576 | tf_op jit(solution)/shard_map/ppermute | solution.py:575
  32.2 3.1 %collective-permute-done.7.rest_8_ = bf16[53,8,128]{2,1,0:T(8,128)(2,1)S(1)} collective-permute-done((bf16[53,8,128]{2,1,0:T(8,128)(2,1)}, bf16[53,8,128]{2,1,0:T(8,128)(2,1)S(1)}, u32[]{:S(2)}, u32[]{:S(2)}) %collective-permute-start.7) | collective-permute-done | bytes 108576 | tf_op jit(solution)/shard_map/ppermute | solution.py:575
  35.3 1.6 %collective-permute-start.14 = (bf16[48,8,128]{2,1,0:T(8,128)(2,1)}, bf16[48,8,128]{2,1,0:T(8,128)(2,1)S(1)}, u32[]{:S(2)}, u32[]{:S(2)}) collective-permute-start(bf16[48,8,128]{2,1,0:T(8,128)(2,1)} %get-tuple-element.47), channel_id=1, source_target_pairs={{0,13},{1,12},{2,15},{3,14},{4,9},{5,8},{6,11},{7,10},{8,5},{9,4},... | collective-permute-start | bytes 294920 | tf_op jit(solution)/shard_map/ppermute | solution.py:575
  37.0 2.4 %collective-permute-start.15 = (bf16[48,8,128]{2,1,0:T(8,128)(2,1)}, bf16[48,8,128]{2,1,0:T(8,128)(2,1)S(1)}, u32[]{:S(2)}, u32[]{:S(2)}) collective-permute-start(bf16[48,8,128]{2,1,0:T(8,128)(2,1)} %get-tuple-element.48), channel_id=1, source_target_pairs={{0,15},{1,14},{2,13},{3,12},{4,11},{5,10},{6,9},{7,8},{8,7},{9,6},... | collective-permute-start | bytes 294920 | tf_op jit(solution)/shard_map/ppermute | solution.py:575
  39.5 0.9 %copy-done = bf16[62,8,128]{2,1,0:T(8,128)(2,1)S(1)} copy-done((bf16[62,8,128]{2,1,0:T(8,128)(2,1)S(1)}, bf16[62,8,128]{2,1,0:T(8,128)(2,1)}, u32[]{:S(2)}) %copy-start) | copy-done | bytes 127000
  40.4 0.5 %make_ready.1 = (bf16[62,8,128]{2,1,0:T(8,128)(2,1)S(1)}, bf16[256,256]{1,0:T(8,128)(2,1)S(1)}, bf16[256,3072]{1,0:T(8,128)(2,1)S(1)}) custom-call(s32[1]{0:T(128)} %bitcast.me_s.turn_s, bf16[62,8,128]{2,1,0:T(8,128)(2,1)S(1)} %copy-done), custom_call_target="tpu_custom_call" | custom-call | tf_op jit(solution)/shard_map/make_ready/pallas_call | solution.py:560
  41.0 1.8 %gains_and_sums.1 = (f32[128,3072]{1,0:T(8,128)S(1)}, f32[64,128]{1,0:T(8,128)S(1)}, s32[16,128]{1,0:T(8,128)S(1)}, f32[3,64,8,128]{3,2,1,0:T(8,128)S(1)}) custom-call(s32[1]{0:T(128)} %bitcast.me_s.turn_s, bf16[256,256]{1,0:T(8,128)(2,1)S(1)} %get-tuple-element.28.choice_ref, bf16[256,3072]{1,0:T(8,128)(2,1)S(1)} %get-tuple-element.29.basis_ref, ...), custom_call_target="tpu_custom_call" | custom-call | tf_op jit(solution)/shard_map/gains_and_sums/pallas_call | solution.py:600
  42.8 2.1 %collective-permute-done.15.rest_1_ = bf16[48,8,128]{2,1,0:T(8,128)(2,1)S(1)} collective-permute-done((bf16[48,8,128]{2,1,0:T(8,128)(2,1)}, bf16[48,8,128]{2,1,0:T(8,128)(2,1)S(1)}, u32[]{:S(2)}, u32[]{:S(2)}) %collective-permute-start.15) | collective-permute-done | bytes 98336 | tf_op jit(solution)/shard_map/ppermute | solution.py:575
  44.9 1.9 %sum_and_apply.1 = bf16[64,8,384]{2,1,0:T(8,128)(2,1)} custom-call(s32[16,128]{1,0:T(8,128)S(1)} %get-tuple-element.43.slots_s, f32[128,3072]{1,0:T(8,128)S(1)} %get-tuple-element.44.gains_ref, f32[64,128]{1,0:T(8,128)S(1)} %get-tuple-element.45.recip_ref, f32[3,64,8,128]{3,2,1,0:T(8,128)S(1)} %get-tuple-element.46.sums_ref, ...), custom_call_target="tpu_custom_call" | custom-call | tf_op jit(solution)/shard_map/sum_and_apply/pallas_call | solution.py:623
  (17 shorter events, 0.2 us)
Async XLA Ops:
  1.8 14.9 %collective-permute-start.12 = (bf16[48,8,128]{2,1,0:T(8,128)(2,1)}, bf16[48,8,128]{2,1,0:T(8,128)(2,1)S(1)}, u32[]{:S(2)}, u32[]{:S(2)}) collective-permute-start(bf16[48,8,128]{2,1,0:T(8,128)(2,1)} %pack_first.1), channel_id=1, source_target_pairs={{0,9},{1,8},{2,11},{3,10},{4,13},{5,12},{6,15},{7,14},{8,1},{9,0},... | collective-permute-start | bytes 294920 | tf_op jit(solution)/shard_map/ppermute | solution.py:575
  8.2 11.8 %collective-permute-start = (bf16[53,8,128]{2,1,0:T(8,128)(2,1)}, bf16[53,8,128]{2,1,0:T(8,128)(2,1)S(1)}, u32[]{:S(2)}, u32[]{:S(2)}) collective-permute-start(bf16[53,8,128]{2,1,0:T(8,128)(2,1)} %get-tuple-element.31), channel_id=1, source_target_pairs={{0,8},{1,9},{2,10},{3,11},{4,12},{5,13},{6,14},{7,15},{8,0},{9,1},... | collective-permute-start | bytes 325640 | tf_op jit(solution)/shard_map/ppermute | solution.py:575
  8.8 14.4 %collective-permute-start.1 = (bf16[53,8,128]{2,1,0:T(8,128)(2,1)}, bf16[53,8,128]{2,1,0:T(8,128)(2,1)S(1)}, u32[]{:S(2)}, u32[]{:S(2)}) collective-permute-start(bf16[53,8,128]{2,1,0:T(8,128)(2,1)} %get-tuple-element.32), channel_id=1, source_target_pairs={{0,10},{1,11},{2,8},{3,9},{4,14},{5,15},{6,12},{7,13},{8,2},{9,3},... | collective-permute-start | bytes 325640 | tf_op jit(solution)/shard_map/ppermute | solution.py:575
  12.2 15.0 %collective-permute-start.2 = (bf16[53,8,128]{2,1,0:T(8,128)(2,1)}, bf16[53,8,128]{2,1,0:T(8,128)(2,1)S(1)}, u32[]{:S(2)}, u32[]{:S(2)}) collective-permute-start(bf16[53,8,128]{2,1,0:T(8,128)(2,1)} %get-tuple-element.33), channel_id=1, source_target_pairs={{0,4},{1,5},{2,6},{3,7},{4,0},{5,1},{6,2},{7,3},{8,12},{9,13},{10,... | collective-permute-start | bytes 325640 | tf_op jit(solution)/shard_map/ppermute | solution.py:575
  13.7 13.4 %collective-permute-start.3 = (bf16[53,8,128]{2,1,0:T(8,128)(2,1)}, bf16[53,8,128]{2,1,0:T(8,128)(2,1)S(1)}, u32[]{:S(2)}, u32[]{:S(2)}) collective-permute-start(bf16[53,8,128]{2,1,0:T(8,128)(2,1)} %get-tuple-element.34), channel_id=1, source_target_pairs={{0,5},{1,4},{2,7},{3,6},{4,1},{5,0},{6,3},{7,2},{8,13},{9,12},{10,... | collective-permute-start | bytes 325640 | tf_op jit(solution)/shard_map/ppermute | solution.py:575
  16.8 11.4 %collective-permute-start.4 = (bf16[53,8,128]{2,1,0:T(8,128)(2,1)}, bf16[53,8,128]{2,1,0:T(8,128)(2,1)S(1)}, u32[]{:S(2)}, u32[]{:S(2)}) collective-permute-start(bf16[53,8,128]{2,1,0:T(8,128)(2,1)} %get-tuple-element.35), channel_id=1, source_target_pairs={{0,12},{1,13},{2,14},{3,15},{4,8},{5,9},{6,10},{7,11},{8,4},{9,5},... | collective-permute-start | bytes 325640 | tf_op jit(solution)/shard_map/ppermute | solution.py:575
  20.0 8.5 %collective-permute-start.5 = (bf16[53,8,128]{2,1,0:T(8,128)(2,1)}, bf16[53,8,128]{2,1,0:T(8,128)(2,1)S(1)}, u32[]{:S(2)}, u32[]{:S(2)}) collective-permute-start(bf16[53,8,128]{2,1,0:T(8,128)(2,1)} %get-tuple-element.36), channel_id=1, source_target_pairs={{0,6},{1,7},{2,4},{3,5},{4,2},{5,3},{6,0},{7,1},{8,14},{9,15},{10,... | collective-permute-start | bytes 325640 | tf_op jit(solution)/shard_map/ppermute | solution.py:575
  23.3 8.9 %collective-permute-start.6 = (bf16[53,8,128]{2,1,0:T(8,128)(2,1)}, bf16[53,8,128]{2,1,0:T(8,128)(2,1)S(1)}, u32[]{:S(2)}, u32[]{:S(2)}) collective-permute-start(bf16[53,8,128]{2,1,0:T(8,128)(2,1)} %get-tuple-element.37), channel_id=1, source_target_pairs={{0,14},{1,15},{2,12},{3,13},{4,10},{5,11},{6,8},{7,9},{8,6},{9,7},... | collective-permute-start | bytes 325640 | tf_op jit(solution)/shard_map/ppermute | solution.py:575
  27.2 8.2 %collective-permute-start.7 = (bf16[53,8,128]{2,1,0:T(8,128)(2,1)}, bf16[53,8,128]{2,1,0:T(8,128)(2,1)S(1)}, u32[]{:S(2)}, u32[]{:S(2)}) collective-permute-start(bf16[53,8,128]{2,1,0:T(8,128)(2,1)} %get-tuple-element.38), channel_id=1, source_target_pairs={{0,7},{1,6},{2,5},{3,4},{4,3},{5,2},{6,1},{7,0},{8,15},{9,14},{10,... | collective-permute-start | bytes 325640 | tf_op jit(solution)/shard_map/ppermute | solution.py:575
  27.2 9.8 %collective-permute-start.8 = (bf16[53,8,128]{2,1,0:T(8,128)(2,1)}, bf16[53,8,128]{2,1,0:T(8,128)(2,1)S(1)}, u32[]{:S(2)}, u32[]{:S(2)}) collective-permute-start(bf16[53,8,128]{2,1,0:T(8,128)(2,1)} %get-tuple-element.39), channel_id=1, source_target_pairs={{0,11},{1,10},{2,9},{3,8},{4,15},{5,14},{6,13},{7,12},{8,3},{9,2},... | collective-permute-start | bytes 325640 | tf_op jit(solution)/shard_map/ppermute | solution.py:575
  28.2 11.2 %collective-permute-start.9 = (bf16[53,8,128]{2,1,0:T(8,128)(2,1)}, bf16[53,8,128]{2,1,0:T(8,128)(2,1)S(1)}, u32[]{:S(2)}, u32[]{:S(2)}) collective-permute-start(bf16[53,8,128]{2,1,0:T(8,128)(2,1)} %get-tuple-element.40), channel_id=1, source_target_pairs={{0,1},{1,0},{2,3},{3,2},{4,5},{5,4},{6,7},{7,6},{8,9},{9,8},{10,11... | collective-permute-start | bytes 325640 | tf_op jit(solution)/shard_map/ppermute | solution.py:575
  28.5 12.4 %collective-permute-start.10 = (bf16[53,8,128]{2,1,0:T(8,128)(2,1)}, bf16[53,8,128]{2,1,0:T(8,128)(2,1)S(1)}, u32[]{:S(2)}, u32[]{:S(2)}) collective-permute-start(bf16[53,8,128]{2,1,0:T(8,128)(2,1)} %get-tuple-element.41), channel_id=1, source_target_pairs={{0,2},{1,3},{2,0},{3,1},{4,6},{5,7},{6,4},{7,5},{8,10},{9,11},{10,... | collective-permute-start | bytes 325640 | tf_op jit(solution)/shard_map/ppermute | solution.py:575
  32.2 8.8 %collective-permute-start.11 = (bf16[53,8,128]{2,1,0:T(8,128)(2,1)}, bf16[53,8,128]{2,1,0:T(8,128)(2,1)S(1)}, u32[]{:S(2)}, u32[]{:S(2)}) collective-permute-start(bf16[53,8,128]{2,1,0:T(8,128)(2,1)} %get-tuple-element.42), channel_id=1, source_target_pairs={{0,3},{1,2},{2,1},{3,0},{4,7},{5,6},{6,5},{7,4},{8,11},{9,10},{10,... | collective-permute-start | bytes 325640 | tf_op jit(solution)/shard_map/ppermute | solution.py:575
  35.3 7.4 %collective-permute-start.14 = (bf16[48,8,128]{2,1,0:T(8,128)(2,1)}, bf16[48,8,128]{2,1,0:T(8,128)(2,1)S(1)}, u32[]{:S(2)}, u32[]{:S(2)}) collective-permute-start(bf16[48,8,128]{2,1,0:T(8,128)(2,1)} %get-tuple-element.47), channel_id=1, source_target_pairs={{0,13},{1,12},{2,15},{3,14},{4,9},{5,8},{6,11},{7,10},{8,5},{9,4},... | collective-permute-start | bytes 294920 | tf_op jit(solution)/shard_map/ppermute | solution.py:575
  37.0 7.9 %collective-permute-start.15 = (bf16[48,8,128]{2,1,0:T(8,128)(2,1)}, bf16[48,8,128]{2,1,0:T(8,128)(2,1)S(1)}, u32[]{:S(2)}, u32[]{:S(2)}) collective-permute-start(bf16[48,8,128]{2,1,0:T(8,128)(2,1)} %get-tuple-element.48), channel_id=1, source_target_pairs={{0,15},{1,14},{2,13},{3,12},{4,11},{5,10},{6,9},{7,8},{8,7},{9,6},... | collective-permute-start | bytes 294920 | tf_op jit(solution)/shard_map/ppermute | solution.py:575
  39.4 1.6 %collective-permute-start.13 = (bf16[20,8,128]{2,1,0:T(8,128)(2,1)S(1)}, bf16[20,8,128]{2,1,0:T(8,128)(2,1)S(1)}, u32[]{:S(2)}, u32[]{:S(2)}) collective-permute-start(bf16[20,8,128]{2,1,0:T(8,128)(2,1)S(1)} %collect_gains.1), channel_id=1, source_target_pairs={{0,1},{1,0},{2,3},{3,2},{4,5},{5,4},{6,7},{7,6},{8,9},{9,8},{10,11... | collective-permute-start | bytes 122888 | tf_op jit(solution)/shard_map/ppermute | solution.py:575
  39.5 0.9 %copy-start = (bf16[62,8,128]{2,1,0:T(8,128)(2,1)S(1)}, bf16[62,8,128]{2,1,0:T(8,128)(2,1)}, u32[]{:S(2)}) copy-start(bf16[62,8,128]{2,1,0:T(8,128)(2,1)} %get-tuple-element.27.own_ref) | copy-start | bytes 380932

commit v14 on v9

--- a/solution.py
+++ b/solution.py
@@ -374,15 +374,24 @@
     sums_ref[...] = one_ref[:, 0:owned] + two_ref[:, 0:owned]
 
 
-def finish_kernel(capacity, late, slots_s, gains_ref, recip_ref, sums_ref, *rest):
-    far = rest[: len(late)]
-    out_hbm, acc_ref, res_ref, out_ref, sems = rest[len(late) :]
+def next_kernel(capacity, x, slots_ref, sums_ref, rows_ref, out_ref, slots_s, sem):
+    move = pltpu.make_async_copy(slots_ref, slots_s, sem)
+    move.start()
+    out_ref[...] = sums_ref[...]
+    move.wait()
+    add_rows((out_ref,), slots_s, x, capacity, rows_ref)
+
+
+def finish_kernel(capacity, last, slots_ref, gains_ref, recip_ref, sums_ref, *rest):
+    far, (out_hbm, slots_s, acc_ref, res_ref, out_ref, sems) = rest[:-6], rest[-6:]
     owned, parts, channels = out_hbm.shape
     chunks = channels // LANES
+    move = pltpu.make_async_copy(slots_ref, slots_s, sems.at[chunks])
+    move.start()
     acc_ref[...] = sums_ref[...]
-    if len(late) > 1:
-        for x, rows_ref in zip(late, far):
-            add_rows((acc_ref,), slots_s, x, capacity, rows_ref)
+    move.wait()
+    if last is not None:
+        add_rows((acc_ref,), slots_s, last, capacity, far[0])
     else:
 
         def from_device(d, carry):
@@ -612,20 +621,34 @@
         compiler_params=some,
         name="gains_and_sums",
     )(me, choice, basis, *[arrived[x] for x in order], *passed)
+    if halves:
+        before, last = late
+        sums = pl.pallas_call(
+            functools.partial(next_kernel, capacity, before),
+            out_shape=shape(sums.shape, f32),
+            in_specs=[anywhere, vmem, vmem],
+            out_specs=vmem,
+            scratch_shapes=[pltpu.SMEM((devices, LANES), i32), dma],
+            compiler_params=some,
+            name="sum_next",
+        )(slots, sums, arrived[before])
+    else:
+        last = None
     return pl.pallas_call(
-        functools.partial(finish_kernel, capacity, late),
+        functools.partial(finish_kernel, capacity, last),
         out_shape=shape((owned, parts, channels), bf16),
-        in_specs=[smem] + [vmem] * (3 + len(late)),
+        in_specs=[anywhere] + [vmem] * 4,
         out_specs=hbm,
         scratch_shapes=[
+            pltpu.SMEM((devices, LANES), i32),
             pltpu.VMEM((chunks, owned, parts, LANES), f32),
             pltpu.VMEM((chunks, owned, parts, LANES), f32),
             pltpu.VMEM((chunks, owned, parts, LANES), bf16),
-            dma((chunks,)),
+            dma((chunks + 1,)),
         ],
         compiler_params=some,
         name="sum_and_apply",
-    )(slots, gains, recip, sums, *[arrived[x] for x in late])
+    )(slots, gains, recip, sums, arrived[late[-1]])
 
 
 def solution(mesh):

time: 47 us -> 46.8 us (level)
  waiting for transfers between devices: 11.9 us -> 10.3 us
  Pallas kernels: 9.58 us -> 11.1 us
    ppermute x16, waiting for transfers between devices: 11.9 us -> 10.3 us  [swap(): return lax.ppermute(array, 'bl', [(d, d ^ x) for d in range(devices)])]
    pallas_call x1 -> x2, Pallas kernels: 2.04 us -> 2.82 us  [the longest x1 1.98 us: on_device(): pl.pallas_call(functools.partial(finish_kernel, capacity, last), out_shap...]
    pallas_call x1, Pallas kernels: 1.95 us -> 2.66 us  [on_device(): pl.pallas_call(functools.partial(middle_kernel, capacity, near, depth, or...]
  transfers between devices with their start and end apart: 16 -> 16, of which waited for: 6 -> 6; matrix products, arithmetic and copies ran while one was open for 0% -> 0% of each run, Pallas kernels for 12% -> 16%
where the time goes in v14:
time: 46.8 us; the launch traced here: 46.7 us
  starting transfers between devices  24.4 us (52%)
  Pallas kernels  11.1 us (24%)
  waiting for transfers between devices  10.3 us (22%)
  local copies, waits for them, and re-layouts  0.9 us (2%)
    ppermute x16, starting transfers between devices, swap(): return lax.ppermute(array, 'bl', [(d, d ^ x) for d in range(devices)])  24.4 us
    ppermute x16, waiting for transfers between devices, swap(): return lax.ppermute(array, 'bl', [(d, d ^ x) for d in range(devices)])  10.3 us
    pallas_call x1, Pallas kernels, on_device(): pl.pallas_call(functools.partial(pack_kernel, capacity, near), out_shape=...  3.2 us
    pallas_call x1, Pallas kernels, on_device(): pl.pallas_call(functools.partial(middle_kernel, capacity, near, depth, or...  2.66 us
    pallas_call x1, Pallas kernels, on_device(): pl.pallas_call(functools.partial(finish_kernel, capacity, last), out_shap...  1.98 us
    pallas_call x1, Pallas kernels, on_device(): pl.pallas_call(functools.partial(first_kernel, capacity, near + 1), out_s...  1.79 us
  transfers between devices with their start and end apart: 16, of which 6 were waited for; matrix products, arithmetic and copies ran while one was open for 0% of the time, Pallas kernels for 16%

profile of v14, /device:TPU:0, one launch (start us, length us, event | category | flops | bytes accessed | tf_op | source)
XLA Modules:
  0.0 46.7 jit_solution(284171973291321071)
XLA Ops:
  0.0 1.8 %pack_first.1 = bf16[48,8,128]{2,1,0:T(8,128)(2,1)} custom-call(s32[1]{0:T(128)} %bitcast.me_s.turn_s, s32[128]{0:T(128)} %bitcast.12, bf16[128,8,384]{2,1,0:T(8,128)(2,1)} %vis_hbm.3), custom_call_target="tpu_custom_call" | custom-call | tf_op jit(solution)/shard_map/pack_first/pallas_call | solution.py:501
  1.8 3.6 %collective-permute-start.12 = (bf16[48,8,128]{2,1,0:T(8,128)(2,1)}, bf16[48,8,128]{2,1,0:T(8,128)(2,1)S(1)}, u32[]{:S(2)}, u32[]{:S(2)}) collective-permute-start(bf16[48,8,128]{2,1,0:T(8,128)(2,1)} %pack_first.1), channel_id=1, source_target_pairs={{0,9},{1,8},{2,11},{3,10},{4,13},{5,12},{6,15},{7,14},{8,1},{9,0},... | collective-permute-start | bytes 294920 | tf_op jit(solution)/shard_map/ppermute | solution.py:576
  5.4 3.2 %pack_rows.1 = (bf16[62,8,128]{2,1,0:T(8,128)(2,1)}, bf16[53,8,128]{2,1,0:T(8,128)(2,1)}, bf16[53,8,128]{2,1,0:T(8,128)(2,1)}, bf16[53,8,128]{2,1,0:T(8,128)(2,1...) custom-call(s32[1]{0:T(128)} %bitcast.me_s.turn_s, ...), custom_call_target="tpu_custom_call" | custom-call | tf_op jit(solution)/shard_map/pack_rows/pallas_call | solution.py:516
  8.6 0.7 %collective-permute-start = (bf16[53,8,128]{2,1,0:T(8,128)(2,1)}, bf16[53,8,128]{2,1,0:T(8,128)(2,1)S(1)}, u32[]{:S(2)}, u32[]{:S(2)}) collective-permute-start(bf16[53,8,128]{2,1,0:T(8,128)(2,1)} %get-tuple-element.31), channel_id=1, source_target_pairs={{0,8},{1,9},{2,10},{3,11},{4,12},{5,13},{6,14},{7,15},{8,0},{9,1},... | collective-permute-start | bytes 325640 | tf_op jit(solution)/shard_map/ppermute | solution.py:576
  9.2 3.3 %collective-permute-start.1 = (bf16[53,8,128]{2,1,0:T(8,128)(2,1)}, bf16[53,8,128]{2,1,0:T(8,128)(2,1)S(1)}, u32[]{:S(2)}, u32[]{:S(2)}) collective-permute-start(bf16[53,8,128]{2,1,0:T(8,128)(2,1)} %get-tuple-element.32), channel_id=1, source_target_pairs={{0,10},{1,11},{2,8},{3,9},{4,14},{5,15},{6,12},{7,13},{8,2},{9,3},... | collective-permute-start | bytes 325640 | tf_op jit(solution)/shard_map/ppermute | solution.py:576
  12.5 1.6 %collective-permute-start.2 = (bf16[53,8,128]{2,1,0:T(8,128)(2,1)}, bf16[53,8,128]{2,1,0:T(8,128)(2,1)S(1)}, u32[]{:S(2)}, u32[]{:S(2)}) collective-permute-start(bf16[53,8,128]{2,1,0:T(8,128)(2,1)} %get-tuple-element.33), channel_id=1, source_target_pairs={{0,4},{1,5},{2,6},{3,7},{4,0},{5,1},{6,2},{7,3},{8,12},{9,13},{10,... | collective-permute-start | bytes 325640 | tf_op jit(solution)/shard_map/ppermute | solution.py:576
  14.1 3.4 %collective-permute-start.4 = (bf16[53,8,128]{2,1,0:T(8,128)(2,1)}, bf16[53,8,128]{2,1,0:T(8,128)(2,1)S(1)}, u32[]{:S(2)}, u32[]{:S(2)}) collective-permute-start(bf16[53,8,128]{2,1,0:T(8,128)(2,1)} %get-tuple-element.35), channel_id=1, source_target_pairs={{0,12},{1,13},{2,14},{3,15},{4,8},{5,9},{6,10},{7,11},{8,4},{9,5},... | collective-permute-start | bytes 325640 | tf_op jit(solution)/shard_map/ppermute | solution.py:576
  17.5 2.9 %collective-permute-done.rest_0_.rest_1_ = bf16[53,8,128]{2,1,0:T(8,128)(2,1)S(1)} collective-permute-done((bf16[53,8,128]{2,1,0:T(8,128)(2,1)}, bf16[53,8,128]{2,1,0:T(8,128)(2,1)S(1)}, u32[]{:S(2)}, u32[]{:S(2)}) %collective-permute-start) | collective-permute-done | bytes 108576 | tf_op jit(solution)/shard_map/ppermute | solution.py:576
  20.4 3.2 %collective-permute-done.1.rest_1_.rest_2_ = bf16[53,8,128]{2,1,0:T(8,128)(2,1)S(1)} collective-permute-done((bf16[53,8,128]{2,1,0:T(8,128)(2,1)}, bf16[53,8,128]{2,1,0:T(8,128)(2,1)S(1)}, u32[]{:S(2)}, u32[]{:S(2)}) %collective-permute-start.1) | collective-permute-done | bytes 108576 | tf_op jit(solution)/shard_map/ppermute | solution.py:576
  23.6 2.4 %collective-permute-start.6 = (bf16[53,8,128]{2,1,0:T(8,128)(2,1)}, bf16[53,8,128]{2,1,0:T(8,128)(2,1)S(1)}, u32[]{:S(2)}, u32[]{:S(2)}) collective-permute-start(bf16[53,8,128]{2,1,0:T(8,128)(2,1)} %get-tuple-element.37), channel_id=1, source_target_pairs={{0,14},{1,15},{2,12},{3,13},{4,10},{5,11},{6,8},{7,9},{8,6},{9,7},... | collective-permute-start | bytes 325640 | tf_op jit(solution)/shard_map/ppermute | solution.py:576
  26.0 2.6 %collective-permute-start.8 = (bf16[53,8,128]{2,1,0:T(8,128)(2,1)}, bf16[53,8,128]{2,1,0:T(8,128)(2,1)S(1)}, u32[]{:S(2)}, u32[]{:S(2)}) collective-permute-start(bf16[53,8,128]{2,1,0:T(8,128)(2,1)} %get-tuple-element.39), channel_id=1, source_target_pairs={{0,11},{1,10},{2,9},{3,8},{4,15},{5,14},{6,13},{7,12},{8,3},{9,2},... | collective-permute-start | bytes 325640 | tf_op jit(solution)/shard_map/ppermute | solution.py:576
  28.6 2.6 %collective-permute-start.10 = (bf16[53,8,128]{2,1,0:T(8,128)(2,1)}, bf16[53,8,128]{2,1,0:T(8,128)(2,1)S(1)}, u32[]{:S(2)}, u32[]{:S(2)}) collective-permute-start(bf16[53,8,128]{2,1,0:T(8,128)(2,1)} %get-tuple-element.41), channel_id=1, source_target_pairs={{0,2},{1,3},{2,0},{3,1},{4,6},{5,7},{6,4},{7,5},{8,10},{9,11},{10,... | collective-permute-start | bytes 325640 | tf_op jit(solution)/shard_map/ppermute | solution.py:576
  31.2 1.3 %collective-permute-done.6.rest_3_.rest_7_ = bf16[53,8,128]{2,1,0:T(8,128)(2,1)S(1)} collective-permute-done((bf16[53,8,128]{2,1,0:T(8,128)(2,1)}, bf16[53,8,128]{2,1,0:T(8,128)(2,1)S(1)}, u32[]{:S(2)}, u32[]{:S(2)}) %collective-permute-start.6) | collective-permute-done | bytes 108576 | tf_op jit(solution)/shard_map/ppermute | solution.py:576
  32.5 2.4 %collective-permute-done.7.rest_8_ = bf16[53,8,128]{2,1,0:T(8,128)(2,1)S(1)} collective-permute-done((bf16[53,8,128]{2,1,0:T(8,128)(2,1)}, bf16[53,8,128]{2,1,0:T(8,128)(2,1)S(1)}, u32[]{:S(2)}, u32[]{:S(2)}) %collective-permute-start.7) | collective-permute-done | bytes 108576 | tf_op jit(solution)/shard_map/ppermute | solution.py:576
  34.9 2.0 %collective-permute-start.14 = (bf16[48,8,128]{2,1,0:T(8,128)(2,1)}, bf16[48,8,128]{2,1,0:T(8,128)(2,1)S(1)}, u32[]{:S(2)}, u32[]{:S(2)}) collective-permute-start(bf16[48,8,128]{2,1,0:T(8,128)(2,1)} %get-tuple-element.47), channel_id=1, source_target_pairs={{0,13},{1,12},{2,15},{3,14},{4,9},{5,8},{6,11},{7,10},{8,5},{9,4},... | collective-permute-start | bytes 294920 | tf_op jit(solution)/shard_map/ppermute | solution.py:576
  36.9 0.1 collective-permute-done.8.rest_9_
  37.1 1.9 %collective-permute-start.15 = (bf16[48,8,128]{2,1,0:T(8,128)(2,1)}, bf16[48,8,128]{2,1,0:T(8,128)(2,1)S(1)}, u32[]{:S(2)}, u32[]{:S(2)}) collective-permute-start(bf16[48,8,128]{2,1,0:T(8,128)(2,1)} %get-tuple-element.48), channel_id=1, source_target_pairs={{0,15},{1,14},{2,13},{3,12},{4,11},{5,10},{6,9},{7,8},{8,7},{9,6},... | collective-permute-start | bytes 294920 | tf_op jit(solution)/shard_map/ppermute | solution.py:576
  39.1 0.3 collective-permute-start.13
  39.4 0.9 %copy-done = bf16[62,8,128]{2,1,0:T(8,128)(2,1)S(1)} copy-done((bf16[62,8,128]{2,1,0:T(8,128)(2,1)S(1)}, bf16[62,8,128]{2,1,0:T(8,128)(2,1)}, u32[]{:S(2)}) %copy-start) | copy-done | bytes 127000
  40.3 0.5 %make_ready.1 = (bf16[62,8,128]{2,1,0:T(8,128)(2,1)S(1)}, bf16[256,256]{1,0:T(8,128)(2,1)S(1)}, bf16[256,3072]{1,0:T(8,128)(2,1)S(1)}) custom-call(s32[1]{0:T(128)} %bitcast.me_s.turn_s, bf16[62,8,128]{2,1,0:T(8,128)(2,1)S(1)} %copy-done), custom_call_target="tpu_custom_call" | custom-call | tf_op jit(solution)/shard_map/make_ready/pallas_call | solution.py:557
  40.9 2.7 %gains_and_sums.1 = (f32[128,3072]{1,0:T(8,128)S(1)}, f32[64,128]{1,0:T(8,128)S(1)}, s32[16,128]{1,0:T(8,128)S(1)}, f32[3,64,8,128]{3,2,1,0:T(8,128)S(1)}) custom-call(s32[1]{0:T(128)} %bitcast.me_s.turn_s, bf16[256,256]{1,0:T(8,128)(2,1)S(1)} %get-tuple-element.28.choice_ref, bf16[256,3072]{1,0:T(8,128)(2,1)S(1)} %get-tuple-element.29.basis_ref, ...), custom_call_target="tpu_custom_call" | custom-call | tf_op jit(solution)/shard_map/gains_and_sums/pallas_call | solution.py:601
  43.5 0.8 %sum_next.1.sums_ref = f32[3,64,8,128]{3,2,1,0:T(8,128)S(1)} custom-call(s32[16,128]{1,0:T(8,128)S(1)} %get-tuple-element.43.slots_ref, f32[3,64,8,128]{3,2,1,0:T(8,128)S(1)} %get-tuple-element.46.sums_ref, bf16[48,8,128]{2,1,0:T(8,128)(2,1)S(1)} %collective-permute-done.14.rows_ref), custom_call_target="tpu_custom_call" | custom-call | tf_op jit(solution)/shard_map/sum_next/pallas_call | solution.py:626
  44.4 0.4 collective-permute-done.15.rest_0_
  44.7 2.0 %sum_and_apply.1 = bf16[64,8,384]{2,1,0:T(8,128)(2,1)} custom-call(s32[16,128]{1,0:T(8,128)S(1)} %get-tuple-element.43.slots_ref, f32[128,3072]{1,0:T(8,128)S(1)} %get-tuple-element.44.gains_ref, f32[64,128]{1,0:T(8,128)S(1)} %get-tuple-element.45.recip_ref, f32[3,64,8,128]{3,2,1,0:T(8,128)S(1)} %sum_next.1.sums_ref, ...), custom_call_target="tpu_custom_call" | custom-call | tf_op jit(solution)/shard_map/sum_and_apply/pallas_call | solution.py:637
  (17 shorter events, 0.1 us)
Async XLA Ops:
  1.8 12.3 %collective-permute-start.12 = (bf16[48,8,128]{2,1,0:T(8,128)(2,1)}, bf16[48,8,128]{2,1,0:T(8,128)(2,1)S(1)}, u32[]{:S(2)}, u32[]{:S(2)}) collective-permute-start(bf16[48,8,128]{2,1,0:T(8,128)(2,1)} %pack_first.1), channel_id=1, source_target_pairs={{0,9},{1,8},{2,11},{3,10},{4,13},{5,12},{6,15},{7,14},{8,1},{9,0},... | collective-permute-start | bytes 294920 | tf_op jit(solution)/shard_map/ppermute | solution.py:576
  8.6 11.8 %collective-permute-start = (bf16[53,8,128]{2,1,0:T(8,128)(2,1)}, bf16[53,8,128]{2,1,0:T(8,128)(2,1)S(1)}, u32[]{:S(2)}, u32[]{:S(2)}) collective-permute-start(bf16[53,8,128]{2,1,0:T(8,128)(2,1)} %get-tuple-element.31), channel_id=1, source_target_pairs={{0,8},{1,9},{2,10},{3,11},{4,12},{5,13},{6,14},{7,15},{8,0},{9,1},... | collective-permute-start | bytes 325640 | tf_op jit(solution)/shard_map/ppermute | solution.py:576
  9.2 14.3 %collective-permute-start.1 = (bf16[53,8,128]{2,1,0:T(8,128)(2,1)}, bf16[53,8,128]{2,1,0:T(8,128)(2,1)S(1)}, u32[]{:S(2)}, u32[]{:S(2)}) collective-permute-start(bf16[53,8,128]{2,1,0:T(8,128)(2,1)} %get-tuple-element.32), channel_id=1, source_target_pairs={{0,10},{1,11},{2,8},{3,9},{4,14},{5,15},{6,12},{7,13},{8,2},{9,3},... | collective-permute-start | bytes 325640 | tf_op jit(solution)/shard_map/ppermute | solution.py:576
  12.5 13.4 %collective-permute-start.2 = (bf16[53,8,128]{2,1,0:T(8,128)(2,1)}, bf16[53,8,128]{2,1,0:T(8,128)(2,1)S(1)}, u32[]{:S(2)}, u32[]{:S(2)}) collective-permute-start(bf16[53,8,128]{2,1,0:T(8,128)(2,1)} %get-tuple-element.33), channel_id=1, source_target_pairs={{0,4},{1,5},{2,6},{3,7},{4,0},{5,1},{6,2},{7,3},{8,12},{9,13},{10,... | collective-permute-start | bytes 325640 | tf_op jit(solution)/shard_map/ppermute | solution.py:576
  14.1 11.9 %collective-permute-start.3 = (bf16[53,8,128]{2,1,0:T(8,128)(2,1)}, bf16[53,8,128]{2,1,0:T(8,128)(2,1)S(1)}, u32[]{:S(2)}, u32[]{:S(2)}) collective-permute-start(bf16[53,8,128]{2,1,0:T(8,128)(2,1)} %get-tuple-element.34), channel_id=1, source_target_pairs={{0,5},{1,4},{2,7},{3,6},{4,1},{5,0},{6,3},{7,2},{8,13},{9,12},{10,... | collective-permute-start | bytes 325640 | tf_op jit(solution)/shard_map/ppermute | solution.py:576
  14.1 14.5 %collective-permute-start.4 = (bf16[53,8,128]{2,1,0:T(8,128)(2,1)}, bf16[53,8,128]{2,1,0:T(8,128)(2,1)S(1)}, u32[]{:S(2)}, u32[]{:S(2)}) collective-permute-start(bf16[53,8,128]{2,1,0:T(8,128)(2,1)} %get-tuple-element.35), channel_id=1, source_target_pairs={{0,12},{1,13},{2,14},{3,15},{4,8},{5,9},{6,10},{7,11},{8,4},{9,5},... | collective-permute-start | bytes 325640 | tf_op jit(solution)/shard_map/ppermute | solution.py:576
  20.4 8.2 %collective-permute-start.5 = (bf16[53,8,128]{2,1,0:T(8,128)(2,1)}, bf16[53,8,128]{2,1,0:T(8,128)(2,1)S(1)}, u32[]{:S(2)}, u32[]{:S(2)}) collective-permute-start(bf16[53,8,128]{2,1,0:T(8,128)(2,1)} %get-tuple-element.36), channel_id=1, source_target_pairs={{0,6},{1,7},{2,4},{3,5},{4,2},{5,3},{6,0},{7,1},{8,14},{9,15},{10,... | collective-permute-start | bytes 325640 | tf_op jit(solution)/shard_map/ppermute | solution.py:576
  23.6 8.9 %collective-permute-start.6 = (bf16[53,8,128]{2,1,0:T(8,128)(2,1)}, bf16[53,8,128]{2,1,0:T(8,128)(2,1)S(1)}, u32[]{:S(2)}, u32[]{:S(2)}) collective-permute-start(bf16[53,8,128]{2,1,0:T(8,128)(2,1)} %get-tuple-element.37), channel_id=1, source_target_pairs={{0,14},{1,15},{2,12},{3,13},{4,10},{5,11},{6,8},{7,9},{8,6},{9,7},... | collective-permute-start | bytes 325640 | tf_op jit(solution)/shard_map/ppermute | solution.py:576
  26.0 8.9 %collective-permute-start.7 = (bf16[53,8,128]{2,1,0:T(8,128)(2,1)}, bf16[53,8,128]{2,1,0:T(8,128)(2,1)S(1)}, u32[]{:S(2)}, u32[]{:S(2)}) collective-permute-start(bf16[53,8,128]{2,1,0:T(8,128)(2,1)} %get-tuple-element.38), channel_id=1, source_target_pairs={{0,7},{1,6},{2,5},{3,4},{4,3},{5,2},{6,1},{7,0},{8,15},{9,14},{10,... | collective-permute-start | bytes 325640 | tf_op jit(solution)/shard_map/ppermute | solution.py:576
  26.0 11.1 %collective-permute-start.8 = (bf16[53,8,128]{2,1,0:T(8,128)(2,1)}, bf16[53,8,128]{2,1,0:T(8,128)(2,1)S(1)}, u32[]{:S(2)}, u32[]{:S(2)}) collective-permute-start(bf16[53,8,128]{2,1,0:T(8,128)(2,1)} %get-tuple-element.39), channel_id=1, source_target_pairs={{0,11},{1,10},{2,9},{3,8},{4,15},{5,14},{6,13},{7,12},{8,3},{9,2},... | collective-permute-start | bytes 325640 | tf_op jit(solution)/shard_map/ppermute | solution.py:576
  28.6 10.5 %collective-permute-start.9 = (bf16[53,8,128]{2,1,0:T(8,128)(2,1)}, bf16[53,8,128]{2,1,0:T(8,128)(2,1)S(1)}, u32[]{:S(2)}, u32[]{:S(2)}) collective-permute-start(bf16[53,8,128]{2,1,0:T(8,128)(2,1)} %get-tuple-element.40), channel_id=1, source_target_pairs={{0,1},{1,0},{2,3},{3,2},{4,5},{5,4},{6,7},{7,6},{8,9},{9,8},{10,11... | collective-permute-start | bytes 325640 | tf_op jit(solution)/shard_map/ppermute | solution.py:576
  28.6 12.2 %collective-permute-start.10 = (bf16[53,8,128]{2,1,0:T(8,128)(2,1)}, bf16[53,8,128]{2,1,0:T(8,128)(2,1)S(1)}, u32[]{:S(2)}, u32[]{:S(2)}) collective-permute-start(bf16[53,8,128]{2,1,0:T(8,128)(2,1)} %get-tuple-element.41), channel_id=1, source_target_pairs={{0,2},{1,3},{2,0},{3,1},{4,6},{5,7},{6,4},{7,5},{8,10},{9,11},{10,... | collective-permute-start | bytes 325640 | tf_op jit(solution)/shard_map/ppermute | solution.py:576
  32.5 8.3 %collective-permute-start.11 = (bf16[53,8,128]{2,1,0:T(8,128)(2,1)}, bf16[53,8,128]{2,1,0:T(8,128)(2,1)S(1)}, u32[]{:S(2)}, u32[]{:S(2)}) collective-permute-start(bf16[53,8,128]{2,1,0:T(8,128)(2,1)} %get-tuple-element.42), channel_id=1, source_target_pairs={{0,3},{1,2},{2,1},{3,0},{4,7},{5,6},{6,5},{7,4},{8,11},{9,10},{10,... | collective-permute-start | bytes 325640 | tf_op jit(solution)/shard_map/ppermute | solution.py:576
  34.9 8.6 %collective-permute-start.14 = (bf16[48,8,128]{2,1,0:T(8,128)(2,1)}, bf16[48,8,128]{2,1,0:T(8,128)(2,1)S(1)}, u32[]{:S(2)}, u32[]{:S(2)}) collective-permute-start(bf16[48,8,128]{2,1,0:T(8,128)(2,1)} %get-tuple-element.47), channel_id=1, source_target_pairs={{0,13},{1,12},{2,15},{3,14},{4,9},{5,8},{6,11},{7,10},{8,5},{9,4},... | collective-permute-start | bytes 294920 | tf_op jit(solution)/shard_map/ppermute | solution.py:576
  37.1 7.7 %collective-permute-start.15 = (bf16[48,8,128]{2,1,0:T(8,128)(2,1)}, bf16[48,8,128]{2,1,0:T(8,128)(2,1)S(1)}, u32[]{:S(2)}, u32[]{:S(2)}) collective-permute-start(bf16[48,8,128]{2,1,0:T(8,128)(2,1)} %get-tuple-element.48), channel_id=1, source_target_pairs={{0,15},{1,14},{2,13},{3,12},{4,11},{5,10},{6,9},{7,8},{8,7},{9,6},... | collective-permute-start | bytes 294920 | tf_op jit(solution)/shard_map/ppermute | solution.py:576
  39.1 1.8 %collective-permute-start.13 = (bf16[20,8,128]{2,1,0:T(8,128)(2,1)S(1)}, bf16[20,8,128]{2,1,0:T(8,128)(2,1)S(1)}, u32[]{:S(2)}, u32[]{:S(2)}) collective-permute-start(bf16[20,8,128]{2,1,0:T(8,128)(2,1)S(1)} %collect_gains.1), channel_id=1, source_target_pairs={{0,1},{1,0},{2,3},{3,2},{4,5},{5,4},{6,7},{7,6},{8,9},{9,8},{10,11... | collective-permute-start | bytes 122888 | tf_op jit(solution)/shard_map/ppermute | solution.py:576
  39.4 0.9 %copy-start = (bf16[62,8,128]{2,1,0:T(8,128)(2,1)S(1)}, bf16[62,8,128]{2,1,0:T(8,128)(2,1)}, u32[]{:S(2)}) copy-start(bf16[62,8,128]{2,1,0:T(8,128)(2,1)} %get-tuple-element.27.own_ref) | copy-start | bytes 380932

commit v15 on v14

--- a/solution.py
+++ b/solution.py
@@ -22,13 +22,7 @@
 def schedule(near):
     even, odd = list(range(near, 2 * near, 2)), list(range(near + 1, 2 * near, 2))
     close = list(range(near // 2, near)) + list(range(1, near // 2))
-    cross, late = even[2:] + odd[1:-2], odd[-2:]
-    order = [0] + even[:2] + close[:2]
-    close = close[2:]
-    while cross:
-        order += cross[:1] + close[:1]
-        cross, close = cross[1:], close[1:]
-    return order + close + odd[:1], late
+    return [0] + even[:2] + close[:2] + even[2:] + close[2:] + odd[:1], odd[1:]
 
 
 def with_gains(near):
@@ -374,12 +368,14 @@
     sums_ref[...] = one_ref[:, 0:owned] + two_ref[:, 0:owned]
 
 
-def next_kernel(capacity, x, slots_ref, sums_ref, rows_ref, out_ref, slots_s, sem):
+def next_kernel(capacity, late, slots_ref, sums_ref, *rest):
+    blocks, (out_ref, slots_s, sem) = rest[:-3], rest[-3:]
     move = pltpu.make_async_copy(slots_ref, slots_s, sem)
     move.start()
     out_ref[...] = sums_ref[...]
     move.wait()
-    add_rows((out_ref,), slots_s, x, capacity, rows_ref)
+    for x, rows_ref in zip(late, blocks):
+        add_rows((out_ref,), slots_s, x, capacity, rows_ref)
 
 
 def finish_kernel(capacity, last, slots_ref, gains_ref, recip_ref, sums_ref, *rest):
@@ -480,7 +476,7 @@
     block = (chunks * capacity, parts, LANES)
     rows_at = chunks * capacity
     if halves:
-        long = with_gains(near) + [near + 3]
+        long = with_gains(near)
         outs = [
             shape((rows_at + (depth if x in long else 0), parts, LANES), bf16)
             for x in range(devices)
@@ -622,16 +618,16 @@
         name="gains_and_sums",
     )(me, choice, basis, *[arrived[x] for x in order], *passed)
     if halves:
-        before, last = late
+        *before, last = late
         sums = pl.pallas_call(
             functools.partial(next_kernel, capacity, before),
             out_shape=shape(sums.shape, f32),
-            in_specs=[anywhere, vmem, vmem],
+            in_specs=[anywhere, vmem] + [vmem] * len(before),
             out_specs=vmem,
             scratch_shapes=[pltpu.SMEM((devices, LANES), i32), dma],
             compiler_params=some,
             name="sum_next",
-        )(slots, sums, arrived[before])
+        )(slots, sums, *[arrived[x] for x in before])
     else:
         last = None
     return pl.pallas_call(

time: 46.8 us -> 51.4 us (1.098)
  the two profiles are of different devices: /device:TPU:0 before, /device:TPU:11 now
where the time goes in v15:
time: 51.4 us; the launch traced here: 51.2 us
  waiting for transfers between devices  20.7 us (40%)
  starting transfers between devices  19.4 us (38%)
  Pallas kernels  10.1 us (20%)
  local copies, waits for them, and re-layouts  0.9 us (2%)
    ppermute x16, waiting for transfers between devices, swap(): return lax.ppermute(array, 'bl', [(d, d ^ x) for d in range(devices)])  20.7 us
    ppermute x16, starting transfers between devices, swap(): return lax.ppermute(array, 'bl', [(d, d ^ x) for d in range(devices)])  19.4 us
    pallas_call x1, Pallas kernels, on_device(): pl.pallas_call(functools.partial(pack_kernel, capacity, near), out_shape=...  3.2 us
    pallas_call x1, Pallas kernels, on_device(): pl.pallas_call(functools.partial(finish_kernel, capacity, last), out_shap...  1.86 us
    pallas_call x1, Pallas kernels, on_device(): pl.pallas_call(functools.partial(middle_kernel, capacity, near, depth, or...  1.79 us
    pallas_call x1, Pallas kernels, on_device(): pl.pallas_call(functools.partial(first_kernel, capacity, near + 1), out_s...  1.79 us
  transfers between devices with their start and end apart: 16, of which 7 were waited for; matrix products, arithmetic and copies ran while one was open for 0% of the time, Pallas kernels for 13%

profile of v15, /device:TPU:11, one launch (start us, length us, event | category | flops | bytes accessed | tf_op | source)
XLA Modules:
  0.0 51.2 jit_solution(8164024907217863570)
XLA Ops:
  0.0 1.8 %pack_first.1 = bf16[48,8,128]{2,1,0:T(8,128)(2,1)} custom-call(s32[1]{0:T(128)} %bitcast.me_s.turn_s, s32[128]{0:T(128)} %bitcast.12, bf16[128,8,384]{2,1,0:T(8,128)(2,1)} %vis_hbm.3), custom_call_target="tpu_custom_call" | custom-call | tf_op jit(solution)/shard_map/pack_first/pallas_call | solution.py:497
  1.8 2.9 %collective-permute-start.11 = (bf16[48,8,128]{2,1,0:T(8,128)(2,1)}, bf16[48,8,128]{2,1,0:T(8,128)(2,1)S(1)}, u32[]{:S(2)}, u32[]{:S(2)}) collective-permute-start(bf16[48,8,128]{2,1,0:T(8,128)(2,1)} %pack_first.1), channel_id=1, source_target_pairs={{0,9},{1,8},{2,11},{3,10},{4,13},{5,12},{6,15},{7,14},{8,1},{9,0},... | collective-permute-start | bytes 294920 | tf_op jit(solution)/shard_map/ppermute | solution.py:572
  4.7 3.2 %pack_rows.1 = (bf16[62,8,128]{2,1,0:T(8,128)(2,1)}, bf16[53,8,128]{2,1,0:T(8,128)(2,1)}, bf16[53,8,128]{2,1,0:T(8,128)(2,1)}, bf16[53,8,128]{2,1,0:T(8,128)(2,1...) custom-call(s32[1]{0:T(128)} %bitcast.me_s.turn_s, ...), custom_call_target="tpu_custom_call" | custom-call | tf_op jit(solution)/shard_map/pack_rows/pallas_call | solution.py:512
  8.1 3.3 %collective-permute-start.1 = (bf16[53,8,128]{2,1,0:T(8,128)(2,1)}, bf16[53,8,128]{2,1,0:T(8,128)(2,1)S(1)}, u32[]{:S(2)}, u32[]{:S(2)}) collective-permute-start(bf16[53,8,128]{2,1,0:T(8,128)(2,1)} %get-tuple-element.32), channel_id=1, source_target_pairs={{0,10},{1,11},{2,8},{3,9},{4,14},{5,15},{6,12},{7,13},{8,2},{9,3},... | collective-permute-start | bytes 325640 | tf_op jit(solution)/shard_map/ppermute | solution.py:572
  11.5 1.8 %collective-permute-start.3 = (bf16[53,8,128]{2,1,0:T(8,128)(2,1)}, bf16[53,8,128]{2,1,0:T(8,128)(2,1)S(1)}, u32[]{:S(2)}, u32[]{:S(2)}) collective-permute-start(bf16[53,8,128]{2,1,0:T(8,128)(2,1)} %get-tuple-element.34), channel_id=1, source_target_pairs={{0,5},{1,4},{2,7},{3,6},{4,1},{5,0},{6,3},{7,2},{8,13},{9,12},{10,... | collective-permute-start | bytes 325640 | tf_op jit(solution)/shard_map/ppermute | solution.py:572
  13.4 3.3 %collective-permute-done.rest_0_.rest_1_ = bf16[53,8,128]{2,1,0:T(8,128)(2,1)S(1)} collective-permute-done((bf16[53,8,128]{2,1,0:T(8,128)(2,1)}, bf16[53,8,128]{2,1,0:T(8,128)(2,1)S(1)}, u32[]{:S(2)}, u32[]{:S(2)}) %collective-permute-start) | collective-permute-done | bytes 108576 | tf_op jit(solution)/shard_map/ppermute | solution.py:572
  16.7 1.0 %collective-permute-start.5 = (bf16[53,8,128]{2,1,0:T(8,128)(2,1)}, bf16[53,8,128]{2,1,0:T(8,128)(2,1)S(1)}, u32[]{:S(2)}, u32[]{:S(2)}) collective-permute-start(bf16[53,8,128]{2,1,0:T(8,128)(2,1)} %get-tuple-element.36), channel_id=1, source_target_pairs={{0,14},{1,15},{2,12},{3,13},{4,10},{5,11},{6,8},{7,9},{8,6},{9,7},... | collective-permute-start | bytes 325640 | tf_op jit(solution)/shard_map/ppermute | solution.py:572
  17.7 1.2 %collective-permute-done.1.rest_1_.rest_2_ = bf16[53,8,128]{2,1,0:T(8,128)(2,1)S(1)} collective-permute-done((bf16[53,8,128]{2,1,0:T(8,128)(2,1)}, bf16[53,8,128]{2,1,0:T(8,128)(2,1)S(1)}, u32[]{:S(2)}, u32[]{:S(2)}) %collective-permute-start.1) | collective-permute-done | bytes 108576 | tf_op jit(solution)/shard_map/ppermute | solution.py:572
  18.9 3.0 %collective-permute-start.6 = (bf16[53,8,128]{2,1,0:T(8,128)(2,1)}, bf16[53,8,128]{2,1,0:T(8,128)(2,1)S(1)}, u32[]{:S(2)}, u32[]{:S(2)}) collective-permute-start(bf16[53,8,128]{2,1,0:T(8,128)(2,1)} %get-tuple-element.37), channel_id=1, source_target_pairs={{0,6},{1,7},{2,4},{3,5},{4,2},{5,3},{6,0},{7,1},{8,14},{9,15},{10,... | collective-permute-start | bytes 325640 | tf_op jit(solution)/shard_map/ppermute | solution.py:572
  21.9 0.9 %collective-permute-start.7 = (bf16[53,8,128]{2,1,0:T(8,128)(2,1)}, bf16[53,8,128]{2,1,0:T(8,128)(2,1)S(1)}, u32[]{:S(2)}, u32[]{:S(2)}) collective-permute-start(bf16[53,8,128]{2,1,0:T(8,128)(2,1)} %get-tuple-element.38), channel_id=1, source_target_pairs={{0,7},{1,6},{2,5},{3,4},{4,3},{5,2},{6,1},{7,0},{8,15},{9,14},{10,... | collective-permute-start | bytes 325640 | tf_op jit(solution)/shard_map/ppermute | solution.py:572
  22.9 0.4 collective-permute-start.8
  23.3 3.3 %collective-permute-done.4.rest_2_.rest_5_ = bf16[53,8,128]{2,1,0:T(8,128)(2,1)S(1)} collective-permute-done((bf16[53,8,128]{2,1,0:T(8,128)(2,1)}, bf16[53,8,128]{2,1,0:T(8,128)(2,1)S(1)}, u32[]{:S(2)}, u32[]{:S(2)}) %collective-permute-start.4) | collective-permute-done | bytes 108576 | tf_op jit(solution)/shard_map/ppermute | solution.py:572
  26.6 1.5 %collective-permute-start.9 = (bf16[53,8,128]{2,1,0:T(8,128)(2,1)}, bf16[53,8,128]{2,1,0:T(8,128)(2,1)S(1)}, u32[]{:S(2)}, u32[]{:S(2)}) collective-permute-start(bf16[53,8,128]{2,1,0:T(8,128)(2,1)} %get-tuple-element.40), channel_id=1, source_target_pairs={{0,2},{1,3},{2,0},{3,1},{4,6},{5,7},{6,4},{7,5},{8,10},{9,11},{10,... | collective-permute-start | bytes 325640 | tf_op jit(solution)/shard_map/ppermute | solution.py:572
  28.1 3.8 %collective-permute-done.5.rest_3_.rest_6_ = bf16[53,8,128]{2,1,0:T(8,128)(2,1)S(1)} collective-permute-done((bf16[53,8,128]{2,1,0:T(8,128)(2,1)}, bf16[53,8,128]{2,1,0:T(8,128)(2,1)S(1)}, u32[]{:S(2)}, u32[]{:S(2)}) %collective-permute-start.5) | collective-permute-done | bytes 108576 | tf_op jit(solution)/shard_map/ppermute | solution.py:572
  31.9 1.5 %collective-permute-start.10 = (bf16[53,8,128]{2,1,0:T(8,128)(2,1)}, bf16[53,8,128]{2,1,0:T(8,128)(2,1)S(1)}, u32[]{:S(2)}, u32[]{:S(2)}) collective-permute-start(bf16[53,8,128]{2,1,0:T(8,128)(2,1)} %get-tuple-element.41), channel_id=1, source_target_pairs={{0,3},{1,2},{2,1},{3,0},{4,7},{5,6},{6,5},{7,4},{8,11},{9,10},{10,... | collective-permute-start | bytes 325640 | tf_op jit(solution)/shard_map/ppermute | solution.py:572
  33.4 0.9 %collective-permute-start.14 = (bf16[48,8,128]{2,1,0:T(8,128)(2,1)}, bf16[48,8,128]{2,1,0:T(8,128)(2,1)S(1)}, u32[]{:S(2)}, u32[]{:S(2)}) collective-permute-start(bf16[48,8,128]{2,1,0:T(8,128)(2,1)} %get-tuple-element.47), channel_id=1, source_target_pairs={{0,13},{1,12},{2,15},{3,14},{4,9},{5,8},{6,11},{7,10},{8,5},{9,4},... | collective-permute-start | bytes 294920 | tf_op jit(solution)/shard_map/ppermute | solution.py:572
  34.3 1.7 %collective-permute-start.15 = (bf16[48,8,128]{2,1,0:T(8,128)(2,1)}, bf16[48,8,128]{2,1,0:T(8,128)(2,1)S(1)}, u32[]{:S(2)}, u32[]{:S(2)}) collective-permute-start(bf16[48,8,128]{2,1,0:T(8,128)(2,1)} %get-tuple-element.48), channel_id=1, source_target_pairs={{0,15},{1,14},{2,13},{3,12},{4,11},{5,10},{6,9},{7,8},{8,7},{9,6},... | collective-permute-start | bytes 294920 | tf_op jit(solution)/shard_map/ppermute | solution.py:572
  36.1 0.9 %copy-done = bf16[62,8,128]{2,1,0:T(8,128)(2,1)S(1)} copy-done((bf16[62,8,128]{2,1,0:T(8,128)(2,1)S(1)}, bf16[62,8,128]{2,1,0:T(8,128)(2,1)}, u32[]{:S(2)}) %copy-start) | copy-done | bytes 127000
  37.0 0.5 %make_ready.1 = (bf16[62,8,128]{2,1,0:T(8,128)(2,1)S(1)}, bf16[256,256]{1,0:T(8,128)(2,1)S(1)}, bf16[256,3072]{1,0:T(8,128)(2,1)S(1)}) custom-call(s32[1]{0:T(128)} %bitcast.me_s.turn_s, bf16[62,8,128]{2,1,0:T(8,128)(2,1)S(1)} %copy-done), custom_call_target="tpu_custom_call" | custom-call | tf_op jit(solution)/shard_map/make_ready/pallas_call | solution.py:553
  37.6 1.8 %gains_and_sums.1 = (f32[128,3072]{1,0:T(8,128)S(1)}, f32[64,128]{1,0:T(8,128)S(1)}, s32[16,128]{1,0:T(8,128)S(1)}, f32[3,64,8,128]{3,2,1,0:T(8,128)S(1)}) custom-call(s32[1]{0:T(128)} %bitcast.me_s.turn_s, bf16[256,256]{1,0:T(8,128)(2,1)S(1)} %get-tuple-element.28.choice_ref, bf16[256,3072]{1,0:T(8,128)(2,1)S(1)} %get-tuple-element.29.basis_ref, ...), custom_call_target="tpu_custom_call" | custom-call | tf_op jit(solution)/shard_map/gains_and_sums/pallas_call | solution.py:597
  39.6 6.6 %collective-permute-done.14.rest_1_ = bf16[48,8,128]{2,1,0:T(8,128)(2,1)S(1)} collective-permute-done((bf16[48,8,128]{2,1,0:T(8,128)(2,1)}, bf16[48,8,128]{2,1,0:T(8,128)(2,1)S(1)}, u32[]{:S(2)}, u32[]{:S(2)}) %collective-permute-start.14) | collective-permute-done | bytes 98336 | tf_op jit(solution)/shard_map/ppermute | solution.py:572
  46.2 0.8 %sum_next.1.sums_ref = f32[3,64,8,128]{3,2,1,0:T(8,128)S(1)} custom-call(s32[16,128]{1,0:T(8,128)S(1)} %get-tuple-element.42.slots_ref, f32[3,64,8,128]{3,2,1,0:T(8,128)S(1)} %get-tuple-element.45.sums_ref, bf16[48,8,128]{2,1,0:T(8,128)(2,1)S(1)} %collective-permute-done.13.rest_0_, bf16[48,8,128]{2,1,0:T(8,128)(2,1)S(1)} %collective-permute-done.14.rest_1_), custom_call_target="tpu_custom_call" | custom-call | tf_op jit(solution)/shard_map/sum_next/pallas_call | solution.py:622
  47.0 2.3 %collective-permute-done.15.rest_0_ = bf16[48,8,128]{2,1,0:T(8,128)(2,1)S(1)} collective-permute-done((bf16[48,8,128]{2,1,0:T(8,128)(2,1)}, bf16[48,8,128]{2,1,0:T(8,128)(2,1)S(1)}, u32[]{:S(2)}, u32[]{:S(2)}) %collective-permute-start.15) | collective-permute-done | bytes 98336 | tf_op jit(solution)/shard_map/ppermute | solution.py:572
  49.3 1.9 %sum_and_apply.1 = bf16[64,8,384]{2,1,0:T(8,128)(2,1)} custom-call(s32[16,128]{1,0:T(8,128)S(1)} %get-tuple-element.42.slots_ref, f32[128,3072]{1,0:T(8,128)S(1)} %get-tuple-element.43.gains_ref, f32[64,128]{1,0:T(8,128)S(1)} %get-tuple-element.44.recip_ref, f32[3,64,8,128]{3,2,1,0:T(8,128)S(1)} %sum_next.1.sums_ref, ...), custom_call_target="tpu_custom_call" | custom-call | tf_op jit(solution)/shard_map/sum_and_apply/pallas_call | solution.py:633
  (17 shorter events, 0.7 us)
Async XLA Ops:
  1.8 11.6 %collective-permute-start.11 = (bf16[48,8,128]{2,1,0:T(8,128)(2,1)}, bf16[48,8,128]{2,1,0:T(8,128)(2,1)S(1)}, u32[]{:S(2)}, u32[]{:S(2)}) collective-permute-start(bf16[48,8,128]{2,1,0:T(8,128)(2,1)} %pack_first.1), channel_id=1, source_target_pairs={{0,9},{1,8},{2,11},{3,10},{4,13},{5,12},{6,15},{7,14},{8,1},{9,0},... | collective-permute-start | bytes 294920 | tf_op jit(solution)/shard_map/ppermute | solution.py:572
  7.9 8.7 %collective-permute-start = (bf16[53,8,128]{2,1,0:T(8,128)(2,1)}, bf16[53,8,128]{2,1,0:T(8,128)(2,1)S(1)}, u32[]{:S(2)}, u32[]{:S(2)}) collective-permute-start(bf16[53,8,128]{2,1,0:T(8,128)(2,1)} %get-tuple-element.31), channel_id=1, source_target_pairs={{0,8},{1,9},{2,10},{3,11},{4,12},{5,13},{6,14},{7,15},{8,0},{9,1},... | collective-permute-start | bytes 325640 | tf_op jit(solution)/shard_map/ppermute | solution.py:572
  8.1 10.8 %collective-permute-start.1 = (bf16[53,8,128]{2,1,0:T(8,128)(2,1)}, bf16[53,8,128]{2,1,0:T(8,128)(2,1)S(1)}, u32[]{:S(2)}, u32[]{:S(2)}) collective-permute-start(bf16[53,8,128]{2,1,0:T(8,128)(2,1)} %get-tuple-element.32), channel_id=1, source_target_pairs={{0,10},{1,11},{2,8},{3,9},{4,14},{5,15},{6,12},{7,13},{8,2},{9,3},... | collective-permute-start | bytes 325640 | tf_op jit(solution)/shard_map/ppermute | solution.py:572
  11.4 10.6 %collective-permute-start.2 = (bf16[53,8,128]{2,1,0:T(8,128)(2,1)}, bf16[53,8,128]{2,1,0:T(8,128)(2,1)S(1)}, u32[]{:S(2)}, u32[]{:S(2)}) collective-permute-start(bf16[53,8,128]{2,1,0:T(8,128)(2,1)} %get-tuple-element.33), channel_id=1, source_target_pairs={{0,4},{1,5},{2,6},{3,7},{4,0},{5,1},{6,2},{7,3},{8,12},{9,13},{10,... | collective-permute-start | bytes 325640 | tf_op jit(solution)/shard_map/ppermute | solution.py:572
  11.5 11.3 %collective-permute-start.3 = (bf16[53,8,128]{2,1,0:T(8,128)(2,1)}, bf16[53,8,128]{2,1,0:T(8,128)(2,1)S(1)}, u32[]{:S(2)}, u32[]{:S(2)}) collective-permute-start(bf16[53,8,128]{2,1,0:T(8,128)(2,1)} %get-tuple-element.34), channel_id=1, source_target_pairs={{0,5},{1,4},{2,7},{3,6},{4,1},{5,0},{6,3},{7,2},{8,13},{9,12},{10,... | collective-permute-start | bytes 325640 | tf_op jit(solution)/shard_map/ppermute | solution.py:572
  13.4 13.2 %collective-permute-start.4 = (bf16[53,8,128]{2,1,0:T(8,128)(2,1)}, bf16[53,8,128]{2,1,0:T(8,128)(2,1)S(1)}, u32[]{:S(2)}, u32[]{:S(2)}) collective-permute-start(bf16[53,8,128]{2,1,0:T(8,128)(2,1)} %get-tuple-element.35), channel_id=1, source_target_pairs={{0,12},{1,13},{2,14},{3,15},{4,8},{5,9},{6,10},{7,11},{8,4},{9,5},... | collective-permute-start | bytes 325640 | tf_op jit(solution)/shard_map/ppermute | solution.py:572
  16.7 15.2 %collective-permute-start.5 = (bf16[53,8,128]{2,1,0:T(8,128)(2,1)}, bf16[53,8,128]{2,1,0:T(8,128)(2,1)S(1)}, u32[]{:S(2)}, u32[]{:S(2)}) collective-permute-start(bf16[53,8,128]{2,1,0:T(8,128)(2,1)} %get-tuple-element.36), channel_id=1, source_target_pairs={{0,14},{1,15},{2,12},{3,13},{4,10},{5,11},{6,8},{7,9},{8,6},{9,7},... | collective-permute-start | bytes 325640 | tf_op jit(solution)/shard_map/ppermute | solution.py:572
  18.9 14.5 %collective-permute-start.6 = (bf16[53,8,128]{2,1,0:T(8,128)(2,1)}, bf16[53,8,128]{2,1,0:T(8,128)(2,1)S(1)}, u32[]{:S(2)}, u32[]{:S(2)}) collective-permute-start(bf16[53,8,128]{2,1,0:T(8,128)(2,1)} %get-tuple-element.37), channel_id=1, source_target_pairs={{0,6},{1,7},{2,4},{3,5},{4,2},{5,3},{6,0},{7,1},{8,14},{9,15},{10,... | collective-permute-start | bytes 325640 | tf_op jit(solution)/shard_map/ppermute | solution.py:572
  21.9 11.4 %collective-permute-start.7 = (bf16[53,8,128]{2,1,0:T(8,128)(2,1)}, bf16[53,8,128]{2,1,0:T(8,128)(2,1)S(1)}, u32[]{:S(2)}, u32[]{:S(2)}) collective-permute-start(bf16[53,8,128]{2,1,0:T(8,128)(2,1)} %get-tuple-element.38), channel_id=1, source_target_pairs={{0,7},{1,6},{2,5},{3,4},{4,3},{5,2},{6,1},{7,0},{8,15},{9,14},{10,... | collective-permute-start | bytes 325640 | tf_op jit(solution)/shard_map/ppermute | solution.py:572
  22.9 11.4 %collective-permute-start.8 = (bf16[53,8,128]{2,1,0:T(8,128)(2,1)}, bf16[53,8,128]{2,1,0:T(8,128)(2,1)S(1)}, u32[]{:S(2)}, u32[]{:S(2)}) collective-permute-start(bf16[53,8,128]{2,1,0:T(8,128)(2,1)} %get-tuple-element.39), channel_id=1, source_target_pairs={{0,1},{1,0},{2,3},{3,2},{4,5},{5,4},{6,7},{7,6},{8,9},{9,8},{10,11... | collective-permute-start | bytes 325640 | tf_op jit(solution)/shard_map/ppermute | solution.py:572
  26.6 9.5 %collective-permute-start.9 = (bf16[53,8,128]{2,1,0:T(8,128)(2,1)}, bf16[53,8,128]{2,1,0:T(8,128)(2,1)S(1)}, u32[]{:S(2)}, u32[]{:S(2)}) collective-permute-start(bf16[53,8,128]{2,1,0:T(8,128)(2,1)} %get-tuple-element.40), channel_id=1, source_target_pairs={{0,2},{1,3},{2,0},{3,1},{4,6},{5,7},{6,4},{7,5},{8,10},{9,11},{10,... | collective-permute-start | bytes 325640 | tf_op jit(solution)/shard_map/ppermute | solution.py:572
  31.9 5.7 %collective-permute-start.10 = (bf16[53,8,128]{2,1,0:T(8,128)(2,1)}, bf16[53,8,128]{2,1,0:T(8,128)(2,1)S(1)}, u32[]{:S(2)}, u32[]{:S(2)}) collective-permute-start(bf16[53,8,128]{2,1,0:T(8,128)(2,1)} %get-tuple-element.41), channel_id=1, source_target_pairs={{0,3},{1,2},{2,1},{3,0},{4,7},{5,6},{6,5},{7,4},{8,11},{9,10},{10,... | collective-permute-start | bytes 325640 | tf_op jit(solution)/shard_map/ppermute | solution.py:572
  33.3 6.2 %collective-permute-start.13 = (bf16[48,8,128]{2,1,0:T(8,128)(2,1)}, bf16[48,8,128]{2,1,0:T(8,128)(2,1)S(1)}, u32[]{:S(2)}, u32[]{:S(2)}) collective-permute-start(bf16[48,8,128]{2,1,0:T(8,128)(2,1)} %get-tuple-element.46), channel_id=1, source_target_pairs={{0,11},{1,10},{2,9},{3,8},{4,15},{5,14},{6,13},{7,12},{8,3},{9,2},... | collective-permute-start | bytes 294920 | tf_op jit(solution)/shard_map/ppermute | solution.py:572
  33.4 12.8 %collective-permute-start.14 = (bf16[48,8,128]{2,1,0:T(8,128)(2,1)}, bf16[48,8,128]{2,1,0:T(8,128)(2,1)S(1)}, u32[]{:S(2)}, u32[]{:S(2)}) collective-permute-start(bf16[48,8,128]{2,1,0:T(8,128)(2,1)} %get-tuple-element.47), channel_id=1, source_target_pairs={{0,13},{1,12},{2,15},{3,14},{4,9},{5,8},{6,11},{7,10},{8,5},{9,4},... | collective-permute-start | bytes 294920 | tf_op jit(solution)/shard_map/ppermute | solution.py:572
  34.3 15.1 %collective-permute-start.15 = (bf16[48,8,128]{2,1,0:T(8,128)(2,1)}, bf16[48,8,128]{2,1,0:T(8,128)(2,1)S(1)}, u32[]{:S(2)}, u32[]{:S(2)}) collective-permute-start(bf16[48,8,128]{2,1,0:T(8,128)(2,1)} %get-tuple-element.48), channel_id=1, source_target_pairs={{0,15},{1,14},{2,13},{3,12},{4,11},{5,10},{6,9},{7,8},{8,7},{9,6},... | collective-permute-start | bytes 294920 | tf_op jit(solution)/shard_map/ppermute | solution.py:572
  36.1 1.5 %collective-permute-start.12 = (bf16[20,8,128]{2,1,0:T(8,128)(2,1)S(1)}, bf16[20,8,128]{2,1,0:T(8,128)(2,1)S(1)}, u32[]{:S(2)}, u32[]{:S(2)}) collective-permute-start(bf16[20,8,128]{2,1,0:T(8,128)(2,1)S(1)} %collect_gains.1), channel_id=1, source_target_pairs={{0,1},{1,0},{2,3},{3,2},{4,5},{5,4},{6,7},{7,6},{8,9},{9,8},{10,11... | collective-permute-start | bytes 122888 | tf_op jit(solution)/shard_map/ppermute | solution.py:572
  36.1 0.9 %copy-start = (bf16[62,8,128]{2,1,0:T(8,128)(2,1)S(1)}, bf16[62,8,128]{2,1,0:T(8,128)(2,1)}, u32[]{:S(2)}) copy-start(bf16[62,8,128]{2,1,0:T(8,128)(2,1)} %get-tuple-element.27.own_ref) | copy-start | bytes 380932

commit v16 on v14

--- a/solution.py
+++ b/solution.py
@@ -22,13 +22,12 @@
 def schedule(near):
     even, odd = list(range(near, 2 * near, 2)), list(range(near + 1, 2 * near, 2))
     close = list(range(near // 2, near)) + list(range(1, near // 2))
-    cross, late = even[2:] + odd[1:-2], odd[-2:]
     order = [0] + even[:2] + close[:2]
-    close = close[2:]
+    cross, close = even[2:], close[2:]
     while cross:
         order += cross[:1] + close[:1]
         cross, close = cross[1:], close[1:]
-    return order + close + odd[:1], late
+    return order + close[:1] + odd[1:-2] + close[1:] + odd[:1], odd[-2:]
 
 
 def with_gains(near):

time: 46.8 us -> 46.7 us (level)
  waiting for transfers between devices: 10.3 us -> 11.8 us
  Pallas kernels: 11.1 us -> 9.88 us
  starting transfers between devices: 24.4 us -> 23.9 us
    ppermute x16, waiting for transfers between devices: 10.3 us -> 11.8 us  [swap(): return lax.ppermute(array, 'bl', [(d, d ^ x) for d in range(devices)])]
    pallas_call x1, Pallas kernels: 2.66 us -> 1.74 us  [on_device(): pl.pallas_call(functools.partial(middle_kernel, capacity, near, depth, or...]
  transfers between devices with their start and end apart: 16 -> 16, of which waited for: 6 -> 6; matrix products, arithmetic and copies ran while one was open for 0% -> 0% of each run, Pallas kernels for 16% -> 13%
where the time goes in v16:
time: 46.7 us; the launch traced here: 46.6 us
  starting transfers between devices  23.9 us (51%)
  waiting for transfers between devices  11.8 us (25%)
  Pallas kernels  9.88 us (21%)
  local copies, waits for them, and re-layouts  0.9 us (2%)
    ppermute x16, starting transfers between devices, swap(): return lax.ppermute(array, 'bl', [(d, d ^ x) for d in range(devices)])  23.9 us
    ppermute x16, waiting for transfers between devices, swap(): return lax.ppermute(array, 'bl', [(d, d ^ x) for d in range(devices)])  11.8 us
    pallas_call x1, Pallas kernels, on_device(): pl.pallas_call(functools.partial(pack_kernel, capacity, near), out_shape=...  3.2 us
    pallas_call x1, Pallas kernels, on_device(): pl.pallas_call(functools.partial(finish_kernel, capacity, last), out_shap...  1.85 us
    pallas_call x1, Pallas kernels, on_device(): pl.pallas_call(functools.partial(first_kernel, capacity, near + 1), out_s...  1.78 us
    pallas_call x1, Pallas kernels, on_device(): pl.pallas_call(functools.partial(middle_kernel, capacity, near, depth, or...  1.74 us
  transfers between devices with their start and end apart: 16, of which 6 were waited for; matrix products, arithmetic and copies ran while one was open for 0% of the time, Pallas kernels for 13%

profile of v16, /device:TPU:0, one launch (start us, length us, event | category | flops | bytes accessed | tf_op | source)
XLA Modules:
  0.0 46.6 jit_solution(18425121599059126113)
XLA Ops:
  0.0 1.8 %pack_first.1 = bf16[48,8,128]{2,1,0:T(8,128)(2,1)} custom-call(s32[1]{0:T(128)} %bitcast.me_s.turn_s, s32[128]{0:T(128)} %bitcast.12, bf16[128,8,384]{2,1,0:T(8,128)(2,1)} %vis_hbm.3), custom_call_target="tpu_custom_call" | custom-call | tf_op jit(solution)/shard_map/pack_first/pallas_call | solution.py:500
  1.8 3.5 %collective-permute-start.12 = (bf16[48,8,128]{2,1,0:T(8,128)(2,1)}, bf16[48,8,128]{2,1,0:T(8,128)(2,1)S(1)}, u32[]{:S(2)}, u32[]{:S(2)}) collective-permute-start(bf16[48,8,128]{2,1,0:T(8,128)(2,1)} %pack_first.1), channel_id=1, source_target_pairs={{0,9},{1,8},{2,11},{3,10},{4,13},{5,12},{6,15},{7,14},{8,1},{9,0},... | collective-permute-start | bytes 294920 | tf_op jit(solution)/shard_map/ppermute | solution.py:575
  5.3 3.2 %pack_rows.1 = (bf16[62,8,128]{2,1,0:T(8,128)(2,1)}, bf16[53,8,128]{2,1,0:T(8,128)(2,1)}, bf16[53,8,128]{2,1,0:T(8,128)(2,1)}, bf16[53,8,128]{2,1,0:T(8,128)(2,1...) custom-call(s32[1]{0:T(128)} %bitcast.me_s.turn_s, ...), custom_call_target="tpu_custom_call" | custom-call | tf_op jit(solution)/shard_map/pack_rows/pallas_call | solution.py:515
  8.5 0.7 %collective-permute-start = (bf16[53,8,128]{2,1,0:T(8,128)(2,1)}, bf16[53,8,128]{2,1,0:T(8,128)(2,1)S(1)}, u32[]{:S(2)}, u32[]{:S(2)}) collective-permute-start(bf16[53,8,128]{2,1,0:T(8,128)(2,1)} %get-tuple-element.31), channel_id=1, source_target_pairs={{0,8},{1,9},{2,10},{3,11},{4,12},{5,13},{6,14},{7,15},{8,0},{9,1},... | collective-permute-start | bytes 325640 | tf_op jit(solution)/shard_map/ppermute | solution.py:575
  9.2 3.3 %collective-permute-start.1 = (bf16[53,8,128]{2,1,0:T(8,128)(2,1)}, bf16[53,8,128]{2,1,0:T(8,128)(2,1)S(1)}, u32[]{:S(2)}, u32[]{:S(2)}) collective-permute-start(bf16[53,8,128]{2,1,0:T(8,128)(2,1)} %get-tuple-element.32), channel_id=1, source_target_pairs={{0,10},{1,11},{2,8},{3,9},{4,14},{5,15},{6,12},{7,13},{8,2},{9,3},... | collective-permute-start | bytes 325640 | tf_op jit(solution)/shard_map/ppermute | solution.py:575
  12.5 1.6 %collective-permute-start.2 = (bf16[53,8,128]{2,1,0:T(8,128)(2,1)}, bf16[53,8,128]{2,1,0:T(8,128)(2,1)S(1)}, u32[]{:S(2)}, u32[]{:S(2)}) collective-permute-start(bf16[53,8,128]{2,1,0:T(8,128)(2,1)} %get-tuple-element.33), channel_id=1, source_target_pairs={{0,4},{1,5},{2,6},{3,7},{4,0},{5,1},{6,2},{7,3},{8,12},{9,13},{10,... | collective-permute-start | bytes 325640 | tf_op jit(solution)/shard_map/ppermute | solution.py:575
  14.1 3.4 %collective-permute-start.4 = (bf16[53,8,128]{2,1,0:T(8,128)(2,1)}, bf16[53,8,128]{2,1,0:T(8,128)(2,1)S(1)}, u32[]{:S(2)}, u32[]{:S(2)}) collective-permute-start(bf16[53,8,128]{2,1,0:T(8,128)(2,1)} %get-tuple-element.35), channel_id=1, source_target_pairs={{0,12},{1,13},{2,14},{3,15},{4,8},{5,9},{6,10},{7,11},{8,4},{9,5},... | collective-permute-start | bytes 325640 | tf_op jit(solution)/shard_map/ppermute | solution.py:575
  17.5 2.9 %collective-permute-done.rest_0_.rest_1_ = bf16[53,8,128]{2,1,0:T(8,128)(2,1)S(1)} collective-permute-done((bf16[53,8,128]{2,1,0:T(8,128)(2,1)}, bf16[53,8,128]{2,1,0:T(8,128)(2,1)S(1)}, u32[]{:S(2)}, u32[]{:S(2)}) %collective-permute-start) | collective-permute-done | bytes 108576 | tf_op jit(solution)/shard_map/ppermute | solution.py:575
  20.4 3.2 %collective-permute-done.1.rest_1_.rest_2_ = bf16[53,8,128]{2,1,0:T(8,128)(2,1)S(1)} collective-permute-done((bf16[53,8,128]{2,1,0:T(8,128)(2,1)}, bf16[53,8,128]{2,1,0:T(8,128)(2,1)S(1)}, u32[]{:S(2)}, u32[]{:S(2)}) %collective-permute-start.1) | collective-permute-done | bytes 108576 | tf_op jit(solution)/shard_map/ppermute | solution.py:575
  23.6 2.2 %collective-permute-start.6 = (bf16[53,8,128]{2,1,0:T(8,128)(2,1)}, bf16[53,8,128]{2,1,0:T(8,128)(2,1)S(1)}, u32[]{:S(2)}, u32[]{:S(2)}) collective-permute-start(bf16[53,8,128]{2,1,0:T(8,128)(2,1)} %get-tuple-element.37), channel_id=1, source_target_pairs={{0,14},{1,15},{2,12},{3,13},{4,10},{5,11},{6,8},{7,9},{8,6},{9,7},... | collective-permute-start | bytes 325640 | tf_op jit(solution)/shard_map/ppermute | solution.py:575
  25.8 0.4 collective-permute-start.8
  26.2 2.7 %collective-permute-start.9 = (bf16[53,8,128]{2,1,0:T(8,128)(2,1)}, bf16[53,8,128]{2,1,0:T(8,128)(2,1)S(1)}, u32[]{:S(2)}, u32[]{:S(2)}) collective-permute-start(bf16[53,8,128]{2,1,0:T(8,128)(2,1)} %get-tuple-element.40), channel_id=1, source_target_pairs={{0,11},{1,10},{2,9},{3,8},{4,15},{5,14},{6,13},{7,12},{8,3},{9,2},... | collective-permute-start | bytes 325640 | tf_op jit(solution)/shard_map/ppermute | solution.py:575
  28.9 2.4 %collective-permute-start.10 = (bf16[53,8,128]{2,1,0:T(8,128)(2,1)}, bf16[53,8,128]{2,1,0:T(8,128)(2,1)S(1)}, u32[]{:S(2)}, u32[]{:S(2)}) collective-permute-start(bf16[53,8,128]{2,1,0:T(8,128)(2,1)} %get-tuple-element.41), channel_id=1, source_target_pairs={{0,2},{1,3},{2,0},{3,1},{4,6},{5,7},{6,4},{7,5},{8,10},{9,11},{10,... | collective-permute-start | bytes 325640 | tf_op jit(solution)/shard_map/ppermute | solution.py:575
  31.2 1.2 %collective-permute-done.6.rest_3_.rest_7_ = bf16[53,8,128]{2,1,0:T(8,128)(2,1)S(1)} collective-permute-done((bf16[53,8,128]{2,1,0:T(8,128)(2,1)}, bf16[53,8,128]{2,1,0:T(8,128)(2,1)S(1)}, u32[]{:S(2)}, u32[]{:S(2)}) %collective-permute-start.6) | collective-permute-done | bytes 108576 | tf_op jit(solution)/shard_map/ppermute | solution.py:575
  32.5 2.5 %collective-permute-done.7.rest_8_ = bf16[53,8,128]{2,1,0:T(8,128)(2,1)S(1)} collective-permute-done((bf16[53,8,128]{2,1,0:T(8,128)(2,1)}, bf16[53,8,128]{2,1,0:T(8,128)(2,1)S(1)}, u32[]{:S(2)}, u32[]{:S(2)}) %collective-permute-start.7) | collective-permute-done | bytes 108576 | tf_op jit(solution)/shard_map/ppermute | solution.py:575
  35.0 1.9 %collective-permute-start.14 = (bf16[48,8,128]{2,1,0:T(8,128)(2,1)}, bf16[48,8,128]{2,1,0:T(8,128)(2,1)S(1)}, u32[]{:S(2)}, u32[]{:S(2)}) collective-permute-start(bf16[48,8,128]{2,1,0:T(8,128)(2,1)} %get-tuple-element.47), channel_id=1, source_target_pairs={{0,13},{1,12},{2,15},{3,14},{4,9},{5,8},{6,11},{7,10},{8,5},{9,4},... | collective-permute-start | bytes 294920 | tf_op jit(solution)/shard_map/ppermute | solution.py:575
  36.9 1.7 %collective-permute-start.15 = (bf16[48,8,128]{2,1,0:T(8,128)(2,1)}, bf16[48,8,128]{2,1,0:T(8,128)(2,1)S(1)}, u32[]{:S(2)}, u32[]{:S(2)}) collective-permute-start(bf16[48,8,128]{2,1,0:T(8,128)(2,1)} %get-tuple-element.48), channel_id=1, source_target_pairs={{0,15},{1,14},{2,13},{3,12},{4,11},{5,10},{6,9},{7,8},{8,7},{9,6},... | collective-permute-start | bytes 294920 | tf_op jit(solution)/shard_map/ppermute | solution.py:575
  38.9 0.9 %copy-done = bf16[62,8,128]{2,1,0:T(8,128)(2,1)S(1)} copy-done((bf16[62,8,128]{2,1,0:T(8,128)(2,1)S(1)}, bf16[62,8,128]{2,1,0:T(8,128)(2,1)}, u32[]{:S(2)}) %copy-start) | copy-done | bytes 127000
  39.8 0.5 %make_ready.1 = (bf16[62,8,128]{2,1,0:T(8,128)(2,1)S(1)}, bf16[256,256]{1,0:T(8,128)(2,1)S(1)}, bf16[256,3072]{1,0:T(8,128)(2,1)S(1)}) custom-call(s32[1]{0:T(128)} %bitcast.me_s.turn_s, bf16[62,8,128]{2,1,0:T(8,128)(2,1)S(1)} %copy-done), custom_call_target="tpu_custom_call" | custom-call | tf_op jit(solution)/shard_map/make_ready/pallas_call | solution.py:556
  40.3 0.3 collective-permute-done.11.rest_12_
  40.6 1.7 %gains_and_sums.1 = (f32[128,3072]{1,0:T(8,128)S(1)}, f32[64,128]{1,0:T(8,128)S(1)}, s32[16,128]{1,0:T(8,128)S(1)}, f32[3,64,8,128]{3,2,1,0:T(8,128)S(1)}) custom-call(s32[1]{0:T(128)} %bitcast.me_s.turn_s, bf16[256,256]{1,0:T(8,128)(2,1)S(1)} %get-tuple-element.28.choice_ref, bf16[256,3072]{1,0:T(8,128)(2,1)S(1)} %get-tuple-element.29.basis_ref, ...), custom_call_target="tpu_custom_call" | custom-call | tf_op jit(solution)/shard_map/gains_and_sums/pallas_call | solution.py:600
  42.4 0.7 %sum_next.1.sums_ref = f32[3,64,8,128]{3,2,1,0:T(8,128)S(1)} custom-call(s32[16,128]{1,0:T(8,128)S(1)} %get-tuple-element.43.slots_ref, f32[3,64,8,128]{3,2,1,0:T(8,128)S(1)} %get-tuple-element.46.sums_ref, bf16[48,8,128]{2,1,0:T(8,128)(2,1)S(1)} %collective-permute-done.14.rows_ref), custom_call_target="tpu_custom_call" | custom-call | tf_op jit(solution)/shard_map/sum_next/pallas_call | solution.py:625
  43.1 1.6 %collective-permute-done.15.rest_0_ = bf16[48,8,128]{2,1,0:T(8,128)(2,1)S(1)} collective-permute-done((bf16[48,8,128]{2,1,0:T(8,128)(2,1)}, bf16[48,8,128]{2,1,0:T(8,128)(2,1)S(1)}, u32[]{:S(2)}, u32[]{:S(2)}) %collective-permute-start.15) | collective-permute-done | bytes 98336 | tf_op jit(solution)/shard_map/ppermute | solution.py:575
  44.7 1.8 %sum_and_apply.1 = bf16[64,8,384]{2,1,0:T(8,128)(2,1)} custom-call(s32[16,128]{1,0:T(8,128)S(1)} %get-tuple-element.43.slots_ref, f32[128,3072]{1,0:T(8,128)S(1)} %get-tuple-element.44.gains_ref, f32[64,128]{1,0:T(8,128)S(1)} %get-tuple-element.45.recip_ref, f32[3,64,8,128]{3,2,1,0:T(8,128)S(1)} %sum_next.1.sums_ref, ...), custom_call_target="tpu_custom_call" | custom-call | tf_op jit(solution)/shard_map/sum_and_apply/pallas_call | solution.py:636
  (17 shorter events, 0.3 us)
Async XLA Ops:
  1.8 12.3 %collective-permute-start.12 = (bf16[48,8,128]{2,1,0:T(8,128)(2,1)}, bf16[48,8,128]{2,1,0:T(8,128)(2,1)S(1)}, u32[]{:S(2)}, u32[]{:S(2)}) collective-permute-start(bf16[48,8,128]{2,1,0:T(8,128)(2,1)} %pack_first.1), channel_id=1, source_target_pairs={{0,9},{1,8},{2,11},{3,10},{4,13},{5,12},{6,15},{7,14},{8,1},{9,0},... | collective-permute-start | bytes 294920 | tf_op jit(solution)/shard_map/ppermute | solution.py:575
  8.5 11.8 %collective-permute-start = (bf16[53,8,128]{2,1,0:T(8,128)(2,1)}, bf16[53,8,128]{2,1,0:T(8,128)(2,1)S(1)}, u32[]{:S(2)}, u32[]{:S(2)}) collective-permute-start(bf16[53,8,128]{2,1,0:T(8,128)(2,1)} %get-tuple-element.31), channel_id=1, source_target_pairs={{0,8},{1,9},{2,10},{3,11},{4,12},{5,13},{6,14},{7,15},{8,0},{9,1},... | collective-permute-start | bytes 325640 | tf_op jit(solution)/shard_map/ppermute | solution.py:575
  9.2 14.4 %collective-permute-start.1 = (bf16[53,8,128]{2,1,0:T(8,128)(2,1)}, bf16[53,8,128]{2,1,0:T(8,128)(2,1)S(1)}, u32[]{:S(2)}, u32[]{:S(2)}) collective-permute-start(bf16[53,8,128]{2,1,0:T(8,128)(2,1)} %get-tuple-element.32), channel_id=1, source_target_pairs={{0,10},{1,11},{2,8},{3,9},{4,14},{5,15},{6,12},{7,13},{8,2},{9,3},... | collective-permute-start | bytes 325640 | tf_op jit(solution)/shard_map/ppermute | solution.py:575
  12.5 13.3 %collective-permute-start.2 = (bf16[53,8,128]{2,1,0:T(8,128)(2,1)}, bf16[53,8,128]{2,1,0:T(8,128)(2,1)S(1)}, u32[]{:S(2)}, u32[]{:S(2)}) collective-permute-start(bf16[53,8,128]{2,1,0:T(8,128)(2,1)} %get-tuple-element.33), channel_id=1, source_target_pairs={{0,4},{1,5},{2,6},{3,7},{4,0},{5,1},{6,2},{7,3},{8,12},{9,13},{10,... | collective-permute-start | bytes 325640 | tf_op jit(solution)/shard_map/ppermute | solution.py:575
  14.1 11.7 %collective-permute-start.3 = (bf16[53,8,128]{2,1,0:T(8,128)(2,1)}, bf16[53,8,128]{2,1,0:T(8,128)(2,1)S(1)}, u32[]{:S(2)}, u32[]{:S(2)}) collective-permute-start(bf16[53,8,128]{2,1,0:T(8,128)(2,1)} %get-tuple-element.34), channel_id=1, source_target_pairs={{0,5},{1,4},{2,7},{3,6},{4,1},{5,0},{6,3},{7,2},{8,13},{9,12},{10,... | collective-permute-start | bytes 325640 | tf_op jit(solution)/shard_map/ppermute | solution.py:575
  14.1 12.1 %collective-permute-start.4 = (bf16[53,8,128]{2,1,0:T(8,128)(2,1)}, bf16[53,8,128]{2,1,0:T(8,128)(2,1)S(1)}, u32[]{:S(2)}, u32[]{:S(2)}) collective-permute-start(bf16[53,8,128]{2,1,0:T(8,128)(2,1)} %get-tuple-element.35), channel_id=1, source_target_pairs={{0,12},{1,13},{2,14},{3,15},{4,8},{5,9},{6,10},{7,11},{8,4},{9,5},... | collective-permute-start | bytes 325640 | tf_op jit(solution)/shard_map/ppermute | solution.py:575
  20.4 8.5 %collective-permute-start.5 = (bf16[53,8,128]{2,1,0:T(8,128)(2,1)}, bf16[53,8,128]{2,1,0:T(8,128)(2,1)S(1)}, u32[]{:S(2)}, u32[]{:S(2)}) collective-permute-start(bf16[53,8,128]{2,1,0:T(8,128)(2,1)} %get-tuple-element.36), channel_id=1, source_target_pairs={{0,6},{1,7},{2,4},{3,5},{4,2},{5,3},{6,0},{7,1},{8,14},{9,15},{10,... | collective-permute-start | bytes 325640 | tf_op jit(solution)/shard_map/ppermute | solution.py:575
  23.6 8.9 %collective-permute-start.6 = (bf16[53,8,128]{2,1,0:T(8,128)(2,1)}, bf16[53,8,128]{2,1,0:T(8,128)(2,1)S(1)}, u32[]{:S(2)}, u32[]{:S(2)}) collective-permute-start(bf16[53,8,128]{2,1,0:T(8,128)(2,1)} %get-tuple-element.37), channel_id=1, source_target_pairs={{0,14},{1,15},{2,12},{3,13},{4,10},{5,11},{6,8},{7,9},{8,6},{9,7},... | collective-permute-start | bytes 325640 | tf_op jit(solution)/shard_map/ppermute | solution.py:575
  25.8 9.2 %collective-permute-start.7 = (bf16[53,8,128]{2,1,0:T(8,128)(2,1)}, bf16[53,8,128]{2,1,0:T(8,128)(2,1)S(1)}, u32[]{:S(2)}, u32[]{:S(2)}) collective-permute-start(bf16[53,8,128]{2,1,0:T(8,128)(2,1)} %get-tuple-element.38), channel_id=1, source_target_pairs={{0,7},{1,6},{2,5},{3,4},{4,3},{5,2},{6,1},{7,0},{8,15},{9,14},{10,... | collective-permute-start | bytes 325640 | tf_op jit(solution)/shard_map/ppermute | solution.py:575
  25.8 11.1 %collective-permute-start.8 = (bf16[53,8,128]{2,1,0:T(8,128)(2,1)}, bf16[53,8,128]{2,1,0:T(8,128)(2,1)S(1)}, u32[]{:S(2)}, u32[]{:S(2)}) collective-permute-start(bf16[53,8,128]{2,1,0:T(8,128)(2,1)} %get-tuple-element.39), channel_id=1, source_target_pairs={{0,1},{1,0},{2,3},{3,2},{4,5},{5,4},{6,7},{7,6},{8,9},{9,8},{10,11... | collective-permute-start | bytes 325640 | tf_op jit(solution)/shard_map/ppermute | solution.py:575
  26.2 12.5 %collective-permute-start.9 = (bf16[53,8,128]{2,1,0:T(8,128)(2,1)}, bf16[53,8,128]{2,1,0:T(8,128)(2,1)S(1)}, u32[]{:S(2)}, u32[]{:S(2)}) collective-permute-start(bf16[53,8,128]{2,1,0:T(8,128)(2,1)} %get-tuple-element.40), channel_id=1, source_target_pairs={{0,11},{1,10},{2,9},{3,8},{4,15},{5,14},{6,13},{7,12},{8,3},{9,2},... | collective-permute-start | bytes 325640 | tf_op jit(solution)/shard_map/ppermute | solution.py:575
  28.9 11.4 %collective-permute-start.10 = (bf16[53,8,128]{2,1,0:T(8,128)(2,1)}, bf16[53,8,128]{2,1,0:T(8,128)(2,1)S(1)}, u32[]{:S(2)}, u32[]{:S(2)}) collective-permute-start(bf16[53,8,128]{2,1,0:T(8,128)(2,1)} %get-tuple-element.41), channel_id=1, source_target_pairs={{0,2},{1,3},{2,0},{3,1},{4,6},{5,7},{6,4},{7,5},{8,10},{9,11},{10,... | collective-permute-start | bytes 325640 | tf_op jit(solution)/shard_map/ppermute | solution.py:575
  32.5 8.2 %collective-permute-start.11 = (bf16[53,8,128]{2,1,0:T(8,128)(2,1)}, bf16[53,8,128]{2,1,0:T(8,128)(2,1)S(1)}, u32[]{:S(2)}, u32[]{:S(2)}) collective-permute-start(bf16[53,8,128]{2,1,0:T(8,128)(2,1)} %get-tuple-element.42), channel_id=1, source_target_pairs={{0,3},{1,2},{2,1},{3,0},{4,7},{5,6},{6,5},{7,4},{8,11},{9,10},{10,... | collective-permute-start | bytes 325640 | tf_op jit(solution)/shard_map/ppermute | solution.py:575
  35.0 7.4 %collective-permute-start.14 = (bf16[48,8,128]{2,1,0:T(8,128)(2,1)}, bf16[48,8,128]{2,1,0:T(8,128)(2,1)S(1)}, u32[]{:S(2)}, u32[]{:S(2)}) collective-permute-start(bf16[48,8,128]{2,1,0:T(8,128)(2,1)} %get-tuple-element.47), channel_id=1, source_target_pairs={{0,13},{1,12},{2,15},{3,14},{4,9},{5,8},{6,11},{7,10},{8,5},{9,4},... | collective-permute-start | bytes 294920 | tf_op jit(solution)/shard_map/ppermute | solution.py:575
  36.9 7.8 %collective-permute-start.15 = (bf16[48,8,128]{2,1,0:T(8,128)(2,1)}, bf16[48,8,128]{2,1,0:T(8,128)(2,1)S(1)}, u32[]{:S(2)}, u32[]{:S(2)}) collective-permute-start(bf16[48,8,128]{2,1,0:T(8,128)(2,1)} %get-tuple-element.48), channel_id=1, source_target_pairs={{0,15},{1,14},{2,13},{3,12},{4,11},{5,10},{6,9},{7,8},{8,7},{9,6},... | collective-permute-start | bytes 294920 | tf_op jit(solution)/shard_map/ppermute | solution.py:575
  38.7 1.9 %collective-permute-start.13 = (bf16[20,8,128]{2,1,0:T(8,128)(2,1)S(1)}, bf16[20,8,128]{2,1,0:T(8,128)(2,1)S(1)}, u32[]{:S(2)}, u32[]{:S(2)}) collective-permute-start(bf16[20,8,128]{2,1,0:T(8,128)(2,1)S(1)} %collect_gains.1), channel_id=1, source_target_pairs={{0,1},{1,0},{2,3},{3,2},{4,5},{5,4},{6,7},{7,6},{8,9},{9,8},{10,11... | collective-permute-start | bytes 122888 | tf_op jit(solution)/shard_map/ppermute | solution.py:575
  38.9 0.9 %copy-start = (bf16[62,8,128]{2,1,0:T(8,128)(2,1)S(1)}, bf16[62,8,128]{2,1,0:T(8,128)(2,1)}, u32[]{:S(2)}) copy-start(bf16[62,8,128]{2,1,0:T(8,128)(2,1)} %get-tuple-element.27.own_ref) | copy-start | bytes 380932

commit v17 on v16

--- a/solution.py
+++ b/solution.py
@@ -114,7 +114,7 @@
         place_s[r] = x * capacity + k
         return carry
 
-    lax.fori_loop(0, rows, rank, 0, unroll=8)
+    lax.fori_loop(0, rows, rank, 0, unroll=32)
     for move in moves[1:]:
         move.wait()
 
@@ -164,7 +164,7 @@
     flat_ref = block_ref.reshape(devices * at, SUB, LANES)
     for i in range(PARTS):
         fetches[i].wait()
-        lax.fori_loop(i * span, (i + 1) * span, place, 0, unroll=8)
+        lax.fori_loop(i * span, (i + 1) * span, place, 0, unroll=32)
     if near > 1:
         pairs = [
             (block_ref.at[x], outs[x].at[pl.ds(0, at)]) for x in range(devices) if x != near + 1
@@ -187,7 +187,7 @@
         list_s[k] = r
         return k + jnp.where(owner_s[r] == wanted, 1, 0)
 
-    count = lax.fori_loop(0, rows, note, 0, unroll=8)
+    count = lax.fori_loop(0, rows, note, 0, unroll=32)
     moves[1].wait()
 
     def place(k, carry):

time: 46.7 us -> 46.9 us (level)
  transfers between devices with their start and end apart: 16 -> 16, of which waited for: 6 -> 6; matrix products, arithmetic and copies ran while one was open for 0% -> 0% of each run, Pallas kernels for 13% -> 14%
where the time goes in v17:
time: 46.9 us; the launch traced here: 46.7 us
  starting transfers between devices  24.1 us (51%)
  waiting for transfers between devices  11.6 us (25%)
  Pallas kernels  10 us (21%)
  local copies, waits for them, and re-layouts  0.9 us (2%)
    ppermute x16, starting transfers between devices, swap(): return lax.ppermute(array, 'bl', [(d, d ^ x) for d in range(devices)])  24.1 us
    ppermute x16, waiting for transfers between devices, swap(): return lax.ppermute(array, 'bl', [(d, d ^ x) for d in range(devices)])  11.6 us
    pallas_call x1, Pallas kernels, on_device(): pl.pallas_call(functools.partial(pack_kernel, capacity, near), out_shape=...  3.04 us
    pallas_call x1, Pallas kernels, on_device(): pl.pallas_call(functools.partial(middle_kernel, capacity, near, depth, or...  1.94 us
    pallas_call x1, Pallas kernels, on_device(): pl.pallas_call(functools.partial(finish_kernel, capacity, last), out_shap...  1.91 us
    pallas_call x1, Pallas kernels, on_device(): pl.pallas_call(functools.partial(first_kernel, capacity, near + 1), out_s...  1.79 us
  transfers between devices with their start and end apart: 16, of which 6 were waited for; matrix products, arithmetic and copies ran while one was open for 0% of the time, Pallas kernels for 14%

profile of v17, /device:TPU:0, one launch (start us, length us, event | category | flops | bytes accessed | tf_op | source)
XLA Modules:
  0.0 46.7 jit_solution(15715816929155217705)
XLA Ops:
  0.0 1.8 %pack_first.1 = bf16[48,8,128]{2,1,0:T(8,128)(2,1)} custom-call(s32[1]{0:T(128)} %bitcast.me_s.turn_s, s32[128]{0:T(128)} %bitcast.12, bf16[128,8,384]{2,1,0:T(8,128)(2,1)} %vis_hbm.3), custom_call_target="tpu_custom_call" | custom-call | tf_op jit(solution)/shard_map/pack_first/pallas_call | solution.py:500
  1.8 3.5 %collective-permute-start.12 = (bf16[48,8,128]{2,1,0:T(8,128)(2,1)}, bf16[48,8,128]{2,1,0:T(8,128)(2,1)S(1)}, u32[]{:S(2)}, u32[]{:S(2)}) collective-permute-start(bf16[48,8,128]{2,1,0:T(8,128)(2,1)} %pack_first.1), channel_id=1, source_target_pairs={{0,9},{1,8},{2,11},{3,10},{4,13},{5,12},{6,15},{7,14},{8,1},{9,0},... | collective-permute-start | bytes 294920 | tf_op jit(solution)/shard_map/ppermute | solution.py:575
  5.3 3.0 %pack_rows.1 = (bf16[62,8,128]{2,1,0:T(8,128)(2,1)}, bf16[53,8,128]{2,1,0:T(8,128)(2,1)}, bf16[53,8,128]{2,1,0:T(8,128)(2,1)}, bf16[53,8,128]{2,1,0:T(8,128)(2,1...) custom-call(s32[1]{0:T(128)} %bitcast.me_s.turn_s, ...), custom_call_target="tpu_custom_call" | custom-call | tf_op jit(solution)/shard_map/pack_rows/pallas_call | solution.py:515
  8.4 0.7 %collective-permute-start = (bf16[53,8,128]{2,1,0:T(8,128)(2,1)}, bf16[53,8,128]{2,1,0:T(8,128)(2,1)S(1)}, u32[]{:S(2)}, u32[]{:S(2)}) collective-permute-start(bf16[53,8,128]{2,1,0:T(8,128)(2,1)} %get-tuple-element.31), channel_id=1, source_target_pairs={{0,8},{1,9},{2,10},{3,11},{4,12},{5,13},{6,14},{7,15},{8,0},{9,1},... | collective-permute-start | bytes 325640 | tf_op jit(solution)/shard_map/ppermute | solution.py:575
  9.0 3.3 %collective-permute-start.1 = (bf16[53,8,128]{2,1,0:T(8,128)(2,1)}, bf16[53,8,128]{2,1,0:T(8,128)(2,1)S(1)}, u32[]{:S(2)}, u32[]{:S(2)}) collective-permute-start(bf16[53,8,128]{2,1,0:T(8,128)(2,1)} %get-tuple-element.32), channel_id=1, source_target_pairs={{0,10},{1,11},{2,8},{3,9},{4,14},{5,15},{6,12},{7,13},{8,2},{9,3},... | collective-permute-start | bytes 325640 | tf_op jit(solution)/shard_map/ppermute | solution.py:575
  12.4 1.6 %collective-permute-start.2 = (bf16[53,8,128]{2,1,0:T(8,128)(2,1)}, bf16[53,8,128]{2,1,0:T(8,128)(2,1)S(1)}, u32[]{:S(2)}, u32[]{:S(2)}) collective-permute-start(bf16[53,8,128]{2,1,0:T(8,128)(2,1)} %get-tuple-element.33), channel_id=1, source_target_pairs={{0,4},{1,5},{2,6},{3,7},{4,0},{5,1},{6,2},{7,3},{8,12},{9,13},{10,... | collective-permute-start | bytes 325640 | tf_op jit(solution)/shard_map/ppermute | solution.py:575
  14.0 3.6 %collective-permute-start.4 = (bf16[53,8,128]{2,1,0:T(8,128)(2,1)}, bf16[53,8,128]{2,1,0:T(8,128)(2,1)S(1)}, u32[]{:S(2)}, u32[]{:S(2)}) collective-permute-start(bf16[53,8,128]{2,1,0:T(8,128)(2,1)} %get-tuple-element.35), channel_id=1, source_target_pairs={{0,12},{1,13},{2,14},{3,15},{4,8},{5,9},{6,10},{7,11},{8,4},{9,5},... | collective-permute-start | bytes 325640 | tf_op jit(solution)/shard_map/ppermute | solution.py:575
  17.5 2.7 %collective-permute-done.rest_0_.rest_1_ = bf16[53,8,128]{2,1,0:T(8,128)(2,1)S(1)} collective-permute-done((bf16[53,8,128]{2,1,0:T(8,128)(2,1)}, bf16[53,8,128]{2,1,0:T(8,128)(2,1)S(1)}, u32[]{:S(2)}, u32[]{:S(2)}) %collective-permute-start) | collective-permute-done | bytes 108576 | tf_op jit(solution)/shard_map/ppermute | solution.py:575
  20.2 0.2 collective-permute-start.5
  20.4 3.1 %collective-permute-done.1.rest_1_.rest_2_ = bf16[53,8,128]{2,1,0:T(8,128)(2,1)S(1)} collective-permute-done((bf16[53,8,128]{2,1,0:T(8,128)(2,1)}, bf16[53,8,128]{2,1,0:T(8,128)(2,1)S(1)}, u32[]{:S(2)}, u32[]{:S(2)}) %collective-permute-start.1) | collective-permute-done | bytes 108576 | tf_op jit(solution)/shard_map/ppermute | solution.py:575
  23.5 2.5 %collective-permute-start.6 = (bf16[53,8,128]{2,1,0:T(8,128)(2,1)}, bf16[53,8,128]{2,1,0:T(8,128)(2,1)S(1)}, u32[]{:S(2)}, u32[]{:S(2)}) collective-permute-start(bf16[53,8,128]{2,1,0:T(8,128)(2,1)} %get-tuple-element.37), channel_id=1, source_target_pairs={{0,14},{1,15},{2,12},{3,13},{4,10},{5,11},{6,8},{7,9},{8,6},{9,7},... | collective-permute-start | bytes 325640 | tf_op jit(solution)/shard_map/ppermute | solution.py:575
  26.1 2.8 %collective-permute-start.9 = (bf16[53,8,128]{2,1,0:T(8,128)(2,1)}, bf16[53,8,128]{2,1,0:T(8,128)(2,1)S(1)}, u32[]{:S(2)}, u32[]{:S(2)}) collective-permute-start(bf16[53,8,128]{2,1,0:T(8,128)(2,1)} %get-tuple-element.40), channel_id=1, source_target_pairs={{0,11},{1,10},{2,9},{3,8},{4,15},{5,14},{6,13},{7,12},{8,3},{9,2},... | collective-permute-start | bytes 325640 | tf_op jit(solution)/shard_map/ppermute | solution.py:575
  28.9 1.9 %collective-permute-start.10 = (bf16[53,8,128]{2,1,0:T(8,128)(2,1)}, bf16[53,8,128]{2,1,0:T(8,128)(2,1)S(1)}, u32[]{:S(2)}, u32[]{:S(2)}) collective-permute-start(bf16[53,8,128]{2,1,0:T(8,128)(2,1)} %get-tuple-element.41), channel_id=1, source_target_pairs={{0,2},{1,3},{2,0},{3,1},{4,6},{5,7},{6,4},{7,5},{8,10},{9,11},{10,... | collective-permute-start | bytes 325640 | tf_op jit(solution)/shard_map/ppermute | solution.py:575
  30.8 1.5 %collective-permute-done.6.rest_3_.rest_7_ = bf16[53,8,128]{2,1,0:T(8,128)(2,1)S(1)} collective-permute-done((bf16[53,8,128]{2,1,0:T(8,128)(2,1)}, bf16[53,8,128]{2,1,0:T(8,128)(2,1)S(1)}, u32[]{:S(2)}, u32[]{:S(2)}) %collective-permute-start.6) | collective-permute-done | bytes 108576 | tf_op jit(solution)/shard_map/ppermute | solution.py:575
  32.4 2.5 %collective-permute-done.7.rest_8_ = bf16[53,8,128]{2,1,0:T(8,128)(2,1)S(1)} collective-permute-done((bf16[53,8,128]{2,1,0:T(8,128)(2,1)}, bf16[53,8,128]{2,1,0:T(8,128)(2,1)S(1)}, u32[]{:S(2)}, u32[]{:S(2)}) %collective-permute-start.7) | collective-permute-done | bytes 108576 | tf_op jit(solution)/shard_map/ppermute | solution.py:575
  34.9 2.1 %collective-permute-start.14 = (bf16[48,8,128]{2,1,0:T(8,128)(2,1)}, bf16[48,8,128]{2,1,0:T(8,128)(2,1)S(1)}, u32[]{:S(2)}, u32[]{:S(2)}) collective-permute-start(bf16[48,8,128]{2,1,0:T(8,128)(2,1)} %get-tuple-element.47), channel_id=1, source_target_pairs={{0,13},{1,12},{2,15},{3,14},{4,9},{5,8},{6,11},{7,10},{8,5},{9,4},... | collective-permute-start | bytes 294920 | tf_op jit(solution)/shard_map/ppermute | solution.py:575
  37.0 1.8 %collective-permute-start.15 = (bf16[48,8,128]{2,1,0:T(8,128)(2,1)}, bf16[48,8,128]{2,1,0:T(8,128)(2,1)S(1)}, u32[]{:S(2)}, u32[]{:S(2)}) collective-permute-start(bf16[48,8,128]{2,1,0:T(8,128)(2,1)} %get-tuple-element.48), channel_id=1, source_target_pairs={{0,15},{1,14},{2,13},{3,12},{4,11},{5,10},{6,9},{7,8},{8,7},{9,6},... | collective-permute-start | bytes 294920 | tf_op jit(solution)/shard_map/ppermute | solution.py:575
  38.9 0.9 %copy-done = bf16[62,8,128]{2,1,0:T(8,128)(2,1)S(1)} copy-done((bf16[62,8,128]{2,1,0:T(8,128)(2,1)S(1)}, bf16[62,8,128]{2,1,0:T(8,128)(2,1)}, u32[]{:S(2)}) %copy-start) | copy-done | bytes 127000
  39.8 0.5 %make_ready.1 = (bf16[62,8,128]{2,1,0:T(8,128)(2,1)S(1)}, bf16[256,256]{1,0:T(8,128)(2,1)S(1)}, bf16[256,3072]{1,0:T(8,128)(2,1)S(1)}) custom-call(s32[1]{0:T(128)} %bitcast.me_s.turn_s, bf16[62,8,128]{2,1,0:T(8,128)(2,1)S(1)} %copy-done), custom_call_target="tpu_custom_call" | custom-call | tf_op jit(solution)/shard_map/make_ready/pallas_call | solution.py:556
  40.4 0.2 collective-permute-done.11.rest_12_
  40.5 1.9 %gains_and_sums.1 = (f32[128,3072]{1,0:T(8,128)S(1)}, f32[64,128]{1,0:T(8,128)S(1)}, s32[16,128]{1,0:T(8,128)S(1)}, f32[3,64,8,128]{3,2,1,0:T(8,128)S(1)}) custom-call(s32[1]{0:T(128)} %bitcast.me_s.turn_s, bf16[256,256]{1,0:T(8,128)(2,1)S(1)} %get-tuple-element.28.choice_ref, bf16[256,3072]{1,0:T(8,128)(2,1)S(1)} %get-tuple-element.29.basis_ref, ...), custom_call_target="tpu_custom_call" | custom-call | tf_op jit(solution)/shard_map/gains_and_sums/pallas_call | solution.py:600
  42.5 0.8 %sum_next.1.sums_ref = f32[3,64,8,128]{3,2,1,0:T(8,128)S(1)} custom-call(s32[16,128]{1,0:T(8,128)S(1)} %get-tuple-element.43.slots_ref, f32[3,64,8,128]{3,2,1,0:T(8,128)S(1)} %get-tuple-element.46.sums_ref, bf16[48,8,128]{2,1,0:T(8,128)(2,1)S(1)} %collective-permute-done.14.rows_ref), custom_call_target="tpu_custom_call" | custom-call | tf_op jit(solution)/shard_map/sum_next/pallas_call | solution.py:625
  43.2 1.6 %collective-permute-done.15.rest_0_ = bf16[48,8,128]{2,1,0:T(8,128)(2,1)S(1)} collective-permute-done((bf16[48,8,128]{2,1,0:T(8,128)(2,1)}, bf16[48,8,128]{2,1,0:T(8,128)(2,1)S(1)}, u32[]{:S(2)}, u32[]{:S(2)}) %collective-permute-start.15) | collective-permute-done | bytes 98336 | tf_op jit(solution)/shard_map/ppermute | solution.py:575
  44.8 1.9 %sum_and_apply.1 = bf16[64,8,384]{2,1,0:T(8,128)(2,1)} custom-call(s32[16,128]{1,0:T(8,128)S(1)} %get-tuple-element.43.slots_ref, f32[128,3072]{1,0:T(8,128)S(1)} %get-tuple-element.44.gains_ref, f32[64,128]{1,0:T(8,128)S(1)} %get-tuple-element.45.recip_ref, f32[3,64,8,128]{3,2,1,0:T(8,128)S(1)} %sum_next.1.sums_ref, ...), custom_call_target="tpu_custom_call" | custom-call | tf_op jit(solution)/shard_map/sum_and_apply/pallas_call | solution.py:636
  (17 shorter events, 0.3 us)
Async XLA Ops:
  1.8 12.2 %collective-permute-start.12 = (bf16[48,8,128]{2,1,0:T(8,128)(2,1)}, bf16[48,8,128]{2,1,0:T(8,128)(2,1)S(1)}, u32[]{:S(2)}, u32[]{:S(2)}) collective-permute-start(bf16[48,8,128]{2,1,0:T(8,128)(2,1)} %pack_first.1), channel_id=1, source_target_pairs={{0,9},{1,8},{2,11},{3,10},{4,13},{5,12},{6,15},{7,14},{8,1},{9,0},... | collective-permute-start | bytes 294920 | tf_op jit(solution)/shard_map/ppermute | solution.py:575
  8.4 11.8 %collective-permute-start = (bf16[53,8,128]{2,1,0:T(8,128)(2,1)}, bf16[53,8,128]{2,1,0:T(8,128)(2,1)S(1)}, u32[]{:S(2)}, u32[]{:S(2)}) collective-permute-start(bf16[53,8,128]{2,1,0:T(8,128)(2,1)} %get-tuple-element.31), channel_id=1, source_target_pairs={{0,8},{1,9},{2,10},{3,11},{4,12},{5,13},{6,14},{7,15},{8,0},{9,1},... | collective-permute-start | bytes 325640 | tf_op jit(solution)/shard_map/ppermute | solution.py:575
  9.0 14.4 %collective-permute-start.1 = (bf16[53,8,128]{2,1,0:T(8,128)(2,1)}, bf16[53,8,128]{2,1,0:T(8,128)(2,1)S(1)}, u32[]{:S(2)}, u32[]{:S(2)}) collective-permute-start(bf16[53,8,128]{2,1,0:T(8,128)(2,1)} %get-tuple-element.32), channel_id=1, source_target_pairs={{0,10},{1,11},{2,8},{3,9},{4,14},{5,15},{6,12},{7,13},{8,2},{9,3},... | collective-permute-start | bytes 325640 | tf_op jit(solution)/shard_map/ppermute | solution.py:575
  12.4 13.6 %collective-permute-start.2 = (bf16[53,8,128]{2,1,0:T(8,128)(2,1)}, bf16[53,8,128]{2,1,0:T(8,128)(2,1)S(1)}, u32[]{:S(2)}, u32[]{:S(2)}) collective-permute-start(bf16[53,8,128]{2,1,0:T(8,128)(2,1)} %get-tuple-element.33), channel_id=1, source_target_pairs={{0,4},{1,5},{2,6},{3,7},{4,0},{5,1},{6,2},{7,3},{8,12},{9,13},{10,... | collective-permute-start | bytes 325640 | tf_op jit(solution)/shard_map/ppermute | solution.py:575
  14.0 12.0 %collective-permute-start.3 = (bf16[53,8,128]{2,1,0:T(8,128)(2,1)}, bf16[53,8,128]{2,1,0:T(8,128)(2,1)S(1)}, u32[]{:S(2)}, u32[]{:S(2)}) collective-permute-start(bf16[53,8,128]{2,1,0:T(8,128)(2,1)} %get-tuple-element.34), channel_id=1, source_target_pairs={{0,5},{1,4},{2,7},{3,6},{4,1},{5,0},{6,3},{7,2},{8,13},{9,12},{10,... | collective-permute-start | bytes 325640 | tf_op jit(solution)/shard_map/ppermute | solution.py:575
  14.0 12.1 %collective-permute-start.4 = (bf16[53,8,128]{2,1,0:T(8,128)(2,1)}, bf16[53,8,128]{2,1,0:T(8,128)(2,1)S(1)}, u32[]{:S(2)}, u32[]{:S(2)}) collective-permute-start(bf16[53,8,128]{2,1,0:T(8,128)(2,1)} %get-tuple-element.35), channel_id=1, source_target_pairs={{0,12},{1,13},{2,14},{3,15},{4,8},{5,9},{6,10},{7,11},{8,4},{9,5},... | collective-permute-start | bytes 325640 | tf_op jit(solution)/shard_map/ppermute | solution.py:575
  20.2 8.7 %collective-permute-start.5 = (bf16[53,8,128]{2,1,0:T(8,128)(2,1)}, bf16[53,8,128]{2,1,0:T(8,128)(2,1)S(1)}, u32[]{:S(2)}, u32[]{:S(2)}) collective-permute-start(bf16[53,8,128]{2,1,0:T(8,128)(2,1)} %get-tuple-element.36), channel_id=1, source_target_pairs={{0,6},{1,7},{2,4},{3,5},{4,2},{5,3},{6,0},{7,1},{8,14},{9,15},{10,... | collective-permute-start | bytes 325640 | tf_op jit(solution)/shard_map/ppermute | solution.py:575
  23.5 8.9 %collective-permute-start.6 = (bf16[53,8,128]{2,1,0:T(8,128)(2,1)}, bf16[53,8,128]{2,1,0:T(8,128)(2,1)S(1)}, u32[]{:S(2)}, u32[]{:S(2)}) collective-permute-start(bf16[53,8,128]{2,1,0:T(8,128)(2,1)} %get-tuple-element.37), channel_id=1, source_target_pairs={{0,14},{1,15},{2,12},{3,13},{4,10},{5,11},{6,8},{7,9},{8,6},{9,7},... | collective-permute-start | bytes 325640 | tf_op jit(solution)/shard_map/ppermute | solution.py:575
  26.0 8.9 %collective-permute-start.7 = (bf16[53,8,128]{2,1,0:T(8,128)(2,1)}, bf16[53,8,128]{2,1,0:T(8,128)(2,1)S(1)}, u32[]{:S(2)}, u32[]{:S(2)}) collective-permute-start(bf16[53,8,128]{2,1,0:T(8,128)(2,1)} %get-tuple-element.38), channel_id=1, source_target_pairs={{0,7},{1,6},{2,5},{3,4},{4,3},{5,2},{6,1},{7,0},{8,15},{9,14},{10,... | collective-permute-start | bytes 325640 | tf_op jit(solution)/shard_map/ppermute | solution.py:575
  26.0 11.0 %collective-permute-start.8 = (bf16[53,8,128]{2,1,0:T(8,128)(2,1)}, bf16[53,8,128]{2,1,0:T(8,128)(2,1)S(1)}, u32[]{:S(2)}, u32[]{:S(2)}) collective-permute-start(bf16[53,8,128]{2,1,0:T(8,128)(2,1)} %get-tuple-element.39), channel_id=1, source_target_pairs={{0,1},{1,0},{2,3},{3,2},{4,5},{5,4},{6,7},{7,6},{8,9},{9,8},{10,11... | collective-permute-start | bytes 325640 | tf_op jit(solution)/shard_map/ppermute | solution.py:575
  26.1 12.7 %collective-permute-start.9 = (bf16[53,8,128]{2,1,0:T(8,128)(2,1)}, bf16[53,8,128]{2,1,0:T(8,128)(2,1)S(1)}, u32[]{:S(2)}, u32[]{:S(2)}) collective-permute-start(bf16[53,8,128]{2,1,0:T(8,128)(2,1)} %get-tuple-element.40), channel_id=1, source_target_pairs={{0,11},{1,10},{2,9},{3,8},{4,15},{5,14},{6,13},{7,12},{8,3},{9,2},... | collective-permute-start | bytes 325640 | tf_op jit(solution)/shard_map/ppermute | solution.py:575
  28.9 11.5 %collective-permute-start.10 = (bf16[53,8,128]{2,1,0:T(8,128)(2,1)}, bf16[53,8,128]{2,1,0:T(8,128)(2,1)S(1)}, u32[]{:S(2)}, u32[]{:S(2)}) collective-permute-start(bf16[53,8,128]{2,1,0:T(8,128)(2,1)} %get-tuple-element.41), channel_id=1, source_target_pairs={{0,2},{1,3},{2,0},{3,1},{4,6},{5,7},{6,4},{7,5},{8,10},{9,11},{10,... | collective-permute-start | bytes 325640 | tf_op jit(solution)/shard_map/ppermute | solution.py:575
  32.4 8.2 %collective-permute-start.11 = (bf16[53,8,128]{2,1,0:T(8,128)(2,1)}, bf16[53,8,128]{2,1,0:T(8,128)(2,1)S(1)}, u32[]{:S(2)}, u32[]{:S(2)}) collective-permute-start(bf16[53,8,128]{2,1,0:T(8,128)(2,1)} %get-tuple-element.42), channel_id=1, source_target_pairs={{0,3},{1,2},{2,1},{3,0},{4,7},{5,6},{6,5},{7,4},{8,11},{9,10},{10,... | collective-permute-start | bytes 325640 | tf_op jit(solution)/shard_map/ppermute | solution.py:575
  34.9 7.6 %collective-permute-start.14 = (bf16[48,8,128]{2,1,0:T(8,128)(2,1)}, bf16[48,8,128]{2,1,0:T(8,128)(2,1)S(1)}, u32[]{:S(2)}, u32[]{:S(2)}) collective-permute-start(bf16[48,8,128]{2,1,0:T(8,128)(2,1)} %get-tuple-element.47), channel_id=1, source_target_pairs={{0,13},{1,12},{2,15},{3,14},{4,9},{5,8},{6,11},{7,10},{8,5},{9,4},... | collective-permute-start | bytes 294920 | tf_op jit(solution)/shard_map/ppermute | solution.py:575
  37.0 7.8 %collective-permute-start.15 = (bf16[48,8,128]{2,1,0:T(8,128)(2,1)}, bf16[48,8,128]{2,1,0:T(8,128)(2,1)S(1)}, u32[]{:S(2)}, u32[]{:S(2)}) collective-permute-start(bf16[48,8,128]{2,1,0:T(8,128)(2,1)} %get-tuple-element.48), channel_id=1, source_target_pairs={{0,15},{1,14},{2,13},{3,12},{4,11},{5,10},{6,9},{7,8},{8,7},{9,6},... | collective-permute-start | bytes 294920 | tf_op jit(solution)/shard_map/ppermute | solution.py:575
  38.8 1.7 %collective-permute-start.13 = (bf16[20,8,128]{2,1,0:T(8,128)(2,1)S(1)}, bf16[20,8,128]{2,1,0:T(8,128)(2,1)S(1)}, u32[]{:S(2)}, u32[]{:S(2)}) collective-permute-start(bf16[20,8,128]{2,1,0:T(8,128)(2,1)S(1)} %collect_gains.1), channel_id=1, source_target_pairs={{0,1},{1,0},{2,3},{3,2},{4,5},{5,4},{6,7},{7,6},{8,9},{9,8},{10,11... | collective-permute-start | bytes 122888 | tf_op jit(solution)/shard_map/ppermute | solution.py:575
  38.9 0.9 %copy-start = (bf16[62,8,128]{2,1,0:T(8,128)(2,1)S(1)}, bf16[62,8,128]{2,1,0:T(8,128)(2,1)}, u32[]{:S(2)}) copy-start(bf16[62,8,128]{2,1,0:T(8,128)(2,1)} %get-tuple-element.27.own_ref) | copy-start | bytes 380932
